TPU v7x, 32 devices: a whole 2x2x4 slice. The times are simulated.
32 devices in a mesh: dp: 8 (over y, x, core), fsdp: 4 (over z).
Axes of the slice: x: 2, y: 2, z: 4, core: 2. Of those that a mesh axis runs over, the one named last changes fastest.
Arguments:
- tokens: bfloat16 [4096, 2048], P(('dp', 'fsdp')), may hold values from -6 to 6
- counts: int32 [8, 4], replicated, may hold values from 64 to 128, as said below
- lengths: int32 [8, 3], replicated, may hold values from 1 to 510, as said below
- gain: bfloat16 [2048], P(('dp', 'fsdp')), may hold values from 0.5 to 1.5
- in_weight: bfloat16 [2048, 8192], P(('dp', 'fsdp')), may hold values from -0.125 to 0.125
- conv_weight: bfloat16 [4, 4096], P(None, ('dp', 'fsdp')), may hold values from -3 to 3
- conv_bias: bfloat16 [4096], P(('dp', 'fsdp')), may hold values from -3 to 3
- x_weight: bfloat16 [4096, 160], P(('dp', 'fsdp')), may hold values from -0.09375 to 0.09375
- dt_weight: bfloat16 [128, 4096], P(None, ('dp', 'fsdp')), may hold values from -0.5 to 0.5
- dt_bias: bfloat16 [4096], P(('dp', 'fsdp')), may hold values from -6.875 to -2.296875
- a_log: bfloat16 [4096, 16], P(('dp', 'fsdp')), may hold values from -4.59375 to 2.796875
- skip: bfloat16 [4096], P(('dp', 'fsdp')), may hold values from 0.5 to 1.5
- out_weight: bfloat16 [4096, 2048], P(('dp', 'fsdp')), may hold values from -0.09375 to 0.09375
- cotangent: bfloat16 [4096, 2048], P(('dp', 'fsdp')), may hold values from -6 to 6
Outputs:
- output: bfloat16 [4096, 2048], P(('dp', 'fsdp'))
- token_grad: float32 [4096, 2048], P(('dp', 'fsdp'))
- gain_grad: float32 [2048], P(('dp', 'fsdp'))
- in_weight_grad: float32 [2048, 8192], P(('dp', 'fsdp'))
- conv_weight_grad: float32 [4, 4096], P(None, ('dp', 'fsdp'))
- conv_bias_grad: float32 [4096], P(('dp', 'fsdp'))
- x_weight_grad: float32 [4096, 160], P(('dp', 'fsdp'))
- dt_weight_grad: float32 [128, 4096], P(None, ('dp', 'fsdp'))
- dt_bias_grad: float32 [4096], P(('dp', 'fsdp'))
- a_log_grad: float32 [4096, 16], P(('dp', 'fsdp'))
- skip_grad: float32 [4096], P(('dp', 'fsdp'))
- out_weight_grad: float32 [4096, 2048], P(('dp', 'fsdp'))
Inputs may be any that keep to these rules, and one draw needn't show every extreme that they name: `counts`: valid slots of a device; in every group some device holds all 128. `lengths`: they sum to the group's valid tokens. The first document ends on the group's first device and the last begins on its last device, so the middle one runs from the first device to the last; the first and last hold at most a quarter of their device's valid tokens. In one group every slot is valid and the first and last documents have one token each.
All inputs are finite; a program needn't handle non-finite values.
Results may differ from a plain program's by a relative error of at most 0.0076.
Values may be sent and summed in bfloat16 or wider, within the bound.
No kernel may reach another device: no remote copies, remote signals or barrier semaphores. Data moves between devices by JAX's collectives and lax.ppermute only.
A program may use at most 320 MiB of HBM per device.

v0:
```python
import jax
import jax.numpy as jnp
from jax import lax
from jax.sharding import PartitionSpec as P

SPAN = 32


EPS = 1e-05


def shifted(value, axis, steps):
    count = lax.axis_size(axis)
    first, last = (max(0, -steps), min(count, count - steps))
    return lax.ppermute(value, axis, [(source, source + steps) for source in range(first, last)])


def entering_2(shard, axis, combine, identity, reverse):
    size, position = (lax.axis_size(axis), lax.axis_index(axis))
    everything = jax.tree.map(
        lambda part, kind: lax.all_gather(part.astype(kind), axis),
        shard,
        (jnp.bfloat16, jnp.bfloat16),
    )
    start = jax.tree.map(
        lambda part, zero: jnp.broadcast_to(jnp.asarray(zero, part.dtype), part.shape),
        shard,
        identity,
    )

    def hop(k, before):
        at = size - 1 - k if reverse else k
        reached = at > position if reverse else at < position
        new = combine(
            before, jax.tree.map(lambda part, own: part[at].astype(own.dtype), everything, shard)
        )
        return jax.tree.map(lambda a, b: jnp.where(reached, a, b), new, before)

    return lax.fori_loop(0, size, hop, start)


def chain(earlier, later):
    return (earlier[0] * later[0], later[0] * earlier[1] + later[1])


def contract_rows(left, right):
    return lax.dot_general(
        left, right, (((0,), (0,)), ((), ())), preferred_element_type=jnp.float32
    )


def contract_cols(left, right):
    return lax.dot_general(
        left, right, (((1,), (1,)), ((), ())), preferred_element_type=jnp.float32
    )


def decays(step_dt, decay_rates, step_keep, step_valid):
    expo = jnp.exp(step_dt[:, None, :] * decay_rates[None])
    return (expo, step_keep[:, None, None] * expo + (1.0 - step_valid)[:, None, None])


def sources(step_dt, step_u, step_b, step_valid):
    return (step_valid[:, None] * step_dt * step_u)[:, None, :] * step_b[:, :, None]


def per_device(
    tokens,
    counts,
    lengths,
    gain,
    in_weight,
    conv_weight,
    conv_bias,
    x_weight,
    dt_weight,
    dt_bias,
    a_log,
    skip,
    out_weight,
    cotangent,
):
    slot_count = tokens.shape[0]
    group_pos = lax.axis_index("dp")
    place = lax.axis_index("fsdp")
    count_row = lax.dynamic_index_in_dim(counts, group_pos, 0, keepdims=False)
    length_row = lax.dynamic_index_in_dim(lengths, group_pos, 0, keepdims=False)
    held = lax.dynamic_index_in_dim(count_row, place, 0, keepdims=False)
    offset = jnp.sum(
        jnp.where(jnp.arange(count_row.shape[0], dtype=jnp.int32) < place, count_row, 0)
    )
    local = jnp.arange(slot_count, dtype=jnp.int32)
    position = offset + local
    second = length_row[0]
    third = length_row[0] + length_row[1]
    begin = jnp.where(position >= third, third, jnp.where(position >= second, second, 0))
    valid = (local < held).astype(jnp.float32)
    keep = valid * (position != begin).astype(jnp.float32)
    weights = (
        lax.all_gather(gain, ("dp", "fsdp"), axis=0, tiled=True),
        lax.all_gather(in_weight, ("dp", "fsdp"), axis=0, tiled=True),
        lax.all_gather(conv_weight, ("dp", "fsdp"), axis=1, tiled=True),
        lax.all_gather(conv_bias, ("dp", "fsdp"), axis=0, tiled=True),
        lax.all_gather(x_weight, ("dp", "fsdp"), axis=0, tiled=True),
        lax.all_gather(dt_weight, ("dp", "fsdp"), axis=1, tiled=True),
        lax.all_gather(dt_bias, ("dp", "fsdp"), axis=0, tiled=True),
        lax.all_gather(a_log, ("dp", "fsdp"), axis=0, tiled=True),
        lax.all_gather(skip, ("dp", "fsdp"), axis=0, tiled=True),
        lax.all_gather(out_weight, ("dp", "fsdp"), axis=0, tiled=True),
    )
    (
        full_gain,
        full_in,
        full_conv,
        full_conv_bias,
        full_x,
        full_dt,
        full_dt_bias,
        full_a_log,
        full_skip,
        full_out,
    ) = weights
    inner_width = full_skip.shape[0]
    rank_width = full_dt.shape[0]
    state_width = full_a_log.shape[1]
    taps = full_conv.shape[0]
    gain_value = full_gain.astype(jnp.float32)
    conv_taps = full_conv.astype(jnp.float32)
    skip_value = full_skip.astype(jnp.float32)
    decay_rates = -jnp.exp(full_a_log.astype(jnp.float32)).T
    inputs_f = tokens.astype(jnp.float32)
    scale = lax.rsqrt(jnp.mean(inputs_f * inputs_f, axis=1, keepdims=True) + EPS)
    unit = inputs_f * scale
    normed = (unit * gain_value).astype(jnp.bfloat16)
    mixed = jnp.dot(normed, full_in, preferred_element_type=jnp.float32)
    inner = mixed[:, :inner_width]
    gate = mixed[:, inner_width:]
    rim_rows = lax.dynamic_slice_in_dim(inner, held - (taps - 1), taps - 1, 0)
    before = shifted(rim_rows.astype(jnp.bfloat16), "fsdp", 1).astype(rim_rows.dtype)
    extended = jnp.concatenate([before, inner], axis=0)
    conv_out = full_conv_bias.astype(jnp.float32)[None, :] + jnp.zeros_like(inner)
    masks = []
    for lag_step in range(taps):
        tapped = lax.slice_in_dim(
            extended, taps - 1 - lag_step, taps - 1 - lag_step + slot_count, axis=0
        )
        allowed = (position - lag_step >= begin).astype(jnp.float32)
        masks.append(allowed)
        conv_out = conv_out + conv_taps[taps - 1 - lag_step][None, :] * tapped * allowed[:, None]
    conv_sig = jax.nn.sigmoid(conv_out)
    activ_low = (conv_out * conv_sig).astype(jnp.bfloat16)
    activ = activ_low.astype(jnp.float32)
    projected = jnp.dot(activ_low, full_x, preferred_element_type=jnp.float32)
    rank_low = projected[:, :rank_width].astype(jnp.bfloat16)
    b_input = projected[:, rank_width : rank_width + state_width]
    c_output = projected[:, rank_width + state_width :]
    pre_step = jnp.dot(rank_low, full_dt, preferred_element_type=jnp.float32) + full_dt_bias.astype(
        jnp.float32
    )
    step_dt = jax.nn.softplus(pre_step)
    span_count = slot_count // SPAN

    def split(value):
        return value.reshape((span_count, SPAN) + value.shape[1:])

    pieces = (
        split(step_dt),
        split(activ),
        split(b_input),
        split(c_output),
        split(keep),
        split(valid),
    )
    ones_state = jnp.ones((state_width, inner_width), jnp.float32)
    zero_state = jnp.zeros((state_width, inner_width), jnp.float32)

    def total_step(running, inputs):
        span_dt, span_u, span_b, span_c, span_keep, span_valid = inputs
        expo, decay = decays(span_dt, decay_rates, span_keep, span_valid)
        cumulative = lax.associative_scan(
            chain, (decay, sources(span_dt, span_u, span_b, span_valid)), axis=0
        )
        return (chain(running, (cumulative[0][-1], cumulative[1][-1])), None)

    (whole_decay, whole_state), _ = lax.scan(total_step, (ones_state, zero_state), pieces)
    _, entering = entering_2(
        (whole_decay, whole_state), "fsdp", chain, (ones_state, zero_state), False
    )

    def state_step(state, inputs):
        span_dt, span_u, span_b, span_c, span_keep, span_valid = inputs
        expo, decay = decays(span_dt, decay_rates, span_keep, span_valid)
        cumulative = lax.associative_scan(
            chain, (decay, sources(span_dt, span_u, span_b, span_valid)), axis=0
        )
        states = cumulative[0] * state[None] + cumulative[1]
        return (states[-1], (state, jnp.sum(states * span_c[:, :, None], axis=1)))

    _, (span_starts, scanned) = lax.scan(state_step, entering, pieces)
    scan_out = scanned.reshape(slot_count, inner_width) + skip_value[None, :] * activ
    gate_sig = jax.nn.sigmoid(gate)
    gate_act = gate * gate_sig
    gated = (scan_out * gate_act).astype(jnp.bfloat16)
    branch = jnp.dot(gated, full_out, preferred_element_type=jnp.float32)
    output = (inputs_f + valid[:, None] * branch).astype(jnp.bfloat16)
    weights = (
        lax.all_gather(gain, ("dp", "fsdp"), axis=0, tiled=True),
        lax.all_gather(in_weight, ("dp", "fsdp"), axis=0, tiled=True),
        lax.all_gather(conv_weight, ("dp", "fsdp"), axis=1, tiled=True),
        lax.all_gather(conv_bias, ("dp", "fsdp"), axis=0, tiled=True),
        lax.all_gather(x_weight, ("dp", "fsdp"), axis=0, tiled=True),
        lax.all_gather(dt_weight, ("dp", "fsdp"), axis=1, tiled=True),
        lax.all_gather(dt_bias, ("dp", "fsdp"), axis=0, tiled=True),
        lax.all_gather(a_log, ("dp", "fsdp"), axis=0, tiled=True),
        lax.all_gather(skip, ("dp", "fsdp"), axis=0, tiled=True),
        lax.all_gather(out_weight, ("dp", "fsdp"), axis=0, tiled=True),
    )
    (
        full_gain,
        full_in,
        full_conv,
        full_conv_bias,
        full_x,
        full_dt,
        full_dt_bias,
        full_a_log,
        full_skip,
        full_out,
    ) = weights
    cot_f = cotangent.astype(jnp.float32)
    masked = (cot_f * valid[:, None]).astype(jnp.bfloat16)
    out_weight_grad = contract_rows(gated, masked)
    grad_gated = contract_cols(masked, full_out)
    grad_scan = grad_gated * gate_act
    grad_gate = grad_gated * scan_out * gate_sig * (1.0 + gate * (1.0 - gate_sig))
    skip_grad = jnp.sum(grad_scan * activ, axis=0)
    grad_activ = grad_scan * skip_value[None, :]
    grad_pieces = split(grad_scan)

    def back_total(running, inputs):
        (span_dt, span_u, span_b, span_c, span_keep, span_valid), span_dy = inputs
        expo, decay = decays(span_dt, decay_rates, span_keep, span_valid)
        source = span_dy[:, None, :] * span_c[:, :, None]
        source = source.at[-1].add(running)
        ahead = jnp.concatenate([decay[1:], jnp.ones_like(decay[:1])], axis=0)
        adjoint = lax.associative_scan(chain, (ahead, source), reverse=True, axis=0)[1]
        return (decay[0] * adjoint[0], None)

    tail_value, _ = lax.scan(back_total, zero_state, (pieces, grad_pieces), reverse=True)
    _, arriving = entering_2(
        (whole_decay, tail_value), "fsdp", chain, (ones_state, zero_state), True
    )

    def back_step(running, inputs):
        incoming, rate_sum = running
        (span_dt, span_u, span_b, span_c, span_keep, span_valid), span_dy, state = inputs
        expo, decay = decays(span_dt, decay_rates, span_keep, span_valid)
        cumulative = lax.associative_scan(
            chain, (decay, sources(span_dt, span_u, span_b, span_valid)), axis=0
        )
        states = cumulative[0] * state[None] + cumulative[1]
        prior = jnp.concatenate([state[None], states[:-1]], axis=0)
        source = span_dy[:, None, :] * span_c[:, :, None]
        source = source.at[-1].add(incoming)
        ahead = jnp.concatenate([decay[1:], jnp.ones_like(decay[:1])], axis=0)
        adjoint = lax.associative_scan(chain, (ahead, source), reverse=True, axis=0)[1]
        through = adjoint * prior * span_keep[:, None, None] * expo
        driven = span_valid[:, None] * span_dt * span_u
        along_b = jnp.sum(adjoint * span_b[:, :, None], axis=1)
        grad_dt = (
            jnp.sum(through * decay_rates[None], axis=1) + span_valid[:, None] * span_u * along_b
        )
        grad_u = span_valid[:, None] * span_dt * along_b
        grad_b = jnp.sum(adjoint * driven[:, None, :], axis=2)
        grad_c = jnp.sum(states * span_dy[:, None, :], axis=2)
        rate_sum = rate_sum + jnp.sum(through * span_dt[:, None, :], axis=0)
        return ((decay[0] * adjoint[0], rate_sum), (grad_dt, grad_u, grad_b, grad_c))

    (_, rate_sum), (span_grad_dt, span_grad_u, span_grad_b, span_grad_c) = lax.scan(
        back_step, (arriving, zero_state), (pieces, grad_pieces, span_starts), reverse=True
    )
    a_log_grad = (rate_sum * decay_rates).T
    grad_activ = grad_activ + span_grad_u.reshape(slot_count, inner_width)
    grad_pre = span_grad_dt.reshape(slot_count, inner_width) * jax.nn.sigmoid(pre_step)
    dt_bias_grad = jnp.sum(grad_pre, axis=0)
    grad_pre_low = grad_pre.astype(jnp.bfloat16)
    dt_weight_grad = contract_rows(rank_low, grad_pre_low)
    grad_rank = contract_cols(grad_pre_low, full_dt)
    grad_projected = jnp.concatenate(
        [
            grad_rank,
            span_grad_b.reshape(slot_count, state_width),
            span_grad_c.reshape(slot_count, state_width),
        ],
        axis=1,
    ).astype(jnp.bfloat16)
    x_weight_grad = contract_rows(activ_low, grad_projected)
    grad_activ = grad_activ + contract_cols(grad_projected, full_x)
    grad_conv = grad_activ * conv_sig * (1.0 + conv_out * (1.0 - conv_sig))
    conv_bias_grad = jnp.sum(grad_conv, axis=0)
    conv_taps = full_conv.astype(jnp.float32)
    tap_grads = [None] * taps
    grad_extended = jnp.zeros_like(extended)
    for lag_step in range(taps):
        tapped = lax.slice_in_dim(
            extended, taps - 1 - lag_step, taps - 1 - lag_step + slot_count, axis=0
        )
        weighted = grad_conv * masks[lag_step][:, None]
        tap_grads[taps - 1 - lag_step] = jnp.sum(weighted * tapped, axis=0)
        grad_extended = grad_extended + jnp.pad(
            conv_taps[taps - 1 - lag_step][None, :] * weighted,
            ((taps - 1 - lag_step, lag_step), (0, 0)),
        )
    conv_weight_grad = jnp.stack(tap_grads, axis=0)
    returned = shifted(grad_extended[: taps - 1].astype(jnp.bfloat16), "fsdp", -1).astype(
        jnp.float32
    )
    grad_inner = grad_extended[taps - 1 :]
    rim_start = held - (taps - 1)
    grad_inner = lax.dynamic_update_slice_in_dim(
        grad_inner,
        lax.dynamic_slice_in_dim(grad_inner, rim_start, taps - 1, 0) + returned,
        rim_start,
        0,
    )
    grad_mixed = jnp.concatenate([grad_inner, grad_gate], axis=1).astype(jnp.bfloat16)
    in_weight_grad = contract_rows(normed, grad_mixed)
    grad_normed = contract_cols(grad_mixed, full_in)
    gain_grad = jnp.sum(grad_normed * unit, axis=0)
    grad_unit = grad_normed * full_gain.astype(jnp.float32)[None, :]
    token_grad = cot_f + scale * (
        grad_unit - unit * jnp.mean(grad_unit * unit, axis=1, keepdims=True)
    )
    owned = (
        lax.psum_scatter(gain_grad, ("dp", "fsdp"), scatter_dimension=0, tiled=True),
        lax.psum_scatter(in_weight_grad, ("dp", "fsdp"), scatter_dimension=0, tiled=True),
        lax.psum_scatter(conv_weight_grad, ("dp", "fsdp"), scatter_dimension=1, tiled=True),
        lax.psum_scatter(conv_bias_grad, ("dp", "fsdp"), scatter_dimension=0, tiled=True),
        lax.psum_scatter(x_weight_grad, ("dp", "fsdp"), scatter_dimension=0, tiled=True),
        lax.psum_scatter(dt_weight_grad, ("dp", "fsdp"), scatter_dimension=1, tiled=True),
        lax.psum_scatter(dt_bias_grad, ("dp", "fsdp"), scatter_dimension=0, tiled=True),
        lax.psum_scatter(a_log_grad, ("dp", "fsdp"), scatter_dimension=0, tiled=True),
        lax.psum_scatter(skip_grad, ("dp", "fsdp"), scatter_dimension=0, tiled=True),
        lax.psum_scatter(out_weight_grad, ("dp", "fsdp"), scatter_dimension=0, tiled=True),
    )
    return (
        output,
        token_grad,
        owned[0],
        owned[1],
        owned[2],
        owned[3],
        owned[4],
        owned[5],
        owned[6],
        owned[7],
        owned[8],
        owned[9],
    )


def solution(mesh):
    return jax.shard_map(
        per_device,
        mesh=mesh,
        in_specs=(
            P(("dp", "fsdp"), None),
            P(),
            P(),
            P(("dp", "fsdp")),
            P(("dp", "fsdp"), None),
            P(None, ("dp", "fsdp")),
            P(("dp", "fsdp")),
            P(("dp", "fsdp"), None),
            P(None, ("dp", "fsdp")),
            P(("dp", "fsdp")),
            P(("dp", "fsdp"), None),
            P(("dp", "fsdp")),
            P(("dp", "fsdp"), None),
            P(("dp", "fsdp"), None),
        ),
        out_specs=(
            P(("dp", "fsdp"), None),
            P(("dp", "fsdp"), None),
            P(("dp", "fsdp")),
            P(("dp", "fsdp"), None),
            P(None, ("dp", "fsdp")),
            P(("dp", "fsdp")),
            P(("dp", "fsdp"), None),
            P(None, ("dp", "fsdp")),
            P(("dp", "fsdp")),
            P(("dp", "fsdp"), None),
            P(("dp", "fsdp")),
            P(("dp", "fsdp"), None),
        ),
        check_vma=False,
    )
```

profile of v0, /device:TPU:0, one launch (start us, length us, event | category | flops | bytes accessed | tf_op | source)
XLA Modules:
  0.0 6223.9 jit_solution(12451649872803818596)
XLA Ops:
  22.9 43.3 all-reduce.86
  66.3 66.9 %all_gather.57 = bf16[4,4096]{1,0:T(4,128)(2,1)S(1)} all-gather(bf16[4,128]{1,0:T(4,128)(2,1)S(1)} %copy-done.164), channel_id=1, replica_groups=mesh['dp'=8,'fsdp'=4] {'dp','fsdp'}, dimensions={1}, use_global_device_ids=true | all-gather | bytes 33792 | tf_op jit(solution)/shard_map/all_gather | solution.py:102
  133.3 66.7 %all_gather.63 = bf16[4096,16]{0,1:T(8,128)(2,1)S(1)} all-gather(bf16[128,16]{0,1:T(8,128)(2,1)S(1)} %copy-done.151), channel_id=1, replica_groups=mesh['dp'=8,'fsdp'=4] {'dp','fsdp'}, dimensions={0}, use_global_device_ids=true | all-gather | bytes 135168 | tf_op jit(solution)/shard_map/all_gather | solution.py:107
  230.2 66.0 %all-gather.3 = bf16[32,1,128]{2,1,0:T(2,128)(2,1)S(1)} all-gather(bf16[1,1,128]{2,1,0:T(2,128)(2,1)S(1)} %bitcast.266), channel_id=1, replica_groups=mesh['dp'=8,'fsdp'=4] {'dp','fsdp'}, dimensions={0}, use_global_device_ids=true | all-gather | bytes 8448 | tf_op jit(solution)/shard_map/all_gather | solution.py:103
  296.2 63.3 %all-gather.4 = bf16[32,1,128]{2,1,0:T(2,128)(2,1)S(1)} all-gather(bf16[1,1,128]{2,1,0:T(2,128)(2,1)S(1)} %bitcast.267), channel_id=1, replica_groups=mesh['dp'=8,'fsdp'=4] {'dp','fsdp'}, dimensions={0}, use_global_device_ids=true | all-gather | bytes 8448 | tf_op jit(solution)/shard_map/all_gather | solution.py:106
  359.6 65.3 %all-gather.5 = bf16[32,1,128]{2,1,0:T(2,128)(2,1)S(1)} all-gather(bf16[1,1,128]{2,1,0:T(2,128)(2,1)S(1)} %bitcast.268), channel_id=1, replica_groups=mesh['dp'=8,'fsdp'=4] {'dp','fsdp'}, dimensions={0}, use_global_device_ids=true | all-gather | bytes 8448 | tf_op jit(solution)/shard_map/all_gather | solution.py:108
  425.7 15.2 multiply_reduce_fusion.6
  450.5 547.2 %while.100 = (s32[]{:T(128)}, f32[16,4096]{1,0:T(8,128)}, f32[16,4096]{1,0:T(8,128)}, f32[4,32]{1,0:T(4,128)S(1)}, f32[4,32,4096]{2,1,0:T(8,128)}, /*index=5*/f3...) while((s32[]{:T(128)}, f32[16,4096]{1,0:T(8,128)}, ...), condition=%wide.region_3.4_spmd.clone, body=%wide.region_2.3_spmd.clone.sunk | while | flops 24641572 | bytes 320085728 | solution.py:185
  1000.0 363.2 %while.99 = (s32[]{:T(128)}, f32[16,4096]{1,0:T(8,128)}, f32[4,32]{1,0:T(4,128)S(1)}, f32[4,32,4096]{2,1,0:T(8,128)}, f32[16,4096]{1,0:T(8,128)S(1)}, /*index=5*...) while((s32[]{:T(128)}, f32[16,4096]{1,0:T(8,128)}, ...), condition=%wide.region_10.11_spmd, body=%wide.region_9.10_spmd.sunk | while | flops 19595300 | bytes 287317152 | solution.py:249
  1365.2 16.4 all-gather
  1381.6 16.0 all-gather.2
  1398.4 14.9 all-gather.1
  1420.8 768.9 %while.98 = (s32[]{:T(128)}, f32[16,4096]{1,0:T(8,128)}, f32[4,16,4096]{2,1,0:T(8,128)}, f32[4,32,4096]{2,1,0:T(8,128)}, f32[4,32]{1,0:T(4,128)S(1)}, /*index=5*...) while((s32[]{:T(128)}, f32[16,4096]{1,0:T(8,128)}, ...), condition=%wide.region_8.9_spmd, body=%wide.region_6.8_spmd.sunk | while | flops 43581472 | bytes 559961984 | solution.py:199
  1598.0 13.8 multiply_reduce_fusion.14
  1790.1 13.8 multiply_reduce_fusion.14
  2194.0 1328.4 %while.103 = (s32[]{:T(128)}, f32[16,4096]{1,0:T(8,128)S(1)}, f32[16,4096]{1,0:T(8,128)}, f32[4,32,4096]{2,1,0:T(8,128)}, f32[4,32,4096]{2,1,0:T(8,128)}, /*inde...) while((s32[]{:T(128)}, f32[16,4096]{1,0:T(8,128)S(1)}, ...), condition=%wide.region_19.20_spmd.clone, body=%wide.region_13.19_spmd.clone.sunk | while | flops 90831904 | bytes 981514496 | solution.py:279
  3574.8 24.5 fusion.67
  3609.7 17.7 fusion.74
  3627.4 38.6 all-reduce.91
  3679.6 132.6 %reduce-scatter.15.cloned.1.call-done = f32[128,16]{0,1:T(8,128)} async-done(((f32[4096,16]{0,1:T(8,128)}), f32[128,16]{0,1:T(8,128)}) %reduce-scatter.15.cloned.1.call-update) | async-done | bytes 8208 | tf_op jit(solution)/shard_map/reduce_scatter | solution.py:342
  3812.1 137.4 %reduce-scatter.13.cloned.1.call-done = f32[128,128]{1,0:T(8,128)} async-done(((f32[128,4096]{1,0:T(8,128)}), f32[128,128]{1,0:T(8,128)}) %reduce-scatter.13.cloned.1.call-update) | async-done | bytes 65552 | tf_op jit(solution)/shard_map/reduce_scatter | solution.py:340
  3949.5 141.4 %reduce-scatter.11.cloned.1.call-done = f32[128,160]{0,1:T(8,128)} async-done(((f32[4096,160]{0,1:T(8,128)}), f32[128,160]{0,1:T(8,128)}) %reduce-scatter.11.cloned.1.call-update) | async-done | bytes 81936 | tf_op jit(solution)/shard_map/reduce_scatter | solution.py:339
  4090.9 713.0 %reduce-scatter.17.cloned.1.call-done = f32[128,2048]{1,0:T(8,128)} async-done(((f32[4096,2048]{1,0:T(8,128)}), f32[128,2048]{1,0:T(8,128)}) %reduce-scatter.17.cloned.1.call-update) | async-done | bytes 1048592 | tf_op jit(solution)/shard_map/reduce_scatter | solution.py:344
  4803.9 1412.9 %reduce-scatter.9.cloned.1.call-done = f32[64,8192]{1,0:T(8,128)} async-done(((f32[2048,8192]{1,0:T(8,128)}), f32[64,8192]{1,0:T(8,128)}) %reduce-scatter.9.cloned.1.call-update) | async-done | bytes 2097168 | tf_op jit(solution)/shard_map/reduce_scatter | solution.py:336
  (2011 shorter events, 3101.9 us)
Async XLA Ops:
  7.2 203.7 %copy-start.90 = (bf16[128,2048]{1,0:T(8,128)(2,1)S(1)}, bf16[128,2048]{1,0:T(8,128)(2,1)}, u32[]{:S(2)}) copy-start(bf16[128,2048]{1,0:T(8,128)(2,1)} %param.30) | copy-start | bytes 1572868
  7.2 203.7 %all-gather.11.cloned.1.call-start = ((), (), s32[]{:S(2)}) async-start(), calls=%async_computation.6 | async-start | bytes 34603008 | tf_op jit(solution)/shard_map/all_gather | solution.py:101
  8.0 417.6 %all-gather.17.cloned.1.call-start = ((), (), s32[]{:S(2)}) async-start(), calls=%async_computation.9 | async-start | bytes 17301504 | tf_op jit(solution)/shard_map/all_gather | solution.py:109
  8.7 432.2 %all-gather.13.cloned.1.call-start = ((), (), s32[]{:S(2)}) async-start(), calls=%async_computation.7 | async-start | bytes 1351680 | tf_op jit(solution)/shard_map/all_gather | solution.py:104
  9.5 436.2 %all-gather.15.cloned.1.call-start = ((), (), s32[]{:S(2)}) async-start(), calls=%async_computation.8 | async-start | bytes 1081344 | tf_op jit(solution)/shard_map/all_gather | solution.py:105
  10.0 3668.1 %reduce-scatter.19.cloned.1.call-start = ((), (), s32[]{:S(2)}) async-start(), calls=%async_computation.15 | async-start | bytes 2162688
  14.8 410.8 %copy-start.154 = (f32[128]{0:T(128)}, f32[128]{0:T(128)S(1)}, u32[]{:S(2)}) copy-start(f32[128]{0:T(128)S(1)} %get-tuple-element.1392) | copy-start | bytes 1540
  14.8 410.8 %copy-start.156 = (f32[128]{0:T(128)}, f32[128]{0:T(128)S(1)}, u32[]{:S(2)}) copy-start(f32[128]{0:T(128)S(1)} %get-tuple-element.1393) | copy-start | bytes 1540
  16.1 409.5 %copy-start.158 = (f32[128]{0:T(128)}, f32[128]{0:T(128)S(1)}, u32[]{:S(2)}) copy-start(f32[128]{0:T(128)S(1)} %get-tuple-element.1394) | copy-start | bytes 1540
  16.1 409.5 %copy-start.161 = (f32[128]{0:T(128)}, f32[128]{0:T(128)S(1)}, u32[]{:S(2)}) copy-start(f32[128]{0:T(128)S(1)} %get-tuple-element.1395) | copy-start | bytes 1540
  22.7 201.5 %copy-start.145 = (f32[128]{0:T(128)}, f32[128]{0:T(128)S(1)}, u32[]{:S(2)}) copy-start(f32[128]{0:T(128)S(1)} %add_rsqrt_fusion) | copy-start | bytes 1540
  133.3 292.4 %copy-start.133 = (f32[1,4096]{1,0:T(1,128)}, f32[1,4096]{1,0:T(1,128)S(1)}, u32[]{:S(2)}) copy-start(f32[1,4096]{1,0:T(1,128)S(1)} %get-tuple-element.1381) | copy-start | bytes 49156
  133.3 292.4 %copy-start.135 = (f32[1,4096]{1,0:T(1,128)}, f32[1,4096]{1,0:T(1,128)S(1)}, u32[]{:S(2)}) copy-start(f32[1,4096]{1,0:T(1,128)S(1)} %get-tuple-element.1382) | copy-start | bytes 49156
  133.3 292.4 %copy-start.137 = (f32[1,4096]{1,0:T(1,128)}, f32[1,4096]{1,0:T(1,128)S(1)}, u32[]{:S(2)}) copy-start(f32[1,4096]{1,0:T(1,128)S(1)} %get-tuple-element.1383) | copy-start | bytes 49156
  133.3 292.4 %copy-start.139 = (f32[1,4096]{1,0:T(1,128)}, f32[1,4096]{1,0:T(1,128)S(1)}, u32[]{:S(2)}) copy-start(f32[1,4096]{1,0:T(1,128)S(1)} %get-tuple-element.1384) | copy-start | bytes 49156
  227.6 198.0 %collective-permute-start = (bf16[3,4096]{1,0:T(4,128)(2,1)S(1)}, bf16[3,4096]{1,0:T(4,128)(2,1)S(1)}, u32[]{:S(2)}, u32[]{:S(2)}) collective-permute-start(bf16[3,4096]{1,0:T(4,128)(2,1)S(1)} %dynamic-slice_convert_fusion), channel_id=1, source_target_pairs={{0,1},{1,2},{2,3},{4,5},{5,6},{6,7},{8,9},{9,10},{10,11},{12,13},{... | collective-permute-start | bytes 73736 | tf_op jit(solution)/shard_map/ppermute | solution.py:15
  230.1 210.8 %copy-start.152 = (f32[128]{0:T(128)}, f32[128]{0:T(128)S(1)}, u32[]{:S(2)}) copy-start(f32[128]{0:T(128)S(1)} %compare_convert_fusion.4) | copy-start | bytes 1540
  3542.8 269.3 %reduce-scatter.15.cloned.1.call-start = ((), (), s32[]{:S(2)}) async-start(), calls=%async_computation.13 | async-start | bytes 270336 | tf_op jit(solution)/shard_map/reduce_scatter | solution.py:342
  3543.7 405.8 %reduce-scatter.13.cloned.1.call-start = ((), (), s32[]{:S(2)}) async-start(), calls=%async_computation.12 | async-start | bytes 2162688 | tf_op jit(solution)/shard_map/reduce_scatter | solution.py:340
  3546.4 544.5 %reduce-scatter.11.cloned.1.call-start = ((), (), s32[]{:S(2)}) async-start(), calls=%async_computation.11 | async-start | bytes 2703360 | tf_op jit(solution)/shard_map/reduce_scatter | solution.py:339
  3548.5 1255.4 %reduce-scatter.17.cloned.1.call-start = ((), (), s32[]{:S(2)}) async-start(), calls=%async_computation.14 | async-start | bytes 34603008 | tf_op jit(solution)/shard_map/reduce_scatter | solution.py:344
  3562.9 2653.9 %reduce-scatter.9.cloned.1.call-start = ((), (), s32[]{:S(2)}) async-start(), calls=%async_computation.10 | async-start | bytes 69206016 | tf_op jit(solution)/shard_map/reduce_scatter | solution.py:336
  3566.5 6.1 collective-permute-start.1
  3609.7 2607.1 %copy-start.1 = (s32[8,3]{0,1:T(4,128)S(1)}, s32[8,3]{0,1:T(4,128)}, u32[]{:S(2)}) copy-start(s32[8,3]{0,1:T(4,128)} %param.32) | copy-start | bytes 292
  (466 other events, 2932.2 us)
Sparse Core Ops, SparseCore 0:
  11.0 199.8 all-gather.10
  213.9 114.5 all-gather.16
  331.3 47.9 all-gather.12
  382.0 48.0 all-gather.14
  3542.9 135.1 reduce-scatter.18
  3680.8 131.2 reduce-scatter.14
  3815.0 134.4 reduce-scatter.12
  3952.5 138.4 reduce-scatter.10
  4093.9 709.9 reduce-scatter.16
  4806.8 1409.9 reduce-scatter.8
where the time goes:
time: 6260 us; the launch traced here: 6220 us
  waiting for transfers between devices  2560 us (41%)
  local copies, waits for them, and re-layouts  1840 us (29%)
  other arithmetic  1200 us (19%)
  blocking collectives  457 us (7%)
  matrix products  113 us (2%)
    reduce_scatter x1, waiting for transfers between devices, per_device(): lax.psum_scatter(in_weight_grad, ('dp', 'fsdp'), scatter_dimension=0, til...  1410 us
    reduce_scatter x1, waiting for transfers between devices, per_device(): lax.psum_scatter(out_weight_grad, ('dp', 'fsdp'), scatter_dimension=0, ti...  713 us
    mul x116, other arithmetic, chain(): return (earlier[0] * later[0], later[0] * earlier[1] + later[1])  430 us
    pad x64, local copies, waits for them, and re-layouts, state_step(): lax.associative_scan(chain, (decay, sources(span_dt, span_u, span_b, span...  410 us
    pad x64, local copies, waits for them, and re-layouts, back_step(): lax.associative_scan(chain, (decay, sources(span_dt, span_u, span_b, span...  404 us
    while x804, local copies, waits for them, and re-layouts  291 us
    pad x32, local copies, waits for them, and re-layouts, back_step(): lax.associative_scan(chain, (ahead, source), reverse=True, axis=0)[1]  198 us
    pad x48, local copies, waits for them, and re-layouts, total_step(): lax.associative_scan(chain, (decay, sources(span_dt, span_u, span_b, span...  189 us
  transfers between devices with their start and end apart: 12, of which 8 were waited for; matrix products, arithmetic and copies ran while one was open for 2% of the time, Pallas kernels for 0%

commit v1 on v0

v1 whole, which is shorter than its diff:
```python
import functools

import jax
import jax.numpy as jnp
from jax import lax
from jax.experimental import pallas as pl
from jax.experimental.pallas import tpu as pltpu
from jax.sharding import PartitionSpec as P

BF, F32 = jnp.bfloat16, jnp.float32
LANES, SUB = 128, 8
LN2 = 0.6931471805599453
FAR = 1.0e5
EPS = 1e-5


def small_cost(flops):
    return pl.CostEstimate(flops=flops, bytes_accessed=1 << 16, transcendentals=0)


def scatter_lanes(ref, value, rows):
    for k in range(value.shape[1] // LANES):
        ref[pl.ds(k, rows, stride=SUB), :] = value[:, k * LANES : (k + 1) * LANES]


def gather_lanes(ref, width, rows):
    return jnp.concatenate(
        [ref[pl.ds(k, rows, stride=SUB), :] for k in range(width // LANES)], axis=1
    )


def softplus(v):
    return jnp.maximum(v, 0.0) + jnp.log1p(jnp.exp(-jnp.abs(v)))


def forward_kernel(bc, rank, dt_w, dt_b, act, valid, rate2, y_out, states, h_ref, dt_s, dtu_s, y_s):
    tb, width = act.shape
    n_state = rate2.shape[0] // SUB

    @pl.when(pl.program_id(0) == 0)
    def _():
        h_ref[...] = jnp.zeros_like(h_ref)
        if width < SUB * LANES:
            dt_s[...] = jnp.zeros_like(dt_s)
            dtu_s[...] = jnp.zeros_like(dtu_s)

    pre = jnp.dot(rank[...], dt_w[...], preferred_element_type=F32) + dt_b[...]
    dt = softplus(pre) * valid[...]
    scatter_lanes(dt_s, dt, tb)
    scatter_lanes(dtu_s, dt * act[...].astype(F32), tb)
    rates = [rate2[n * SUB : (n + 1) * SUB, :] for n in range(n_state)]
    first = [h_ref[n * SUB : (n + 1) * SUB, :] for n in range(n_state)]
    for n in range(n_state):
        states[0, n, 0:SUB, :] = first[n]

    def token(t, h):
        at = pl.multiple_of(t * SUB, SUB)
        dt_t = dt_s[pl.ds(at, SUB), :] + bc[t, 2 * n_state]
        dtu_t = dtu_s[pl.ds(at, SUB), :]
        new, parts = [], [None, None]
        for n in range(n_state):
            hn = jnp.exp2(dt_t * rates[n]) * h[n] + dtu_t * bc[t, n]
            states[0, n, pl.ds(at + SUB, SUB), :] = hn
            term = hn * bc[t, n_state + n]
            parts[n % 2] = term if parts[n % 2] is None else parts[n % 2] + term
            new.append(hn)
        y_s[pl.ds(at, SUB), :] = parts[0] + parts[1]
        return tuple(new)

    last = lax.fori_loop(0, tb, token, tuple(first), unroll=2)
    for n in range(n_state):
        h_ref[n * SUB : (n + 1) * SUB, :] = last[n]
    y_out[...] = gather_lanes(y_s, width, tb)


def scan_forward(bc, rank, dt_w, dt_b, act, valid, rate2, tb):
    slots, width = act.shape
    n_state = rate2.shape[0] // SUB
    nb = slots // tb
    whole = lambda i: (0, 0)
    row = lambda i: (i, 0)
    return pl.pallas_call(
        forward_kernel,
        grid=(nb,),
        in_specs=[
            pl.BlockSpec((tb, bc.shape[1]), row, memory_space=pltpu.SMEM),
            pl.BlockSpec((tb, rank.shape[1]), row),
            pl.BlockSpec(dt_w.shape, whole),
            pl.BlockSpec((1, width), whole),
            pl.BlockSpec((tb, width), row),
            pl.BlockSpec((tb, 1), row),
            pl.BlockSpec(rate2.shape, whole),
        ],
        out_specs=[
            pl.BlockSpec((tb, width), row),
            pl.BlockSpec((1, n_state, (tb + 1) * SUB, LANES), lambda i: (i, 0, 0, 0)),
        ],
        out_shape=[
            jax.ShapeDtypeStruct((slots, width), F32),
            jax.ShapeDtypeStruct((nb, n_state, (tb + 1) * SUB, LANES), F32),
        ],
        scratch_shapes=[pltpu.VMEM(rate2.shape, F32)] + [pltpu.VMEM((tb * SUB, LANES), F32)] * 3,
        compiler_params=pltpu.CompilerParams(vmem_limit_bytes=48 << 20),
        cost_estimate=small_cost(1 << 20),
        name="scan_forward",
    )(bc, rank, dt_w, dt_b, act, valid, rate2)


def backward_kernel(
    bc, rank, dt_w, dt_b, act, valid, rate2, skip, gs, states, fold,
    part_out, gu_out, dtw_out, vec_out, rate_out,
    g_ref, dt_s, dtu_s, gs_s, gdt_s, ab_s, lam_s,
):
    tb, width = act.shape
    n_state = rate2.shape[0] // SUB
    half = n_state // 2

    @pl.when(pl.program_id(0) == 0)
    def _():
        g_ref[...] = jnp.zeros_like(g_ref)
        rate_out[...] = jnp.zeros_like(rate_out)
        vec_out[...] = jnp.zeros_like(vec_out)
        dtw_out[...] = jnp.zeros_like(dtw_out)
        if width < SUB * LANES:
            for ref in (dt_s, dtu_s, gs_s):
                ref[...] = jnp.zeros_like(ref)

    u = act[...].astype(F32)
    ok = valid[...]
    pre = jnp.dot(rank[...], dt_w[...], preferred_element_type=F32) + dt_b[...]
    dt = softplus(pre) * ok
    gs_v = gs[...]
    scatter_lanes(dt_s, dt, tb)
    scatter_lanes(dtu_s, dt * u, tb)
    scatter_lanes(gs_s, gs_v, tb)

    for group in range(2):
        index = range(group * half, (group + 1) * half)
        rates = [rate2[n * SUB : (n + 1) * SUB, :] for n in index]

        def token(i, carry):
            g, acc = carry
            t = tb - 1 - i
            at = pl.multiple_of(t * SUB, SUB)
            dt_t = dt_s[pl.ds(at, SUB), :]
            dtd = dt_t + bc[t, 2 * n_state]
            gs_t = gs_s[pl.ds(at, SUB), :]
            new_g, new_acc = [], []
            gdt = ab = None
            for j, n in enumerate(index):
                lam = gs_t * bc[t, n_state + n] + g[j]
                lam_s[n, pl.ds(at, SUB), :] = lam
                back = jnp.exp2(dtd * rates[j]) * lam
                thr = back * states[0, n, pl.ds(at, SUB), :]
                gdt = thr * rates[j] if gdt is None else gdt + thr * rates[j]
                ab = lam * bc[t, n] if ab is None else ab + lam * bc[t, n]
                new_g.append(back)
                new_acc.append(acc[j] + thr * dt_t)
            if group == 0:
                gdt_s[pl.ds(at, SUB), :] = gdt
                ab_s[pl.ds(at, SUB), :] = ab
            else:
                gdt_s[pl.ds(at, SUB), :] += gdt
                ab_s[pl.ds(at, SUB), :] += ab
            return tuple(new_g), tuple(new_acc)

        start = (
            tuple(g_ref[n * SUB : (n + 1) * SUB, :] for n in index),
            tuple(rate_out[n * SUB : (n + 1) * SUB, :] for n in index),
        )
        g, acc = lax.fori_loop(0, tb, token, start, unroll=2)
        for j, n in enumerate(index):
            g_ref[n * SUB : (n + 1) * SUB, :] = g[j]
            rate_out[n * SUB : (n + 1) * SUB, :] = acc[j]

    ab = gather_lanes(ab_s, width, tb)
    gdt = gather_lanes(gdt_s, width, tb)
    gu_out[...] = gs_v * skip[...] + dt * ab
    grad_pre = ok * (gdt * LN2 + u * ab) * jax.nn.sigmoid(pre)
    vec_out[0:1, :] += jnp.sum(grad_pre, axis=0, keepdims=True)
    vec_out[1:2, :] += jnp.sum(gs_v * u, axis=0, keepdims=True)
    low = grad_pre.astype(BF)
    dtw_out[...] += lax.dot_general(rank[...], low, (((0,), (0,)), ((), ())), preferred_element_type=F32)
    rank_w = rank.shape[1]
    part_out[:, 0:rank_w] = lax.dot_general(low, dt_w[...], (((1,), (1,)), ((), ())), preferred_element_type=F32)

    lane = lax.broadcasted_iota(jnp.int32, (tb, LANES), 1)
    tail = jnp.zeros((tb, LANES), F32)
    dtu_v = dtu_s[...]
    gs_l = gs_s[...]
    for n in range(n_state):
        for at, value in ((n, lam_s[n] * dtu_v), (n_state + n, states[0, n, SUB:, :] * gs_l)):
            summed = jnp.dot(fold[...], value.astype(BF), preferred_element_type=F32)
            tail = jnp.where(lane == at, jnp.sum(summed, axis=1, keepdims=True), tail)
    part_out[:, rank_w:] = tail[:, 0 : 2 * n_state]


def scan_backward(bc, rank, dt_w, dt_b, act, valid, rate2, skip, gs, states, tb):
    slots, width = act.shape
    n_state = rate2.shape[0] // SUB
    nb = slots // tb
    whole = lambda i: (0, 0)
    row = lambda i: (nb - 1 - i, 0)
    rank_w = rank.shape[1]
    fold = (jnp.arange(tb * SUB)[None, :] // SUB == jnp.arange(tb)[:, None]).astype(BF)
    return pl.pallas_call(
        backward_kernel,
        grid=(nb,),
        in_specs=[
            pl.BlockSpec((tb, bc.shape[1]), row, memory_space=pltpu.SMEM),
            pl.BlockSpec((tb, rank_w), row),
            pl.BlockSpec(dt_w.shape, whole),
            pl.BlockSpec((1, width), whole),
            pl.BlockSpec((tb, width), row),
            pl.BlockSpec((tb, 1), row),
            pl.BlockSpec(rate2.shape, whole),
            pl.BlockSpec((1, width), whole),
            pl.BlockSpec((tb, width), row),
            pl.BlockSpec((1, n_state, (tb + 1) * SUB, LANES), lambda i: (nb - 1 - i, 0, 0, 0)),
            pl.BlockSpec(fold.shape, whole),
        ],
        out_specs=[
            pl.BlockSpec((tb, rank_w + 2 * n_state), row),
            pl.BlockSpec((tb, width), row),
            pl.BlockSpec(dt_w.shape, whole),
            pl.BlockSpec((2, width), whole),
            pl.BlockSpec(rate2.shape, whole),
        ],
        out_shape=[
            jax.ShapeDtypeStruct((slots, rank_w + 2 * n_state), F32),
            jax.ShapeDtypeStruct((slots, width), F32),
            jax.ShapeDtypeStruct(dt_w.shape, F32),
            jax.ShapeDtypeStruct((2, width), F32),
            jax.ShapeDtypeStruct(rate2.shape, F32),
        ],
        scratch_shapes=[pltpu.VMEM(rate2.shape, F32)]
        + [pltpu.VMEM((tb * SUB, LANES), F32)] * 5
        + [pltpu.VMEM((n_state, tb * SUB, LANES), F32)],
        compiler_params=pltpu.CompilerParams(vmem_limit_bytes=56 << 20),
        cost_estimate=small_cost(1 << 20),
        name="scan_backward",
    )(bc, rank, dt_w, dt_b, act, valid, rate2, skip, gs, states, fold)


def silu_grad(value, sig):
    return sig * (1.0 + value * (1.0 - sig))


def place_blocks(ref, own, other, index):
    chips, rows, _ = own.shape
    core = lax.rem(index, 2)
    for q in range(chips):
        ref[pl.ds(pl.multiple_of((2 * q + core) * rows, rows), rows), :] = own[q]
        ref[pl.ds(pl.multiple_of((2 * q + 1 - core) * rows, rows), rows), :] = other[q]


def read_row(ref, row, cols):
    base = pl.multiple_of(row // SUB * SUB, SUB)
    rows = ref[pl.ds(base, SUB), cols]
    mine = lax.broadcasted_iota(jnp.int32, rows.shape, 0) == row - base
    return jnp.sum(jnp.where(mine, rows, 0.0), axis=0, keepdims=True)


def add_row(ref, row, value):
    base = pl.multiple_of(row // SUB * SUB, SUB)
    rows = ref[pl.ds(base, SUB), :]
    mine = lax.broadcasted_iota(jnp.int32, rows.shape, 0) == row - base
    ref[pl.ds(base, SUB), :] = rows + jnp.where(mine, value, 0.0)


def split_kernel(n_dp, in_w, out):
    rows = in_w.shape[0]
    n_line, _, width = out.shape
    owned = width // n_dp
    for to in range(n_line):
        for half in range(2):
            for d in range(n_dp):
                at = ((half * n_dp + d) * n_line + to) * owned
                out[to, half * rows : (half + 1) * rows, d * owned : (d + 1) * owned] = in_w[:, at : at + owned]


def split_columns(in_w, n_dp, n_line):
    rows, both = in_w.shape
    width = both // (2 * n_line)
    if width // n_dp % LANES:
        blocks = in_w.reshape(rows, 2, n_dp, n_line, width // n_dp).transpose(3, 1, 0, 2, 4)
        return blocks.reshape(n_line, 2 * rows, width)
    vmem = pl.BlockSpec(memory_space=pltpu.VMEM)
    return pl.pallas_call(
        functools.partial(split_kernel, n_dp),
        in_specs=[vmem],
        out_specs=vmem,
        out_shape=jax.ShapeDtypeStruct((n_line, 2 * rows, width), in_w.dtype),
        cost_estimate=small_cost(1 << 10),
        name="split_columns",
    )(in_w)


def join_kernel(n_dp, inner, gate, in_w, gain, out, gain_out):
    n_line, rows, width = inner.shape
    owned = width // n_dp
    total = jnp.zeros((rows, LANES), F32)
    for half, parts in enumerate((inner, gate)):
        for line in range(n_line):
            for d in range(n_dp):
                at = ((half * n_dp + d) * n_line + line) * owned
                block = parts[line, :, d * owned : (d + 1) * owned].astype(F32)
                out[:, at : at + owned] = block
                term = block * in_w[:, at : at + owned].astype(F32)
                for low in range(0, owned, LANES):
                    total = total + term[:, low : low + LANES]
    gain_out[...] = jnp.sum(total, axis=1, keepdims=True) / gain[...]


def join_columns(inner, gate, in_w, gain, n_dp):
    rows, both = in_w.shape
    n_line, _, width = inner.shape
    if width // n_dp % LANES:
        blocks = jnp.stack([inner, gate]).astype(F32)
        full = blocks.reshape(2, n_line, rows, n_dp, -1).transpose(2, 0, 3, 1, 4).reshape(rows, both)
        return full, jnp.sum(full * in_w.astype(F32), axis=1) / gain.astype(F32)
    vmem = pl.BlockSpec(memory_space=pltpu.VMEM)
    full, gain_grad = pl.pallas_call(
        functools.partial(join_kernel, n_dp),
        in_specs=[vmem] * 4,
        out_specs=[vmem] * 2,
        out_shape=[jax.ShapeDtypeStruct((rows, both), F32), jax.ShapeDtypeStruct((rows, 1), F32)],
        cost_estimate=small_cost(1 << 10),
        name="join_columns",
    )(inner, gate, in_w, gain.astype(F32)[:, None])
    return full, gain_grad[:, 0]


def column_block(width, slots):
    return 256 if width % 256 == 0 and slots <= 1024 else LANES


def from_place(place, move, n_line, body):
    steps, sign = move
    if sign == 0:
        body(lax.rem(place - steps + n_line, n_line))
        return
    source = place - sign * steps

    @pl.when(jnp.logical_and(source >= 0, source < n_line))
    def _():
        body(source)


def split_cores(ref, kept, sent, index, n_dp):
    size = ref.shape[1] // n_dp
    core = lax.rem(index, 2)
    for q in range(kept.shape[1] // size):
        cols = slice(q * size, (q + 1) * size)
        kept[:, cols] = ref[:, pl.ds(pl.multiple_of((2 * q + core) * size, size), size)]
        sent[:, cols] = ref[:, pl.ds(pl.multiple_of((2 * q + 1 - core) * size, size), size)]


def project_kernel(n_line, n_dp, moves, info, *refs):
    toks, refs = refs[: len(moves)], refs[len(moves) :]
    own, other, gain, conv_w, conv_b, x_t, allowed, normed, kept, sent, inner, conv_out, activ, part32, w_nat, ext = refs
    held, model = toks[0].shape
    slots = held * n_line
    width = w_nat.shape[1]
    taps = conv_w.shape[0]
    rim = taps - 1
    step = 32
    for move, tok in zip(moves, toks):

        def normalise(source, tok=tok):
            base = source * held

            @pl.loop(0, held // step)
            def _(i):
                x = tok[pl.ds(pl.multiple_of(i * step, step), step), :].astype(F32)
                scale = lax.rsqrt(jnp.mean(x * x, axis=1, keepdims=True) + EPS)
                rows = pl.ds(pl.multiple_of(base + i * step, step), step)
                normed[rows, :] = (x * scale * gain[...]).astype(BF)

        from_place(info[1], move, n_line, normalise)

    split_cores(normed, kept, sent, info[0], n_dp)
    place_blocks(w_nat, own, other, info[0])
    cb = column_block(width, slots)

    @pl.loop(0, width // cb)
    def _(c):
        cols = pl.ds(pl.multiple_of(c * cb, cb), cb)
        inner[:, cols] = jnp.dot(normed[...], w_nat[:, cols], preferred_element_type=F32)
        for f in range(n_line):
            rows = slice(f * held, (f + 1) * held)
            ext[SUB : SUB + held, :] = inner[rows, cols]
            for k in range(1, rim + 1):
                if f == 0:
                    ext[SUB - k : SUB - k + 1, :] = jnp.zeros((1, cb), F32)
                else:
                    ext[SUB - k : SUB - k + 1, :] = read_row(inner, (f - 1) * held + info[1 + f] - k, cols)
            total = conv_b[:, cols]
            for lag in range(taps):
                tapped = ext[SUB - lag : SUB - lag + held, :]
                total = total + conv_w[rim - lag : rim - lag + 1, cols] * tapped * allowed[rows, lag : lag + 1]
            conv_out[rows, cols] = total
            activ[rows, cols] = (total * jax.nn.sigmoid(total)).astype(BF)

    part = lax.dot_general(activ[...], x_t[...], (((1,), (1,)), ((), ())), preferred_element_type=F32)
    part32[...] = part


def project(info, n_line, n_dp, moves, toks, own, other, gain, conv_w, conv_b, x_t, allowed):
    held, model = toks[0].shape
    slots = held * n_line
    width, proj = x_t.shape[1], x_t.shape[0]
    vmem = pl.BlockSpec(memory_space=pltpu.VMEM)
    shapes = [
        ((slots, model), BF), ((slots, model // 2), BF), ((slots, model // 2), BF),
        ((slots, width), F32), ((slots, width), F32), ((slots, width), BF),
        ((slots, proj), F32), ((model, width), BF),
    ]
    return pl.pallas_call(
        functools.partial(project_kernel, n_line, n_dp, moves),
        in_specs=[pl.BlockSpec(memory_space=pltpu.SMEM)] + [vmem] * (7 + len(toks)),
        out_specs=[vmem] * len(shapes),
        out_shape=[jax.ShapeDtypeStruct(s, t) for s, t in shapes],
        scratch_shapes=[pltpu.VMEM((SUB + slots // n_line, column_block(width, slots)), F32)],
        compiler_params=pltpu.CompilerParams(vmem_limit_bytes=56 << 20),
        cost_estimate=small_cost(1 << 20),
        name="project",
    )(info, *toks, own, other, gain, conv_w, conv_b, x_t, allowed)


def gate_kernel(n_line, n_dp, moves, info, *refs):
    cots, refs = refs[: len(moves)], refs[len(moves) :]
    own, other, o_nat, normed, y, act, skip, valid, gated, branch, gs, grad_gate, dout, w_nat, *halves = refs
    slots, width = y.shape
    held, model = cots[0].shape
    place_blocks(w_nat, own, other, info[0])
    for move, cot in zip(moves, cots):

        def mask(source, cot=cot):
            rows = pl.ds(pl.multiple_of(source * held, held), held)
            dout[rows, :] = (cot[...].astype(F32) * valid[rows, :]).astype(BF)

        from_place(info[1], move, n_line, mask)

    cb = column_block(width, slots)

    @pl.loop(0, width // cb)
    def _(c):
        cols = pl.ds(pl.multiple_of(c * cb, cb), cb)
        gate = jnp.dot(normed[...], w_nat[:, cols], preferred_element_type=F32)
        grad = lax.dot_general(dout[...], o_nat[cols, :], (((1,), (1,)), ((), ())), preferred_element_type=F32)
        sig = jax.nn.sigmoid(gate)
        scan_out = y[:, cols] + skip[:, cols] * act[:, cols].astype(F32)
        gated[:, cols] = (scan_out * gate * sig).astype(BF)
        gs[:, cols] = grad * gate * sig
        grad_gate[:, cols] = (grad * scan_out * silu_grad(gate, sig)).astype(BF)

    mb = column_block(model, slots)

    @pl.loop(0, model // mb)
    def _(c):
        cols = pl.ds(pl.multiple_of(c * mb, mb), mb)
        branch[:, cols] = jnp.dot(gated[...], o_nat[:, cols], preferred_element_type=F32).astype(BF)

    if halves:
        split_cores(gated, *halves, info[0], n_dp)


def gate_block(info, n_line, n_dp, moves, cots, own, other, out_w, normed, y, act, skip, valid):
    slots, width = y.shape
    model = normed.shape[1]
    vmem = pl.BlockSpec(memory_space=pltpu.VMEM)
    shapes = [
        ((slots, width), BF), ((slots, model), BF), ((slots, width), F32), ((slots, width), BF),
        ((slots, model), BF), ((model, width), BF),
    ]
    if width // n_dp % LANES == 0:
        shapes += [((slots, width // 2), BF)] * 2
    *outs, = pl.pallas_call(
        functools.partial(gate_kernel, n_line, n_dp, moves),
        in_specs=[pl.BlockSpec(memory_space=pltpu.SMEM)] + [vmem] * (8 + len(cots)),
        out_specs=[vmem] * len(shapes),
        out_shape=[jax.ShapeDtypeStruct(s, t) for s, t in shapes],
        compiler_params=pltpu.CompilerParams(vmem_limit_bytes=58 << 20),
        cost_estimate=small_cost(1 << 20),
        name="gate_block",
    )(info, *cots, own, other, out_w, normed, y, act, skip, valid)
    return outs[:6] + (outs[6:] or cores(outs[0], 1))


def conv_back_kernel(n_line, info, gp, gu, x_t, act, conv_out, inner, conv_w, allowed, gi_low, x_grad, vec, ext, gi, tail):
    slots, width = gu.shape
    held = slots // n_line
    taps = conv_w.shape[0]
    rim = taps - 1
    cb = column_block(width, slots)
    x_grad[...] = lax.dot_general(gp[...], act[...], (((0,), (0,)), ((), ())), preferred_element_type=F32)
    vec[...] = jnp.zeros_like(vec)
    for lag in range(taps):
        tail[lag, held : held + SUB, :] = jnp.zeros((SUB, cb), F32)

    @pl.loop(0, width // cb)
    def _(c):
        cols = pl.ds(pl.multiple_of(c * cb, cb), cb)
        for f in range(n_line - 1, -1, -1):
            rows = slice(f * held, (f + 1) * held)
            ext[SUB : SUB + held, :] = inner[rows, cols]
            for k in range(1, rim + 1):
                if f == 0:
                    ext[SUB - k : SUB - k + 1, :] = jnp.zeros((1, cb), F32)
                else:
                    ext[SUB - k : SUB - k + 1, :] = read_row(inner, (f - 1) * held + info[1 + f] - k, cols)
            grad = gu[rows, cols] + jnp.dot(gp[rows, :], x_t[:, cols], preferred_element_type=F32)
            co = conv_out[rows, cols]
            grad = grad * silu_grad(co, jax.nn.sigmoid(co))
            vec[taps : taps + 1, cols] += jnp.sum(grad, axis=0, keepdims=True)
            for lag in range(taps):
                weighted = grad * allowed[rows, lag : lag + 1]
                vec[rim - lag : rim - lag + 1, cols] += jnp.sum(
                    weighted * ext[SUB - lag : SUB - lag + held, :], axis=0, keepdims=True
                )
                tail[lag, 0:held, :] = weighted * conv_w[rim - lag : rim - lag + 1, cols]
            total = tail[0, 0:held, :]
            for lag in range(1, taps):
                total = total + tail[lag, lag : lag + held, :]
            gi[rows, :] = total
            if f + 1 < n_line:
                for k in range(1, rim + 1):
                    add_row(gi, f * held + info[2 + f] - k, gi[slots + k : slots + k + 1, :])
            for k in range(1, rim + 1):
                row = tail[k, 0:1, :]
                for lag in range(k + 1, taps):
                    row = row + tail[lag, lag - k : lag - k + 1, :]
                gi[slots + k : slots + k + 1, :] = row
        gi_low[:, cols] = gi[0:slots, :].astype(BF)


def conv_back(info, n_line, gp, gu, x_t, act, conv_out, inner, conv_w, allowed):
    slots, width = gu.shape
    held = slots // n_line
    taps = conv_w.shape[0]
    cb = column_block(width, slots)
    vmem = pl.BlockSpec(memory_space=pltpu.VMEM)
    shapes = [((slots, width), BF), (x_t.shape, F32), ((SUB, width), F32)]
    return pl.pallas_call(
        functools.partial(conv_back_kernel, n_line),
        in_specs=[pl.BlockSpec(memory_space=pltpu.SMEM)] + [vmem] * 8,
        out_specs=[vmem] * len(shapes),
        out_shape=[jax.ShapeDtypeStruct(s, t) for s, t in shapes],
        scratch_shapes=[
            pltpu.VMEM((SUB + held, cb), F32),
            pltpu.VMEM((slots + SUB, cb), F32),
            pltpu.VMEM((taps, held + SUB, cb), F32),
        ],
        compiler_params=pltpu.CompilerParams(vmem_limit_bytes=48 << 20),
        cost_estimate=small_cost(1 << 20),
        name="conv_back",
    )(info, gp, gu, x_t, act, conv_out, inner, conv_w, allowed)


def swap(value, axis, mask):
    count = lax.axis_size(axis)
    return lax.ppermute(value, axis, [(i, i ^ mask) for i in range(count)])


def shift(value, axis, steps):
    count = lax.axis_size(axis)
    return lax.ppermute(value, axis, [(i, (i + steps) % count) for i in range(count)])


def chips_of(axis):
    return [list(range(core, lax.axis_size(axis), 2)) for core in range(2)]


def to_line(blocks):
    return lax.all_to_all(blocks, "fsdp", 0, 0)


def to_chips(blocks):
    return lax.all_to_all(blocks, "dp", 0, 0, axis_index_groups=chips_of("dp"))


def repeated(value, count):
    return jnp.broadcast_to(value[None], (count,) + value.shape)


def in_order(parts, axis):
    count, me = lax.axis_size(axis), lax.axis_index(axis)
    up = jnp.stack([parts[-k % count] for k in range(count)] * 2)
    return lax.dynamic_slice_in_dim(up, lax.rem(count - me, count), count, 0)


def by_chip(parts):
    chip, count = lax.div(lax.axis_index("dp"), 2), len(parts)
    bits = count.bit_length() - 1
    cube = jnp.stack(parts).reshape((2,) * bits + parts[0].shape)
    for place in range(bits):
        mine = lax.rem(chip >> (bits - 1 - place), 2) == 1
        cube = jnp.where(mine, jnp.flip(cube, place), cube)
    return cube.reshape((count,) + parts[0].shape)


def by_device(own, other):
    core = lax.rem(lax.axis_index("dp"), 2) == 1
    both = jnp.where(core, jnp.stack([other, own], axis=1), jnp.stack([own, other], axis=1))
    return lax.optimization_barrier(both.reshape((-1,) + own.shape[1:]))


def total_line(value):
    reach = 1
    while reach < lax.axis_size("fsdp"):
        value = value + swap(value.astype(BF), "fsdp", reach).astype(F32)
        reach *= 2
    return value


def fence(*values):
    flat, shape = jax.tree.flatten(values)
    return jax.tree.unflatten(shape, lax.optimization_barrier(tuple(flat)))


def cores(value, axis):
    cut = value.shape[:axis] + (lax.axis_size("dp") // 2, 2, -1) + value.shape[axis + 1 :]
    cube = value.reshape(cut)
    core = lax.rem(lax.axis_index("dp"), 2)
    found = [lax.dynamic_index_in_dim(cube, at, axis + 1, keepdims=False) for at in (core, 1 - core)]
    flat = value.shape[:axis] + (value.shape[axis] // 2,) + value.shape[axis + 1 :]
    return [part.reshape(flat) for part in found]


def weight_grad(kept, sent, right):
    return contract_rows(kept, right), contract_rows(sent, right).astype(BF)


def add_core(kept, sent):
    total = kept + swap(sent, "dp", 1).astype(F32)
    return total.reshape((lax.axis_size("dp") // 2, -1) + kept.shape[1:])


def add_chips(blocks):
    return jnp.sum(to_chips(blocks.astype(BF)).astype(F32), axis=0)


def add_chips_near(blocks):
    count, chip = lax.axis_size("dp") // 2, lax.div(lax.axis_index("dp"), 2)
    total = lax.dynamic_index_in_dim(blocks, chip, 0, keepdims=False)
    for u in range(1, count):
        total = total + far(blocks, u).astype(F32)
    return total


def far(blocks, u):
    chip = lax.div(lax.axis_index("dp"), 2)
    block = lax.dynamic_index_in_dim(blocks, jnp.bitwise_xor(chip, u), 0, keepdims=False)
    return swap(block.astype(BF), "dp", 2 * u)


class Gather:
    def __init__(self, value):
        self.count = lax.axis_size("fsdp")
        self.hops = self.count <= 4
        self.found = {(0, 0): value}

    def hop(self, steps):
        if not self.hops:
            self.found[steps, 0] = shift(self.found[0, 0], "fsdp", steps)
            return
        for sign in (1, -1):
            last = self.found[(0, 0) if steps == 1 else (steps - 1, sign)]
            pairs = [(i, i + 1) for i in range(steps - 1, self.count - 1)]
            if sign < 0:
                pairs = [(self.count - 1 - i, self.count - 1 - j) for i, j in pairs]
            self.found[steps, sign] = lax.ppermute(last, "fsdp", pairs)

    def fenced(self, *others):
        self.found, *others = fence(self.found, *others)
        return others

    def moves(self):
        return tuple(sorted(self.found))

    def blocks(self):
        return [self.found[move] for move in sorted(self.found)]

def contract_rows(left, right):
    return lax.dot_general(left, right, (((0,), (0,)), ((), ())), preferred_element_type=F32)


def contract_cols(left, right):
    return lax.dot_general(left, right, (((1,), (1,)), ((), ())), preferred_element_type=F32)


def per_device(
    tokens, counts, lengths, gain, in_weight, conv_weight, conv_bias, x_weight,
    dt_weight, dt_bias, a_log, skip, out_weight, cotangent,
):
    n_dp, n_line = lax.axis_size("dp"), lax.axis_size("fsdp")
    group, place = lax.axis_index("dp"), lax.axis_index("fsdp")
    held_slots, model = tokens.shape
    slots = held_slots * n_line
    owned = skip.shape[0]
    width = owned * n_dp
    in_rows = in_weight.shape[0]
    taps, rank_w, n_state = conv_weight.shape[0], dt_weight.shape[0], a_log.shape[1]
    proj = x_weight.shape[1]
    tb = 64 if slots % 64 == 0 else slots

    count_row = lax.dynamic_index_in_dim(counts, group, 0, keepdims=False)
    length_row = lax.dynamic_index_in_dim(lengths, group, 0, keepdims=False)
    info = jnp.concatenate([jnp.stack([group, place]).astype(jnp.int32), count_row])
    offsets = jnp.cumsum(count_row) - count_row
    within = lax.broadcasted_iota(jnp.int32, (n_line, held_slots), 1)
    present = within < count_row[:, None]
    position = offsets[:, None] + within
    second, third = length_row[0], length_row[0] + length_row[1]
    begin = jnp.where(position >= third, third, jnp.where(position >= second, second, 0))
    marks = jnp.stack(
        [position - lag >= begin for lag in range(taps)] + [present, present & (position == begin)]
    ).astype(F32).reshape(taps + 2, slots).T
    allowed, valid, opens = marks[:, :taps], marks[:, taps : taps + 1], marks[:, taps + 1 :] * FAR

    own_tokens, own_cot = tokens, cotangent
    steps = range(1, n_line)
    chips = range(1, n_dp // 2)
    out_w = lax.all_gather(out_weight, "dp", tiled=True)

    parts = split_columns(in_weight, n_dp, n_line)
    parts, tokens, gain_in = fence(parts, tokens, gain)
    parts = to_line(parts)
    toks = Gather(tokens)
    toks.hop(1)
    gains = [gain_in] + [shift(gain_in, "fsdp", s) for s in steps]
    parts, gains = toks.fenced(parts, gains)

    line_gain = in_order(gains, "fsdp").reshape(-1, owned)
    rest = jnp.concatenate([conv_weight, conv_bias[None], dt_bias[None], skip[None], line_gain], axis=0)
    rest = jnp.pad(rest, ((0, -rest.shape[0] % 16), (0, 0)))
    small = jnp.concatenate([dt_weight, x_weight.T, a_log.T, rest], axis=0)
    inner_rep = repeated(parts[:, :in_rows].reshape(-1, width), n_dp // 2)
    inner_rep, small, gate_in = toks.fenced(inner_rep, small, parts[:, in_rows:].reshape(-1, width))
    inner_own = to_chips(inner_rep)
    toks.hop(2)
    near = [small] + [swap(small, "dp", 2 * u) for u in chips]
    near, gate_in, cotangent = toks.fenced(near, gate_in, cotangent)
    for s in steps[2:]:
        toks.hop(s)
    near = by_chip(near)
    near_other = swap(near, "dp", 1)
    inner_own, near, near_other = toks.fenced(inner_own, near, near_other)

    cots = Gather(cotangent)
    inner_own, near, near_other = cots.fenced(inner_own, near, near_other)
    inner_other = swap(inner_own, "dp", 1)
    cots.hop(1)
    gate_rep = repeated(gate_in, n_dp // 2)
    small = by_device(near, near_other)
    first = rank_w + proj + n_state
    at_gain = first + taps + 3
    full_gain = small[:, at_gain : at_gain + line_gain.shape[0]].reshape(1, model).astype(F32)
    small = lax.optimization_barrier(small.transpose(1, 0, 2).reshape(-1, width))
    cuts = [0]
    for size in (rank_w, proj, n_state, taps, 1, 1, 1):
        cuts.append(cuts[-1] + size)
    dt_w, x_t, a_t, conv_w, conv_b, dt_b, skip_w = [small[a:b] for a, b in zip(cuts[:-1], cuts[1:])]
    conv_w, conv_b, dt_b, skip_w = [v.astype(F32) for v in (conv_w, conv_b, dt_b, skip_w)]
    rates = -jnp.exp(a_t.astype(F32))
    chunks = width // LANES
    rate2 = jnp.pad(
        (rates * (1.0 / LN2)).reshape(n_state, chunks, LANES), ((0, 0), (0, SUB - chunks), (0, 0))
    ).reshape(n_state * SUB, LANES)

    gate_rep, inner_own, inner_other, full_gain, x_t, conv_w = cots.fenced(
        gate_rep, inner_own, inner_other, full_gain, x_t, conv_w
    )
    gate_own = to_chips(gate_rep)
    cots.hop(2)
    normed, normed_kept, normed_sent, inner, conv_out, activ, part, inner_nat = project(
        info, n_line, n_dp, toks.moves(), toks.blocks(), inner_own, inner_other, full_gain, conv_w, conv_b, x_t, allowed
    )
    part, = cots.fenced(part)

    projected = total_line(part)
    projected, gate_own = cots.fenced(projected, gate_own)

    gate_other = swap(gate_own, "dp", 1)
    for s in steps[2:]:
        cots.hop(s)
    rank_low = projected[:, :rank_w].astype(BF)
    bc = jnp.concatenate([projected[:, rank_w:], opens], axis=1)
    scanned, states = scan_forward(bc, rank_low, dt_w, dt_b, activ, valid, rate2, tb)
    scanned, gate_own, gate_other = cots.fenced(scanned, gate_own, gate_other)

    gated, branch, grad_scan, grad_gate, dout, gate_nat, gated_kept, gated_sent = gate_block(
        info, n_line, n_dp, cots.moves(), cots.blocks(), gate_own, gate_other, out_w, normed, scanned, activ, skip_w, valid
    )
    branch = branch.reshape(n_line, held_slots, model)

    def sent_to(blocks, s):
        return lax.dynamic_index_in_dim(blocks, lax.rem(place + s, n_line), 0, keepdims=False)

    branches = [sent_to(branch, s) for s in range(n_line)]
    branches, gated_kept, gated_sent, dout, grad_gate = fence(branches, gated_kept, gated_sent, dout, grad_gate)
    branches[1] = shift(branches[1], "fsdp", 1)
    gate_grad = weight_grad(normed_kept, normed_sent, grad_gate)
    gate_grad = add_core(*gate_grad).astype(BF)
    out_grad = weight_grad(gated_kept, gated_sent, dout)
    branches, out_grad, gate_grad, grad_scan = fence(branches, out_grad, gate_grad, grad_scan)

    gate_rows = add_chips(gate_grad).astype(BF)
    for s in steps[1:]:
        branches[s] = shift(branches[s], "fsdp", s)
    out_grad = add_core(*out_grad)
    part, grad_u, dt_w_grad, vectors, rate_sum = scan_backward(
        bc, rank_low, dt_w, dt_b, activ, valid, rate2, skip_w, grad_scan, states, tb
    )
    part, branches, out_grad, gate_rows = fence(part, branches, out_grad, gate_rows)

    out_far = {u: far(out_grad, u) for u in chips[:-1]}
    out_weight_grad = lax.dynamic_index_in_dim(out_grad, lax.div(group, 2), 0, keepdims=False)
    normed_gate = contract_cols(grad_gate, gate_nat)
    own_valid = lax.dynamic_slice_in_dim(valid, place * held_slots, held_slots, 0)
    own_f = own_tokens.astype(F32)
    output = (own_f + own_valid * sum(p.astype(F32) for p in branches)).astype(BF)
    grad_projected = total_line(part).astype(BF)
    grad_projected, out_far, output, normed_gate = fence(grad_projected, out_far, output, normed_gate)

    gate_got = to_line(gate_rows.reshape(n_line, in_rows, width))
    rate_sum = rate_sum.reshape(n_state, SUB, LANES)[:, :chunks].reshape(n_state, width)
    grad_inner, x_t_grad, conv_grads = conv_back(
        info, n_line, grad_projected, grad_u, x_t, activ, conv_out, inner, conv_w, allowed
    )
    inner_grad = weight_grad(normed_kept, normed_sent, grad_inner)
    grad_normed = (contract_cols(grad_inner, inner_nat) + normed_gate).astype(BF)
    grad_normed = grad_normed.reshape(n_line, held_slots, model)
    grads = [sent_to(grad_normed, s) for s in range(n_line)]
    inner_grad, grads, gate_got, x_t_grad, conv_grads = fence(inner_grad, grads, gate_got, x_t_grad, conv_grads)

    grads[1] = shift(grads[1], "fsdp", 1)
    inner_grad = add_core(*inner_grad).astype(BF)
    for u in chips[-1:]:
        out_far[u] = far(out_grad, u)
    small_grads = jnp.concatenate(
        [dt_w_grad, x_t_grad, rate_sum * rates, conv_grads[: taps + 1], vectors], axis=0
    )
    small_grads = jnp.pad(small_grads, ((0, -cuts[-1] % 32), (0, 0)))
    small_rows = small_grads.shape[0]
    small_kept, small_sent = cores(small_grads, 1)
    small_grads = (small_kept + swap(small_sent.astype(BF), "dp", 1).astype(F32)).reshape(small_rows, n_dp // 2, owned)
    small_grads = small_grads.transpose(1, 0, 2)
    inner_grad, grads, small_grads, out_far = fence(inner_grad, grads, small_grads, out_far)
    out_weight_grad = out_weight_grad + sum(out_far[u].astype(F32) for u in chips)

    inner_rows = add_chips(inner_grad).astype(BF)
    for s in steps[1:]:
        grads[s] = shift(grads[s], "fsdp", s)
    small_grads = add_chips_near(small_grads)
    inner_rows, grads, small_grads = fence(inner_rows, grads, small_grads)

    inner_got = to_line(inner_rows.reshape(n_line, in_rows, width))
    grad_normed = sum(p.astype(F32) for p in grads)
    own_scale = lax.rsqrt(jnp.mean(own_f * own_f, axis=1, keepdims=True) + EPS)
    unit = own_f * own_scale
    grad_unit = grad_normed * full_gain
    token_grad = own_cot.astype(F32) + own_scale * (
        grad_unit - unit * jnp.mean(grad_unit * unit, axis=1, keepdims=True)
    )
    dt_g, x_g, a_g, conv_g, conv_b_g, dt_b_g, skip_g = [
        small_grads[a:b] for a, b in zip(cuts[:-1], cuts[1:])
    ]
    in_weight_grad, gain_grad = join_columns(inner_got, gate_got, in_weight, gain, n_dp)
    return (
        output, token_grad, gain_grad, in_weight_grad, conv_g, conv_b_g[0], x_g.T, dt_g, dt_b_g[0], a_g.T,
        skip_g[0], out_weight_grad,
    )


def solution(mesh):
    both = ("dp", "fsdp")
    rows, cols, vec = P(both, None), P(None, both), P(both)
    return jax.shard_map(
        per_device,
        mesh=mesh,
        in_specs=(rows, P(), P(), vec, rows, cols, vec, rows, cols, vec, rows, vec, rows, rows),
        out_specs=(rows, rows, vec, rows, cols, vec, rows, cols, vec, rows, vec, rows),
        check_vma=False,
    )
```

time: 6260 us -> 479 us (0.08)
  waiting for transfers between devices: 2560 us -> 151 us
  local copies, waits for them, and re-layouts: 1840 us -> 33.8 us
  other arithmetic: 1200 us -> 34.3 us
  blocking collectives: 457 us -> 0 us
  Pallas kernels: 0 us -> 110 us
  starting transfers between devices: 3.56 us -> 98.2 us
  matrix products: 113 us -> 27.4 us
    reduce_scatter x5 -> x0, waiting for transfers between devices: 2540 us -> none  [the longest x1 1410 us: per_device(): lax.psum_scatter(in_weight_grad, ('dp', 'fsdp'), scatter_dimension=0, til...]
    pad x232 -> x1, local copies, waits for them, and re-layouts: 1300 us -> 1.4 us  [per_device(): small_grads = jnp.pad(small_grads, ((0, -cuts[-1] % 32), (0, 0)))]
    mul x158 -> x2, other arithmetic: 493 us -> 0.04 us  [the longest x1 0.02 us: per_device(): rate_sum * rates]
    all_gather x8 -> x0, blocking collectives: 376 us -> none  [the longest x1 66.9 us: per_device(): lax.all_gather(conv_weight, ('dp', 'fsdp'), axis=1, tiled=True)]
    add x176 -> x6, other arithmetic: 378 us -> 9.49 us  [the longest x1 3.5 us: add_core(): total = kept + swap(sent, 'dp', 1).astype(F32)]
    while x805 -> x0, local copies, waits for them, and re-layouts: 292 us -> none
    slice x130 -> x8, local copies, waits for them, and re-layouts: 157 us -> 3.65 us  [the longest x2 1.21 us: per_device(): small_grads[a:b]]
    reduce_sum x15 -> x4, other arithmetic: 156 us -> 7.15 us  [the longest x2 2.69 us: add_chips(): return jnp.sum(to_chips(blocks.astype(BF)).astype(F32), axis=0)]
  transfers between devices with their start and end apart: 12 -> 49, of which waited for: 8 -> 18; matrix products, arithmetic and copies ran while one was open for 2% -> 17% of each run, Pallas kernels for 0% -> 17%
where the time goes in v1:
time: 479 us; the launch traced here: 471 us
  waiting for transfers between devices  151 us (32%)
  Pallas kernels  110 us (23%)
  starting transfers between devices  98.2 us (21%)
  other arithmetic  34.3 us (7%)
  local copies, waits for them, and re-layouts  33.8 us (7%)
  matrix products  27.4 us (6%)
  between operations  16.9 us (4%)
    ppermute x20, waiting for transfers between devices, swap(): return lax.ppermute(value, axis, [(i, i ^ mask) for i in range(count)])  94.2 us
    pallas_call x1, Pallas kernels, scan_backward(): pl.pallas_call(backward_kernel, grid=(nb,), in_specs=[pl.BlockSpec((tb, b...  40 us
    ppermute x9, waiting for transfers between devices, shift(): lax.ppermute(value, axis, [(i, (i + steps) % count) for i in range(count)])  30.5 us
    ppermute x20, starting transfers between devices, swap(): return lax.ppermute(value, axis, [(i, i ^ mask) for i in range(count)])  23 us
    ppermute x12, starting transfers between devices, hop(): self.found[steps, sign] = lax.ppermute(last, 'fsdp', pairs)  22.9 us
    all_to_all x3, starting transfers between devices, to_line(): return lax.all_to_all(blocks, 'fsdp', 0, 0)  22.4 us
    pallas_call x1, Pallas kernels, gate_block(): pl.pallas_call(functools.partial(gate_kernel, n_line, n_dp, moves), in_sp...  22.1 us
    pallas_call x1, Pallas kernels, scan_forward(): pl.pallas_call(forward_kernel, grid=(nb,), in_specs=[pl.BlockSpec((tb, bc...  19.7 us
  transfers between devices with their start and end apart: 49, of which 18 were waited for; matrix products, arithmetic and copies ran while one was open for 17% of the time, Pallas kernels for 17%

profile of v1, /device:TPU:0, one launch (start us, length us, event | category | flops | bytes accessed | tf_op | source)
XLA Modules:
  0.0 471.2 jit_solution(17868889708394404846)
XLA Ops:
  9.7 6.5 %all-to-all-start = ((bf16[4,128,1024]{2,1,0:T(8,128)(2,1)}), bf16[4,128,1024]{2,1,0:T(8,128)(2,1)S(1)}, u32[]{:S(2)}, u32[]{:S(2)}) async-start(bf16[4,128,1024]{2,1,0:T(8,128)(2,1)} %split_columns.1), calls=%async_computation | async-start | bytes 2097152 | tf_op jit(solution)/shard_map/all_to_all | solution.py:576
  17.4 4.6 collective-permute-start.1
  27.9 20.5 %collective-permute-done.2 = bf16[64]{0:T(256)(128)(2,1)S(1)} collective-permute-done((bf16[64]{0:T(256)(128)(2,1)S(1)}, bf16[64]{0:T(256)(128)(2,1)S(1)}, u32[]{:S(2)}, u32[]{:S(2)}) %collective-permute-start.2) | collective-permute-done | bytes 160 | tf_op jit(solution)/shard_map/ppermute | solution.py:568
  48.5 4.7 collective-permute-done.3
  66.8 25.2 %collective-permute-done.7 = bf16[320,128]{1,0:T(8,128)(2,1)S(1)} collective-permute-done((bf16[320,128]{1,0:T(8,128)(2,1)S(1)}, bf16[320,128]{1,0:T(8,128)(2,1)S(1)}, u32[]{:S(2)}, u32[]{:S(2)}) %collective-permute-start.7) | collective-permute-done | bytes 81952 | tf_op jit(solution)/shard_map/ppermute | solution.py:563
  98.4 8.7 %collective-permute-done.10.refs_5_ = bf16[128,2048]{1,0:T(8,128)(2,1)S(1)} collective-permute-done((bf16[128,2048]{1,0:T(8,128)(2,1)}, bf16[128,2048]{1,0:T(8,128)(2,1)S(1)}, u32[]{:S(2)}, u32[]{:S(2)}) %collective-permute-start.10) | collective-permute-done | bytes 524320 | tf_op jit(solution)/shard_map/ppermute | solution.py:673
  118.7 7.9 %collective-permute-done.13.refs_1_ = bf16[128,2048]{1,0:T(8,128)(2,1)S(1)} collective-permute-done((bf16[128,2048]{1,0:T(8,128)(2,1)S(1)}, bf16[128,2048]{1,0:T(8,128)(2,1)S(1)}, u32[]{:S(2)}, u32[]{:S(2)}) %collective-permute-start.13) | collective-permute-done | bytes 524320 | tf_op jit(solution)/shard_map/ppermute | solution.py:673
  130.3 4.6 all-to-all-start.2
  141.2 15.5 %project.1 = (bf16[512,2048]{1,0:T(8,128)(2,1)}, bf16[512,1024]{1,0:T(8,128)(2,1)}, bf16[512,1024]{1,0:T(8,128)(2,1)}, f32[512,1024]{1,0:T(8,128)}, f32[512,1024...) custom-call(s32[6]{0:T(128)} %pad_add_fusion.info, ...), custom_call_target="tpu_custom_call" | custom-call | flops 1048576 | bytes 65536 | tf_op jit(solution)/shard_map/project/pallas_call | solution.py:419
  157.9 7.2 %collective-permute-start.18 = (bf16[512,160]{1,0:T(8,128)(2,1)S(1)}, bf16[512,160]{1,0:T(8,128)(2,1)S(1)}, u32[]{:S(2)}, u32[]{:S(2)}) collective-permute-start(bf16[512,160]{1,0:T(8,128)(2,1)S(1)} %convert_element_type.204), channel_id=1, source_target_pairs={{0,1},{1,0},{2,3},{3,2},{4,5},{5,4},{6,7},{7,6},{8,9},{9,8},{10,11... | collective-permute-start | bytes 491528 | tf_op jit(solution)/shard_map/ppermute | solution.py:563
  165.1 5.1 %collective-permute-done.18 = bf16[512,160]{1,0:T(8,128)(2,1)S(1)} collective-permute-done((bf16[512,160]{1,0:T(8,128)(2,1)S(1)}, bf16[512,160]{1,0:T(8,128)(2,1)S(1)}, u32[]{:S(2)}, u32[]{:S(2)}) %collective-permute-start.18) | collective-permute-done | bytes 163872 | tf_op jit(solution)/shard_map/ppermute | solution.py:563
  172.1 12.1 %collective-permute-done.19 = bf16[512,160]{1,0:T(8,128)(2,1)S(1)} collective-permute-done((bf16[512,160]{1,0:T(8,128)(2,1)S(1)}, bf16[512,160]{1,0:T(8,128)(2,1)S(1)}, u32[]{:S(2)}, u32[]{:S(2)}) %collective-permute-start.19) | collective-permute-done | bytes 163872 | tf_op jit(solution)/shard_map/ppermute | solution.py:563
  189.6 19.7 %scan_forward.1 = (f32[512,1024]{1,0:T(8,128)S(1)}, f32[8,16,520,128]{3,2,1,0:T(8,128)}) custom-call(f32[512,33]{1,0:T(8,128)S(1)} %pad_maximum_fusion.1.bc, bf16[512,128]{1,0:T(8,128)(2,1)S(1)} %slice.130.rank, bf16[128,1024]{1,0:T(8,128)(2,1)S(1)} %slice.111.dt_w, f32[1,1024]{1,0:T(1,128)S(1)} %get-tuple-element.340.dt_b, bf16[512,1024]{1,0:T(8,128)(2,1)S(1)} %copy-done.2, ...), custom_call_target="tpu_custom_call" | custom-call | flops 1048576 | bytes 65536 | tf_op jit(solution)/shard_map/scan_forward/pallas_call | solution.py:82
  210.7 22.1 %gate_block.1 = (bf16[512,1024]{1,0:T(8,128)(2,1)}, bf16[512,2048]{1,0:T(8,128)(2,1)}, f32[512,1024]{1,0:T(8,128)}, bf16[512,1024]{1,0:T(8,128)(2,1)}, bf16[512,...) custom-call(s32[6]{0:T(128)} %pad_add_fusion.info, ...), custom_call_target="tpu_custom_call" | custom-call | flops 1048576 | bytes 65536 | tf_op jit(solution)/shard_map/gate_block/pallas_call | solution.py:479
  258.5 6.9 %fusion.27 = f32[512,2048]{1,0:T(8,128)} fusion(bf16[512,1024]{1,0:T(8,128)(2,1)} %get-tuple-element.256, bf16[2048,1024]{1,0:T(8,128)(2,1)} %get-tuple-element.275), kind=kOutput, calls=%fused_computation.106 | convolution fusion | flops 2147483648 | bytes 9437184 | tf_op jit(solution)/shard_map/dot_general | solution.py:690
  269.6 40.0 %scan_backward.1 = (f32[512,160]{1,0:T(8,128)}, f32[512,1024]{1,0:T(8,128)}, f32[128,1024]{1,0:T(8,128)}, f32[2,1024]{1,0:T(2,128)}, f32[128,128]{1,0:T(8,128)}) custom-call(f32[512,33]{1,0:T(8,128)} %copy-done.7, bf16[512,128]{1,0:T(8,128)(2,1)} %copy-done.11, bf16[128,1024]{1,0:T(8,128)(2,1)} %copy-done.8, f32[1,1024]{1,0:T(1,128)} %copy-done.14, ...), custom_call_target="tpu_custom_call" | custom-call | flops 1048576 | bytes 65536 | tf_op jit(solution)/shard_map/scan_backward/pallas_call | solution.py:206
  330.4 19.6 %collective-permute-done.29 = bf16[512,160]{1,0:T(8,128)(2,1)S(1)} collective-permute-done((bf16[512,160]{1,0:T(8,128)(2,1)S(1)}, bf16[512,160]{1,0:T(8,128)(2,1)S(1)}, u32[]{:S(2)}, u32[]{:S(2)}) %collective-permute-start.29) | collective-permute-done | bytes 163872 | tf_op jit(solution)/shard_map/ppermute | solution.py:563
  350.1 7.0 %conv_back.1 = (bf16[512,1024]{1,0:T(8,128)(2,1)S(1)}, f32[160,1024]{1,0:T(8,128)S(1)}, f32[8,1024]{1,0:T(8,128)S(1)}) custom-call(s32[6]{0:T(128)S(1)} %copy-done.15, bf16[512,160]{1,0:T(8,128)(2,1)S(1)} %add_convert_fusion.3.gp, f32[512,1024]{1,0:T(8,128)S(1)} %copy-done.9, bf16[160,1024]{1,0:T(8,128)(2,1)S(1)} %copy-done.6, ...), custom_call_target="tpu_custom_call" | custom-call | flops 1048576 | bytes 65536 | tf_op jit(solution)/shard_map/conv_back/pallas_call | solution.py:545
  357.2 4.7 %fusion.29 = f32[512,2048]{1,0:T(8,128)S(1)} fusion(bf16[512,1024]{1,0:T(8,128)(2,1)S(1)} %get-tuple-element.281, bf16[2048,1024]{1,0:T(8,128)(2,1)} %get-tuple-element.282), kind=kOutput, calls=%fused_computation.108 | convolution fusion | flops 2147483648 | bytes 9437184 | tf_op jit(solution)/shard_map/dot_general | solution.py:690
  382.0 5.0 %add_convert_fusion = bf16[1024,1024]{1,0:T(8,128)(2,1)} fusion(f32[1024,1024]{1,0:T(8,128)} %fusion.28, bf16[1024,1024]{1,0:T(8,128)(2,1)} %collective-permute-done.32), kind=kLoop, calls=%fused_computation | loop fusion | flops 3145728 | bytes 8388608 | tf_op jit(solution)/shard_map/convert_element_type | solution.py:839
  387.0 8.4 %collective-permute-done.35 = bf16[128,2048]{1,0:T(8,128)(2,1)} collective-permute-done((bf16[128,2048]{1,0:T(8,128)(2,1)S(1)}, bf16[128,2048]{1,0:T(8,128)(2,1)}, u32[]{:S(2)}, u32[]{:S(2)}) %collective-permute-start.35) | collective-permute-done | bytes 524320 | tf_op jit(solution)/shard_map/ppermute | solution.py:563
  410.0 17.7 %collective-permute-done.38 = bf16[320,128]{1,0:T(8,128)(2,1)S(1)} collective-permute-done((bf16[320,128]{1,0:T(8,128)(2,1)S(1)}, bf16[320,128]{1,0:T(8,128)(2,1)S(1)}, u32[]{:S(2)}, u32[]{:S(2)}) %collective-permute-start.38) | collective-permute-done | bytes 81952 | tf_op jit(solution)/shard_map/ppermute | solution.py:563
  432.0 12.5 %all-to-all-start.6 = ((bf16[4,64,1024]{2,1,0:T(8,128)(2,1)}), bf16[4,64,1024]{2,1,0:T(8,128)(2,1)S(1)}, u32[]{:S(2)}, u32[]{:S(2)}) async-start(bf16[4,64,1024]{2,1,0:T(8,128)(2,1)} %bitcast.140), calls=%async_computation.6 | async-start | bytes 1048576 | tf_op jit(solution)/shard_map/all_to_all | solution.py:576
  451.1 7.5 %all-to-all-done.6.inner = bf16[4,64,1024]{2,1,0:T(8,128)(2,1)S(1)} async-done(((bf16[4,64,1024]{2,1,0:T(8,128)(2,1)}), bf16[4,64,1024]{2,1,0:T(8,128)(2,1)S(1)}, u32[]{:S(2)}, u32[]{:S(2)}) %all-to-all-start.6) | async-done | bytes 524320 | tf_op jit(solution)/shard_map/all_to_all | solution.py:576
  (296 shorter events, 160.7 us)
Async XLA Ops:
  9.7 43.5 %all-to-all-start = ((bf16[4,128,1024]{2,1,0:T(8,128)(2,1)}), bf16[4,128,1024]{2,1,0:T(8,128)(2,1)S(1)}, u32[]{:S(2)}, u32[]{:S(2)}) async-start(bf16[4,128,1024]{2,1,0:T(8,128)(2,1)} %split_columns.1), calls=%async_computation | async-start | bytes 2097152 | tf_op jit(solution)/shard_map/all_to_all | solution.py:576
  16.2 37.0 %collective-permute-start = (bf16[128,2048]{1,0:T(8,128)(2,1)S(1)}, bf16[128,2048]{1,0:T(8,128)(2,1)S(1)}, u32[]{:S(2)}, u32[]{:S(2)}) collective-permute-start(bf16[128,2048]{1,0:T(8,128)(2,1)S(1)} %copy-done.18), channel_id=1, source_target_pairs={{3,2},{2,1},{1,0},{7,6},{6,5},{5,4},{11,10},{10,9},{9,8},{15,14},{... | collective-permute-start | bytes 1572872 | tf_op jit(solution)/shard_map/ppermute | solution.py:673
  17.4 35.7 %collective-permute-start.1 = (bf16[128,2048]{1,0:T(8,128)(2,1)S(1)}, bf16[128,2048]{1,0:T(8,128)(2,1)S(1)}, u32[]{:S(2)}, u32[]{:S(2)}) collective-permute-start(bf16[128,2048]{1,0:T(8,128)(2,1)S(1)} %copy-done.18), channel_id=1, source_target_pairs={{0,1},{1,2},{2,3},{4,5},{5,6},{6,7},{8,9},{9,10},{10,11},{12,13},{... | collective-permute-start | bytes 1572872 | tf_op jit(solution)/shard_map/ppermute | solution.py:673
  22.1 26.4 %collective-permute-start.2 = (bf16[64]{0:T(256)(128)(2,1)S(1)}, bf16[64]{0:T(256)(128)(2,1)S(1)}, u32[]{:S(2)}, u32[]{:S(2)}) collective-permute-start(bf16[64]{0:T(256)(128)(2,1)S(1)} %copy-done.50), channel_id=1, source_target_pairs={{0,1},{1,2},{2,3},{3,0},{4,5},{5,6},{6,7},{7,4},{8,9},{9,10},{10,1... | collective-permute-start | bytes 392 | tf_op jit(solution)/shard_map/ppermute | solution.py:568
  24.1 29.1 %collective-permute-start.3 = (bf16[64]{0:T(256)(128)(2,1)S(1)}, bf16[64]{0:T(256)(128)(2,1)S(1)}, u32[]{:S(2)}, u32[]{:S(2)}) collective-permute-start(bf16[64]{0:T(256)(128)(2,1)S(1)} %copy-done.50), channel_id=1, source_target_pairs={{0,2},{1,3},{2,0},{3,1},{4,6},{5,7},{6,4},{7,5},{8,10},{9,11},{10,... | collective-permute-start | bytes 392 | tf_op jit(solution)/shard_map/ppermute | solution.py:568
  25.1 28.1 %collective-permute-start.4 = (bf16[64]{0:T(256)(128)(2,1)S(1)}, bf16[64]{0:T(256)(128)(2,1)S(1)}, u32[]{:S(2)}, u32[]{:S(2)}) collective-permute-start(bf16[64]{0:T(256)(128)(2,1)S(1)} %copy-done.50), channel_id=1, source_target_pairs={{0,3},{1,0},{2,1},{3,2},{4,7},{5,4},{6,5},{7,6},{8,11},{9,8},{10,9... | collective-permute-start | bytes 392 | tf_op jit(solution)/shard_map/ppermute | solution.py:568
  56.1 51.9 %all-to-all-start.1 = ((bf16[4,256,1024]{2,1,0:T(8,128)(2,1)}), bf16[4,256,1024]{2,1,0:T(8,128)(2,1)S(1)}, u32[]{:S(2)}, u32[]{:S(2)}) async-start(bf16[4,256,1024]{2,1,0:T(8,128)(2,1)} %broadcast_in_dim.42), calls=%async_computation.1 | async-start | bytes 4194304 | tf_op jit(solution)/shard_map/all_to_all | solution.py:580
  59.8 150.8 %all-gather.2.cloned.1.call-start = ((), (), s32[]{:S(2)}) async-start(), calls=%async_computation.7 | async-start | bytes 4718592 | tf_op jit(solution)/shard_map/all_gather | solution.py:725
  60.6 33.2 %collective-permute-start.5 = (bf16[128,2048]{1,0:T(8,128)(2,1)S(1)}, bf16[128,2048]{1,0:T(8,128)(2,1)}, u32[]{:S(2)}, u32[]{:S(2)}) collective-permute-start(bf16[128,2048]{1,0:T(8,128)(2,1)S(1)} %collective-permute-done.refs_1_), channel_id=1, source_target_pairs={{2,1},{1,0},{6,5},{5,4},{10,9},{9,8},{14,13},{13,12},{18,17},{17,1... | collective-permute-start | bytes 1572872 | tf_op jit(solution)/shard_map/ppermute | solution.py:673
  61.9 31.9 %collective-permute-start.6 = (bf16[128,2048]{1,0:T(8,128)(2,1)}, bf16[128,2048]{1,0:T(8,128)(2,1)}, u32[]{:S(2)}, u32[]{:S(2)}) collective-permute-start(bf16[128,2048]{1,0:T(8,128)(2,1)} %copy-done.35), channel_id=1, source_target_pairs={{1,2},{2,3},{5,6},{6,7},{9,10},{10,11},{13,14},{14,15},{17,18},{18... | collective-permute-start | bytes 1572872 | tf_op jit(solution)/shard_map/ppermute | solution.py:673
  63.3 28.7 %collective-permute-start.7 = (bf16[320,128]{1,0:T(8,128)(2,1)S(1)}, bf16[320,128]{1,0:T(8,128)(2,1)S(1)}, u32[]{:S(2)}, u32[]{:S(2)}) collective-permute-start(bf16[320,128]{1,0:T(8,128)(2,1)S(1)} %fusion.15), channel_id=1, source_target_pairs={{0,8},{4,12},{8,0},{12,4},{16,24},{20,28},{24,16},{28,20},{1,9},{5... | collective-permute-start | bytes 245768 | tf_op jit(solution)/shard_map/ppermute | solution.py:563
  65.3 26.7 %collective-permute-start.8 = (bf16[320,128]{1,0:T(8,128)(2,1)S(1)}, bf16[320,128]{1,0:T(8,128)(2,1)S(1)}, u32[]{:S(2)}, u32[]{:S(2)}) collective-permute-start(bf16[320,128]{1,0:T(8,128)(2,1)S(1)} %fusion.15), channel_id=1, source_target_pairs={{0,16},{4,20},{8,24},{12,28},{16,0},{20,4},{24,8},{28,12},{1,17},{... | collective-permute-start | bytes 245768 | tf_op jit(solution)/shard_map/ppermute | solution.py:563
  66.8 27.0 %collective-permute-start.9 = (bf16[320,128]{1,0:T(8,128)(2,1)S(1)}, bf16[320,128]{1,0:T(8,128)(2,1)S(1)}, u32[]{:S(2)}, u32[]{:S(2)}) collective-permute-start(bf16[320,128]{1,0:T(8,128)(2,1)S(1)} %fusion.15), channel_id=1, source_target_pairs={{0,24},{4,28},{8,16},{12,20},{16,8},{20,12},{24,0},{28,4},{1,25},{... | collective-permute-start | bytes 245768 | tf_op jit(solution)/shard_map/ppermute | solution.py:563
  130.3 54.0 %all-to-all-start.2 = ((bf16[4,256,1024]{2,1,0:T(8,128)(2,1)}), bf16[4,256,1024]{2,1,0:T(8,128)(2,1)}, u32[]{:S(2)}, u32[]{:S(2)}) async-start(bf16[4,256,1024]{2,1,0:T(8,128)(2,1)} %broadcast_in_dim.46), calls=%async_computation.2 | async-start | bytes 4194304 | tf_op jit(solution)/shard_map/all_to_all | solution.py:580
  184.3 26.4 %collective-permute-start.22 = (bf16[4,256,1024]{2,1,0:T(8,128)(2,1)}, bf16[4,256,1024]{2,1,0:T(8,128)(2,1)}, u32[]{:S(2)}, u32[]{:S(2)}) collective-permute-start(bf16[4,256,1024]{2,1,0:T(8,128)(2,1)} %all-to-all-done.2.refs_7_), channel_id=1, source_target_pairs={{0,4},{4,0},{8,12},{12,8},{16,20},{20,16},{24,28},{28,24},{1,5},{5... | collective-permute-start | bytes 6291464 | tf_op jit(solution)/shard_map/ppermute | solution.py:563
  253.3 57.7 %collective-permute-start.27 = (bf16[512,2048]{1,0:T(8,128)(2,1)}, bf16[512,2048]{1,0:T(8,128)(2,1)}, u32[]{:S(2)}, u32[]{:S(2)}) collective-permute-start(bf16[512,2048]{1,0:T(8,128)(2,1)} %convolution_convert_fusion), channel_id=1, source_target_pairs={{0,4},{4,0},{8,12},{12,8},{16,20},{20,16},{24,28},{28,24},{1,5},{5... | collective-permute-start | bytes 6291464 | tf_op jit(solution)/shard_map/ppermute | solution.py:563
  253.3 56.3 %all-to-all-start.3 = ((bf16[4,256,1024]{2,1,0:T(8,128)(2,1)}), bf16[4,256,1024]{2,1,0:T(8,128)(2,1)S(1)}, u32[]{:S(2)}, u32[]{:S(2)}) async-start(bf16[4,256,1024]{2,1,0:T(8,128)(2,1)} %bitcast.136), calls=%async_computation.3 | async-start | bytes 4194304 | tf_op jit(solution)/shard_map/all_to_all | solution.py:580
  265.4 49.0 %collective-permute-start.25 = (bf16[128,2048]{1,0:T(8,128)(2,1)}, bf16[128,2048]{1,0:T(8,128)(2,1)}, u32[]{:S(2)}, u32[]{:S(2)}) collective-permute-start(bf16[128,2048]{1,0:T(8,128)(2,1)} %get-tuple-element.264), channel_id=1, source_target_pairs={{0,2},{1,3},{2,0},{3,1},{4,6},{5,7},{6,4},{7,5},{8,10},{9,11},{10,... | collective-permute-start | bytes 1572872 | tf_op jit(solution)/shard_map/ppermute | solution.py:568
  266.8 47.7 %collective-permute-start.26 = (bf16[128,2048]{1,0:T(8,128)(2,1)}, bf16[128,2048]{1,0:T(8,128)(2,1)}, u32[]{:S(2)}, u32[]{:S(2)}) collective-permute-start(bf16[128,2048]{1,0:T(8,128)(2,1)} %get-tuple-element.265), channel_id=1, source_target_pairs={{0,3},{1,0},{2,1},{3,2},{4,7},{5,4},{6,5},{7,6},{8,11},{9,8},{10,9... | collective-permute-start | bytes 1572872 | tf_op jit(solution)/shard_map/ppermute | solution.py:568
  317.9 32.2 %collective-permute-start.30 = (bf16[128,2048]{1,0:T(8,128)(2,1)}, bf16[128,2048]{1,0:T(8,128)(2,1)}, u32[]{:S(2)}, u32[]{:S(2)}) collective-permute-start(bf16[128,2048]{1,0:T(8,128)(2,1)} %get-tuple-element.323), channel_id=1, source_target_pairs={{0,8},{4,12},{8,0},{12,4},{16,24},{20,28},{24,16},{28,20},{1,9},{5... | collective-permute-start | bytes 1572872 | tf_op jit(solution)/shard_map/ppermute | solution.py:563
  319.8 30.3 %collective-permute-start.31 = (bf16[128,2048]{1,0:T(8,128)(2,1)}, bf16[128,2048]{1,0:T(8,128)(2,1)}, u32[]{:S(2)}, u32[]{:S(2)}) collective-permute-start(bf16[128,2048]{1,0:T(8,128)(2,1)} %get-tuple-element.322), channel_id=1, source_target_pairs={{0,16},{4,20},{8,24},{12,28},{16,0},{20,4},{24,8},{28,12},{1,17},{... | collective-permute-start | bytes 1572872 | tf_op jit(solution)/shard_map/ppermute | solution.py:563
  321.3 49.4 %all-to-all-start.4 = ((bf16[4,64,1024]{2,1,0:T(8,128)(2,1)}), bf16[4,64,1024]{2,1,0:T(8,128)(2,1)S(1)}, u32[]{:S(2)}, u32[]{:S(2)}) async-start(bf16[4,64,1024]{2,1,0:T(8,128)(2,1)} %bitcast.45), calls=%async_computation.4 | async-start | bytes 1048576 | tf_op jit(solution)/shard_map/all_to_all | solution.py:576
  397.2 32.3 %all-to-all-start.5 = ((bf16[4,256,1024]{2,1,0:T(8,128)(2,1)}), bf16[4,256,1024]{2,1,0:T(8,128)(2,1)S(1)}, u32[]{:S(2)}, u32[]{:S(2)}) async-start(bf16[4,256,1024]{2,1,0:T(8,128)(2,1)} %bitcast.129), calls=%async_computation.5 | async-start | bytes 4194304 | tf_op jit(solution)/shard_map/all_to_all | solution.py:580
  432.0 26.6 %all-to-all-start.6 = ((bf16[4,64,1024]{2,1,0:T(8,128)(2,1)}), bf16[4,64,1024]{2,1,0:T(8,128)(2,1)S(1)}, u32[]{:S(2)}, u32[]{:S(2)}) async-start(bf16[4,64,1024]{2,1,0:T(8,128)(2,1)} %bitcast.140), calls=%async_computation.6 | async-start | bytes 1048576 | tf_op jit(solution)/shard_map/all_to_all | solution.py:576
  (85 other events, 1595.7 us)
Sparse Core Ops, SparseCore 0:
  62.5 50.1 all-gather.1

commit v2 on v1

v2 whole, which is shorter than its diff:
```python
import functools

import jax
import jax.numpy as jnp
from jax import lax
from jax.experimental import pallas as pl
from jax.experimental.pallas import tpu as pltpu
from jax.sharding import PartitionSpec as P

BF, F32 = jnp.bfloat16, jnp.float32
LANES, SUB = 128, 8
LN2 = 0.6931471805599453
FAR = 1.0e5
EPS = 1e-5


def small_cost(flops):
    return pl.CostEstimate(flops=flops, bytes_accessed=1 << 16, transcendentals=0)


class Small:
    def __init__(self, rank, proj, state, taps):
        self.dt_w = slice(0, rank)
        self.x_t = slice(rank, rank + proj)
        self.a_t = slice(rank + proj, rank + proj + state)
        self.rest = slice(rank + proj + state, rank + proj + state + 16)
        self.taps, self.rows = taps, rank + proj + state + 16

    def fold(self, parts):
        rows = -(-self.rows // parts)
        return rows + -rows % 16

    def vector(self, ref, at):
        return ref[self.rest, :].astype(F32)[at : at + 1, :]


def scatter_lanes(ref, value, rows):
    for k in range(value.shape[1] // LANES):
        ref[pl.ds(k, rows, stride=SUB), :] = value[:, k * LANES : (k + 1) * LANES]


def gather_lanes(ref, width, rows):
    return jnp.concatenate(
        [ref[pl.ds(k, rows, stride=SUB), :] for k in range(width // LANES)], axis=1
    )


def softplus(v):
    return jnp.maximum(v, 0.0) + jnp.log1p(jnp.exp(-jnp.abs(v)))


def forward_kernel(at, bc, rank, small, act, valid, rate2, y_out, states, h_ref, dt_s, dtu_s, y_s):
    tb, width = act.shape
    n_state = rate2.shape[0] // SUB

    @pl.when(pl.program_id(0) == 0)
    def _():
        h_ref[...] = jnp.zeros_like(h_ref)
        if width < SUB * LANES:
            dt_s[...] = jnp.zeros_like(dt_s)
            dtu_s[...] = jnp.zeros_like(dtu_s)

    dt_b = at.vector(small, at.taps + 1)
    pre = jnp.dot(rank[...], small[at.dt_w, :], preferred_element_type=F32) + dt_b
    dt = softplus(pre) * valid[...]
    scatter_lanes(dt_s, dt, tb)
    scatter_lanes(dtu_s, dt * act[...].astype(F32), tb)
    rates = [rate2[n * SUB : (n + 1) * SUB, :] for n in range(n_state)]
    first = [h_ref[n * SUB : (n + 1) * SUB, :] for n in range(n_state)]
    for n in range(n_state):
        states[0, n, 0:SUB, :] = first[n]

    def token(t, h):
        at = pl.multiple_of(t * SUB, SUB)
        dt_t = dt_s[pl.ds(at, SUB), :] + bc[t, 2 * n_state]
        dtu_t = dtu_s[pl.ds(at, SUB), :]
        new, parts = [], [None, None]
        for n in range(n_state):
            hn = jnp.exp2(dt_t * rates[n]) * h[n] + dtu_t * bc[t, n]
            states[0, n, pl.ds(at + SUB, SUB), :] = hn
            term = hn * bc[t, n_state + n]
            parts[n % 2] = term if parts[n % 2] is None else parts[n % 2] + term
            new.append(hn)
        y_s[pl.ds(at, SUB), :] = parts[0] + parts[1]
        return tuple(new)

    last = lax.fori_loop(0, tb, token, tuple(first), unroll=8)
    for n in range(n_state):
        h_ref[n * SUB : (n + 1) * SUB, :] = last[n]
    y_out[...] = gather_lanes(y_s, width, tb)


def scan_forward(at, bc, rank, small, act, valid, rate2, tb):
    slots, width = act.shape
    n_state = rate2.shape[0] // SUB
    nb = slots // tb
    whole = lambda i: (0, 0)
    row = lambda i: (i, 0)
    return pl.pallas_call(
        functools.partial(forward_kernel, at),
        grid=(nb,),
        in_specs=[
            pl.BlockSpec((tb, bc.shape[1]), row, memory_space=pltpu.SMEM),
            pl.BlockSpec((tb, rank.shape[1]), row),
            pl.BlockSpec(small.shape, whole),
            pl.BlockSpec((tb, width), row),
            pl.BlockSpec((tb, 1), row),
            pl.BlockSpec(rate2.shape, whole),
        ],
        out_specs=[
            pl.BlockSpec((tb, width), row),
            pl.BlockSpec((1, n_state, (tb + 1) * SUB, LANES), lambda i: (i, 0, 0, 0)),
        ],
        out_shape=[
            jax.ShapeDtypeStruct((slots, width), F32),
            jax.ShapeDtypeStruct((nb, n_state, (tb + 1) * SUB, LANES), F32),
        ],
        scratch_shapes=[pltpu.VMEM(rate2.shape, F32)] + [pltpu.VMEM((tb * SUB, LANES), F32)] * 3,
        compiler_params=pltpu.CompilerParams(vmem_limit_bytes=48 << 20),
        cost_estimate=small_cost(1 << 20),
        name="scan_forward",
    )(bc, rank, small, act, valid, rate2)


def backward_kernel(
    at_small, bc, rank, small, act, valid, rate2, gs, states, fold,
    part_out, gu_out, dtw_out, vec_out, rate_out,
    g_ref, dt_s, dtu_s, gs_s, gdt_s, ab_s, lam_s,
):
    tb, width = act.shape
    n_state = rate2.shape[0] // SUB
    half = n_state // 2

    @pl.when(pl.program_id(0) == 0)
    def _():
        g_ref[...] = jnp.zeros_like(g_ref)
        rate_out[...] = jnp.zeros_like(rate_out)
        vec_out[...] = jnp.zeros_like(vec_out)
        dtw_out[...] = jnp.zeros_like(dtw_out)
        if width < SUB * LANES:
            for ref in (dt_s, dtu_s, gs_s):
                ref[...] = jnp.zeros_like(ref)

    u = act[...].astype(F32)
    ok = valid[...]
    dt_b, skip = at_small.vector(small, at_small.taps + 1), at_small.vector(small, at_small.taps + 2)
    pre = jnp.dot(rank[...], small[at_small.dt_w, :], preferred_element_type=F32) + dt_b
    dt = softplus(pre) * ok
    gs_v = gs[...]
    scatter_lanes(dt_s, dt, tb)
    scatter_lanes(dtu_s, dt * u, tb)
    scatter_lanes(gs_s, gs_v, tb)

    for group in range(2):
        index = range(group * half, (group + 1) * half)
        rates = [rate2[n * SUB : (n + 1) * SUB, :] for n in index]

        def token(i, carry):
            g, acc = carry
            t = tb - 1 - i
            at = pl.multiple_of(t * SUB, SUB)
            dt_t = dt_s[pl.ds(at, SUB), :]
            dtd = dt_t + bc[t, 2 * n_state]
            gs_t = gs_s[pl.ds(at, SUB), :]
            new_g, new_acc = [], []
            gdt = ab = None
            for j, n in enumerate(index):
                lam = gs_t * bc[t, n_state + n] + g[j]
                lam_s[n, pl.ds(at, SUB), :] = lam
                back = jnp.exp2(dtd * rates[j]) * lam
                thr = back * states[0, n, pl.ds(at, SUB), :]
                gdt = thr * rates[j] if gdt is None else gdt + thr * rates[j]
                ab = lam * bc[t, n] if ab is None else ab + lam * bc[t, n]
                new_g.append(back)
                new_acc.append(acc[j] + thr * dt_t)
            if group == 0:
                gdt_s[pl.ds(at, SUB), :] = gdt
                ab_s[pl.ds(at, SUB), :] = ab
            else:
                gdt_s[pl.ds(at, SUB), :] += gdt
                ab_s[pl.ds(at, SUB), :] += ab
            return tuple(new_g), tuple(new_acc)

        start = (
            tuple(g_ref[n * SUB : (n + 1) * SUB, :] for n in index),
            tuple(rate_out[n * SUB : (n + 1) * SUB, :] for n in index),
        )
        g, acc = lax.fori_loop(0, tb, token, start, unroll=8)
        for j, n in enumerate(index):
            g_ref[n * SUB : (n + 1) * SUB, :] = g[j]
            rate_out[n * SUB : (n + 1) * SUB, :] = acc[j]

    ab = gather_lanes(ab_s, width, tb)
    gdt = gather_lanes(gdt_s, width, tb)
    gu_out[...] = gs_v * skip + dt * ab
    grad_pre = ok * (gdt * LN2 + u * ab) * jax.nn.sigmoid(pre)
    vec_out[0:1, :] += jnp.sum(grad_pre, axis=0, keepdims=True)
    vec_out[1:2, :] += jnp.sum(gs_v * u, axis=0, keepdims=True)
    low = grad_pre.astype(BF)
    dtw_out[...] += lax.dot_general(rank[...], low, (((0,), (0,)), ((), ())), preferred_element_type=F32)
    rank_w = rank.shape[1]
    part_out[:, 0:rank_w] = lax.dot_general(low, small[at_small.dt_w, :], (((1,), (1,)), ((), ())), preferred_element_type=F32)

    lane = lax.broadcasted_iota(jnp.int32, (tb, LANES), 1)
    tail = jnp.zeros((tb, LANES), F32)
    dtu_v = dtu_s[...]
    gs_l = gs_s[...]
    for n in range(n_state):
        for at, value in ((n, lam_s[n] * dtu_v), (n_state + n, states[0, n, SUB:, :] * gs_l)):
            summed = jnp.dot(fold[...], value.astype(BF), preferred_element_type=F32)
            tail = jnp.where(lane == at, jnp.sum(summed, axis=1, keepdims=True), tail)
    part_out[:, rank_w:] = tail[:, 0 : 2 * n_state]


def scan_backward(at, bc, rank, small, act, valid, rate2, gs, states, tb):
    slots, width = act.shape
    n_state = rate2.shape[0] // SUB
    nb = slots // tb
    whole = lambda i: (0, 0)
    row = lambda i: (nb - 1 - i, 0)
    rank_w = rank.shape[1]
    fold = (jnp.arange(tb * SUB)[None, :] // SUB == jnp.arange(tb)[:, None]).astype(BF)
    return pl.pallas_call(
        functools.partial(backward_kernel, at),
        grid=(nb,),
        in_specs=[
            pl.BlockSpec((tb, bc.shape[1]), row, memory_space=pltpu.SMEM),
            pl.BlockSpec((tb, rank_w), row),
            pl.BlockSpec(small.shape, whole),
            pl.BlockSpec((tb, width), row),
            pl.BlockSpec((tb, 1), row),
            pl.BlockSpec(rate2.shape, whole),
            pl.BlockSpec((tb, width), row),
            pl.BlockSpec((1, n_state, (tb + 1) * SUB, LANES), lambda i: (nb - 1 - i, 0, 0, 0)),
            pl.BlockSpec(fold.shape, whole),
        ],
        out_specs=[
            pl.BlockSpec((tb, rank_w + 2 * n_state), row),
            pl.BlockSpec((tb, width), row),
            pl.BlockSpec((rank_w, width), whole),
            pl.BlockSpec((2, width), whole),
            pl.BlockSpec(rate2.shape, whole),
        ],
        out_shape=[
            jax.ShapeDtypeStruct((slots, rank_w + 2 * n_state), F32),
            jax.ShapeDtypeStruct((slots, width), F32),
            jax.ShapeDtypeStruct((rank_w, width), F32),
            jax.ShapeDtypeStruct((2, width), F32),
            jax.ShapeDtypeStruct(rate2.shape, F32),
        ],
        scratch_shapes=[pltpu.VMEM(rate2.shape, F32)]
        + [pltpu.VMEM((tb * SUB, LANES), F32)] * 5
        + [pltpu.VMEM((n_state, tb * SUB, LANES), F32)],
        compiler_params=pltpu.CompilerParams(vmem_limit_bytes=56 << 20),
        cost_estimate=small_cost(1 << 20),
        name="scan_backward",
    )(bc, rank, small, act, valid, rate2, gs, states, fold)


def silu_grad(value, sig):
    return sig * (1.0 + value * (1.0 - sig))


def place_blocks(ref, own, other, index):
    chips = own.shape[0]
    rows = ref.shape[0] // (2 * chips)
    core = lax.rem(index, 2)
    for q in range(chips):
        ref[pl.ds(pl.multiple_of((2 * q + core) * rows, rows), rows), :] = own[q, 0:rows, :]
        ref[pl.ds(pl.multiple_of((2 * q + 1 - core) * rows, rows), rows), :] = other[q, 0:rows, :]


def read_row(ref, row, cols):
    base = pl.multiple_of(row // SUB * SUB, SUB)
    rows = ref[pl.ds(base, SUB), cols]
    mine = lax.broadcasted_iota(jnp.int32, rows.shape, 0) == row - base
    return jnp.sum(jnp.where(mine, rows, 0.0), axis=0, keepdims=True)


def add_row(ref, row, value):
    base = pl.multiple_of(row // SUB * SUB, SUB)
    rows = ref[pl.ds(base, SUB), :]
    mine = lax.broadcasted_iota(jnp.int32, rows.shape, 0) == row - base
    ref[pl.ds(base, SUB), :] = rows + jnp.where(mine, value, 0.0)


def split_kernel(n_dp, in_w, gain, out):
    rows = in_w.shape[0]
    n_line, full, width = out.shape
    owned = width // n_dp
    top = jnp.broadcast_to(gain[...].astype(F32), (full - 2 * rows, rows)).astype(in_w.dtype)
    for to in range(n_line):
        for half in range(2):
            for d in range(n_dp):
                at = ((half * n_dp + d) * n_line + to) * owned
                out[to, half * rows : (half + 1) * rows, d * owned : (d + 1) * owned] = in_w[:, at : at + owned]
        out[to, 2 * rows :, :] = jnp.zeros((full - 2 * rows, width), in_w.dtype)
        out[to, 2 * rows :, 0:rows] = top


def split_columns(in_w, gain, n_dp, n_line):
    rows, both = in_w.shape
    width = both // (2 * n_line)
    if width // n_dp % LANES:
        blocks = in_w.reshape(rows, 2, n_dp, n_line, width // n_dp).transpose(3, 1, 0, 2, 4)
        top = jnp.broadcast_to(jnp.pad(gain, (0, width - rows)), (n_line, 16, width))
        return jnp.concatenate([blocks.reshape(n_line, 2 * rows, width), top], axis=1)
    vmem = pl.BlockSpec(memory_space=pltpu.VMEM)
    return pl.pallas_call(
        functools.partial(split_kernel, n_dp),
        in_specs=[vmem] * 2,
        out_specs=vmem,
        out_shape=jax.ShapeDtypeStruct((n_line, 2 * rows + 16, width), in_w.dtype),
        cost_estimate=small_cost(1 << 10),
        name="split_columns",
    )(in_w, gain[None])


def join_kernel(n_dp, inner, gate, in_w, gain, out, gain_out):
    n_line, rows, width = inner.shape
    owned = width // n_dp
    total = jnp.zeros((rows, LANES), F32)
    for half, got in enumerate((inner, gate)):
        for line in range(n_line):
            for d in range(n_dp):
                at = ((half * n_dp + d) * n_line + line) * owned
                block = got[line, :, d * owned : (d + 1) * owned].astype(F32)
                out[:, at : at + owned] = block
                term = block * in_w[:, at : at + owned].astype(F32)
                for low in range(0, owned, LANES):
                    total = total + term[:, low : low + LANES]
    ones = jnp.ones((SUB, LANES), F32)
    sums = lax.dot_general(
        ones, total, (((1,), (1,)), ((), ())), precision=lax.Precision.HIGHEST, preferred_element_type=F32
    )
    gain_out[...] = sums[0:1, :] / gain[...].astype(F32)


def join_columns(inner, gate, in_w, gain, n_dp):
    rows, both = in_w.shape
    n_line, _, width = inner.shape
    if width // n_dp % LANES:
        blocks = jnp.stack([inner, gate]).astype(F32).reshape(2, n_line, rows, n_dp, -1)
        full = blocks.transpose(2, 0, 3, 1, 4).reshape(rows, both)
        return full, jnp.sum(full * in_w.astype(F32), axis=1) / gain.astype(F32)
    vmem = pl.BlockSpec(memory_space=pltpu.VMEM)
    full, gain_grad = pl.pallas_call(
        functools.partial(join_kernel, n_dp),
        in_specs=[vmem] * 4,
        out_specs=[vmem] * 2,
        out_shape=[jax.ShapeDtypeStruct((rows, both), F32), jax.ShapeDtypeStruct((1, rows), F32)],
        cost_estimate=small_cost(1 << 10),
        name="join_columns",
    )(inner, gate, in_w, gain[None])
    return full, gain_grad[0]


def column_block(width, slots):
    return 256 if width % 256 == 0 and slots <= 1024 else LANES


def from_place(place, steps, n_line):
    return lax.rem(place - steps + n_line, n_line)


def outer(kept, sent, right, kept_out, sent_out):
    rows = min(256, kept.shape[1])

    @pl.loop(0, kept.shape[1] // rows)
    def _(r):
        at = pl.ds(pl.multiple_of(r * rows, rows), rows)
        for left, out in ((kept, kept_out), (sent, sent_out)):
            found = lax.dot_general(left[:, at], right[...], (((0,), (0,)), ((), ())), preferred_element_type=F32)
            out[at, :] = found.astype(out.dtype)


def outer_kernel(kept, sent, right, kept_out, sent_out):
    outer(kept, sent, right, kept_out, sent_out)


def outer_product(kept, sent, right):
    shape = (kept.shape[1], right.shape[1])
    vmem = pl.BlockSpec(memory_space=pltpu.VMEM)
    return pl.pallas_call(
        outer_kernel,
        in_specs=[vmem] * 3,
        out_specs=[vmem] * 2,
        out_shape=[jax.ShapeDtypeStruct(shape, BF)] * 2,
        compiler_params=pltpu.CompilerParams(vmem_limit_bytes=48 << 20),
        cost_estimate=small_cost(1 << 20),
        name="outer_product",
    )(kept, sent, right)


def to_shifts(source, outs, place):
    rows = outs[0].shape[0]
    for s, out in enumerate(outs):
        at = pl.multiple_of(lax.rem(place + s, len(outs)) * rows, rows)
        out[...] = source[pl.ds(at, rows), :]


def split_cores(ref, kept, sent, index, n_dp):
    size = ref.shape[1] // n_dp
    core = lax.rem(index, 2)
    for q in range(kept.shape[1] // size):
        cols = slice(q * size, (q + 1) * size)
        kept[:, cols] = ref[:, pl.ds(pl.multiple_of((2 * q + core) * size, size), size)]
        sent[:, cols] = ref[:, pl.ds(pl.multiple_of((2 * q + 1 - core) * size, size), size)]


def project_kernel(n_line, n_dp, at, info, *refs):
    toks, refs = refs[:n_line], refs[n_line:]
    own, other, small, allowed, gain, normed, kept, sent, inner, conv_out, activ, part32, w_nat, ext = refs
    held, model = toks[0].shape
    slots = held * n_line
    width = w_nat.shape[1]
    taps = at.taps
    rim = taps - 1
    rows_dp = model // n_dp
    core = lax.rem(info[0], 2)
    for q in range(n_dp // 2):
        for blocks, d in ((own, 2 * q + core), (other, 2 * q + 1 - core)):
            found = blocks[q, rows_dp:, 0:rows_dp].astype(F32)[0:1, :]
            gain[:, pl.ds(pl.multiple_of(d * rows_dp, rows_dp), rows_dp)] = found
    step = 32
    for s, tok in enumerate(toks):
        base = from_place(info[1], s, n_line) * held

        @pl.loop(0, held // step)
        def _(i):
            x = tok[pl.ds(pl.multiple_of(i * step, step), step), :].astype(F32)
            scale = lax.rsqrt(jnp.mean(x * x, axis=1, keepdims=True) + EPS)
            normed[pl.ds(pl.multiple_of(base + i * step, step), step), :] = (x * scale * gain[...]).astype(BF)

    split_cores(normed, kept, sent, info[0], n_dp)
    place_blocks(w_nat, own, other, info[0])
    cb = column_block(width, slots)

    @pl.loop(0, width // cb)
    def _(c):
        cols = pl.ds(pl.multiple_of(c * cb, cb), cb)
        inner[:, cols] = jnp.dot(normed[...], w_nat[:, cols], preferred_element_type=F32)
        vectors = small[at.rest, cols].astype(F32)
        for f in range(n_line):
            rows = slice(f * held, (f + 1) * held)
            ext[SUB : SUB + held, :] = inner[rows, cols]
            for k in range(1, rim + 1):
                if f == 0:
                    ext[SUB - k : SUB - k + 1, :] = jnp.zeros((1, cb), F32)
                else:
                    ext[SUB - k : SUB - k + 1, :] = read_row(inner, (f - 1) * held + info[1 + f] - k, cols)
            total = vectors[taps : taps + 1, :]
            for lag in range(taps):
                tapped = ext[SUB - lag : SUB - lag + held, :]
                total = total + vectors[rim - lag : rim - lag + 1, :] * tapped * allowed[rows, lag : lag + 1]
            conv_out[rows, cols] = total
            activ[rows, cols] = (total * jax.nn.sigmoid(total)).astype(BF)

    part32[...] = lax.dot_general(
        activ[...], small[at.x_t, :], (((1,), (1,)), ((), ())), preferred_element_type=F32
    )


def project(info, n_line, n_dp, toks, own, other, at, small, allowed):
    held, model = toks[0].shape
    slots = held * n_line
    width, proj = small.shape[1], at.x_t.stop - at.x_t.start
    vmem = pl.BlockSpec(memory_space=pltpu.VMEM)
    shapes = [
        ((1, model), F32), ((slots, model), BF), ((slots, model // 2), BF), ((slots, model // 2), BF),
        ((slots, width), F32), ((slots, width), F32), ((slots, width), BF), ((slots, proj), F32), ((model, width), BF),
    ]
    return pl.pallas_call(
        functools.partial(project_kernel, n_line, n_dp, at),
        in_specs=[pl.BlockSpec(memory_space=pltpu.SMEM)] + [vmem] * (4 + len(toks)),
        out_specs=[vmem] * len(shapes),
        out_shape=[jax.ShapeDtypeStruct(s, t) for s, t in shapes],
        scratch_shapes=[pltpu.VMEM((SUB + slots // n_line, column_block(width, slots)), F32)],
        compiler_params=pltpu.CompilerParams(vmem_limit_bytes=56 << 20),
        cost_estimate=small_cost(1 << 20),
        name="project",
    )(info, *toks, own, other, small, allowed)


def gate_kernel(n_line, n_dp, at, info, own, other, normed, y, act, small, *refs):
    out_own, out_other, refs = refs[: n_dp // 2], refs[n_dp // 2 : n_dp], refs[n_dp:]
    branches, refs = refs[:n_line], refs[n_line:]
    gate, gated, w_nat, o_nat, *halves, branch = refs
    slots, width = y.shape
    model = normed.shape[1]
    place_blocks(w_nat, own, other, info[0])
    rows = width // n_dp
    core, chip = lax.rem(info[0], 2), lax.div(info[0], 2)
    for u in range(n_dp // 2):
        first = 2 * jnp.bitwise_xor(chip, u)
        o_nat[pl.ds(pl.multiple_of((first + core) * rows, rows), rows), :] = out_own[u][0:rows, :]
        o_nat[pl.ds(pl.multiple_of((first + 1 - core) * rows, rows), rows), :] = out_other[u][0:rows, :]
    cb = column_block(width, slots)

    @pl.loop(0, width // cb)
    def _(c):
        cols = pl.ds(pl.multiple_of(c * cb, cb), cb)
        value = jnp.dot(normed[...], w_nat[:, cols], preferred_element_type=F32)
        gate[:, cols] = value
        skip = small[at.rest, cols].astype(F32)[at.taps + 2 : at.taps + 3, :]
        scan_out = y[:, cols] + skip * act[:, cols].astype(F32)
        gated[:, cols] = (scan_out * value * jax.nn.sigmoid(value)).astype(BF)

    mb = column_block(model, slots)

    @pl.loop(0, model // mb)
    def _(c):
        cols = pl.ds(pl.multiple_of(c * mb, mb), mb)
        branch[:, cols] = jnp.dot(gated[...], o_nat[:, cols], preferred_element_type=F32).astype(BF)

    to_shifts(branch, branches, info[1])
    if halves:
        split_cores(gated, *halves, info[0], n_dp)


def gate_block(info, n_line, n_dp, own, other, out_own, out_other, normed, y, act, at, small):
    slots, width = y.shape
    model = normed.shape[1]
    vmem = pl.BlockSpec(memory_space=pltpu.VMEM)
    shapes = [((slots // n_line, model), BF)] * n_line
    shapes += [((slots, width), F32), ((slots, width), BF), ((model, width), BF), ((width, model), BF)]
    if width // n_dp % LANES == 0:
        shapes += [((slots, width // 2), BF)] * 2
    outs = pl.pallas_call(
        functools.partial(gate_kernel, n_line, n_dp, at),
        in_specs=[pl.BlockSpec(memory_space=pltpu.SMEM)] + [vmem] * (6 + n_dp),
        out_specs=[vmem] * len(shapes),
        out_shape=[jax.ShapeDtypeStruct(s, t) for s, t in shapes],
        scratch_shapes=[pltpu.VMEM((slots, model), BF)],
        compiler_params=pltpu.CompilerParams(vmem_limit_bytes=58 << 20),
        cost_estimate=small_cost(1 << 20),
        name="gate_block",
    )(info, own, other, normed, y, act, small, *out_own, *out_other)
    branches, (gate, gated, w_nat, o_nat), halves = list(outs[:n_line]), outs[n_line : n_line + 4], outs[n_line + 4 :]
    return branches, gate, w_nat, o_nat, *(halves or cores(gated, 1))


def gate_back_kernel(n_line, at, info, *refs):
    cots, refs = refs[:n_line], refs[n_line:]
    o_nat, gate, y, act, small, valid, normed_k, normed_s, gs, grad_gate, dout, gate_k, gate_s = refs
    slots, width = y.shape
    held, model = cots[0].shape
    for s, cot in enumerate(cots):
        rows = pl.ds(pl.multiple_of(from_place(info[1], s, n_line) * held, held), held)
        dout[rows, :] = (cot[...].astype(F32) * valid[rows, :]).astype(BF)

    cb = column_block(width, slots)

    @pl.loop(0, width // cb)
    def _(c):
        cols = pl.ds(pl.multiple_of(c * cb, cb), cb)
        grad = lax.dot_general(dout[...], o_nat[cols, :], (((1,), (1,)), ((), ())), preferred_element_type=F32)
        value = gate[:, cols]
        sig = jax.nn.sigmoid(value)
        skip = small[at.rest, cols].astype(F32)[at.taps + 2 : at.taps + 3, :]
        scan_out = y[:, cols] + skip * act[:, cols].astype(F32)
        gs[:, cols] = grad * value * sig
        grad_gate[:, cols] = (grad * scan_out * silu_grad(value, sig)).astype(BF)

    outer(normed_k, normed_s, grad_gate, gate_k, gate_s)


def gate_back(info, n_line, cots, o_nat, gate, y, act, at, small, valid, normed_k, normed_s):
    slots, width = y.shape
    model = o_nat.shape[1]
    vmem = pl.BlockSpec(memory_space=pltpu.VMEM)
    shapes = [((slots, width), F32), ((slots, width), BF), ((slots, model), BF)]
    shapes += [((model // 2, width), BF)] * 2
    return pl.pallas_call(
        functools.partial(gate_back_kernel, n_line, at),
        in_specs=[pl.BlockSpec(memory_space=pltpu.SMEM)] + [vmem] * (8 + len(cots)),
        out_specs=[vmem] * len(shapes),
        out_shape=[jax.ShapeDtypeStruct(s, t) for s, t in shapes],
        compiler_params=pltpu.CompilerParams(vmem_limit_bytes=58 << 20),
        cost_estimate=small_cost(1 << 20),
        name="gate_back",
    )(info, *cots, o_nat, gate, y, act, small, valid, normed_k, normed_s)


def together(slots):
    return slots <= 1024


def conv_back_kernel(n_line, n_dp, at, info, gp, gu, small, act, conv_out, inner, allowed, dtw, rate_grad, scan_vec,
                     w_nat, normed_gate, *refs):
    halves, refs = (refs[:2], refs[2:]) if together(gu.shape[0]) else ((), refs)
    grads, refs = refs[:n_line], refs[n_line:]
    gi_low, kept, sent, *products, x_grad, vec, ext, gi, tail, grad_normed, column = refs
    slots, width = gu.shape
    held = slots // n_line
    taps = at.taps
    rim = taps - 1
    cb = column_block(width, slots)
    x_grad[...] = lax.dot_general(gp[...], act[...], (((0,), (0,)), ((), ())), preferred_element_type=F32)
    vec[...] = jnp.zeros_like(vec)
    for lag in range(taps):
        tail[lag, held : held + SUB, :] = jnp.zeros((SUB, cb), F32)

    @pl.loop(0, width // cb)
    def _(c):
        cols = pl.ds(pl.multiple_of(c * cb, cb), cb)
        vectors = small[at.rest, cols].astype(F32)
        for f in range(n_line - 1, -1, -1):
            rows = slice(f * held, (f + 1) * held)
            ext[SUB : SUB + held, :] = inner[rows, cols]
            for k in range(1, rim + 1):
                if f == 0:
                    ext[SUB - k : SUB - k + 1, :] = jnp.zeros((1, cb), F32)
                else:
                    ext[SUB - k : SUB - k + 1, :] = read_row(inner, (f - 1) * held + info[1 + f] - k, cols)
            grad = gu[rows, cols] + jnp.dot(gp[rows, :], small[at.x_t, cols], preferred_element_type=F32)
            co = conv_out[rows, cols]
            grad = grad * silu_grad(co, jax.nn.sigmoid(co))
            vec[taps : taps + 1, cols] += jnp.sum(grad, axis=0, keepdims=True)
            for lag in range(taps):
                weighted = grad * allowed[rows, lag : lag + 1]
                vec[rim - lag : rim - lag + 1, cols] += jnp.sum(
                    weighted * ext[SUB - lag : SUB - lag + held, :], axis=0, keepdims=True
                )
                tail[lag, 0:held, :] = weighted * vectors[rim - lag : rim - lag + 1, :]
            total = tail[0, 0:held, :]
            for lag in range(1, taps):
                total = total + tail[lag, lag : lag + held, :]
            gi[rows, :] = total
            if f + 1 < n_line:
                for k in range(1, rim + 1):
                    add_row(gi, f * held + info[2 + f] - k, gi[slots + k : slots + k + 1, :])
            for k in range(1, rim + 1):
                row = tail[k, 0:1, :]
                for lag in range(k + 1, taps):
                    row = row + tail[lag, lag - k : lag - k + 1, :]
                gi[slots + k : slots + k + 1, :] = row
        gi_low[:, cols] = gi[0:slots, :].astype(BF)

    model = w_nat.shape[0]
    mb = column_block(model, slots)

    @pl.loop(0, model // mb)
    def _(c):
        cols = pl.ds(pl.multiple_of(c * mb, mb), mb)
        found = lax.dot_general(gi_low[...], w_nat[cols, :], (((1,), (1,)), ((), ())), preferred_element_type=F32)
        grad_normed[:, cols] = (found + normed_gate[:, cols]).astype(BF)

    to_shifts(grad_normed, grads, info[1])
    if halves:
        outer(*halves, gi_low, *products)
    vec[taps + 1 : taps + 3, :] = scan_vec[...]
    owned = width // n_dp
    if kept.shape[0] == 1:
        kept[0, at.dt_w, :], kept[0, at.x_t, :], kept[0, at.a_t, :], kept[0, at.rest, :] = (
            dtw[...], x_grad[...], rate_grad[...], vec[...]
        )
        return
    core = lax.rem(info[0], 2)
    fold = kept.shape[1]
    for q in range(n_dp // 2):
        for ref, d in ((kept, 2 * q + core), (sent, 2 * q + 1 - core)):
            cols = pl.ds(pl.multiple_of(d * owned, owned), owned)
            for rows, source in ((at.dt_w, dtw), (at.x_t, x_grad), (at.a_t, rate_grad), (at.rest, vec)):
                column[rows, :] = source[:, cols]
            for b in range(width // owned):
                ref[q, :, b * owned : (b + 1) * owned] = column[b * fold : (b + 1) * fold, :].astype(ref.dtype)


def conv_back(info, n_line, n_dp, gp, gu, at, small, act, conv_out, inner, allowed, dtw, rate_grad, scan_vec, w_nat, normed_gate,
              normed_k, normed_s):
    slots, width = gu.shape
    held = slots // n_line
    cb = column_block(width, slots)
    owned = width // n_dp
    tiles = owned % LANES == 0
    vmem = pl.BlockSpec(memory_space=pltpu.VMEM)
    fold = at.fold(n_dp)
    shape = (n_dp // 2, fold, width) if tiles else (1, at.rows, width)
    model = w_nat.shape[0]
    halves = [normed_k, normed_s] if together(slots) else []
    outs = pl.pallas_call(
        functools.partial(conv_back_kernel, n_line, n_dp, at),
        in_specs=[pl.BlockSpec(memory_space=pltpu.SMEM)] + [vmem] * (12 + len(halves)),
        out_specs=[vmem] * (n_line + 3 + len(halves)),
        out_shape=[jax.ShapeDtypeStruct((held, model), BF)] * n_line
        + [
            jax.ShapeDtypeStruct((slots, width), BF),
            jax.ShapeDtypeStruct(shape, F32),
            jax.ShapeDtypeStruct(shape if tiles else (SUB, LANES), BF if tiles else F32),
        ]
        + [jax.ShapeDtypeStruct((model // 2, width), BF)] * len(halves),
        scratch_shapes=[
            pltpu.VMEM((at.x_t.stop - at.x_t.start, width), F32),
            pltpu.VMEM((16, width), F32),
            pltpu.VMEM((SUB + held, cb), F32),
            pltpu.VMEM((slots + SUB, cb), F32),
            pltpu.VMEM((at.taps, held + SUB, cb), F32),
            pltpu.VMEM((slots, model), BF),
            pltpu.VMEM((n_dp * fold, owned), F32),
        ],
        compiler_params=pltpu.CompilerParams(vmem_limit_bytes=58 << 20),
        cost_estimate=small_cost(1 << 20),
        name="conv_back",
    )(info, gp, gu, small, act, conv_out, inner, allowed, dtw, rate_grad, scan_vec, w_nat, normed_gate, *halves)
    grads, (gi_low, kept, sent, *products) = outs[:n_line], outs[n_line:]
    if not products:
        products = outer_product(normed_k, normed_s, gi_low)
    if not tiles:
        kept, sent = [
            part.reshape(at.rows, n_dp // 2, owned).transpose(1, 0, 2) for part in cores(kept[0], 1)
        ]
    return list(grads), *products, kept, sent.astype(BF)


def swap(value, axis, mask):
    count = lax.axis_size(axis)
    return lax.ppermute(value, axis, [(i, i ^ mask) for i in range(count)])


def shift(value, axis, steps):
    count = lax.axis_size(axis)
    return lax.ppermute(value, axis, [(i, (i + steps) % count) for i in range(count)])


def chips_of(axis):
    return [list(range(core, lax.axis_size(axis), 2)) for core in range(2)]


def to_line(blocks):
    return lax.all_to_all(blocks, "fsdp", 0, 0)


def to_chips(blocks):
    return lax.all_to_all(blocks, "dp", 0, 0, axis_index_groups=chips_of("dp"))


def repeated(value, count):
    return jnp.broadcast_to(value[None], (count,) + value.shape)


def in_order(parts, axis):
    count, me = lax.axis_size(axis), lax.axis_index(axis)
    up = jnp.stack([parts[-k % count] for k in range(count)] * 2)
    return lax.dynamic_slice_in_dim(up, lax.rem(count - me, count), count, 0)


def by_chip(parts):
    chip, count = lax.div(lax.axis_index("dp"), 2), len(parts)
    bits = count.bit_length() - 1
    cube = jnp.stack(parts).reshape((2,) * bits + parts[0].shape)
    for place in range(bits):
        mine = lax.rem(chip >> (bits - 1 - place), 2) == 1
        cube = jnp.where(mine, jnp.flip(cube, place), cube)
    return cube.reshape((count,) + parts[0].shape)


def by_device(own, other):
    core = lax.rem(lax.axis_index("dp"), 2) == 1
    both = jnp.where(core, jnp.stack([other, own], axis=1), jnp.stack([own, other], axis=1))
    return lax.optimization_barrier(both.reshape((-1,) + own.shape[1:]))


def total_line(value):
    reach = 1
    while reach < lax.axis_size("fsdp"):
        value = value + swap(value.astype(BF), "fsdp", reach).astype(F32)
        reach *= 2
    return value


def fence(*values):
    flat, shape = jax.tree.flatten(values)
    return jax.tree.unflatten(shape, lax.optimization_barrier(tuple(flat)))


def cores(value, axis):
    cut = value.shape[:axis] + (lax.axis_size("dp") // 2, 2, -1) + value.shape[axis + 1 :]
    cube = value.reshape(cut)
    core = lax.rem(lax.axis_index("dp"), 2)
    found = [lax.dynamic_index_in_dim(cube, at, axis + 1, keepdims=False) for at in (core, 1 - core)]
    flat = value.shape[:axis] + (value.shape[axis] // 2,) + value.shape[axis + 1 :]
    return [part.reshape(flat) for part in found]


def add_core_kernel(kept, got, *refs):
    *small, out = refs
    chips, rows, width = out.shape
    whole = kept.shape[0] // chips

    @pl.loop(0, chips)
    def _(q):
        at = pl.ds(pl.multiple_of(q * whole, whole), whole)
        out[q, 0:whole, :] = (kept[at, :].astype(F32) + got[at, :].astype(F32)).astype(BF)
        if small:
            out[q, whole:rows, :] = (small[0][q] + small[1][q].astype(F32)).astype(BF)


def add_core(kept, got, *small):
    chips = lax.axis_size("dp") // 2
    rows = kept.shape[0] // chips + (small[0].shape[1] if small else 0)
    vmem = pl.BlockSpec(memory_space=pltpu.VMEM)
    return pl.pallas_call(
        add_core_kernel,
        in_specs=[vmem] * (2 + len(small)),
        out_specs=vmem,
        out_shape=jax.ShapeDtypeStruct((chips, rows, kept.shape[1]), BF),
        compiler_params=pltpu.CompilerParams(vmem_limit_bytes=32 << 20),
        cost_estimate=small_cost(1 << 10),
        name="add_core",
    )(kept, got, *small)


def add_chips(blocks):
    return jnp.sum(to_chips(blocks.astype(BF)).astype(F32), axis=0)


def add_chips_near(blocks):
    count, chip = lax.axis_size("dp") // 2, lax.div(lax.axis_index("dp"), 2)
    total = lax.dynamic_index_in_dim(blocks, chip, 0, keepdims=False)
    for u in range(1, count):
        total = total + far(blocks, u).astype(F32)
    return total


def sent_far(blocks, u):
    chip = lax.div(lax.axis_index("dp"), 2)
    return lax.dynamic_index_in_dim(blocks, jnp.bitwise_xor(chip, u), 0, keepdims=False).astype(BF)


def far(blocks, u):
    return swap(sent_far(blocks, u), "dp", 2 * u)


def contract_cols(left, right):
    return lax.dot_general(left, right, (((1,), (1,)), ((), ())), preferred_element_type=F32)


def per_device(
    tokens, counts, lengths, gain, in_weight, conv_weight, conv_bias, x_weight,
    dt_weight, dt_bias, a_log, skip, out_weight, cotangent,
):
    n_dp, n_line = lax.axis_size("dp"), lax.axis_size("fsdp")
    group, place = lax.axis_index("dp"), lax.axis_index("fsdp")
    held_slots, model = tokens.shape
    slots = held_slots * n_line
    owned = skip.shape[0]
    width = owned * n_dp
    in_rows = in_weight.shape[0]
    taps, rank_w, n_state = conv_weight.shape[0], dt_weight.shape[0], a_log.shape[1]
    proj = x_weight.shape[1]
    tb = 64 if slots % 64 == 0 else slots

    count_row = lax.dynamic_index_in_dim(counts, group, 0, keepdims=False)
    length_row = lax.dynamic_index_in_dim(lengths, group, 0, keepdims=False)
    info = jnp.concatenate([jnp.stack([group, place]).astype(jnp.int32), count_row])
    offsets = jnp.cumsum(count_row) - count_row
    within = lax.broadcasted_iota(jnp.int32, (n_line, held_slots), 1)
    present = within < count_row[:, None]
    position = offsets[:, None] + within
    second, third = length_row[0], length_row[0] + length_row[1]
    begin = jnp.where(position >= third, third, jnp.where(position >= second, second, 0))
    marks = jnp.stack(
        [position - lag >= begin for lag in range(taps)] + [present, present & (position == begin)]
    ).astype(F32).reshape(taps + 2, slots).T
    allowed, valid, opens = marks[:, :taps], marks[:, taps : taps + 1], marks[:, taps + 1 :] * FAR

    own_tokens, own_cot = tokens, cotangent
    steps = range(1, n_line)
    chips = range(1, n_dp // 2)
    at = Small(rank_w, proj, n_state, taps)

    parts = split_columns(in_weight, gain, n_dp, n_line)
    rest = jnp.concatenate([conv_weight, conv_bias[None], dt_bias[None], skip[None]], axis=0)
    rest = jnp.pad(rest, ((0, 16 - rest.shape[0]), (0, 0)))
    small = jnp.concatenate([dt_weight, x_weight.T, a_log.T, rest], axis=0)
    small_rows = -(-at.rows * owned // model)
    small_rows += -small_rows % 16
    small = jnp.pad(small, ((0, small_rows * model // owned - at.rows), (0, 0))).reshape(small_rows, model)
    packed = jnp.concatenate([out_weight, small], axis=0)
    parts, tokens = fence(parts, tokens)
    parts = to_line(parts)
    toks = {0: tokens, 1: shift(tokens, "fsdp", 1)}
    near = [packed] + [swap(packed, "dp", 2 * u) for u in chips]
    parts, toks, near, info, allowed, valid, opens = fence(parts, toks, near, info, allowed, valid, opens)

    gain_rows = jnp.pad(parts[:, 2 * in_rows, :in_rows].reshape(1, -1), ((0, 15), (0, width - n_line * in_rows)))
    inner_block = jnp.concatenate([parts[:, :in_rows].reshape(-1, width), gain_rows], axis=0)
    gate_in = parts[:, in_rows : 2 * in_rows].reshape(-1, width)
    inner_rep, gate_in, toks = fence(repeated(inner_block, n_dp // 2), gate_in, toks)
    inner_own = to_chips(inner_rep)
    for s in steps[1:]:
        toks[s] = shift(toks[0], "fsdp", s)
    gate_rep = repeated(gate_in, n_dp // 2)
    small = by_chip([block[owned:].reshape(-1, owned)[: at.rows] for block in near])
    small_other = swap(small, "dp", 1)
    inner_own, toks, near, gate_rep, cotangent, small, small_other = fence(
        inner_own, toks, near, gate_rep, cotangent, small, small_other
    )

    inner_other = swap(inner_own, "dp", 1)
    small = by_device(small, small_other).transpose(1, 0, 2).reshape(-1, width)
    inner_own, inner_other, toks, cotangent, near, small = fence(inner_own, inner_other, toks, cotangent, near, small)
    rates = -jnp.exp(small[at.a_t].astype(F32))
    chunks = width // LANES
    rate2 = jnp.pad(
        (rates * (1.0 / LN2)).reshape(n_state, chunks, LANES), ((0, 0), (0, SUB - chunks), (0, 0))
    ).reshape(n_state * SUB, LANES)

    gate_own = to_chips(gate_rep)
    cots = {0: cotangent, 1: shift(cotangent, "fsdp", 1)}
    full_gain, normed, normed_kept, normed_sent, inner, conv_out, activ, part, inner_nat = project(
        info, n_line, n_dp, [toks[s] for s in range(n_line)], inner_own, inner_other, at, small, allowed
    )
    part, rate2, cots, near, gate_own = fence(part, rate2, cots, near, gate_own)

    projected = total_line(part)
    out_near, out_other = near, [swap(block, "dp", 1) for block in near]
    projected, cots, out_near, out_other = fence(projected, cots, out_near, out_other)

    gate_other = swap(gate_own, "dp", 1)
    for s in steps[1:]:
        cots[s] = shift(cots[0], "fsdp", s)
    rank_low = projected[:, :rank_w].astype(BF)
    bc = jnp.concatenate([projected[:, rank_w:], opens], axis=1)
    scanned, states = scan_forward(at, bc, rank_low, small, activ, valid, rate2, tb)
    scanned, gate_own, gate_other, cots[n_line - 1] = fence(scanned, gate_own, gate_other, cots[n_line - 1])

    branches, gate, gate_nat, out_nat, *gated = gate_block(
        info, n_line, n_dp, gate_own, gate_other, out_near, out_other, normed, scanned, activ, at, small
    )
    branches, gate, gated, gate_nat, out_nat, cots = fence(branches, gate, gated, gate_nat, out_nat, cots)

    branches[1] = shift(branches[1], "fsdp", 1)
    grad_scan, grad_gate, dout, gate_kept, gate_sent = gate_back(
        info, n_line, [cots[s] for s in range(n_line)], out_nat, gate, scanned, activ, at, small, valid,
        normed_kept, normed_sent,
    )
    branches, grad_scan, grad_gate, dout, gated, gate_kept, gate_sent = fence(
        branches, grad_scan, grad_gate, dout, gated, gate_kept, gate_sent
    )
    gate_grad = add_core(gate_kept, swap(gate_sent, "dp", 1))
    gate_grad, grad_scan, branches = fence(gate_grad, grad_scan, branches)

    gate_rows = add_chips(gate_grad).astype(BF)
    for s in steps[1:]:
        branches[s] = shift(branches[s], "fsdp", s)
    part, grad_u, dt_w_grad, vectors, rate_sum = scan_backward(
        at, bc, rank_low, small, activ, valid, rate2, grad_scan, states, tb
    )
    part, branches, gated, dout, grad_gate, rate_sum, gate_rows = fence(
        part, branches, gated, dout, grad_gate, rate_sum, gate_rows
    )

    out_kept, out_sent = outer_product(*gated, dout)
    reach = 1
    while reach < n_line:
        part = part + swap(part.astype(BF), "fsdp", reach).astype(F32)
        reach *= 2
        if reach == 2:
            part, out_kept, out_sent, grad_gate = fence(part, out_kept, out_sent, grad_gate)
            out_got = swap(out_sent, "dp", 1)
            normed_gate = contract_cols(grad_gate, gate_nat)
    rate_grad = rate_sum.reshape(n_state, SUB, LANES)[:, :chunks].reshape(n_state, width) * rates
    grad_projected, out_kept, out_got, normed_gate, rate_grad, gate_rows = fence(
        part.astype(BF), out_kept, out_got, normed_gate, rate_grad, gate_rows
    )

    gate_got = to_line(gate_rows.reshape(n_line, in_rows, width))
    out_grad = add_core(out_kept, out_got)
    grads, inner_kept, inner_sent, small_kept, small_sent = conv_back(
        info, n_line, n_dp, grad_projected, grad_u, at, small, activ, conv_out, inner, allowed,
        dt_w_grad, rate_grad, vectors, inner_nat, normed_gate, normed_kept, normed_sent,
    )
    out_far = {u: sent_far(out_grad, u) for u in chips}
    grads, gate_got, inner_kept, inner_sent, small_kept, small_sent, out_grad, out_far = fence(
        grads, gate_got, inner_kept, inner_sent, small_kept, small_sent, out_grad, out_far
    )

    folded = owned % LANES == 0
    grads[1] = shift(grads[1], "fsdp", 1)
    for u in chips[2:]:
        out_far[u] = swap(out_far[u], "dp", 2 * u)
    inner_got, small_got = swap(inner_sent, "dp", 1), swap(small_sent, "dp", 1)
    inner_grad = add_core(inner_kept, inner_got, *((small_kept, small_got) if folded else ()))
    inner_grad, grads, small_kept, small_got, out_grad, out_far, branches = fence(
        inner_grad, grads, small_kept, small_got, out_grad, out_far, branches
    )

    got = to_chips(inner_grad)
    inner_rows = jnp.sum(got[:, : n_line * in_rows].astype(F32), axis=0).astype(BF)
    small_sum = jnp.sum(got[:, n_line * in_rows :].astype(F32), axis=0)
    for s in steps[1:]:
        grads[s] = shift(grads[s], "fsdp", s)
    inner_rows, small_sum, grads, small_kept, small_got, out_grad, out_far, branches = fence(
        inner_rows, small_sum, grads, small_kept, small_got, out_grad, out_far, branches
    )

    inner_got = to_line(inner_rows.reshape(n_line, in_rows, width))
    for u in chips[:2]:
        out_far[u] = swap(out_far[u], "dp", 2 * u)
    grad_normed = sum(p.astype(F32) for p in grads)
    grad_normed, small_sum, small_kept, small_got, branches = fence(
        grad_normed, small_sum, small_kept, small_got, branches
    )
    out_weight_grad = lax.dynamic_index_in_dim(out_grad, lax.div(group, 2), 0, keepdims=False).astype(F32)
    out_weight_grad = out_weight_grad + sum(out_far[u].astype(F32) for u in chips)
    if folded:
        small_grads = small_sum.reshape(-1, n_dp, owned).transpose(1, 0, 2).reshape(-1, owned)
    else:
        small_grads = add_chips_near(small_kept + small_got.astype(F32))
    own_valid = lax.dynamic_slice_in_dim(valid, place * held_slots, held_slots, 0)
    own_f = own_tokens.astype(F32)
    output = (own_f + own_valid * sum(p.astype(F32) for p in branches)).astype(BF)
    own_scale = lax.rsqrt(jnp.mean(own_f * own_f, axis=1, keepdims=True) + EPS)
    unit = own_f * own_scale
    grad_unit = grad_normed * full_gain
    token_grad = own_cot.astype(F32) + own_scale * (
        grad_unit - unit * jnp.mean(grad_unit * unit, axis=1, keepdims=True)
    )
    dt_g, x_g, a_g = small_grads[at.dt_w], small_grads[at.x_t], small_grads[at.a_t]
    tail_g = small_grads[at.rest]
    conv_g, conv_b_g, dt_b_g, skip_g = tail_g[:taps], tail_g[taps : taps + 1], tail_g[taps + 1 : taps + 2], tail_g[taps + 2 : taps + 3]
    in_weight_grad, gain_grad = join_columns(inner_got, gate_got, in_weight, gain, n_dp)
    return (
        output, token_grad, gain_grad, in_weight_grad, conv_g, conv_b_g[0], x_g.T, dt_g, dt_b_g[0], a_g.T,
        skip_g[0], out_weight_grad,
    )


def solution(mesh):
    both = ("dp", "fsdp")
    rows, cols, vec = P(both, None), P(None, both), P(both)
    return jax.shard_map(
        per_device,
        mesh=mesh,
        in_specs=(rows, P(), P(), vec, rows, cols, vec, rows, cols, vec, rows, vec, rows, rows),
        out_specs=(rows, rows, vec, rows, cols, vec, rows, cols, vec, rows, vec, rows),
        check_vma=False,
    )
```

time: 479 us -> 405 us (0.85); the launches traced: 471 us -> 403 us
  Pallas kernels: 110 us -> 141 us
  waiting for transfers between devices: 151 us -> 120 us
  matrix products: 27.4 us -> 6.9 us
  starting transfers between devices: 98.2 us -> 79.7 us
  between operations: 16.9 us -> 2.94 us
  other arithmetic: 34.3 us -> 26.6 us
  local copies, waits for them, and re-layouts: 33.8 us -> 26.5 us
    ppermute x20 -> x21, waiting for transfers between devices: 94.2 us -> 38.7 us  [swap(): return lax.ppermute(value, axis, [(i, i ^ mask) for i in range(count)])]
    pallas_call x6 -> x11, Pallas kernels: 107 us -> 138 us  [the longest x1 38.4 us: scan_backward(): pl.pallas_call(functools.partial(backward_kernel, at), grid=(nb,), in_spe...]
    all_to_all x4, waiting for transfers between devices: 0.01 us -> 25.1 us  [to_chips(): return lax.all_to_all(blocks, 'dp', 0, 0, axis_index_groups=chips_of('dp'))]
    ppermute x12 -> x0, starting transfers between devices: 22.9 us -> none  [hop(): self.found[steps, sign] = lax.ppermute(last, 'fsdp', pairs)]
    ppermute x9 -> x12, waiting for transfers between devices: 30.5 us -> 49 us  [shift(): lax.ppermute(value, axis, [(i, (i + steps) % count) for i in range(count)])]
    ppermute x12 -> x0, waiting for transfers between devices: 17.9 us -> none  [hop(): self.found[steps, sign] = lax.ppermute(last, 'fsdp', pairs)]
    dot_general x6 -> x0, matrix products: 15.8 us -> none  [contract_rows(): lax.dot_general(left, right, (((0,), (0,)), ((), ())), preferred_element_...]
    ppermute x9 -> x12, starting transfers between devices: 14.1 us -> 26.9 us  [shift(): lax.ppermute(value, axis, [(i, (i + steps) % count) for i in range(count)])]
  transfers between devices with their start and end apart: 49 -> 40, of which waited for: 18 -> 16; matrix products, arithmetic and copies ran while one was open for 17% -> 10% of each run, Pallas kernels for 17% -> 33%
where the time goes in v2:
time: 405 us; the launch traced here: 403 us
  Pallas kernels  141 us (35%)
  waiting for transfers between devices  120 us (30%)
  starting transfers between devices  79.7 us (20%)
  other arithmetic  26.6 us (7%)
  local copies, waits for them, and re-layouts  26.5 us (7%)
  matrix products  6.9 us (2%)
    ppermute x12, waiting for transfers between devices, shift(): lax.ppermute(value, axis, [(i, (i + steps) % count) for i in range(count)])  49 us
    ppermute x21, waiting for transfers between devices, swap(): return lax.ppermute(value, axis, [(i, i ^ mask) for i in range(count)])  38.7 us
    pallas_call x1, Pallas kernels, scan_backward(): pl.pallas_call(functools.partial(backward_kernel, at), grid=(nb,), in_spe...  38.4 us
    ppermute x12, starting transfers between devices, shift(): lax.ppermute(value, axis, [(i, (i + steps) % count) for i in range(count)])  26.9 us
    all_to_all x4, waiting for transfers between devices, to_chips(): return lax.all_to_all(blocks, 'dp', 0, 0, axis_index_groups=chips_of('dp'))  25.1 us
    pallas_call x1, Pallas kernels, conv_back(): pl.pallas_call(functools.partial(conv_back_kernel, n_line, n_dp, at), in_...  21.1 us
    ppermute x21, starting transfers between devices, swap(): return lax.ppermute(value, axis, [(i, i ^ mask) for i in range(count)])  18.2 us
    all_to_all x3, starting transfers between devices, to_line(): return lax.all_to_all(blocks, 'fsdp', 0, 0)  18.2 us
  transfers between devices with their start and end apart: 40, of which 16 were waited for; matrix products, arithmetic and copies ran while one was open for 10% of the time, Pallas kernels for 33%

profile of v2, /device:TPU:0, one launch (start us, length us, event | category | flops | bytes accessed | tf_op | source)
XLA Modules:
  0.0 403.2 jit_solution(18012952785051457998)
XLA Ops:
  3.2 6.4 %all-to-all-start = ((bf16[4,144,1024]{2,1,0:T(8,128)(2,1)}), bf16[4,144,1024]{2,1,0:T(8,128)(2,1)S(1)}, u32[]{:S(2)}, u32[]{:S(2)}) async-start(bf16[4,144,1024]{2,1,0:T(8,128)(2,1)} %split_columns.1), calls=%async_computation | async-start | bytes 2359296 | tf_op jit(solution)/shard_map/all_to_all | solution.py:731
  21.0 23.3 %collective-permute-done.refs_1_ = bf16[128,2048]{1,0:T(8,128)(2,1)} collective-permute-done((bf16[128,2048]{1,0:T(8,128)(2,1)S(1)}, bf16[128,2048]{1,0:T(8,128)(2,1)}, u32[]{:S(2)}, u32[]{:S(2)}) %collective-permute-start) | collective-permute-done | bytes 524320 | tf_op jit(solution)/shard_map/ppermute | solution.py:723
  44.3 5.2 %all-to-all-done = bf16[4,144,1024]{2,1,0:T(8,128)(2,1)S(1)} async-done(((bf16[4,144,1024]{2,1,0:T(8,128)(2,1)}), bf16[4,144,1024]{2,1,0:T(8,128)(2,1)S(1)}, u32[]{:S(2)}, u32[]{:S(2)}) %all-to-all-start) | async-done | bytes 1179680 | tf_op jit(solution)/shard_map/all_to_all | solution.py:731
  53.2 4.6 %all-to-all-start.1 = ((bf16[4,272,1024]{2,1,0:T(8,128)(2,1)}), bf16[4,272,1024]{2,1,0:T(8,128)(2,1)}, u32[]{:S(2)}, u32[]{:S(2)}) async-start(bf16[4,272,1024]{2,1,0:T(8,128)(2,1)} %broadcast_in_dim.44), calls=%async_computation.1 | async-start | bytes 4456448 | tf_op jit(solution)/shard_map/all_to_all | solution.py:735
  63.9 17.8 %collective-permute-done.4.refs_2_ = bf16[128,2048]{1,0:T(8,128)(2,1)S(1)} collective-permute-done((bf16[128,2048]{1,0:T(8,128)(2,1)S(1)}, bf16[128,2048]{1,0:T(8,128)(2,1)S(1)}, u32[]{:S(2)}, u32[]{:S(2)}) %collective-permute-start.4) | collective-permute-done | bytes 524320 | tf_op jit(solution)/shard_map/ppermute | solution.py:723
  85.3 3.6 all-to-all-start.2
  90.5 10.0 %collective-permute-start.8 = (bf16[128,2048]{1,0:T(8,128)(2,1)}, bf16[128,2048]{1,0:T(8,128)(2,1)}, u32[]{:S(2)}, u32[]{:S(2)}) collective-permute-start(bf16[128,2048]{1,0:T(8,128)(2,1)} %refs_0_.1), channel_id=1, source_target_pairs={{0,1},{1,2},{2,3},{3,0},{4,5},{5,6},{6,7},{7,4},{8,9},{9,10},{10,1... | collective-permute-start | bytes 1572872 | tf_op jit(solution)/shard_map/ppermute | solution.py:723
  100.6 15.3 %project.1 = (f32[1,2048]{1,0:T(1,128)}, bf16[512,2048]{1,0:T(8,128)(2,1)}, bf16[512,1024]{1,0:T(8,128)(2,1)}, bf16[512,1024]{1,0:T(8,128)(2,1)}, f32[512,1024]{...) custom-call(s32[6]{0:T(128)} %pad_add_fusion.info, ...), custom_call_target="tpu_custom_call" | custom-call | flops 1048576 | bytes 65536 | tf_op jit(solution)/shard_map/project/pallas_call | solution.py:473
  117.9 8.4 %collective-permute-start.9 = (bf16[512,160]{1,0:T(8,128)(2,1)S(1)}, bf16[512,160]{1,0:T(8,128)(2,1)S(1)}, u32[]{:S(2)}, u32[]{:S(2)}) collective-permute-start(bf16[512,160]{1,0:T(8,128)(2,1)S(1)} %convert_element_type.99), channel_id=1, source_target_pairs={{0,1},{1,0},{2,3},{3,2},{4,5},{5,4},{6,7},{7,6},{8,9},{9,8},{10,11... | collective-permute-start | bytes 491528 | tf_op jit(solution)/shard_map/ppermute | solution.py:718
  126.3 6.4 %collective-permute-done.9 = bf16[512,160]{1,0:T(8,128)(2,1)S(1)} collective-permute-done((bf16[512,160]{1,0:T(8,128)(2,1)S(1)}, bf16[512,160]{1,0:T(8,128)(2,1)S(1)}, u32[]{:S(2)}, u32[]{:S(2)}) %collective-permute-start.9) | collective-permute-done | bytes 163872 | tf_op jit(solution)/shard_map/ppermute | solution.py:718
  135.0 13.0 %collective-permute-done.10 = bf16[512,160]{1,0:T(8,128)(2,1)S(1)} collective-permute-done((bf16[512,160]{1,0:T(8,128)(2,1)S(1)}, bf16[512,160]{1,0:T(8,128)(2,1)S(1)}, u32[]{:S(2)}, u32[]{:S(2)}) %collective-permute-start.10) | collective-permute-done | bytes 163872 | tf_op jit(solution)/shard_map/ppermute | solution.py:718
  151.8 17.7 %scan_forward.1 = (f32[512,1024]{1,0:T(8,128)S(1)}, f32[8,16,520,128]{3,2,1,0:T(8,128)}) custom-call(f32[512,33]{1,0:T(8,128)S(1)} %pad_maximum_fusion.1.bc, bf16[512,128]{1,0:T(8,128)(2,1)S(1)} %slice.142.rank, bf16[320,1024]{1,0:T(8,128)(2,1)S(1)} %copy-done.3, bf16[512,1024]{1,0:T(8,128)(2,1)S(1)} %copy-done.4, ...), custom_call_target="tpu_custom_call" | custom-call | flops 1048576 | bytes 65536 | tf_op jit(solution)/shard_map/scan_forward/pallas_call | solution.py:99
  172.2 18.0 %gate_block.1 = (bf16[128,2048]{1,0:T(8,128)(2,1)}, bf16[128,2048]{1,0:T(8,128)(2,1)}, bf16[128,2048]{1,0:T(8,128)(2,1)}, bf16[128,2048]{1,0:T(8,128)(2,1)}, f32...) custom-call(s32[6]{0:T(128)} %pad_add_fusion.info, ...), custom_call_target="tpu_custom_call" | custom-call | flops 1048576 | bytes 65536 | tf_op jit(solution)/shard_map/gate_block/pallas_call | solution.py:529
  191.2 15.0 %gate_back.1 = (f32[512,1024]{1,0:T(8,128)}, bf16[512,1024]{1,0:T(8,128)(2,1)}, bf16[512,2048]{1,0:T(8,128)(2,1)}, bf16[1024,1024]{1,0:T(8,128)(2,1)}, bf16[1024,1024]{1,0:T(8,128)(2,1)}) custom-call(s32[6]{0:T(128)} %pad_add_fusion.info, bf16[128,2048]{1,0:T(8,128)(2,1)} %refs_0_.1, bf16[128,2048]{1,0:T(8,128)(2,1)} %collective-permute-done.8.refs_1_, ...), custom_call_target="tpu_custom_call" | custom-call | flops 1048576 | bytes 65536 | tf_op jit(solution)/shard_map/gate_back/pallas_call | solution.py:574
  206.3 4.4 %collective-permute-done.19.got = bf16[1024,1024]{1,0:T(8,128)(2,1)S(1)} collective-permute-done((bf16[1024,1024]{1,0:T(8,128)(2,1)}, bf16[1024,1024]{1,0:T(8,128)(2,1)S(1)}, u32[]{:S(2)}, u32[]{:S(2)}) %collective-permute-start.19) | collective-permute-done | bytes 2097184 | tf_op jit(solution)/shard_map/ppermute | solution.py:718
  223.4 38.4 %scan_backward.1 = (f32[512,160]{1,0:T(8,128)}, f32[512,1024]{1,0:T(8,128)}, f32[128,1024]{1,0:T(8,128)}, f32[2,1024]{1,0:T(2,128)}, f32[128,128]{1,0:T(8,128)}) custom-call(f32[512,33]{1,0:T(8,128)} %copy-done.7, bf16[512,128]{1,0:T(8,128)(2,1)} %copy-done.14, bf16[320,1024]{1,0:T(8,128)(2,1)} %copy-done.2, ...), custom_call_target="tpu_custom_call" | custom-call | flops 1048576 | bytes 65536 | tf_op jit(solution)/shard_map/scan_backward/pallas_call | solution.py:223
  264.3 5.5 %outer_product.1 = (bf16[512,2048]{1,0:T(8,128)(2,1)S(1)}, bf16[512,2048]{1,0:T(8,128)(2,1)}) custom-call(bf16[512,512]{1,0:T(8,128)(2,1)S(1)} %copy-done.17, bf16[512,512]{1,0:T(8,128)(2,1)S(1)} %copy-done.18, bf16[512,2048]{1,0:T(8,128)(2,1)} %get-tuple-element.338.right), custom_call_target="tpu_custom_call" | custom-call | flops 1048576 | bytes 65536 | tf_op jit(solution)/shard_map/outer_product/pallas_call | solution.py:384
  273.8 6.9 %fusion.34.normed_gate = f32[512,2048]{1,0:T(8,128)} fusion(bf16[512,1024]{1,0:T(8,128)(2,1)} %get-tuple-element.345, bf16[2048,1024]{1,0:T(8,128)(2,1)} %get-tuple-element.346), kind=kOutput, calls=%fused_computation.86 | convolution fusion | flops 2147483648 | bytes 9437184 | tf_op jit(solution)/shard_map/dot_general | solution.py:836
  280.7 8.3 %collective-permute-done.23 = bf16[512,160]{1,0:T(8,128)(2,1)S(1)} collective-permute-done((bf16[512,160]{1,0:T(8,128)(2,1)S(1)}, bf16[512,160]{1,0:T(8,128)(2,1)S(1)}, u32[]{:S(2)}, u32[]{:S(2)}) %collective-permute-start.23) | collective-permute-done | bytes 163872 | tf_op jit(solution)/shard_map/ppermute | solution.py:718
  298.2 21.1 %conv_back.1 = (bf16[128,2048]{1,0:T(8,128)(2,1)}, bf16[128,2048]{1,0:T(8,128)(2,1)}, bf16[128,2048]{1,0:T(8,128)(2,1)}, bf16[128,2048]{1,0:T(8,128)(2,1)}, bf16...) custom-call(s32[6]{0:T(128)} %pad_add_fusion.info, ...), custom_call_target="tpu_custom_call" | custom-call | flops 1048576 | bytes 65536 | tf_op jit(solution)/shard_map/conv_back/pallas_call | solution.py:682
  330.6 6.5 %collective-permute-done.27 = bf16[128,2048]{1,0:T(8,128)(2,1)S(1)} collective-permute-done((bf16[128,2048]{1,0:T(8,128)(2,1)}, bf16[128,2048]{1,0:T(8,128)(2,1)S(1)}, u32[]{:S(2)}, u32[]{:S(2)}) %collective-permute-start.27) | collective-permute-done | bytes 524320 | tf_op jit(solution)/shard_map/ppermute | solution.py:723
  337.9 4.5 %all-to-all-start.5 = ((bf16[4,304,1024]{2,1,0:T(8,128)(2,1)}), bf16[4,304,1024]{2,1,0:T(8,128)(2,1)}, u32[]{:S(2)}, u32[]{:S(2)}) async-start(bf16[4,304,1024]{2,1,0:T(8,128)(2,1)} %add_core.5), calls=%async_computation.5 | async-start | bytes 4980736 | tf_op jit(solution)/shard_map/all_to_all | solution.py:735
  347.3 24.5 %all-to-all-done.5 = bf16[4,304,1024]{2,1,0:T(8,128)(2,1)} async-done(((bf16[4,304,1024]{2,1,0:T(8,128)(2,1)}), bf16[4,304,1024]{2,1,0:T(8,128)(2,1)}, u32[]{:S(2)}, u32[]{:S(2)}) %all-to-all-start.5) | async-done | bytes 2490400 | tf_op jit(solution)/shard_map/all_to_all | solution.py:735
  377.9 8.3 %all-to-all-start.6 = ((bf16[4,64,1024]{2,1,0:T(8,128)(2,1)}), bf16[4,64,1024]{2,1,0:T(8,128)(2,1)S(1)}, u32[]{:S(2)}, u32[]{:S(2)}) async-start(bf16[4,64,1024]{2,1,0:T(8,128)(2,1)} %bitcast.28), calls=%async_computation.6 | async-start | bytes 1048576 | tf_op jit(solution)/shard_map/all_to_all | solution.py:731
  (255 shorter events, 107.3 us)
Async XLA Ops:
  3.2 46.2 %all-to-all-start = ((bf16[4,144,1024]{2,1,0:T(8,128)(2,1)}), bf16[4,144,1024]{2,1,0:T(8,128)(2,1)S(1)}, u32[]{:S(2)}, u32[]{:S(2)}) async-start(bf16[4,144,1024]{2,1,0:T(8,128)(2,1)} %split_columns.1), calls=%async_computation | async-start | bytes 2359296 | tf_op jit(solution)/shard_map/all_to_all | solution.py:731
  9.9 34.4 %collective-permute-start.1 = (bf16[160,2048]{1,0:T(8,128)(2,1)S(1)}, bf16[160,2048]{1,0:T(8,128)(2,1)S(1)}, u32[]{:S(2)}, u32[]{:S(2)}) collective-permute-start(bf16[160,2048]{1,0:T(8,128)(2,1)S(1)} %constant_dynamic-update-slice_fusion.refs_0_), channel_id=1, source_target_pairs={{0,8},{4,12},{8,0},{12,4},{16,24},{20,28},{24,16},{28,20},{1,9},{5... | collective-permute-start | bytes 1966088 | tf_op jit(solution)/shard_map/ppermute | solution.py:718
  11.5 32.8 %collective-permute-start.2 = (bf16[160,2048]{1,0:T(8,128)(2,1)S(1)}, bf16[160,2048]{1,0:T(8,128)(2,1)}, u32[]{:S(2)}, u32[]{:S(2)}) collective-permute-start(bf16[160,2048]{1,0:T(8,128)(2,1)S(1)} %constant_dynamic-update-slice_fusion.refs_0_), channel_id=1, source_target_pairs={{0,16},{4,20},{8,24},{12,28},{16,0},{20,4},{24,8},{28,12},{1,17},{... | collective-permute-start | bytes 1966088 | tf_op jit(solution)/shard_map/ppermute | solution.py:718
  13.0 31.3 %collective-permute-start.3 = (bf16[160,2048]{1,0:T(8,128)(2,1)S(1)}, bf16[160,2048]{1,0:T(8,128)(2,1)}, u32[]{:S(2)}, u32[]{:S(2)}) collective-permute-start(bf16[160,2048]{1,0:T(8,128)(2,1)S(1)} %constant_dynamic-update-slice_fusion.refs_0_), channel_id=1, source_target_pairs={{0,24},{4,28},{8,16},{12,20},{16,8},{20,12},{24,0},{28,4},{1,25},{... | collective-permute-start | bytes 1966088 | tf_op jit(solution)/shard_map/ppermute | solution.py:718
  13.5 30.8 %collective-permute-start = (bf16[128,2048]{1,0:T(8,128)(2,1)S(1)}, bf16[128,2048]{1,0:T(8,128)(2,1)}, u32[]{:S(2)}, u32[]{:S(2)}) collective-permute-start(bf16[128,2048]{1,0:T(8,128)(2,1)S(1)} %copy-done.19), channel_id=1, source_target_pairs={{0,1},{1,2},{2,3},{3,0},{4,5},{5,6},{6,7},{7,4},{8,9},{9,10},{10,1... | collective-permute-start | bytes 1572872 | tf_op jit(solution)/shard_map/ppermute | solution.py:723
  53.2 30.5 %all-to-all-start.1 = ((bf16[4,272,1024]{2,1,0:T(8,128)(2,1)}), bf16[4,272,1024]{2,1,0:T(8,128)(2,1)}, u32[]{:S(2)}, u32[]{:S(2)}) async-start(bf16[4,272,1024]{2,1,0:T(8,128)(2,1)} %broadcast_in_dim.44), calls=%async_computation.1 | async-start | bytes 4456448 | tf_op jit(solution)/shard_map/all_to_all | solution.py:735
  57.9 23.8 %collective-permute-start.4 = (bf16[128,2048]{1,0:T(8,128)(2,1)S(1)}, bf16[128,2048]{1,0:T(8,128)(2,1)S(1)}, u32[]{:S(2)}, u32[]{:S(2)}) collective-permute-start(bf16[128,2048]{1,0:T(8,128)(2,1)S(1)} %copy-done.19), channel_id=1, source_target_pairs={{0,2},{1,3},{2,0},{3,1},{4,6},{5,7},{6,4},{7,5},{8,10},{9,11},{10,... | collective-permute-start | bytes 1572872 | tf_op jit(solution)/shard_map/ppermute | solution.py:723
  59.5 23.5 %collective-permute-start.5 = (bf16[128,2048]{1,0:T(8,128)(2,1)S(1)}, bf16[128,2048]{1,0:T(8,128)(2,1)}, u32[]{:S(2)}, u32[]{:S(2)}) collective-permute-start(bf16[128,2048]{1,0:T(8,128)(2,1)S(1)} %copy-done.19), channel_id=1, source_target_pairs={{0,3},{1,0},{2,1},{3,2},{4,7},{5,4},{6,5},{7,6},{8,11},{9,8},{10,9... | collective-permute-start | bytes 1572872 | tf_op jit(solution)/shard_map/ppermute | solution.py:723
  85.3 30.6 %all-to-all-start.2 = ((bf16[4,256,1024]{2,1,0:T(8,128)(2,1)}), bf16[4,256,1024]{2,1,0:T(8,128)(2,1)S(1)}, u32[]{:S(2)}, u32[]{:S(2)}) async-start(bf16[4,256,1024]{2,1,0:T(8,128)(2,1)} %broadcast_in_dim.45), calls=%async_computation.2 | async-start | bytes 4194304 | tf_op jit(solution)/shard_map/all_to_all | solution.py:735
  90.5 25.4 %collective-permute-start.8 = (bf16[128,2048]{1,0:T(8,128)(2,1)}, bf16[128,2048]{1,0:T(8,128)(2,1)}, u32[]{:S(2)}, u32[]{:S(2)}) collective-permute-start(bf16[128,2048]{1,0:T(8,128)(2,1)} %refs_0_.1), channel_id=1, source_target_pairs={{0,1},{1,2},{2,3},{3,0},{4,5},{5,6},{6,7},{7,4},{8,9},{9,10},{10,1... | collective-permute-start | bytes 1572872 | tf_op jit(solution)/shard_map/ppermute | solution.py:723
  115.9 55.0 %collective-permute-start.15 = (bf16[4,256,1024]{2,1,0:T(8,128)(2,1)S(1)}, bf16[4,256,1024]{2,1,0:T(8,128)(2,1)S(1)}, u32[]{:S(2)}, u32[]{:S(2)}) collective-permute-start(bf16[4,256,1024]{2,1,0:T(8,128)(2,1)S(1)} %all-to-all-done.2.own), channel_id=1, source_target_pairs={{0,4},{4,0},{8,12},{12,8},{16,20},{20,16},{24,28},{28,24},{1,5},{5... | collective-permute-start | bytes 6291464 | tf_op jit(solution)/shard_map/ppermute | solution.py:718
  150.3 20.5 %collective-permute-start.16 = (bf16[128,2048]{1,0:T(8,128)(2,1)}, bf16[128,2048]{1,0:T(8,128)(2,1)S(1)}, u32[]{:S(2)}, u32[]{:S(2)}) collective-permute-start(bf16[128,2048]{1,0:T(8,128)(2,1)} %refs_0_.1), channel_id=1, source_target_pairs={{0,3},{1,0},{2,1},{3,2},{4,7},{5,4},{6,5},{7,6},{8,11},{9,8},{10,9... | collective-permute-start | bytes 1572872 | tf_op jit(solution)/shard_map/ppermute | solution.py:723
  151.5 38.8 %collective-permute-start.17 = (bf16[128,2048]{1,0:T(8,128)(2,1)}, bf16[128,2048]{1,0:T(8,128)(2,1)}, u32[]{:S(2)}, u32[]{:S(2)}) collective-permute-start(bf16[128,2048]{1,0:T(8,128)(2,1)} %refs_0_.1), channel_id=1, source_target_pairs={{0,2},{1,3},{2,0},{3,1},{4,6},{5,7},{6,4},{7,5},{8,10},{9,11},{10,... | collective-permute-start | bytes 1572872 | tf_op jit(solution)/shard_map/ppermute | solution.py:723
  214.1 47.7 %all-to-all-start.3 = ((bf16[4,256,1024]{2,1,0:T(8,128)(2,1)}), bf16[4,256,1024]{2,1,0:T(8,128)(2,1)S(1)}, u32[]{:S(2)}, u32[]{:S(2)}) async-start(bf16[4,256,1024]{2,1,0:T(8,128)(2,1)} %add_core.3), calls=%async_computation.3 | async-start | bytes 4194304 | tf_op jit(solution)/shard_map/all_to_all | solution.py:735
  217.7 45.4 %collective-permute-start.20 = (bf16[128,2048]{1,0:T(8,128)(2,1)}, bf16[128,2048]{1,0:T(8,128)(2,1)}, u32[]{:S(2)}, u32[]{:S(2)}) collective-permute-start(bf16[128,2048]{1,0:T(8,128)(2,1)} %get-tuple-element.327), channel_id=1, source_target_pairs={{0,2},{1,3},{2,0},{3,1},{4,6},{5,7},{6,4},{7,5},{8,10},{9,11},{10,... | collective-permute-start | bytes 1572872 | tf_op jit(solution)/shard_map/ppermute | solution.py:723
  220.7 42.4 %collective-permute-start.21 = (bf16[128,2048]{1,0:T(8,128)(2,1)}, bf16[128,2048]{1,0:T(8,128)(2,1)}, u32[]{:S(2)}, u32[]{:S(2)}) collective-permute-start(bf16[128,2048]{1,0:T(8,128)(2,1)} %get-tuple-element.328), channel_id=1, source_target_pairs={{0,3},{1,0},{2,1},{3,2},{4,7},{5,4},{6,5},{7,6},{8,11},{9,8},{10,9... | collective-permute-start | bytes 1572872 | tf_op jit(solution)/shard_map/ppermute | solution.py:723
  272.1 17.6 %collective-permute-start.24 = (bf16[512,2048]{1,0:T(8,128)(2,1)}, bf16[512,2048]{1,0:T(8,128)(2,1)S(1)}, u32[]{:S(2)}, u32[]{:S(2)}) collective-permute-start(bf16[512,2048]{1,0:T(8,128)(2,1)} %get-tuple-element.344), channel_id=1, source_target_pairs={{0,4},{4,0},{8,12},{12,8},{16,20},{20,16},{24,28},{28,24},{1,5},{5... | collective-permute-start | bytes 6291464 | tf_op jit(solution)/shard_map/ppermute | solution.py:718
  291.1 29.5 %all-to-all-start.4 = ((bf16[4,64,1024]{2,1,0:T(8,128)(2,1)}), bf16[4,64,1024]{2,1,0:T(8,128)(2,1)S(1)}, u32[]{:S(2)}, u32[]{:S(2)}) async-start(bf16[4,64,1024]{2,1,0:T(8,128)(2,1)} %bitcast.67), calls=%async_computation.4 | async-start | bytes 1048576 | tf_op jit(solution)/shard_map/all_to_all | solution.py:731
  337.9 33.9 %all-to-all-start.5 = ((bf16[4,304,1024]{2,1,0:T(8,128)(2,1)}), bf16[4,304,1024]{2,1,0:T(8,128)(2,1)}, u32[]{:S(2)}, u32[]{:S(2)}) async-start(bf16[4,304,1024]{2,1,0:T(8,128)(2,1)} %add_core.5), calls=%async_computation.5 | async-start | bytes 4980736 | tf_op jit(solution)/shard_map/all_to_all | solution.py:735
  342.6 33.2 %collective-permute-start.29 = (bf16[128,2048]{1,0:T(8,128)(2,1)}, bf16[128,2048]{1,0:T(8,128)(2,1)S(1)}, u32[]{:S(2)}, u32[]{:S(2)}) collective-permute-start(bf16[128,2048]{1,0:T(8,128)(2,1)} %get-tuple-element.388), channel_id=1, source_target_pairs={{0,2},{1,3},{2,0},{3,1},{4,6},{5,7},{6,4},{7,5},{8,10},{9,11},{10,... | collective-permute-start | bytes 1572872 | tf_op jit(solution)/shard_map/ppermute | solution.py:723
  344.9 30.9 %collective-permute-start.30 = (bf16[128,2048]{1,0:T(8,128)(2,1)}, bf16[128,2048]{1,0:T(8,128)(2,1)}, u32[]{:S(2)}, u32[]{:S(2)}) collective-permute-start(bf16[128,2048]{1,0:T(8,128)(2,1)} %get-tuple-element.389), channel_id=1, source_target_pairs={{0,3},{1,0},{2,1},{3,2},{4,7},{5,4},{6,5},{7,6},{8,11},{9,8},{10,9... | collective-permute-start | bytes 1572872 | tf_op jit(solution)/shard_map/ppermute | solution.py:723
  375.8 19.0 %collective-permute-start.31 = (bf16[128,2048]{1,0:T(8,128)(2,1)}, bf16[128,2048]{1,0:T(8,128)(2,1)}, u32[]{:S(2)}, u32[]{:S(2)}) collective-permute-start(bf16[128,2048]{1,0:T(8,128)(2,1)} %get-tuple-element.419), channel_id=1, source_target_pairs={{0,8},{4,12},{8,0},{12,4},{16,24},{20,28},{24,16},{28,20},{1,9},{5... | collective-permute-start | bytes 1572872 | tf_op jit(solution)/shard_map/ppermute | solution.py:718
  377.3 17.5 %collective-permute-start.32 = (bf16[128,2048]{1,0:T(8,128)(2,1)}, bf16[128,2048]{1,0:T(8,128)(2,1)}, u32[]{:S(2)}, u32[]{:S(2)}) collective-permute-start(bf16[128,2048]{1,0:T(8,128)(2,1)} %get-tuple-element.420), channel_id=1, source_target_pairs={{0,16},{4,20},{8,24},{12,28},{16,0},{20,4},{24,8},{28,12},{1,17},{... | collective-permute-start | bytes 1572872 | tf_op jit(solution)/shard_map/ppermute | solution.py:718
  377.9 21.4 %all-to-all-start.6 = ((bf16[4,64,1024]{2,1,0:T(8,128)(2,1)}), bf16[4,64,1024]{2,1,0:T(8,128)(2,1)S(1)}, u32[]{:S(2)}, u32[]{:S(2)}) async-start(bf16[4,64,1024]{2,1,0:T(8,128)(2,1)} %bitcast.28), calls=%async_computation.6 | async-start | bytes 1048576 | tf_op jit(solution)/shard_map/all_to_all | solution.py:731
  (72 other events, 1001.3 us)

commit v3 on v2

--- a/solution.py
+++ b/solution.py
@@ -32,6 +32,10 @@
 
     def vector(self, ref, at):
         return ref[self.rest, :].astype(F32)[at : at + 1, :]
+
+
+def contract_cols(left, right):
+    return lax.dot_general(left, right, (((1,), (1,)), ((), ())), preferred_element_type=F32)
 
 
 def scatter_lanes(ref, value, rows):
@@ -116,20 +120,20 @@
             jax.ShapeDtypeStruct((nb, n_state, (tb + 1) * SUB, LANES), F32),
         ],
         scratch_shapes=[pltpu.VMEM(rate2.shape, F32)] + [pltpu.VMEM((tb * SUB, LANES), F32)] * 3,
-        compiler_params=pltpu.CompilerParams(vmem_limit_bytes=48 << 20),
+        compiler_params=pltpu.CompilerParams(vmem_limit_bytes=61 << 20),
         cost_estimate=small_cost(1 << 20),
         name="scan_forward",
     )(bc, rank, small, act, valid, rate2)
 
 
 def backward_kernel(
-    at_small, bc, rank, small, act, valid, rate2, gs, states, fold,
-    part_out, gu_out, dtw_out, vec_out, rate_out,
-    g_ref, dt_s, dtu_s, gs_s, gdt_s, ab_s, lam_s,
+    at_small, bc, rank, small, act, valid, rate2, gs, states,
+    packed_out, gu_out, dtw_out, vec_out, rate_out,
+    part_s, g_ref, dt_s, dtu_s, gs_s, gdt_s, ab_s, both_s, sums,
 ):
     tb, width = act.shape
     n_state = rate2.shape[0] // SUB
-    half = n_state // 2
+    part = 4
 
     @pl.when(pl.program_id(0) == 0)
     def _():
@@ -151,24 +155,35 @@
     scatter_lanes(dtu_s, dt * u, tb)
     scatter_lanes(gs_s, gs_v, tb)
 
-    for group in range(2):
-        index = range(group * half, (group + 1) * half)
+    row = lax.broadcasted_iota(jnp.int32, (SUB, 2 * LANES), 0)
+    lane = lax.broadcasted_iota(jnp.int32, (SUB, 2 * LANES), 1)
+    pick = (lane // LANES == row).astype(F32).astype(BF)
+    run = SUB
+    span = run * SUB
+
+    def add_lanes(group, i):
+        rows = pl.ds(pl.multiple_of(i * span, span), span)
+        pairs = jnp.concatenate([both_s[group % 2, j, rows, :] for j in range(part)], axis=0)
+        sums[group, pl.ds(pl.multiple_of(i * SUB, SUB), SUB), :] = contract_cols(pick, pairs)
+
+    for group in range(n_state // part):
+        index = range(group * part, (group + 1) * part)
         rates = [rate2[n * SUB : (n + 1) * SUB, :] for n in index]
 
-        def token(i, carry):
+        def token(t, carry, after):
             g, acc = carry
-            t = tb - 1 - i
             at = pl.multiple_of(t * SUB, SUB)
-            dt_t = dt_s[pl.ds(at, SUB), :]
+            dt_t, dtu_t, gs_t = [ref[pl.ds(at, SUB), :] for ref in (dt_s, dtu_s, gs_s)]
             dtd = dt_t + bc[t, 2 * n_state]
-            gs_t = gs_s[pl.ds(at, SUB), :]
-            new_g, new_acc = [], []
+            new_g, new_acc, before, sources, reads = [], [], [], [], []
             gdt = ab = None
             for j, n in enumerate(index):
                 lam = gs_t * bc[t, n_state + n] + g[j]
-                lam_s[n, pl.ds(at, SUB), :] = lam
+                sources.append(lam * dtu_t)
+                reads.append(after[j] * gs_t)
                 back = jnp.exp2(dtd * rates[j]) * lam
-                thr = back * states[0, n, pl.ds(at, SUB), :]
+                before.append(states[0, n, pl.ds(at, SUB), :])
+                thr = back * before[j]
                 gdt = thr * rates[j] if gdt is None else gdt + thr * rates[j]
                 ab = lam * bc[t, n] if ab is None else ab + lam * bc[t, n]
                 new_g.append(back)
@@ -179,37 +194,73 @@
             else:
                 gdt_s[pl.ds(at, SUB), :] += gdt
                 ab_s[pl.ds(at, SUB), :] += ab
-            return tuple(new_g), tuple(new_acc)
+            return (tuple(new_g), tuple(new_acc)), before, sources, reads
+
+        def some_tokens(i, carry):
+            i = tb // run - 1 - i
+            if group:
+                add_lanes(group - 1, i)
+            late = pl.multiple_of((i + 1) * span, SUB)
+            after = [states[0, n, pl.ds(late, SUB), :] for n in index]
+            for k in range(run - 1, 0, -2):
+                t = i * run + k
+                carry, after, sources1, reads1 = token(t, carry, after)
+                carry, after, sources0, reads0 = token(t - 1, carry, after)
+                rows = pl.ds(pl.multiple_of((t - 1) * SUB, 2 * SUB), 2 * SUB)
+                for j in range(part):
+                    both_s[group % 2, j, rows, 0:LANES] = jnp.concatenate([sources0[j], sources1[j]], axis=0).astype(BF)
+                    both_s[group % 2, j, rows, LANES:] = jnp.concatenate([reads0[j], reads1[j]], axis=0).astype(BF)
+            return carry
 
         start = (
             tuple(g_ref[n * SUB : (n + 1) * SUB, :] for n in index),
             tuple(rate_out[n * SUB : (n + 1) * SUB, :] for n in index),
         )
-        g, acc = lax.fori_loop(0, tb, token, start, unroll=8)
+        g, acc = lax.fori_loop(0, tb // run, some_tokens, start, unroll=tb // run)
         for j, n in enumerate(index):
             g_ref[n * SUB : (n + 1) * SUB, :] = g[j]
             rate_out[n * SUB : (n + 1) * SUB, :] = acc[j]
+    for i in range(tb // run):
+        add_lanes(n_state // part - 1, i)
 
     ab = gather_lanes(ab_s, width, tb)
     gdt = gather_lanes(gdt_s, width, tb)
-    gu_out[...] = gs_v * skip + dt * ab
+    gu_out[...] = (gs_v * skip + dt * ab).astype(BF)
     grad_pre = ok * (gdt * LN2 + u * ab) * jax.nn.sigmoid(pre)
     vec_out[0:1, :] += jnp.sum(grad_pre, axis=0, keepdims=True)
     vec_out[1:2, :] += jnp.sum(gs_v * u, axis=0, keepdims=True)
     low = grad_pre.astype(BF)
     dtw_out[...] += lax.dot_general(rank[...], low, (((0,), (0,)), ((), ())), preferred_element_type=F32)
     rank_w = rank.shape[1]
-    part_out[:, 0:rank_w] = lax.dot_general(low, small[at_small.dt_w, :], (((1,), (1,)), ((), ())), preferred_element_type=F32)
-
-    lane = lax.broadcasted_iota(jnp.int32, (tb, LANES), 1)
-    tail = jnp.zeros((tb, LANES), F32)
-    dtu_v = dtu_s[...]
-    gs_l = gs_s[...]
-    for n in range(n_state):
-        for at, value in ((n, lam_s[n] * dtu_v), (n_state + n, states[0, n, SUB:, :] * gs_l)):
-            summed = jnp.dot(fold[...], value.astype(BF), preferred_element_type=F32)
-            tail = jnp.where(lane == at, jnp.sum(summed, axis=1, keepdims=True), tail)
-    part_out[:, rank_w:] = tail[:, 0 : 2 * n_state]
+    rows = pl.ds(pl.multiple_of((pl.num_programs(0) - 1 - pl.program_id(0)) * tb, tb), tb)
+    part_s[rows, 0:rank_w] = contract_cols(low, small[at_small.dt_w, :]).astype(BF)
+
+    take_row = lax.broadcasted_iota(jnp.int32, (2 * tb, tb // run * SUB), 0)
+    take_lane = lax.broadcasted_iota(jnp.int32, (2 * tb, tb // run * SUB), 1)
+    take = (take_lane == take_row % tb // run * SUB + take_row // tb).astype(F32).astype(BF)
+    keep_row = lax.broadcasted_iota(jnp.int32, (2 * tb, part * span), 0)
+    keep_lane = lax.broadcasted_iota(jnp.int32, (2 * tb, part * span), 1)
+    keep = keep_lane // SUB % run == keep_row % run
+    from_lane = lax.broadcasted_iota(jnp.int32, (part * span, LANES), 0)
+    to_lane = lax.broadcasted_iota(jnp.int32, (part * span, LANES), 1)
+    tail = jnp.zeros((2 * tb, LANES), F32)
+    for group in range(n_state // part):
+        chosen = jnp.dot(take, sums[group].astype(BF), preferred_element_type=F32)
+        chosen = jnp.where(keep, chosen, 0.0).astype(BF)
+        fold = (to_lane == group * part + from_lane // span).astype(F32).astype(BF)
+        tail = tail + jnp.dot(chosen, fold, preferred_element_type=F32)
+    part_s[rows, rank_w : rank_w + n_state] = tail[0:tb, 0:n_state].astype(BF)
+    part_s[rows, rank_w + n_state :] = tail[tb:, 0:n_state].astype(BF)
+
+    @pl.when(pl.program_id(0) == pl.num_programs(0) - 1)
+    def _():
+        proj = part_s.shape[1]
+        across = lax.broadcasted_iota(jnp.int32, (proj, proj), 0) == lax.broadcasted_iota(jnp.int32, (proj, proj), 1)
+        one = across.astype(F32).astype(BF)
+        for b in range(part_s.shape[0] // LANES):
+            packed_out[b * proj : (b + 1) * proj, :] = contract_cols(
+                one, part_s[b * LANES : (b + 1) * LANES, :]
+            ).astype(BF)
 
 
 def scan_backward(at, bc, rank, small, act, valid, rate2, gs, states, tb):
@@ -219,7 +270,7 @@
     whole = lambda i: (0, 0)
     row = lambda i: (nb - 1 - i, 0)
     rank_w = rank.shape[1]
-    fold = (jnp.arange(tb * SUB)[None, :] // SUB == jnp.arange(tb)[:, None]).astype(BF)
+    proj = rank_w + 2 * n_state
     return pl.pallas_call(
         functools.partial(backward_kernel, at),
         grid=(nb,),
@@ -232,29 +283,28 @@
             pl.BlockSpec(rate2.shape, whole),
             pl.BlockSpec((tb, width), row),
             pl.BlockSpec((1, n_state, (tb + 1) * SUB, LANES), lambda i: (nb - 1 - i, 0, 0, 0)),
-            pl.BlockSpec(fold.shape, whole),
         ],
         out_specs=[
-            pl.BlockSpec((tb, rank_w + 2 * n_state), row),
+            pl.BlockSpec((proj * slots // LANES, LANES), whole),
             pl.BlockSpec((tb, width), row),
             pl.BlockSpec((rank_w, width), whole),
             pl.BlockSpec((2, width), whole),
             pl.BlockSpec(rate2.shape, whole),
         ],
         out_shape=[
-            jax.ShapeDtypeStruct((slots, rank_w + 2 * n_state), F32),
-            jax.ShapeDtypeStruct((slots, width), F32),
+            jax.ShapeDtypeStruct((proj * slots // LANES, LANES), BF),
+            jax.ShapeDtypeStruct((slots, width), BF),
             jax.ShapeDtypeStruct((rank_w, width), F32),
             jax.ShapeDtypeStruct((2, width), F32),
             jax.ShapeDtypeStruct(rate2.shape, F32),
         ],
-        scratch_shapes=[pltpu.VMEM(rate2.shape, F32)]
+        scratch_shapes=[pltpu.VMEM((slots, proj), BF), pltpu.VMEM(rate2.shape, F32)]
         + [pltpu.VMEM((tb * SUB, LANES), F32)] * 5
-        + [pltpu.VMEM((n_state, tb * SUB, LANES), F32)],
-        compiler_params=pltpu.CompilerParams(vmem_limit_bytes=56 << 20),
+        + [pltpu.VMEM((2, 4, tb * SUB, 2 * LANES), BF), pltpu.VMEM((n_state // 4, tb, 4 * SUB * SUB), F32)],
+        compiler_params=pltpu.CompilerParams(vmem_limit_bytes=61 << 20),
         cost_estimate=small_cost(1 << 20),
         name="scan_backward",
-    )(bc, rank, small, act, valid, rate2, gs, states, fold)
+    )(bc, rank, small, act, valid, rate2, gs, states)
 
 
 def silu_grad(value, sig):
@@ -270,9 +320,24 @@
         ref[pl.ds(pl.multiple_of((2 * q + 1 - core) * rows, rows), rows), :] = other[q, 0:rows, :]
 
 
+def block_copies(ref, own, other, index, sems, first):
+    chips = own.shape[0]
+    rows = ref.shape[0] // (2 * chips)
+    core = lax.rem(index, 2)
+    found = []
+    for q in range(chips):
+        for blocks, d in ((own, 2 * q + core), (other, 2 * q + 1 - core)):
+            at = pl.ds(pl.multiple_of(d * rows, rows), rows)
+            found.append(
+                pltpu.make_async_copy(blocks.at[q, pl.ds(0, rows)], ref.at[at], sems.at[first + len(found)])
+            )
+    return found
+
+
 def read_row(ref, row, cols):
-    base = pl.multiple_of(row // SUB * SUB, SUB)
-    rows = ref[pl.ds(base, SUB), cols]
+    tile = SUB if ref.dtype == F32 else 2 * SUB
+    base = pl.multiple_of(row // tile * tile, tile)
+    rows = ref[pl.ds(base, tile), cols].astype(F32)
     mine = lax.broadcasted_iota(jnp.int32, rows.shape, 0) == row - base
     return jnp.sum(jnp.where(mine, rows, 0.0), axis=0, keepdims=True)
 
@@ -363,19 +428,19 @@
     return lax.rem(place - steps + n_line, n_line)
 
 
-def outer(kept, sent, right, kept_out, sent_out):
-    rows = min(256, kept.shape[1])
-
-    @pl.loop(0, kept.shape[1] // rows)
+def outer(lefts, right, outs):
+    rows = min(256, lefts[0].shape[1])
+
+    @pl.loop(0, lefts[0].shape[1] // rows)
     def _(r):
         at = pl.ds(pl.multiple_of(r * rows, rows), rows)
-        for left, out in ((kept, kept_out), (sent, sent_out)):
+        for left, out in zip(lefts, outs):
             found = lax.dot_general(left[:, at], right[...], (((0,), (0,)), ((), ())), preferred_element_type=F32)
             out[at, :] = found.astype(out.dtype)
 
 
 def outer_kernel(kept, sent, right, kept_out, sent_out):
-    outer(kept, sent, right, kept_out, sent_out)
+    outer((kept, sent), right, (kept_out, sent_out))
 
 
 def outer_product(kept, sent, right):
@@ -386,7 +451,7 @@
         in_specs=[vmem] * 3,
         out_specs=[vmem] * 2,
         out_shape=[jax.ShapeDtypeStruct(shape, BF)] * 2,
-        compiler_params=pltpu.CompilerParams(vmem_limit_bytes=48 << 20),
+        compiler_params=pltpu.CompilerParams(vmem_limit_bytes=61 << 20),
         cost_estimate=small_cost(1 << 20),
         name="outer_product",
     )(kept, sent, right)
@@ -410,7 +475,7 @@
 
 def project_kernel(n_line, n_dp, at, info, *refs):
     toks, refs = refs[:n_line], refs[n_line:]
-    own, other, small, allowed, gain, normed, kept, sent, inner, conv_out, activ, part32, w_nat, ext = refs
+    own, other, small, allowed, gain, normed, kept, sent, inner, conv_out, activ, part, w_nat, inner_s, ext = refs
     held, model = toks[0].shape
     slots = held * n_line
     width = w_nat.shape[1]
@@ -439,26 +504,28 @@
     @pl.loop(0, width // cb)
     def _(c):
         cols = pl.ds(pl.multiple_of(c * cb, cb), cb)
-        inner[:, cols] = jnp.dot(normed[...], w_nat[:, cols], preferred_element_type=F32)
+        inner_s[...] = jnp.dot(normed[...], w_nat[:, cols], preferred_element_type=F32)
+        inner[:, cols] = inner_s[...].astype(BF)
         vectors = small[at.rest, cols].astype(F32)
         for f in range(n_line):
             rows = slice(f * held, (f + 1) * held)
-            ext[SUB : SUB + held, :] = inner[rows, cols]
+            ext[SUB : SUB + held, :] = inner_s[rows, :]
             for k in range(1, rim + 1):
                 if f == 0:
                     ext[SUB - k : SUB - k + 1, :] = jnp.zeros((1, cb), F32)
                 else:
-                    ext[SUB - k : SUB - k + 1, :] = read_row(inner, (f - 1) * held + info[1 + f] - k, cols)
+                    ext[SUB - k : SUB - k + 1, :] = read_row(inner_s, (f - 1) * held + info[1 + f] - k, slice(None))
             total = vectors[taps : taps + 1, :]
             for lag in range(taps):
                 tapped = ext[SUB - lag : SUB - lag + held, :]
                 total = total + vectors[rim - lag : rim - lag + 1, :] * tapped * allowed[rows, lag : lag + 1]
-            conv_out[rows, cols] = total
+            conv_out[rows, cols] = total.astype(BF)
             activ[rows, cols] = (total * jax.nn.sigmoid(total)).astype(BF)
 
-    part32[...] = lax.dot_general(
-        activ[...], small[at.x_t, :], (((1,), (1,)), ((), ())), preferred_element_type=F32
-    )
+    proj = part.shape[0] * LANES // slots
+    for b in range(slots // LANES):
+        found = contract_cols(small[at.x_t, :], activ[b * LANES : (b + 1) * LANES, :])
+        part[b * proj : (b + 1) * proj, :] = found.astype(BF)
 
 
 def project(info, n_line, n_dp, toks, own, other, at, small, allowed):
@@ -468,15 +535,19 @@
     vmem = pl.BlockSpec(memory_space=pltpu.VMEM)
     shapes = [
         ((1, model), F32), ((slots, model), BF), ((slots, model // 2), BF), ((slots, model // 2), BF),
-        ((slots, width), F32), ((slots, width), F32), ((slots, width), BF), ((slots, proj), F32), ((model, width), BF),
+        ((slots, width), BF), ((slots, width), BF), ((slots, width), BF), ((proj * slots // LANES, LANES), BF),
     ]
     return pl.pallas_call(
         functools.partial(project_kernel, n_line, n_dp, at),
         in_specs=[pl.BlockSpec(memory_space=pltpu.SMEM)] + [vmem] * (4 + len(toks)),
         out_specs=[vmem] * len(shapes),
         out_shape=[jax.ShapeDtypeStruct(s, t) for s, t in shapes],
-        scratch_shapes=[pltpu.VMEM((SUB + slots // n_line, column_block(width, slots)), F32)],
-        compiler_params=pltpu.CompilerParams(vmem_limit_bytes=56 << 20),
+        scratch_shapes=[
+            pltpu.VMEM((model, width), BF),
+            pltpu.VMEM((slots, column_block(width, slots)), F32),
+            pltpu.VMEM((SUB + slots // n_line, column_block(width, slots)), F32),
+        ],
+        compiler_params=pltpu.CompilerParams(vmem_limit_bytes=61 << 20),
         cost_estimate=small_cost(1 << 20),
         name="project",
     )(info, *toks, own, other, small, allowed)
@@ -485,7 +556,7 @@
 def gate_kernel(n_line, n_dp, at, info, own, other, normed, y, act, small, *refs):
     out_own, out_other, refs = refs[: n_dp // 2], refs[n_dp // 2 : n_dp], refs[n_dp:]
     branches, refs = refs[:n_line], refs[n_line:]
-    gate, gated, w_nat, o_nat, *halves, branch = refs
+    gate, gated, o_nat, *halves, branch, w_nat = refs
     slots, width = y.shape
     model = normed.shape[1]
     place_blocks(w_nat, own, other, info[0])
@@ -523,7 +594,7 @@
     model = normed.shape[1]
     vmem = pl.BlockSpec(memory_space=pltpu.VMEM)
     shapes = [((slots // n_line, model), BF)] * n_line
-    shapes += [((slots, width), F32), ((slots, width), BF), ((model, width), BF), ((width, model), BF)]
+    shapes += [((slots, width), F32), ((slots, width), BF), ((width, model), BF)]
     if width // n_dp % LANES == 0:
         shapes += [((slots, width // 2), BF)] * 2
     outs = pl.pallas_call(
@@ -531,18 +602,18 @@
         in_specs=[pl.BlockSpec(memory_space=pltpu.SMEM)] + [vmem] * (6 + n_dp),
         out_specs=[vmem] * len(shapes),
         out_shape=[jax.ShapeDtypeStruct(s, t) for s, t in shapes],
-        scratch_shapes=[pltpu.VMEM((slots, model), BF)],
-        compiler_params=pltpu.CompilerParams(vmem_limit_bytes=58 << 20),
+        scratch_shapes=[pltpu.VMEM((slots, model), BF), pltpu.VMEM((model, width), BF)],
+        compiler_params=pltpu.CompilerParams(vmem_limit_bytes=61 << 20),
         cost_estimate=small_cost(1 << 20),
         name="gate_block",
     )(info, own, other, normed, y, act, small, *out_own, *out_other)
-    branches, (gate, gated, w_nat, o_nat), halves = list(outs[:n_line]), outs[n_line : n_line + 4], outs[n_line + 4 :]
-    return branches, gate, w_nat, o_nat, *(halves or cores(gated, 1))
+    branches, (gate, gated, o_nat), halves = list(outs[:n_line]), outs[n_line : n_line + 3], outs[n_line + 3 :]
+    return branches, gate, o_nat, *(halves or cores(gated, 1))
 
 
 def gate_back_kernel(n_line, at, info, *refs):
     cots, refs = refs[:n_line], refs[n_line:]
-    o_nat, gate, y, act, small, valid, normed_k, normed_s, gs, grad_gate, dout, gate_k, gate_s = refs
+    o_nat, gate, y, act, small, valid, normed, gs, grad_gate, dout, product = refs
     slots, width = y.shape
     held, model = cots[0].shape
     for s, cot in enumerate(cots):
@@ -562,41 +633,66 @@
         gs[:, cols] = grad * value * sig
         grad_gate[:, cols] = (grad * scan_out * silu_grad(value, sig)).astype(BF)
 
-    outer(normed_k, normed_s, grad_gate, gate_k, gate_s)
-
-
-def gate_back(info, n_line, cots, o_nat, gate, y, act, at, small, valid, normed_k, normed_s):
+    outer((normed,), grad_gate, (product,))
+
+
+def gate_back(info, n_line, cots, o_nat, gate, y, act, at, small, valid, normed):
     slots, width = y.shape
     model = o_nat.shape[1]
     vmem = pl.BlockSpec(memory_space=pltpu.VMEM)
     shapes = [((slots, width), F32), ((slots, width), BF), ((slots, model), BF)]
-    shapes += [((model // 2, width), BF)] * 2
+    shapes += [((model, width), BF)]
     return pl.pallas_call(
         functools.partial(gate_back_kernel, n_line, at),
-        in_specs=[pl.BlockSpec(memory_space=pltpu.SMEM)] + [vmem] * (8 + len(cots)),
+        in_specs=[pl.BlockSpec(memory_space=pltpu.SMEM)] + [vmem] * (7 + len(cots)),
         out_specs=[vmem] * len(shapes),
         out_shape=[jax.ShapeDtypeStruct(s, t) for s, t in shapes],
-        compiler_params=pltpu.CompilerParams(vmem_limit_bytes=58 << 20),
+        compiler_params=pltpu.CompilerParams(vmem_limit_bytes=61 << 20),
         cost_estimate=small_cost(1 << 20),
         name="gate_back",
-    )(info, *cots, o_nat, gate, y, act, small, valid, normed_k, normed_s)
+    )(info, *cots, o_nat, gate, y, act, small, valid, normed)
 
 
 def together(slots):
     return slots <= 1024
 
 
-def conv_back_kernel(n_line, n_dp, at, info, gp, gu, small, act, conv_out, inner, allowed, dtw, rate_grad, scan_vec,
-                     w_nat, normed_gate, *refs):
-    halves, refs = (refs[:2], refs[2:]) if together(gu.shape[0]) else ((), refs)
+def conv_back_kernel(n_line, n_dp, at, info, gp_part, gp_got, gu, small, act, conv_out, inner, allowed, dtw, rate_grad, scan_vec,
+                     grad_gate, *refs):
+    slots, width = gu.shape
+    inner_own, inner_other, gate_own, gate_other, *refs = refs
+    halves_far, refs = (refs[:2], refs[2:]) if together(slots) else ((), refs)
     grads, refs = refs[:n_line], refs[n_line:]
-    gi_low, kept, sent, *products, x_grad, vec, ext, gi, tail, grad_normed, column = refs
-    slots, width = gu.shape
+    products_far, refs = (refs[:2], refs[2:]) if together(slots) else ((), refs)
+    gi_low, refs = (None, refs) if together(slots) else (refs[0], refs[1:])
+    kept, sent, x_grad, vec, ext, gi, tail, grad_normed, column, gp, arrived, left, w_nat, gate_nat, *refs = refs
+    halves = ()
+    copies = block_copies(w_nat, inner_own, inner_other, info[0], arrived, 0)
+    copies += block_copies(gate_nat, gate_own, gate_other, info[0], arrived, n_dp)
+    if together(slots):
+        gi_low, *refs = refs
+        halves, products = refs[:2], refs[2:]
+        for i, (src, dst) in enumerate(zip(halves_far, halves)):
+            copies.append(pltpu.make_async_copy(src, dst, arrived.at[2 * n_dp + i]))
+    for copy in copies:
+        copy.start()
+    leaving = []
+
+    def leave(src, dst):
+        copy = pltpu.make_async_copy(src, dst, left.at[len(leaving)])
+        copy.start()
+        leaving.append(copy)
+
+    gp[...] = (gp_part[...] + gp_got[...].astype(F32)).astype(BF)
     held = slots // n_line
     taps = at.taps
     rim = taps - 1
     cb = column_block(width, slots)
-    x_grad[...] = lax.dot_general(gp[...], act[...], (((0,), (0,)), ((), ())), preferred_element_type=F32)
+    proj = x_grad.shape[0]
+    x_grad[...] = sum(
+        jnp.dot(gp[b * proj : (b + 1) * proj, :], act[b * LANES : (b + 1) * LANES, :], preferred_element_type=F32)
+        for b in range(slots // LANES)
+    )
     vec[...] = jnp.zeros_like(vec)
     for lag in range(taps):
         tail[lag, held : held + SUB, :] = jnp.zeros((SUB, cb), F32)
@@ -607,14 +703,21 @@
         vectors = small[at.rest, cols].astype(F32)
         for f in range(n_line - 1, -1, -1):
             rows = slice(f * held, (f + 1) * held)
-            ext[SUB : SUB + held, :] = inner[rows, cols]
+            ext[SUB : SUB + held, :] = inner[rows, cols].astype(F32)
             for k in range(1, rim + 1):
                 if f == 0:
                     ext[SUB - k : SUB - k + 1, :] = jnp.zeros((1, cb), F32)
                 else:
                     ext[SUB - k : SUB - k + 1, :] = read_row(inner, (f - 1) * held + info[1 + f] - k, cols)
-            grad = gu[rows, cols] + jnp.dot(gp[rows, :], small[at.x_t, cols], preferred_element_type=F32)
-            co = conv_out[rows, cols]
+            back = [
+                lax.dot_general(
+                    gp[b * proj : (b + 1) * proj, :], small[at.x_t, cols], (((0,), (0,)), ((), ())),
+                    preferred_element_type=F32,
+                )
+                for b in range(f * held // LANES, (f + 1) * held // LANES)
+            ]
+            grad = gu[rows, cols].astype(F32) + jnp.concatenate(back, axis=0)
+            co = conv_out[rows, cols].astype(F32)
             grad = grad * silu_grad(co, jax.nn.sigmoid(co))
             vec[taps : taps + 1, cols] += jnp.sum(grad, axis=0, keepdims=True)
             for lag in range(taps):
@@ -637,24 +740,37 @@
                 gi[slots + k : slots + k + 1, :] = row
         gi_low[:, cols] = gi[0:slots, :].astype(BF)
 
+    for copy in copies:
+        copy.wait()
     model = w_nat.shape[0]
     mb = column_block(model, slots)
 
     @pl.loop(0, model // mb)
     def _(c):
         cols = pl.ds(pl.multiple_of(c * mb, mb), mb)
-        found = lax.dot_general(gi_low[...], w_nat[cols, :], (((1,), (1,)), ((), ())), preferred_element_type=F32)
-        grad_normed[:, cols] = (found + normed_gate[:, cols]).astype(BF)
-
-    to_shifts(grad_normed, grads, info[1])
+        found = contract_cols(gi_low[...], w_nat[cols, :]) + contract_cols(grad_gate[...], gate_nat[cols, :])
+        grad_normed[:, cols] = found.astype(BF)
+
+    for s, grad in enumerate(grads):
+        first = pl.multiple_of(lax.rem(info[1] + s, n_line) * held, held)
+        leave(grad_normed.at[pl.ds(first, held)], grad)
     if halves:
-        outer(*halves, gi_low, *products)
+        step = model // 2 // 4
+        for r in range(4):
+            rows = slice(r * step, (r + 1) * step)
+            for half, product, out in zip(halves, products, products_far):
+                product[rows, :] = lax.dot_general(
+                    half[:, rows], gi_low[...], (((0,), (0,)), ((), ())), preferred_element_type=F32
+                ).astype(BF)
+                leave(product.at[pl.ds(r * step, step)], out.at[pl.ds(r * step, step)])
     vec[taps + 1 : taps + 3, :] = scan_vec[...]
     owned = width // n_dp
     if kept.shape[0] == 1:
         kept[0, at.dt_w, :], kept[0, at.x_t, :], kept[0, at.a_t, :], kept[0, at.rest, :] = (
             dtw[...], x_grad[...], rate_grad[...], vec[...]
         )
+        for copy in leaving:
+            copy.wait()
         return
     core = lax.rem(info[0], 2)
     fold = kept.shape[1]
@@ -665,31 +781,32 @@
                 column[rows, :] = source[:, cols]
             for b in range(width // owned):
                 ref[q, :, b * owned : (b + 1) * owned] = column[b * fold : (b + 1) * fold, :].astype(ref.dtype)
-
-
-def conv_back(info, n_line, n_dp, gp, gu, at, small, act, conv_out, inner, allowed, dtw, rate_grad, scan_vec, w_nat, normed_gate,
-              normed_k, normed_s):
+    for copy in leaving:
+        copy.wait()
+
+
+def conv_back(info, n_line, n_dp, gp_part, gp_got, gu, at, small, act, conv_out, inner, allowed, dtw, rate_grad, scan_vec, grad_gate,
+              inner_blocks, gate_blocks, normed_k, normed_s):
     slots, width = gu.shape
-    held = slots // n_line
+    held, model = slots // n_line, 2 * normed_k.shape[1]
     cb = column_block(width, slots)
     owned = width // n_dp
-    tiles = owned % LANES == 0
-    vmem = pl.BlockSpec(memory_space=pltpu.VMEM)
+    tiles, one = owned % LANES == 0, together(slots)
+    vmem, away = pl.BlockSpec(memory_space=pltpu.VMEM), pl.BlockSpec(memory_space=pl.ANY)
     fold = at.fold(n_dp)
     shape = (n_dp // 2, fold, width) if tiles else (1, at.rows, width)
-    model = w_nat.shape[0]
-    halves = [normed_k, normed_s] if together(slots) else []
+    later = [*inner_blocks, *gate_blocks] + ([normed_k, normed_s] if one else [])
+    low, half = jax.ShapeDtypeStruct((slots, width), BF), jax.ShapeDtypeStruct((model // 2, width), BF)
     outs = pl.pallas_call(
         functools.partial(conv_back_kernel, n_line, n_dp, at),
-        in_specs=[pl.BlockSpec(memory_space=pltpu.SMEM)] + [vmem] * (12 + len(halves)),
-        out_specs=[vmem] * (n_line + 3 + len(halves)),
+        in_specs=[pl.BlockSpec(memory_space=pltpu.SMEM)] + [vmem] * 12 + [away] * len(later),
+        out_specs=[away] * n_line + ([away] * 2 if one else [vmem]) + [vmem] * 2,
         out_shape=[jax.ShapeDtypeStruct((held, model), BF)] * n_line
+        + ([half] * 2 if one else [low])
         + [
-            jax.ShapeDtypeStruct((slots, width), BF),
             jax.ShapeDtypeStruct(shape, F32),
             jax.ShapeDtypeStruct(shape if tiles else (SUB, LANES), BF if tiles else F32),
-        ]
-        + [jax.ShapeDtypeStruct((model // 2, width), BF)] * len(halves),
+        ],
         scratch_shapes=[
             pltpu.VMEM((at.x_t.stop - at.x_t.start, width), F32),
             pltpu.VMEM((16, width), F32),
@@ -698,14 +815,20 @@
             pltpu.VMEM((at.taps, held + SUB, cb), F32),
             pltpu.VMEM((slots, model), BF),
             pltpu.VMEM((n_dp * fold, owned), F32),
-        ],
-        compiler_params=pltpu.CompilerParams(vmem_limit_bytes=58 << 20),
+            pltpu.VMEM(gp_got.shape, BF),
+            pltpu.SemaphoreType.DMA((2 * n_dp + 2,)),
+            pltpu.SemaphoreType.DMA((n_line + 8,)),
+        ]
+        + [pltpu.VMEM((model, width), BF)] * 2
+        + ([pltpu.VMEM((slots, width), BF)] + [pltpu.VMEM((slots, model // 2), BF)] * 2 if one else [])
+        + ([pltpu.VMEM((model // 2, width), BF)] * 2 if one else []),
+        compiler_params=pltpu.CompilerParams(vmem_limit_bytes=61 << 20),
         cost_estimate=small_cost(1 << 20),
         name="conv_back",
-    )(info, gp, gu, small, act, conv_out, inner, allowed, dtw, rate_grad, scan_vec, w_nat, normed_gate, *halves)
-    grads, (gi_low, kept, sent, *products) = outs[:n_line], outs[n_line:]
-    if not products:
-        products = outer_product(normed_k, normed_s, gi_low)
+    )(info, gp_part, gp_got, gu, small, act, conv_out, inner, allowed, dtw, rate_grad, scan_vec, grad_gate, *later)
+    grads, (*products, kept, sent) = outs[:n_line], outs[n_line:]
+    if not one:
+        products = outer_product(normed_k, normed_s, products[0])
     if not tiles:
         kept, sent = [
             part.reshape(at.rows, n_dp // 2, owned).transpose(1, 0, 2) for part in cores(kept[0], 1)
@@ -761,12 +884,13 @@
     return lax.optimization_barrier(both.reshape((-1,) + own.shape[1:]))
 
 
-def total_line(value):
-    reach = 1
-    while reach < lax.axis_size("fsdp"):
-        value = value + swap(value.astype(BF), "fsdp", reach).astype(F32)
+def last_line(value, reach):
+    while True:
+        got = swap(value.astype(BF), "fsdp", reach)
         reach *= 2
-    return value
+        if reach >= lax.axis_size("fsdp"):
+            return value, got
+        value = value + got.astype(F32)
 
 
 def fence(*values):
@@ -785,27 +909,24 @@
 
 def add_core_kernel(kept, got, *refs):
     *small, out = refs
-    chips, rows, width = out.shape
+    whole = kept.shape[0]
+    out[0, 0:whole, :] = (kept[...].astype(F32) + got[...].astype(F32)).astype(BF)
+    if small:
+        out[0, whole:, :] = (small[0][0] + small[1][0].astype(F32)).astype(BF)
+
+
+def add_core(kept, got, *small):
+    chips, width = lax.axis_size("dp") // 2, kept.shape[1]
     whole = kept.shape[0] // chips
-
-    @pl.loop(0, chips)
-    def _(q):
-        at = pl.ds(pl.multiple_of(q * whole, whole), whole)
-        out[q, 0:whole, :] = (kept[at, :].astype(F32) + got[at, :].astype(F32)).astype(BF)
-        if small:
-            out[q, whole:rows, :] = (small[0][q] + small[1][q].astype(F32)).astype(BF)
-
-
-def add_core(kept, got, *small):
-    chips = lax.axis_size("dp") // 2
-    rows = kept.shape[0] // chips + (small[0].shape[1] if small else 0)
-    vmem = pl.BlockSpec(memory_space=pltpu.VMEM)
+    more = small[0].shape[1] if small else 0
     return pl.pallas_call(
         add_core_kernel,
-        in_specs=[vmem] * (2 + len(small)),
-        out_specs=vmem,
-        out_shape=jax.ShapeDtypeStruct((chips, rows, kept.shape[1]), BF),
-        compiler_params=pltpu.CompilerParams(vmem_limit_bytes=32 << 20),
+        grid=(chips,),
+        in_specs=[pl.BlockSpec((whole, width), lambda q: (q, 0))] * 2
+        + [pl.BlockSpec((1, more, width), lambda q: (q, 0, 0))] * len(small),
+        out_specs=pl.BlockSpec((1, whole + more, width), lambda q: (q, 0, 0)),
+        out_shape=jax.ShapeDtypeStruct((chips, whole + more, width), BF),
+        compiler_params=pltpu.CompilerParams(vmem_limit_bytes=61 << 20),
         cost_estimate=small_cost(1 << 10),
         name="add_core",
     )(kept, got, *small)
@@ -823,17 +944,15 @@
     return total
 
 
-def sent_far(blocks, u):
-    chip = lax.div(lax.axis_index("dp"), 2)
-    return lax.dynamic_index_in_dim(blocks, jnp.bitwise_xor(chip, u), 0, keepdims=False).astype(BF)
+def sent_far(kept, got, u):
+    rows = kept.shape[0] // (lax.axis_size("dp") // 2)
+    at = jnp.bitwise_xor(lax.div(lax.axis_index("dp"), 2), u) * rows
+    return sum(lax.dynamic_slice_in_dim(part, at, rows, 0).astype(F32) for part in (kept, got)).astype(BF)
 
 
 def far(blocks, u):
-    return swap(sent_far(blocks, u), "dp", 2 * u)
-
-
-def contract_cols(left, right):
-    return lax.dot_general(left, right, (((1,), (1,)), ((), ())), preferred_element_type=F32)
+    block = lax.dynamic_index_in_dim(blocks, jnp.bitwise_xor(lax.div(lax.axis_index("dp"), 2), u), 0, keepdims=False)
+    return swap(block.astype(BF), "dp", 2 * u)
 
 
 def per_device(
@@ -909,82 +1028,76 @@
 
     gate_own = to_chips(gate_rep)
     cots = {0: cotangent, 1: shift(cotangent, "fsdp", 1)}
-    full_gain, normed, normed_kept, normed_sent, inner, conv_out, activ, part, inner_nat = project(
+    full_gain, normed, normed_kept, normed_sent, inner, conv_out, activ, low = project(
         info, n_line, n_dp, [toks[s] for s in range(n_line)], inner_own, inner_other, at, small, allowed
     )
-    part, rate2, cots, near, gate_own = fence(part, rate2, cots, near, gate_own)
-
-    projected = total_line(part)
+    low, rate2, cots, near = fence(low, rate2, cots, near)
+
+    part = low.astype(F32) + swap(low, "fsdp", 1).astype(F32)
+    part, gate_own, near = fence(part, gate_own, near)
+    part, got = last_line(part, 2)
     out_near, out_other = near, [swap(block, "dp", 1) for block in near]
-    projected, cots, out_near, out_other = fence(projected, cots, out_near, out_other)
+    part, got, cots, out_near, out_other = fence(part, got, cots, out_near, out_other)
+    projected = part + got.astype(F32)
 
     gate_other = swap(gate_own, "dp", 1)
     for s in steps[1:]:
         cots[s] = shift(cots[0], "fsdp", s)
+    projected = projected.reshape(-1, proj, LANES).transpose(0, 2, 1).reshape(slots, proj)
     rank_low = projected[:, :rank_w].astype(BF)
     bc = jnp.concatenate([projected[:, rank_w:], opens], axis=1)
     scanned, states = scan_forward(at, bc, rank_low, small, activ, valid, rate2, tb)
     scanned, gate_own, gate_other, cots[n_line - 1] = fence(scanned, gate_own, gate_other, cots[n_line - 1])
 
-    branches, gate, gate_nat, out_nat, *gated = gate_block(
+    branches, gate, out_nat, *gated = gate_block(
         info, n_line, n_dp, gate_own, gate_other, out_near, out_other, normed, scanned, activ, at, small
     )
-    branches, gate, gated, gate_nat, out_nat, cots = fence(branches, gate, gated, gate_nat, out_nat, cots)
+    branches, gate, gated, out_nat, cots = fence(branches, gate, gated, out_nat, cots)
 
     branches[1] = shift(branches[1], "fsdp", 1)
-    grad_scan, grad_gate, dout, gate_kept, gate_sent = gate_back(
-        info, n_line, [cots[s] for s in range(n_line)], out_nat, gate, scanned, activ, at, small, valid,
-        normed_kept, normed_sent,
-    )
-    branches, grad_scan, grad_gate, dout, gated, gate_kept, gate_sent = fence(
-        branches, grad_scan, grad_gate, dout, gated, gate_kept, gate_sent
-    )
-    gate_grad = add_core(gate_kept, swap(gate_sent, "dp", 1))
-    gate_grad, grad_scan, branches = fence(gate_grad, grad_scan, branches)
-
-    gate_rows = add_chips(gate_grad).astype(BF)
+    grad_scan, grad_gate, dout, gate_grad = gate_back(
+        info, n_line, [cots[s] for s in range(n_line)], out_nat, gate, scanned, activ, at, small, valid, normed
+    )
+    branches, grad_scan, grad_gate, dout, gated, gate_grad = fence(
+        branches, grad_scan, grad_gate, dout, gated, gate_grad
+    )
+
+    gate_sums = lax.all_to_all(gate_grad.reshape(n_dp, -1, width), "dp", 0, 0)
     for s in steps[1:]:
         branches[s] = shift(branches[s], "fsdp", s)
-    part, grad_u, dt_w_grad, vectors, rate_sum = scan_backward(
+    low, grad_u, dt_w_grad, vectors, rate_sum = scan_backward(
         at, bc, rank_low, small, activ, valid, rate2, grad_scan, states, tb
     )
-    part, branches, gated, dout, grad_gate, rate_sum, gate_rows = fence(
-        part, branches, gated, dout, grad_gate, rate_sum, gate_rows
-    )
+    low, branches, gated, dout, grad_gate, rate_sum = fence(low, branches, gated, dout, grad_gate, rate_sum)
 
     out_kept, out_sent = outer_product(*gated, dout)
-    reach = 1
-    while reach < n_line:
-        part = part + swap(part.astype(BF), "fsdp", reach).astype(F32)
-        reach *= 2
-        if reach == 2:
-            part, out_kept, out_sent, grad_gate = fence(part, out_kept, out_sent, grad_gate)
-            out_got = swap(out_sent, "dp", 1)
-            normed_gate = contract_cols(grad_gate, gate_nat)
+    part = low.astype(F32) + swap(low, "fsdp", 1).astype(F32)
+    part, out_kept, out_sent, grad_gate = fence(part, out_kept, out_sent, grad_gate)
+    out_got = swap(out_sent, "dp", 1)
+    out_far = {u: sent_far(out_kept, out_got, u) for u in range(n_dp // 2)}
+    gate_rows = jnp.sum(gate_sums.astype(F32), axis=0).astype(BF)
     rate_grad = rate_sum.reshape(n_state, SUB, LANES)[:, :chunks].reshape(n_state, width) * rates
-    grad_projected, out_kept, out_got, normed_gate, rate_grad, gate_rows = fence(
-        part.astype(BF), out_kept, out_got, normed_gate, rate_grad, gate_rows
-    )
+    part, got = last_line(part, 2)
+    part, got, out_far, rate_grad, gate_rows = fence(part, got, out_far, rate_grad, gate_rows)
 
     gate_got = to_line(gate_rows.reshape(n_line, in_rows, width))
-    out_grad = add_core(out_kept, out_got)
     grads, inner_kept, inner_sent, small_kept, small_sent = conv_back(
-        info, n_line, n_dp, grad_projected, grad_u, at, small, activ, conv_out, inner, allowed,
-        dt_w_grad, rate_grad, vectors, inner_nat, normed_gate, normed_kept, normed_sent,
-    )
-    out_far = {u: sent_far(out_grad, u) for u in chips}
-    grads, gate_got, inner_kept, inner_sent, small_kept, small_sent, out_grad, out_far = fence(
-        grads, gate_got, inner_kept, inner_sent, small_kept, small_sent, out_grad, out_far
+        info, n_line, n_dp, part, got, grad_u, at, small, activ, conv_out, inner, allowed,
+        dt_w_grad, rate_grad, vectors, grad_gate, (inner_own, inner_other), (gate_own, gate_other),
+        normed_kept, normed_sent,
+    )
+    grads, gate_got, inner_kept, inner_sent, small_kept, small_sent, out_far, branches = fence(
+        grads, gate_got, inner_kept, inner_sent, small_kept, small_sent, out_far, branches
     )
 
     folded = owned % LANES == 0
     grads[1] = shift(grads[1], "fsdp", 1)
-    for u in chips[2:]:
+    for u in chips[:2]:
         out_far[u] = swap(out_far[u], "dp", 2 * u)
     inner_got, small_got = swap(inner_sent, "dp", 1), swap(small_sent, "dp", 1)
     inner_grad = add_core(inner_kept, inner_got, *((small_kept, small_got) if folded else ()))
-    inner_grad, grads, small_kept, small_got, out_grad, out_far, branches = fence(
-        inner_grad, grads, small_kept, small_got, out_grad, out_far, branches
+    inner_grad, grads, small_kept, small_got, out_far, branches = fence(
+        inner_grad, grads, small_kept, small_got, out_far, branches
     )
 
     got = to_chips(inner_grad)
@@ -992,23 +1105,22 @@
     small_sum = jnp.sum(got[:, n_line * in_rows :].astype(F32), axis=0)
     for s in steps[1:]:
         grads[s] = shift(grads[s], "fsdp", s)
-    inner_rows, small_sum, grads, small_kept, small_got, out_grad, out_far, branches = fence(
-        inner_rows, small_sum, grads, small_kept, small_got, out_grad, out_far, branches
-    )
-
-    inner_got = to_line(inner_rows.reshape(n_line, in_rows, width))
-    for u in chips[:2]:
+    for u in chips[2:]:
         out_far[u] = swap(out_far[u], "dp", 2 * u)
-    grad_normed = sum(p.astype(F32) for p in grads)
-    grad_normed, small_sum, small_kept, small_got, branches = fence(
-        grad_normed, small_sum, small_kept, small_got, branches
-    )
-    out_weight_grad = lax.dynamic_index_in_dim(out_grad, lax.div(group, 2), 0, keepdims=False).astype(F32)
-    out_weight_grad = out_weight_grad + sum(out_far[u].astype(F32) for u in chips)
     if folded:
         small_grads = small_sum.reshape(-1, n_dp, owned).transpose(1, 0, 2).reshape(-1, owned)
     else:
         small_grads = add_chips_near(small_kept + small_got.astype(F32))
+    dt_g, x_g, a_g = small_grads[at.dt_w], small_grads[at.x_t], small_grads[at.a_t]
+    tail_g = small_grads[at.rest]
+    conv_g, conv_b_g, dt_b_g, skip_g = tail_g[:taps], tail_g[taps : taps + 1], tail_g[taps + 1 : taps + 2], tail_g[taps + 2 : taps + 3]
+    small_out = [conv_g, conv_b_g[0], x_g.T, dt_g, dt_b_g[0], a_g.T, skip_g[0]]
+    inner_rows, grads, out_far, branches, small_out = fence(inner_rows, grads, out_far, branches, small_out)
+
+    inner_got = to_line(inner_rows.reshape(n_line, in_rows, width))
+    grad_normed = sum(p.astype(F32) for p in grads)
+    grad_normed, branches, out_far = fence(grad_normed, branches, out_far)
+    out_weight_grad = sum(part.astype(F32) for part in out_far.values())
     own_valid = lax.dynamic_slice_in_dim(valid, place * held_slots, held_slots, 0)
     own_f = own_tokens.astype(F32)
     output = (own_f + own_valid * sum(p.astype(F32) for p in branches)).astype(BF)
@@ -1018,14 +1130,8 @@
     token_grad = own_cot.astype(F32) + own_scale * (
         grad_unit - unit * jnp.mean(grad_unit * unit, axis=1, keepdims=True)
     )
-    dt_g, x_g, a_g = small_grads[at.dt_w], small_grads[at.x_t], small_grads[at.a_t]
-    tail_g = small_grads[at.rest]
-    conv_g, conv_b_g, dt_b_g, skip_g = tail_g[:taps], tail_g[taps : taps + 1], tail_g[taps + 1 : taps + 2], tail_g[taps + 2 : taps + 3]
     in_weight_grad, gain_grad = join_columns(inner_got, gate_got, in_weight, gain, n_dp)
-    return (
-        output, token_grad, gain_grad, in_weight_grad, conv_g, conv_b_g[0], x_g.T, dt_g, dt_b_g[0], a_g.T,
-        skip_g[0], out_weight_grad,
-    )
+    return output, token_grad, gain_grad, in_weight_grad, *small_out, out_weight_grad
 
 
 def solution(mesh):

time: 405 us -> 365 us (0.901)
  waiting for transfers between devices: 120 us -> 107 us
  Pallas kernels: 141 us -> 134 us
  matrix products: 6.9 us -> 0 us
  local copies, waits for them, and re-layouts: 26.5 us -> 21.1 us
  starting transfers between devices: 79.7 us -> 74.8 us
    ppermute x21 -> x20, waiting for transfers between devices: 38.7 us -> 28.8 us  [swap(): return lax.ppermute(value, axis, [(i, i ^ mask) for i in range(count)])]
    unnamed x112 -> x104, local copies, waits for them, and re-layouts: 13.6 us -> 5 us
    dot_general x1 -> x0, matrix products: 6.9 us -> none  [contract_cols(): lax.dot_general(left, right, (((1,), (1,)), ((), ())), preferred_element_...]
    ppermute x12, waiting for transfers between devices: 49 us -> 42.7 us  [shift(): lax.ppermute(value, axis, [(i, (i + steps) % count) for i in range(count)])]
    all_to_all x3, waiting for transfers between devices: 6.95 us -> 12.2 us  [to_line(): return lax.all_to_all(blocks, 'fsdp', 0, 0)]
    all_to_all x3, starting transfers between devices: 18.2 us -> 13.5 us  [to_line(): return lax.all_to_all(blocks, 'fsdp', 0, 0)]
    all_to_all x0 -> x1, starting transfers between devices: none -> 4.56 us  [per_device(): gate_sums = lax.all_to_all(gate_grad.reshape(n_dp, -1, width), 'dp', 0, 0)]
    all_to_all x4 -> x3, starting transfers between devices: 16.4 us -> 12.2 us  [to_chips(): return lax.all_to_all(blocks, 'dp', 0, 0, axis_index_groups=chips_of('dp'))]
  transfers between devices with their start and end apart: 40 -> 39, of which waited for: 16 -> 17; matrix products, arithmetic and copies ran while one was open for 10% -> 10% of each run, Pallas kernels for 33% -> 35%
where the time goes in v3:
time: 365 us; the launch traced here: 363 us
  Pallas kernels  134 us (37%)
  waiting for transfers between devices  107 us (29%)
  starting transfers between devices  74.8 us (20%)
  other arithmetic  23.4 us (6%)
  local copies, waits for them, and re-layouts  21.1 us (6%)
    ppermute x12, waiting for transfers between devices, shift(): lax.ppermute(value, axis, [(i, (i + steps) % count) for i in range(count)])  42.7 us
    pallas_call x1, Pallas kernels, scan_backward(): pl.pallas_call(functools.partial(backward_kernel, at), grid=(nb,), in_spe...  34.4 us
    ppermute x12, starting transfers between devices, shift(): lax.ppermute(value, axis, [(i, (i + steps) % count) for i in range(count)])  29.3 us
    ppermute x20, waiting for transfers between devices, swap(): return lax.ppermute(value, axis, [(i, i ^ mask) for i in range(count)])  28.8 us
    all_to_all x3, waiting for transfers between devices, to_chips(): return lax.all_to_all(blocks, 'dp', 0, 0, axis_index_groups=chips_of('dp'))  23.1 us
    pallas_call x1, Pallas kernels, conv_back(): pl.pallas_call(functools.partial(conv_back_kernel, n_line, n_dp, at), in_...  18.8 us
    pallas_call x1, Pallas kernels, scan_forward(): pl.pallas_call(functools.partial(forward_kernel, at), grid=(nb,), in_spec...  18.3 us
    pallas_call x1, Pallas kernels, gate_block(): pl.pallas_call(functools.partial(gate_kernel, n_line, n_dp, at), in_specs...  16.8 us
  transfers between devices with their start and end apart: 39, of which 17 were waited for; matrix products, arithmetic and copies ran while one was open for 10% of the time, Pallas kernels for 35%

profile of v3, /device:TPU:0, one launch (start us, length us, event | category | flops | bytes accessed | tf_op | source)
XLA Modules:
  0.0 363.3 jit_solution(4057460107113344798)
XLA Ops:
  3.2 6.4 %all-to-all-start = ((bf16[4,144,1024]{2,1,0:T(8,128)(2,1)}), bf16[4,144,1024]{2,1,0:T(8,128)(2,1)S(1)}, u32[]{:S(2)}, u32[]{:S(2)}) async-start(bf16[4,144,1024]{2,1,0:T(8,128)(2,1)} %split_columns.1), calls=%async_computation | async-start | bytes 2359296 | tf_op jit(solution)/shard_map/all_to_all | solution.py:854
  21.1 23.2 %collective-permute-done.refs_1_ = bf16[128,2048]{1,0:T(8,128)(2,1)} collective-permute-done((bf16[128,2048]{1,0:T(8,128)(2,1)S(1)}, bf16[128,2048]{1,0:T(8,128)(2,1)}, u32[]{:S(2)}, u32[]{:S(2)}) %collective-permute-start) | collective-permute-done | bytes 524320 | tf_op jit(solution)/shard_map/ppermute | solution.py:846
  44.3 5.2 %all-to-all-done = bf16[4,144,1024]{2,1,0:T(8,128)(2,1)S(1)} async-done(((bf16[4,144,1024]{2,1,0:T(8,128)(2,1)}), bf16[4,144,1024]{2,1,0:T(8,128)(2,1)S(1)}, u32[]{:S(2)}, u32[]{:S(2)}) %all-to-all-start) | async-done | bytes 1179680 | tf_op jit(solution)/shard_map/all_to_all | solution.py:854
  52.1 3.8 %all-to-all-start.1 = ((bf16[4,272,1024]{2,1,0:T(8,128)(2,1)}), bf16[4,272,1024]{2,1,0:T(8,128)(2,1)S(1)}, u32[]{:S(2)}, u32[]{:S(2)}) async-start(bf16[4,272,1024]{2,1,0:T(8,128)(2,1)} %broadcast_in_dim.42), calls=%async_computation.1 | async-start | bytes 4456448 | tf_op jit(solution)/shard_map/all_to_all | solution.py:858
  65.7 14.1 %collective-permute-done.4.refs_2_ = bf16[128,2048]{1,0:T(8,128)(2,1)} collective-permute-done((bf16[128,2048]{1,0:T(8,128)(2,1)S(1)}, bf16[128,2048]{1,0:T(8,128)(2,1)}, u32[]{:S(2)}, u32[]{:S(2)}) %collective-permute-start.4) | collective-permute-done | bytes 524320 | tf_op jit(solution)/shard_map/ppermute | solution.py:846
  83.7 4.5 %all-to-all-start.2 = ((bf16[4,256,1024]{2,1,0:T(8,128)(2,1)}), bf16[4,256,1024]{2,1,0:T(8,128)(2,1)}, u32[]{:S(2)}, u32[]{:S(2)}) async-start(bf16[4,256,1024]{2,1,0:T(8,128)(2,1)} %broadcast_in_dim.43), calls=%async_computation.2 | async-start | bytes 4194304 | tf_op jit(solution)/shard_map/all_to_all | solution.py:858
  88.4 9.9 %collective-permute-start.8 = (bf16[128,2048]{1,0:T(8,128)(2,1)}, bf16[128,2048]{1,0:T(8,128)(2,1)S(1)}, u32[]{:S(2)}, u32[]{:S(2)}) collective-permute-start(bf16[128,2048]{1,0:T(8,128)(2,1)} %refs_0_.1), channel_id=1, source_target_pairs={{0,1},{1,2},{2,3},{3,0},{4,5},{5,6},{6,7},{7,4},{8,9},{9,10},{10,1... | collective-permute-start | bytes 1572872 | tf_op jit(solution)/shard_map/ppermute | solution.py:846
  99.0 13.2 %project.1 = (f32[1,2048]{1,0:T(1,128)}, bf16[512,2048]{1,0:T(8,128)(2,1)}, bf16[512,1024]{1,0:T(8,128)(2,1)}, bf16[512,1024]{1,0:T(8,128)(2,1)}, bf16[512,1024]...) custom-call(s32[6]{0:T(128)} %pad_add_fusion.info, ...), custom_call_target="tpu_custom_call" | custom-call | flops 1048576 | bytes 65536 | tf_op jit(solution)/shard_map/project/pallas_call | solution.py:540
  112.7 6.0 %collective-permute-done.9 = bf16[640,128]{1,0:T(8,128)(2,1)S(1)} collective-permute-done((bf16[640,128]{1,0:T(8,128)(2,1)}, bf16[640,128]{1,0:T(8,128)(2,1)S(1)}, u32[]{:S(2)}, u32[]{:S(2)}) %collective-permute-start.9) | collective-permute-done | bytes 163872 | tf_op jit(solution)/shard_map/ppermute | solution.py:841
  123.3 7.6 %collective-permute-done.10 = bf16[640,128]{1,0:T(8,128)(2,1)S(1)} collective-permute-done((bf16[640,128]{1,0:T(8,128)(2,1)S(1)}, bf16[640,128]{1,0:T(8,128)(2,1)S(1)}, u32[]{:S(2)}, u32[]{:S(2)}) %collective-permute-start.10) | collective-permute-done | bytes 163872 | tf_op jit(solution)/shard_map/ppermute | solution.py:841
  139.6 18.3 %scan_forward.1 = (f32[512,1024]{1,0:T(8,128)}, f32[8,16,520,128]{3,2,1,0:T(8,128)}) custom-call(f32[512,33]{1,0:T(8,128)} %pad_maximum_fusion.1.bc, bf16[512,128]{1,0:T(8,128)(2,1)} %slice.143.rank, bf16[320,1024]{1,0:T(8,128)(2,1)} %copy-done.2, bf16[512,1024]{1,0:T(8,128)(2,1)} %get-tuple-element.283.act.refs_7_, ...), custom_call_target="tpu_custom_call" | custom-call | flops 1048576 | bytes 65536 | tf_op jit(solution)/shard_map/scan_forward/pallas_call | solution.py:103
  159.2 16.8 %gate_block.1 = (bf16[128,2048]{1,0:T(8,128)(2,1)}, bf16[128,2048]{1,0:T(8,128)(2,1)}, bf16[128,2048]{1,0:T(8,128)(2,1)}, bf16[128,2048]{1,0:T(8,128)(2,1)}, f32...) custom-call(s32[6]{0:T(128)} %pad_add_fusion.info, ...), custom_call_target="tpu_custom_call" | custom-call | flops 1048576 | bytes 65536 | tf_op jit(solution)/shard_map/gate_block/pallas_call | solution.py:600
  177.4 16.0 %gate_back.1 = (f32[512,1024]{1,0:T(8,128)}, bf16[512,1024]{1,0:T(8,128)(2,1)}, bf16[512,2048]{1,0:T(8,128)(2,1)}, bf16[2048,1024]{1,0:T(8,128)(2,1)}) custom-call(s32[6]{0:T(128)} %pad_add_fusion.info, bf16[128,2048]{1,0:T(8,128)(2,1)} %refs_0_.1, bf16[128,2048]{1,0:T(8,128)(2,1)} %copy-done.27, bf16[128,2048]{1,0:T(8,128)(2,1)} %collective-permute-done.17.refs_2_, ...), custom_call_target="tpu_custom_call" | custom-call | flops 1048576 | bytes 65536 | tf_op jit(solution)/shard_map/gate_back/pallas_call | solution.py:645
  194.3 4.6 %all-to-all-start.3 = ((bf16[8,256,1024]{2,1,0:T(8,128)(2,1)}), bf16[8,256,1024]{2,1,0:T(8,128)(2,1)}, u32[]{:S(2)}, u32[]{:S(2)}) async-start(bf16[8,256,1024]{2,1,0:T(8,128)(2,1)} %bitcast.58), calls=%async_computation.3 | async-start | bytes 8388608 | tf_op jit(solution)/shard_map/all_to_all | solution.py:1065
  203.4 34.4 %scan_backward.1 = (bf16[640,128]{1,0:T(8,128)(2,1)}, bf16[512,1024]{1,0:T(8,128)(2,1)}, f32[128,1024]{1,0:T(8,128)}, f32[2,1024]{1,0:T(2,128)}, f32[128,128]{1,0:T(8,128)}) custom-call(f32[512,33]{1,0:T(8,128)} %pad_maximum_fusion.1.bc, bf16[512,128]{1,0:T(8,128)(2,1)} %slice.143.rank, bf16[320,1024]{1,0:T(8,128)(2,1)} %copy-done.2, ...), custom_call_target="tpu_custom_call" | custom-call | flops 1048576 | bytes 65536 | tf_op jit(solution)/shard_map/scan_backward/pallas_call | solution.py:274
  238.0 6.4 %outer_product.1 = (bf16[512,2048]{1,0:T(8,128)(2,1)}, bf16[512,2048]{1,0:T(8,128)(2,1)}) custom-call(bf16[512,512]{1,0:T(8,128)(2,1)} %get-tuple-element.339.kept, bf16[512,512]{1,0:T(8,128)(2,1)} %get-tuple-element.340.sent, bf16[512,2048]{1,0:T(8,128)(2,1)} %get-tuple-element.341.right), custom_call_target="tpu_custom_call" | custom-call | flops 1048576 | bytes 65536 | tf_op jit(solution)/shard_map/outer_product/pallas_call | solution.py:449
  252.2 4.0 %reduce_sum.51 = bf16[256,1024]{1,0:T(8,128)(2,1)} reduce(bf16[8,256,1024]{2,1,0:T(8,128)(2,1)} %all-to-all-done.3, bf16[]{:T(256)} %constant.47.clone.1), dimensions={0}, to_apply=%region_1.2 | reduce | flops 1835008 | bytes 4718594 | tf_op jit(solution)/shard_map/reduce_sum | solution.py:1078
  260.5 18.8 %conv_back.1 = (bf16[128,2048]{1,0:T(8,128)(2,1)}, bf16[128,2048]{1,0:T(8,128)(2,1)}, bf16[128,2048]{1,0:T(8,128)(2,1)}, bf16[128,2048]{1,0:T(8,128)(2,1)}, bf16...) custom-call(s32[6]{0:T(128)} %pad_add_fusion.info, ...), custom_call_target="tpu_custom_call" | custom-call | flops 1048576 | bytes 65536 | tf_op jit(solution)/shard_map/conv_back/pallas_call | solution.py:800
  287.4 4.6 %add_core.1 = bf16[4,304,1024]{2,1,0:T(8,128)(2,1)} custom-call(bf16[1024,1024]{1,0:T(8,128)(2,1)} %get-tuple-element.378.kept, bf16[1024,1024]{1,0:T(8,128)(2,1)} %collective-permute-done.24.got, f32[4,48,1024]{2,1,0:T(8,128)} %get-tuple-element.380.refs_0_, bf16[4,48,1024]{2,1,0:T(8,128)(2,1)} %copy-done.34), custom_call_target="tpu_custom_call" | custom-call | flops 1024 | bytes 65536 | tf_op jit(solution)/shard_map/add_core/pallas_call | solution.py:922
  292.0 4.1 %collective-permute-done.26 = bf16[128,2048]{1,0:T(8,128)(2,1)} collective-permute-done((bf16[128,2048]{1,0:T(8,128)(2,1)}, bf16[128,2048]{1,0:T(8,128)(2,1)}, u32[]{:S(2)}, u32[]{:S(2)}) %collective-permute-start.26) | collective-permute-done | bytes 524320 | tf_op jit(solution)/shard_map/ppermute | solution.py:846
  297.7 3.9 %all-to-all-start.5 = ((bf16[4,304,1024]{2,1,0:T(8,128)(2,1)}), bf16[4,304,1024]{2,1,0:T(8,128)(2,1)S(1)}, u32[]{:S(2)}, u32[]{:S(2)}) async-start(bf16[4,304,1024]{2,1,0:T(8,128)(2,1)} %add_core.1), calls=%async_computation.5 | async-start | bytes 4980736 | tf_op jit(solution)/shard_map/all_to_all | solution.py:858
  309.5 22.5 %all-to-all-done.5 = bf16[4,304,1024]{2,1,0:T(8,128)(2,1)S(1)} async-done(((bf16[4,304,1024]{2,1,0:T(8,128)(2,1)}), bf16[4,304,1024]{2,1,0:T(8,128)(2,1)S(1)}, u32[]{:S(2)}, u32[]{:S(2)}) %all-to-all-start.5) | async-done | bytes 2490400 | tf_op jit(solution)/shard_map/all_to_all | solution.py:858
  336.4 6.1 %collective-permute-done.31 = bf16[128,2048]{1,0:T(8,128)(2,1)} collective-permute-done((bf16[128,2048]{1,0:T(8,128)(2,1)}, bf16[128,2048]{1,0:T(8,128)(2,1)}, u32[]{:S(2)}, u32[]{:S(2)}) %collective-permute-start.31) | collective-permute-done | bytes 524320 | tf_op jit(solution)/shard_map/ppermute | solution.py:841
  352.3 7.1 %all-to-all-done.6.inner = bf16[4,64,1024]{2,1,0:T(8,128)(2,1)S(1)} async-done(((bf16[4,64,1024]{2,1,0:T(8,128)(2,1)}), bf16[4,64,1024]{2,1,0:T(8,128)(2,1)S(1)}, u32[]{:S(2)}, u32[]{:S(2)}) %all-to-all-start.6) | async-done | bytes 524320 | tf_op jit(solution)/shard_map/all_to_all | solution.py:854
  (238 shorter events, 98.9 us)
Async XLA Ops:
  3.2 46.2 %all-to-all-start = ((bf16[4,144,1024]{2,1,0:T(8,128)(2,1)}), bf16[4,144,1024]{2,1,0:T(8,128)(2,1)S(1)}, u32[]{:S(2)}, u32[]{:S(2)}) async-start(bf16[4,144,1024]{2,1,0:T(8,128)(2,1)} %split_columns.1), calls=%async_computation | async-start | bytes 2359296 | tf_op jit(solution)/shard_map/all_to_all | solution.py:854
  9.9 34.4 %collective-permute-start.1 = (bf16[160,2048]{1,0:T(8,128)(2,1)S(1)}, bf16[160,2048]{1,0:T(8,128)(2,1)S(1)}, u32[]{:S(2)}, u32[]{:S(2)}) collective-permute-start(bf16[160,2048]{1,0:T(8,128)(2,1)S(1)} %constant_dynamic-update-slice_fusion.refs_0_), channel_id=1, source_target_pairs={{0,8},{4,12},{8,0},{12,4},{16,24},{20,28},{24,16},{28,20},{1,9},{5... | collective-permute-start | bytes 1966088 | tf_op jit(solution)/shard_map/ppermute | solution.py:841
  11.5 32.8 %collective-permute-start.2 = (bf16[160,2048]{1,0:T(8,128)(2,1)S(1)}, bf16[160,2048]{1,0:T(8,128)(2,1)}, u32[]{:S(2)}, u32[]{:S(2)}) collective-permute-start(bf16[160,2048]{1,0:T(8,128)(2,1)S(1)} %constant_dynamic-update-slice_fusion.refs_0_), channel_id=1, source_target_pairs={{0,16},{4,20},{8,24},{12,28},{16,0},{20,4},{24,8},{28,12},{1,17},{... | collective-permute-start | bytes 1966088 | tf_op jit(solution)/shard_map/ppermute | solution.py:841
  13.0 31.3 %collective-permute-start.3 = (bf16[160,2048]{1,0:T(8,128)(2,1)S(1)}, bf16[160,2048]{1,0:T(8,128)(2,1)}, u32[]{:S(2)}, u32[]{:S(2)}) collective-permute-start(bf16[160,2048]{1,0:T(8,128)(2,1)S(1)} %constant_dynamic-update-slice_fusion.refs_0_), channel_id=1, source_target_pairs={{0,24},{4,28},{8,16},{12,20},{16,8},{20,12},{24,0},{28,4},{1,25},{... | collective-permute-start | bytes 1966088 | tf_op jit(solution)/shard_map/ppermute | solution.py:841
  13.5 30.8 %collective-permute-start = (bf16[128,2048]{1,0:T(8,128)(2,1)S(1)}, bf16[128,2048]{1,0:T(8,128)(2,1)}, u32[]{:S(2)}, u32[]{:S(2)}) collective-permute-start(bf16[128,2048]{1,0:T(8,128)(2,1)S(1)} %copy-done.4), channel_id=1, source_target_pairs={{0,1},{1,2},{2,3},{3,0},{4,5},{5,6},{6,7},{7,4},{8,9},{9,10},{10,1... | collective-permute-start | bytes 1572872 | tf_op jit(solution)/shard_map/ppermute | solution.py:846
  52.1 29.5 %all-to-all-start.1 = ((bf16[4,272,1024]{2,1,0:T(8,128)(2,1)}), bf16[4,272,1024]{2,1,0:T(8,128)(2,1)S(1)}, u32[]{:S(2)}, u32[]{:S(2)}) async-start(bf16[4,272,1024]{2,1,0:T(8,128)(2,1)} %broadcast_in_dim.42), calls=%async_computation.1 | async-start | bytes 4456448 | tf_op jit(solution)/shard_map/all_to_all | solution.py:858
  56.0 23.8 %collective-permute-start.4 = (bf16[128,2048]{1,0:T(8,128)(2,1)S(1)}, bf16[128,2048]{1,0:T(8,128)(2,1)}, u32[]{:S(2)}, u32[]{:S(2)}) collective-permute-start(bf16[128,2048]{1,0:T(8,128)(2,1)S(1)} %copy-done.4), channel_id=1, source_target_pairs={{0,2},{1,3},{2,0},{3,1},{4,6},{5,7},{6,4},{7,5},{8,10},{9,11},{10,... | collective-permute-start | bytes 1572872 | tf_op jit(solution)/shard_map/ppermute | solution.py:846
  57.5 23.5 %collective-permute-start.5 = (bf16[128,2048]{1,0:T(8,128)(2,1)S(1)}, bf16[128,2048]{1,0:T(8,128)(2,1)}, u32[]{:S(2)}, u32[]{:S(2)}) collective-permute-start(bf16[128,2048]{1,0:T(8,128)(2,1)S(1)} %copy-done.4), channel_id=1, source_target_pairs={{0,3},{1,0},{2,1},{3,2},{4,7},{5,4},{6,5},{7,6},{8,11},{9,8},{10,9... | collective-permute-start | bytes 1572872 | tf_op jit(solution)/shard_map/ppermute | solution.py:846
  83.7 36.0 %all-to-all-start.2 = ((bf16[4,256,1024]{2,1,0:T(8,128)(2,1)}), bf16[4,256,1024]{2,1,0:T(8,128)(2,1)}, u32[]{:S(2)}, u32[]{:S(2)}) async-start(bf16[4,256,1024]{2,1,0:T(8,128)(2,1)} %broadcast_in_dim.43), calls=%async_computation.2 | async-start | bytes 4194304 | tf_op jit(solution)/shard_map/all_to_all | solution.py:858
  88.4 23.8 %collective-permute-start.8 = (bf16[128,2048]{1,0:T(8,128)(2,1)}, bf16[128,2048]{1,0:T(8,128)(2,1)S(1)}, u32[]{:S(2)}, u32[]{:S(2)}) collective-permute-start(bf16[128,2048]{1,0:T(8,128)(2,1)} %refs_0_.1), channel_id=1, source_target_pairs={{0,1},{1,2},{2,3},{3,0},{4,5},{5,6},{6,7},{7,4},{8,9},{9,10},{10,1... | collective-permute-start | bytes 1572872 | tf_op jit(solution)/shard_map/ppermute | solution.py:846
  119.7 38.2 %collective-permute-start.15 = (bf16[4,256,1024]{2,1,0:T(8,128)(2,1)}, bf16[4,256,1024]{2,1,0:T(8,128)(2,1)S(1)}, u32[]{:S(2)}, u32[]{:S(2)}) collective-permute-start(bf16[4,256,1024]{2,1,0:T(8,128)(2,1)} %all-to-all-done.2.own.refs_2_), channel_id=1, source_target_pairs={{0,4},{4,0},{8,12},{12,8},{16,20},{20,16},{24,28},{28,24},{1,5},{5... | collective-permute-start | bytes 6291464 | tf_op jit(solution)/shard_map/ppermute | solution.py:841
  133.3 24.6 %collective-permute-start.16 = (bf16[128,2048]{1,0:T(8,128)(2,1)}, bf16[128,2048]{1,0:T(8,128)(2,1)}, u32[]{:S(2)}, u32[]{:S(2)}) collective-permute-start(bf16[128,2048]{1,0:T(8,128)(2,1)} %refs_0_.1), channel_id=1, source_target_pairs={{0,3},{1,0},{2,1},{3,2},{4,7},{5,4},{6,5},{7,6},{8,11},{9,8},{10,9... | collective-permute-start | bytes 1572872 | tf_op jit(solution)/shard_map/ppermute | solution.py:846
  136.8 39.2 %collective-permute-start.17 = (bf16[128,2048]{1,0:T(8,128)(2,1)}, bf16[128,2048]{1,0:T(8,128)(2,1)}, u32[]{:S(2)}, u32[]{:S(2)}) collective-permute-start(bf16[128,2048]{1,0:T(8,128)(2,1)} %refs_0_.1), channel_id=1, source_target_pairs={{0,2},{1,3},{2,0},{3,1},{4,6},{5,7},{6,4},{7,5},{8,10},{9,11},{10,... | collective-permute-start | bytes 1572872 | tf_op jit(solution)/shard_map/ppermute | solution.py:846
  176.1 17.4 %collective-permute-start.18 = (bf16[128,2048]{1,0:T(8,128)(2,1)}, bf16[128,2048]{1,0:T(8,128)(2,1)S(1)}, u32[]{:S(2)}, u32[]{:S(2)}) collective-permute-start(bf16[128,2048]{1,0:T(8,128)(2,1)} %get-tuple-element.311), channel_id=1, source_target_pairs={{0,1},{1,2},{2,3},{3,0},{4,5},{5,6},{6,7},{7,4},{8,9},{9,10},{10,1... | collective-permute-start | bytes 1572872 | tf_op jit(solution)/shard_map/ppermute | solution.py:846
  194.3 57.9 %all-to-all-start.3 = ((bf16[8,256,1024]{2,1,0:T(8,128)(2,1)}), bf16[8,256,1024]{2,1,0:T(8,128)(2,1)}, u32[]{:S(2)}, u32[]{:S(2)}) async-start(bf16[8,256,1024]{2,1,0:T(8,128)(2,1)} %bitcast.58), calls=%async_computation.3 | async-start | bytes 8388608 | tf_op jit(solution)/shard_map/all_to_all | solution.py:1065
  198.8 39.0 %collective-permute-start.19 = (bf16[128,2048]{1,0:T(8,128)(2,1)S(1)}, bf16[128,2048]{1,0:T(8,128)(2,1)S(1)}, u32[]{:S(2)}, u32[]{:S(2)}) collective-permute-start(bf16[128,2048]{1,0:T(8,128)(2,1)S(1)} %copy-done.50), channel_id=1, source_target_pairs={{0,2},{1,3},{2,0},{3,1},{4,6},{5,7},{6,4},{7,5},{8,10},{9,11},{10,... | collective-permute-start | bytes 1572872 | tf_op jit(solution)/shard_map/ppermute | solution.py:846
  200.5 37.4 %collective-permute-start.20 = (bf16[128,2048]{1,0:T(8,128)(2,1)S(1)}, bf16[128,2048]{1,0:T(8,128)(2,1)S(1)}, u32[]{:S(2)}, u32[]{:S(2)}) collective-permute-start(bf16[128,2048]{1,0:T(8,128)(2,1)S(1)} %copy-done.49), channel_id=1, source_target_pairs={{0,3},{1,0},{2,1},{3,2},{4,7},{5,4},{6,5},{7,6},{8,11},{9,8},{10,9... | collective-permute-start | bytes 1572872 | tf_op jit(solution)/shard_map/ppermute | solution.py:846
  257.0 22.3 %all-to-all-start.4 = ((bf16[4,64,1024]{2,1,0:T(8,128)(2,1)}), bf16[4,64,1024]{2,1,0:T(8,128)(2,1)S(1)}, u32[]{:S(2)}, u32[]{:S(2)}) async-start(bf16[4,64,1024]{2,1,0:T(8,128)(2,1)} %bitcast.28), calls=%async_computation.4 | async-start | bytes 1048576 | tf_op jit(solution)/shard_map/all_to_all | solution.py:854
  279.4 16.7 %collective-permute-start.26 = (bf16[128,2048]{1,0:T(8,128)(2,1)}, bf16[128,2048]{1,0:T(8,128)(2,1)}, u32[]{:S(2)}, u32[]{:S(2)}) collective-permute-start(bf16[128,2048]{1,0:T(8,128)(2,1)} %get-tuple-element.383), channel_id=1, source_target_pairs={{0,1},{1,2},{2,3},{3,0},{4,5},{5,6},{6,7},{7,4},{8,9},{9,10},{10,1... | collective-permute-start | bytes 1572872 | tf_op jit(solution)/shard_map/ppermute | solution.py:846
  297.7 34.3 %all-to-all-start.5 = ((bf16[4,304,1024]{2,1,0:T(8,128)(2,1)}), bf16[4,304,1024]{2,1,0:T(8,128)(2,1)S(1)}, u32[]{:S(2)}, u32[]{:S(2)}) async-start(bf16[4,304,1024]{2,1,0:T(8,128)(2,1)} %add_core.1), calls=%async_computation.5 | async-start | bytes 4980736 | tf_op jit(solution)/shard_map/all_to_all | solution.py:858
  302.8 33.7 %collective-permute-start.29 = (bf16[128,2048]{1,0:T(8,128)(2,1)}, bf16[128,2048]{1,0:T(8,128)(2,1)}, u32[]{:S(2)}, u32[]{:S(2)}) collective-permute-start(bf16[128,2048]{1,0:T(8,128)(2,1)} %get-tuple-element.397), channel_id=1, source_target_pairs={{0,2},{1,3},{2,0},{3,1},{4,6},{5,7},{6,4},{7,5},{8,10},{9,11},{10,... | collective-permute-start | bytes 1572872 | tf_op jit(solution)/shard_map/ppermute | solution.py:846
  305.2 31.2 %collective-permute-start.30 = (bf16[128,2048]{1,0:T(8,128)(2,1)}, bf16[128,2048]{1,0:T(8,128)(2,1)}, u32[]{:S(2)}, u32[]{:S(2)}) collective-permute-start(bf16[128,2048]{1,0:T(8,128)(2,1)} %get-tuple-element.398), channel_id=1, source_target_pairs={{0,3},{1,0},{2,1},{3,2},{4,7},{5,4},{6,5},{7,6},{8,11},{9,8},{10,9... | collective-permute-start | bytes 1572872 | tf_op jit(solution)/shard_map/ppermute | solution.py:846
  306.6 35.9 %collective-permute-start.31 = (bf16[128,2048]{1,0:T(8,128)(2,1)}, bf16[128,2048]{1,0:T(8,128)(2,1)}, u32[]{:S(2)}, u32[]{:S(2)}) collective-permute-start(bf16[128,2048]{1,0:T(8,128)(2,1)} %get-tuple-element.402), channel_id=1, source_target_pairs={{0,24},{4,28},{8,16},{12,20},{16,8},{20,12},{24,0},{28,4},{1,25},{... | collective-permute-start | bytes 1572872 | tf_op jit(solution)/shard_map/ppermute | solution.py:841
  342.5 16.8 %all-to-all-start.6 = ((bf16[4,64,1024]{2,1,0:T(8,128)(2,1)}), bf16[4,64,1024]{2,1,0:T(8,128)(2,1)S(1)}, u32[]{:S(2)}, u32[]{:S(2)}) async-start(bf16[4,64,1024]{2,1,0:T(8,128)(2,1)} %bitcast.60), calls=%async_computation.6 | async-start | bytes 1048576 | tf_op jit(solution)/shard_map/all_to_all | solution.py:854
  (67 other events, 545.9 us)

commit v4 on v3

--- a/solution.py
+++ b/solution.py
@@ -128,8 +128,8 @@
 
 def backward_kernel(
     at_small, bc, rank, small, act, valid, rate2, gs, states,
-    packed_out, gu_out, dtw_out, vec_out, rate_out,
-    part_s, g_ref, dt_s, dtu_s, gs_s, gdt_s, ab_s, both_s, sums,
+    packed_out, gu_out, dtw_out, vec_out, rate_grad,
+    part_s, rate_out, g_ref, dt_s, dtu_s, gs_s, gdt_s, ab_s, both_s, sums,
 ):
     tb, width = act.shape
     n_state = rate2.shape[0] // SUB
@@ -261,6 +261,9 @@
             packed_out[b * proj : (b + 1) * proj, :] = contract_cols(
                 one, part_s[b * LANES : (b + 1) * LANES, :]
             ).astype(BF)
+        for k in range(width // LANES):
+            rows = pl.ds(k, n_state, stride=SUB)
+            rate_grad[:, k * LANES : (k + 1) * LANES] = rate_out[rows, :] * rate2[rows, :] * LN2
 
 
 def scan_backward(at, bc, rank, small, act, valid, rate2, gs, states, tb):
@@ -289,16 +292,16 @@
             pl.BlockSpec((tb, width), row),
             pl.BlockSpec((rank_w, width), whole),
             pl.BlockSpec((2, width), whole),
-            pl.BlockSpec(rate2.shape, whole),
+            pl.BlockSpec((n_state, width), whole),
         ],
         out_shape=[
             jax.ShapeDtypeStruct((proj * slots // LANES, LANES), BF),
             jax.ShapeDtypeStruct((slots, width), BF),
             jax.ShapeDtypeStruct((rank_w, width), F32),
             jax.ShapeDtypeStruct((2, width), F32),
-            jax.ShapeDtypeStruct(rate2.shape, F32),
+            jax.ShapeDtypeStruct((n_state, width), F32),
         ],
-        scratch_shapes=[pltpu.VMEM((slots, proj), BF), pltpu.VMEM(rate2.shape, F32)]
+        scratch_shapes=[pltpu.VMEM((slots, proj), BF)] + [pltpu.VMEM(rate2.shape, F32)] * 2
         + [pltpu.VMEM((tb * SUB, LANES), F32)] * 5
         + [pltpu.VMEM((2, 4, tb * SUB, 2 * LANES), BF), pltpu.VMEM((n_state // 4, tb, 4 * SUB * SUB), F32)],
         compiler_params=pltpu.CompilerParams(vmem_limit_bytes=61 << 20),
@@ -381,17 +384,21 @@
     )(in_w, gain[None])
 
 
-def join_kernel(n_dp, inner, gate, in_w, gain, out, gain_out):
-    n_line, rows, width = inner.shape
+def join_kernel(n_dp, place, *refs):
+    *inner, gate, in_w, gain, out, gain_out = refs
+    n_line, rows, width = gate.shape
     owned = width // n_dp
     total = jnp.zeros((rows, LANES), F32)
-    for half, got in enumerate((inner, gate)):
-        for line in range(n_line):
+    for s in range(n_line):
+        for half in range(2):
+            line = from_place(place[0], s, n_line) if half == 0 else s
             for d in range(n_dp):
+                cols = slice(d * owned, (d + 1) * owned)
+                block = (inner[s][:, cols] if half == 0 else gate[s, :, cols]).astype(F32)
                 at = ((half * n_dp + d) * n_line + line) * owned
-                block = got[line, :, d * owned : (d + 1) * owned].astype(F32)
-                out[:, at : at + owned] = block
-                term = block * in_w[:, at : at + owned].astype(F32)
+                at = pl.ds(pl.multiple_of(at, owned), owned) if half == 0 else slice(at, at + owned)
+                out[:, at] = block
+                term = block * in_w[:, at].astype(F32)
                 for low in range(0, owned, LANES):
                     total = total + term[:, low : low + LANES]
     ones = jnp.ones((SUB, LANES), F32)
@@ -401,22 +408,22 @@
     gain_out[...] = sums[0:1, :] / gain[...].astype(F32)
 
 
-def join_columns(inner, gate, in_w, gain, n_dp):
+def join_columns(place, inner, gate, in_w, gain, n_dp):
     rows, both = in_w.shape
-    n_line, _, width = inner.shape
+    n_line, _, width = gate.shape
     if width // n_dp % LANES:
-        blocks = jnp.stack([inner, gate]).astype(F32).reshape(2, n_line, rows, n_dp, -1)
+        blocks = jnp.stack([in_order(inner, "fsdp"), gate]).astype(F32).reshape(2, n_line, rows, n_dp, -1)
         full = blocks.transpose(2, 0, 3, 1, 4).reshape(rows, both)
         return full, jnp.sum(full * in_w.astype(F32), axis=1) / gain.astype(F32)
     vmem = pl.BlockSpec(memory_space=pltpu.VMEM)
     full, gain_grad = pl.pallas_call(
         functools.partial(join_kernel, n_dp),
-        in_specs=[vmem] * 4,
+        in_specs=[pl.BlockSpec(memory_space=pltpu.SMEM)] + [vmem] * (n_line + 3),
         out_specs=[vmem] * 2,
         out_shape=[jax.ShapeDtypeStruct((rows, both), F32), jax.ShapeDtypeStruct((1, rows), F32)],
         cost_estimate=small_cost(1 << 10),
         name="join_columns",
-    )(inner, gate, in_w, gain[None])
+    )(place[None], *inner, gate, in_w, gain[None])
     return full, gain_grad[0]
 
 
@@ -662,7 +669,7 @@
     slots, width = gu.shape
     inner_own, inner_other, gate_own, gate_other, *refs = refs
     halves_far, refs = (refs[:2], refs[2:]) if together(slots) else ((), refs)
-    grads, refs = refs[:n_line], refs[n_line:]
+    normed_far, *refs = refs
     products_far, refs = (refs[:2], refs[2:]) if together(slots) else ((), refs)
     gi_low, refs = (None, refs) if together(slots) else (refs[0], refs[1:])
     kept, sent, x_grad, vec, ext, gi, tail, grad_normed, column, gp, arrived, left, w_nat, gate_nat, *refs = refs
@@ -751,9 +758,7 @@
         found = contract_cols(gi_low[...], w_nat[cols, :]) + contract_cols(grad_gate[...], gate_nat[cols, :])
         grad_normed[:, cols] = found.astype(BF)
 
-    for s, grad in enumerate(grads):
-        first = pl.multiple_of(lax.rem(info[1] + s, n_line) * held, held)
-        leave(grad_normed.at[pl.ds(first, held)], grad)
+    leave(grad_normed, normed_far)
     if halves:
         step = model // 2 // 4
         for r in range(4):
@@ -800,8 +805,8 @@
     outs = pl.pallas_call(
         functools.partial(conv_back_kernel, n_line, n_dp, at),
         in_specs=[pl.BlockSpec(memory_space=pltpu.SMEM)] + [vmem] * 12 + [away] * len(later),
-        out_specs=[away] * n_line + ([away] * 2 if one else [vmem]) + [vmem] * 2,
-        out_shape=[jax.ShapeDtypeStruct((held, model), BF)] * n_line
+        out_specs=[away] + ([away] * 2 if one else [vmem]) + [vmem] * 2,
+        out_shape=[jax.ShapeDtypeStruct((slots, model), BF)]
         + ([half] * 2 if one else [low])
         + [
             jax.ShapeDtypeStruct(shape, F32),
@@ -817,7 +822,7 @@
             pltpu.VMEM((n_dp * fold, owned), F32),
             pltpu.VMEM(gp_got.shape, BF),
             pltpu.SemaphoreType.DMA((2 * n_dp + 2,)),
-            pltpu.SemaphoreType.DMA((n_line + 8,)),
+            pltpu.SemaphoreType.DMA((9,)),
         ]
         + [pltpu.VMEM((model, width), BF)] * 2
         + ([pltpu.VMEM((slots, width), BF)] + [pltpu.VMEM((slots, model // 2), BF)] * 2 if one else [])
@@ -826,14 +831,14 @@
         cost_estimate=small_cost(1 << 20),
         name="conv_back",
     )(info, gp_part, gp_got, gu, small, act, conv_out, inner, allowed, dtw, rate_grad, scan_vec, grad_gate, *later)
-    grads, (*products, kept, sent) = outs[:n_line], outs[n_line:]
+    grad_normed, *products, kept, sent = outs
     if not one:
         products = outer_product(normed_k, normed_s, products[0])
     if not tiles:
         kept, sent = [
             part.reshape(at.rows, n_dp // 2, owned).transpose(1, 0, 2) for part in cores(kept[0], 1)
         ]
-    return list(grads), *products, kept, sent.astype(BF)
+    return grad_normed, *products, kept, sent.astype(BF)
 
 
 def swap(value, axis, mask):
@@ -907,33 +912,28 @@
     return [part.reshape(flat) for part in found]
 
 
-def add_core_kernel(kept, got, *refs):
-    *small, out = refs
-    whole = kept.shape[0]
-    out[0, 0:whole, :] = (kept[...].astype(F32) + got[...].astype(F32)).astype(BF)
-    if small:
-        out[0, whole:, :] = (small[0][0] + small[1][0].astype(F32)).astype(BF)
-
-
-def add_core(kept, got, *small):
+def add_core_kernel(chip, kept, got, small_kept, small_got, *outs):
+    rows = kept.shape[0] // len(outs)
+    for u, out in enumerate(outs):
+        q = jnp.bitwise_xor(chip[0], u)
+        at = pl.ds(pl.multiple_of(q * rows, rows), rows)
+        out[0:rows, :] = (kept[at, :].astype(F32) + got[at, :].astype(F32)).astype(BF)
+        out[rows:, :] = (small_kept[q] + small_got[q].astype(F32)).astype(BF)
+
+
+def add_core(kept, got, small_kept, small_got):
     chips, width = lax.axis_size("dp") // 2, kept.shape[1]
-    whole = kept.shape[0] // chips
-    more = small[0].shape[1] if small else 0
+    rows = kept.shape[0] // chips + small_kept.shape[1]
+    vmem = pl.BlockSpec(memory_space=pltpu.VMEM)
     return pl.pallas_call(
         add_core_kernel,
-        grid=(chips,),
-        in_specs=[pl.BlockSpec((whole, width), lambda q: (q, 0))] * 2
-        + [pl.BlockSpec((1, more, width), lambda q: (q, 0, 0))] * len(small),
-        out_specs=pl.BlockSpec((1, whole + more, width), lambda q: (q, 0, 0)),
-        out_shape=jax.ShapeDtypeStruct((chips, whole + more, width), BF),
+        in_specs=[pl.BlockSpec(memory_space=pltpu.SMEM)] + [vmem] * 4,
+        out_specs=[vmem] * chips,
+        out_shape=[jax.ShapeDtypeStruct((rows, width), BF)] * chips,
         compiler_params=pltpu.CompilerParams(vmem_limit_bytes=61 << 20),
         cost_estimate=small_cost(1 << 10),
         name="add_core",
-    )(kept, got, *small)
-
-
-def add_chips(blocks):
-    return jnp.sum(to_chips(blocks.astype(BF)).astype(F32), axis=0)
+    )(lax.div(lax.axis_index("dp"), 2)[None], kept, got, small_kept, small_got)
 
 
 def add_chips_near(blocks):
@@ -944,6 +944,32 @@
     return total
 
 
+def sum_chips_kernel(count, place, *refs):
+    blocks, (*outs, small) = refs[:count], refs[count:]
+    rows = outs[0].shape[0]
+    for s, out in enumerate(outs):
+        at = pl.ds(pl.multiple_of(lax.rem(place[0] + s, len(outs)) * rows, rows), rows)
+        out[...] = sum(block[at, :].astype(F32) for block in blocks).astype(BF)
+    first = rows * len(outs)
+    small[...] = sum(block[first:, :].astype(F32) for block in blocks)
+
+
+def sum_chips(place, blocks, n_line, rows):
+    full, width = blocks[0].shape
+    vmem = pl.BlockSpec(memory_space=pltpu.VMEM)
+    *parts, small = pl.pallas_call(
+        functools.partial(sum_chips_kernel, len(blocks)),
+        in_specs=[pl.BlockSpec(memory_space=pltpu.SMEM)] + [vmem] * len(blocks),
+        out_specs=[vmem] * (n_line + 1),
+        out_shape=[jax.ShapeDtypeStruct((rows, width), BF)] * n_line
+        + [jax.ShapeDtypeStruct((full - n_line * rows, width), F32)],
+        compiler_params=pltpu.CompilerParams(vmem_limit_bytes=61 << 20),
+        cost_estimate=small_cost(1 << 10),
+        name="sum_chips",
+    )(place[None], *blocks)
+    return parts, small
+
+
 def sent_far(kept, got, u):
     rows = kept.shape[0] // (lax.axis_size("dp") // 2)
     at = jnp.bitwise_xor(lax.div(lax.axis_index("dp"), 2), u) * rows
@@ -953,6 +979,68 @@
 def far(blocks, u):
     block = lax.dynamic_index_in_dim(blocks, jnp.bitwise_xor(lax.div(lax.axis_index("dp"), 2), u), 0, keepdims=False)
     return swap(block.astype(BF), "dp", 2 * u)
+
+
+def halves_kernel(chip, kept, got, first, second, *held):
+    rows, half = held[0].shape
+    outs = {
+        (0, 0): held[0], (2, 0): held[1], (0, 1): held[2], (1, 1): held[3],
+        (1, 0): first.at[0:rows], (3, 0): first.at[rows : 2 * rows],
+        (2, 1): second.at[0:rows], (3, 1): second.at[rows : 2 * rows],
+    }
+    for (u, side), out in outs.items():
+        at = pl.ds(pl.multiple_of(jnp.bitwise_xor(chip[0], u) * rows, rows), rows)
+        cols = slice(side * half, (side + 1) * half)
+        out[...] = (kept[at, cols].astype(F32) + got[at, cols].astype(F32)).astype(BF)
+
+
+def chip_sum(kept, got):
+    chips, (rows, width) = lax.axis_size("dp") // 2, kept.shape
+    if chips != 4 or rows // chips % LANES:
+        return ChipSum([sent_far(kept, got, u) for u in range(chips)])
+    rows, half = rows // chips, width // 2
+    vmem = pl.BlockSpec(memory_space=pltpu.VMEM)
+    first, second, *held = pl.pallas_call(
+        halves_kernel,
+        in_specs=[pl.BlockSpec(memory_space=pltpu.SMEM)] + [vmem] * 2,
+        out_specs=[vmem] * 6,
+        out_shape=[jax.ShapeDtypeStruct((2 * rows, half), BF)] * 2 + [jax.ShapeDtypeStruct((rows, half), BF)] * 4,
+        compiler_params=pltpu.CompilerParams(vmem_limit_bytes=61 << 20),
+        cost_estimate=small_cost(1 << 10),
+        name="chip_halves",
+    )(lax.div(lax.axis_index("dp"), 2)[None], kept, got)
+    return ChipSum(held, [first, second])
+
+
+class ChipSum:
+    def __init__(self, held, sends=None):
+        self.direct = sends is None
+        self.held, self.sends, self.got = held, sends or held[1:], []
+
+    def fenced(self, *others):
+        (self.held, self.sends, self.got), *others = fence((self.held, self.sends, self.got), *others)
+        return others
+
+    def first(self):
+        self.got = [swap(send, "dp", 2 * u) for u, send in enumerate(self.sends, 1)]
+        self.sends = []
+
+    def add(self):
+        if self.direct:
+            return
+        rows = self.held[0].shape[0]
+        own = [h.astype(F32) + got[:rows].astype(F32) for h, got in zip(self.held[::2], self.got)]
+        self.sends = [(h.astype(F32) + got[rows:].astype(F32)).astype(BF) for h, got in zip(self.held[1::2], self.got)]
+        self.held, self.got = own, []
+
+    def second(self):
+        if not self.direct:
+            self.got = [swap(send, "dp", 2 * u) for u, send in zip((2, 1), self.sends)]
+
+    def total(self):
+        if self.direct:
+            return sum(part.astype(F32) for part in (self.held[0], *self.got))
+        return jnp.concatenate([h + got.astype(F32) for h, got in zip(self.held, self.got)], axis=1)
 
 
 def per_device(
@@ -1001,7 +1089,10 @@
     parts = to_line(parts)
     toks = {0: tokens, 1: shift(tokens, "fsdp", 1)}
     near = [packed] + [swap(packed, "dp", 2 * u) for u in chips]
-    parts, toks, near, info, allowed, valid, opens = fence(parts, toks, near, info, allowed, valid, opens)
+    own_valid = lax.dynamic_slice_in_dim(valid, place * held_slots, held_slots, 0)
+    parts, toks, near, info, allowed, valid, opens, own_valid = fence(
+        parts, toks, near, info, allowed, valid, opens, own_valid
+    )
 
     gain_rows = jnp.pad(parts[:, 2 * in_rows, :in_rows].reshape(1, -1), ((0, 15), (0, width - n_line * in_rows)))
     inner_block = jnp.concatenate([parts[:, :in_rows].reshape(-1, width), gain_rows], axis=0)
@@ -1028,15 +1119,16 @@
 
     gate_own = to_chips(gate_rep)
     cots = {0: cotangent, 1: shift(cotangent, "fsdp", 1)}
+    out_other = [swap(block, "dp", 1) for block in near[: len(near) // 2]]
     full_gain, normed, normed_kept, normed_sent, inner, conv_out, activ, low = project(
         info, n_line, n_dp, [toks[s] for s in range(n_line)], inner_own, inner_other, at, small, allowed
     )
-    low, rate2, cots, near = fence(low, rate2, cots, near)
+    low, rate2, cots, near, out_other = fence(low, rate2, cots, near, out_other)
 
     part = low.astype(F32) + swap(low, "fsdp", 1).astype(F32)
-    part, gate_own, near = fence(part, gate_own, near)
+    part, gate_own, near, out_other = fence(part, gate_own, near, out_other)
     part, got = last_line(part, 2)
-    out_near, out_other = near, [swap(block, "dp", 1) for block in near]
+    out_near, out_other = near, out_other + [swap(block, "dp", 1) for block in near[len(near) // 2 :]]
     part, got, cots, out_near, out_other = fence(part, got, cots, out_near, out_other)
     projected = part + got.astype(F32)
 
@@ -1065,63 +1157,65 @@
     gate_sums = lax.all_to_all(gate_grad.reshape(n_dp, -1, width), "dp", 0, 0)
     for s in steps[1:]:
         branches[s] = shift(branches[s], "fsdp", s)
-    low, grad_u, dt_w_grad, vectors, rate_sum = scan_backward(
+    low, grad_u, dt_w_grad, vectors, rate_grad = scan_backward(
         at, bc, rank_low, small, activ, valid, rate2, grad_scan, states, tb
     )
-    low, branches, gated, dout, grad_gate, rate_sum = fence(low, branches, gated, dout, grad_gate, rate_sum)
+    low, branches, gated, dout, grad_gate = fence(low, branches, gated, dout, grad_gate)
 
     out_kept, out_sent = outer_product(*gated, dout)
     part = low.astype(F32) + swap(low, "fsdp", 1).astype(F32)
     part, out_kept, out_sent, grad_gate = fence(part, out_kept, out_sent, grad_gate)
     out_got = swap(out_sent, "dp", 1)
-    out_far = {u: sent_far(out_kept, out_got, u) for u in range(n_dp // 2)}
     gate_rows = jnp.sum(gate_sums.astype(F32), axis=0).astype(BF)
-    rate_grad = rate_sum.reshape(n_state, SUB, LANES)[:, :chunks].reshape(n_state, width) * rates
+    out_kept, out_got, gate_rows = fence(out_kept, out_got, gate_rows)
+    out_sum = chip_sum(out_kept, out_got)
     part, got = last_line(part, 2)
-    part, got, out_far, rate_grad, gate_rows = fence(part, got, out_far, rate_grad, gate_rows)
+    part, got, out_sum.held, out_sum.sends, gate_rows = fence(part, got, out_sum.held, out_sum.sends, gate_rows)
 
     gate_got = to_line(gate_rows.reshape(n_line, in_rows, width))
-    grads, inner_kept, inner_sent, small_kept, small_sent = conv_back(
+    grad_normed, inner_kept, inner_sent, small_kept, small_sent = conv_back(
         info, n_line, n_dp, part, got, grad_u, at, small, activ, conv_out, inner, allowed,
         dt_w_grad, rate_grad, vectors, grad_gate, (inner_own, inner_other), (gate_own, gate_other),
         normed_kept, normed_sent,
     )
-    grads, gate_got, inner_kept, inner_sent, small_kept, small_sent, out_far, branches = fence(
-        grads, gate_got, inner_kept, inner_sent, small_kept, small_sent, out_far, branches
-    )
-
+    grad_normed, gate_got, inner_kept, inner_sent, small_kept, small_sent, branches = out_sum.fenced(
+        grad_normed, gate_got, inner_kept, inner_sent, small_kept, small_sent, branches
+    )
+
+    grad_normed = to_line(grad_normed.reshape(n_line, held_slots, model))
     folded = owned % LANES == 0
-    grads[1] = shift(grads[1], "fsdp", 1)
-    for u in chips[:2]:
-        out_far[u] = swap(out_far[u], "dp", 2 * u)
+    out_sum.first()
     inner_got, small_got = swap(inner_sent, "dp", 1), swap(small_sent, "dp", 1)
-    inner_grad = add_core(inner_kept, inner_got, *((small_kept, small_got) if folded else ()))
-    inner_grad, grads, small_kept, small_got, out_far, branches = fence(
-        inner_grad, grads, small_kept, small_got, out_far, branches
-    )
-
-    got = to_chips(inner_grad)
-    inner_rows = jnp.sum(got[:, : n_line * in_rows].astype(F32), axis=0).astype(BF)
-    small_sum = jnp.sum(got[:, n_line * in_rows :].astype(F32), axis=0)
-    for s in steps[1:]:
-        grads[s] = shift(grads[s], "fsdp", s)
-    for u in chips[2:]:
-        out_far[u] = swap(out_far[u], "dp", 2 * u)
+    if folded:
+        blocks = add_core(inner_kept, inner_got, small_kept, small_got)
+    else:
+        blocks = [sent_far(inner_kept, inner_got, u) for u in range(n_dp // 2)]
+    blocks, small_kept, small_got, branches = out_sum.fenced(blocks, small_kept, small_got, branches)
+
+    blocks = [swap(block, "dp", 2 * u) if u else block for u, block in enumerate(blocks)]
+    out_sum.add()
+    if folded:
+        inner_sent, small_sum = sum_chips(place, blocks, n_line, in_rows)
+    else:
+        rows = sum(block.astype(F32) for block in blocks).astype(BF).reshape(n_line, in_rows, width)
+        inner_sent = [
+            lax.dynamic_index_in_dim(rows, lax.rem(place + s, n_line), 0, keepdims=False) for s in range(n_line)
+        ]
+        small_sum = add_chips_near(small_kept + small_got.astype(F32))
+    inner_sent, small_sum, branches = out_sum.fenced(inner_sent, small_sum, branches)
+
+    inner_got = [shift(block, "fsdp", s) if s else block for s, block in enumerate(inner_sent)]
+    out_sum.second()
+    grad_normed, small_sum = fence(grad_normed, small_sum)
+    grad_normed = jnp.sum(grad_normed.astype(F32), axis=0)
+    out_weight_grad = out_sum.total()
+    small_grads = small_sum
     if folded:
         small_grads = small_sum.reshape(-1, n_dp, owned).transpose(1, 0, 2).reshape(-1, owned)
-    else:
-        small_grads = add_chips_near(small_kept + small_got.astype(F32))
     dt_g, x_g, a_g = small_grads[at.dt_w], small_grads[at.x_t], small_grads[at.a_t]
     tail_g = small_grads[at.rest]
-    conv_g, conv_b_g, dt_b_g, skip_g = tail_g[:taps], tail_g[taps : taps + 1], tail_g[taps + 1 : taps + 2], tail_g[taps + 2 : taps + 3]
-    small_out = [conv_g, conv_b_g[0], x_g.T, dt_g, dt_b_g[0], a_g.T, skip_g[0]]
-    inner_rows, grads, out_far, branches, small_out = fence(inner_rows, grads, out_far, branches, small_out)
-
-    inner_got = to_line(inner_rows.reshape(n_line, in_rows, width))
-    grad_normed = sum(p.astype(F32) for p in grads)
-    grad_normed, branches, out_far = fence(grad_normed, branches, out_far)
-    out_weight_grad = sum(part.astype(F32) for part in out_far.values())
-    own_valid = lax.dynamic_slice_in_dim(valid, place * held_slots, held_slots, 0)
+    conv_g, conv_b_g, dt_b_g, skip_g = tail_g[:taps], tail_g[taps], tail_g[taps + 1], tail_g[taps + 2]
+    small_out = [conv_g, conv_b_g, x_g.T, dt_g, dt_b_g, a_g.T, skip_g]
     own_f = own_tokens.astype(F32)
     output = (own_f + own_valid * sum(p.astype(F32) for p in branches)).astype(BF)
     own_scale = lax.rsqrt(jnp.mean(own_f * own_f, axis=1, keepdims=True) + EPS)
@@ -1130,7 +1224,10 @@
     token_grad = own_cot.astype(F32) + own_scale * (
         grad_unit - unit * jnp.mean(grad_unit * unit, axis=1, keepdims=True)
     )
-    in_weight_grad, gain_grad = join_columns(inner_got, gate_got, in_weight, gain, n_dp)
+    inner_got, token_grad, output, out_weight_grad, small_out = fence(
+        inner_got, token_grad, output, out_weight_grad, small_out
+    )
+    in_weight_grad, gain_grad = join_columns(place, inner_got, gate_got, in_weight, gain, n_dp)
     return output, token_grad, gain_grad, in_weight_grad, *small_out, out_weight_grad
 
 

time: 365 us -> 354 us (0.970)
  starting transfers between devices: 74.8 us -> 57.1 us
  Pallas kernels: 134 us -> 140 us
    all_to_all x3 -> x2, waiting for transfers between devices: 23.1 us -> 1.86 us  [to_chips(): return lax.all_to_all(blocks, 'dp', 0, 0, axis_index_groups=chips_of('dp'))]
    ppermute x20 -> x24, waiting for transfers between devices: 28.8 us -> 49.1 us  [swap(): return lax.ppermute(value, axis, [(i, i ^ mask) for i in range(count)])]
    ppermute x12, starting transfers between devices: 29.3 us -> 16.1 us  [shift(): lax.ppermute(value, axis, [(i, (i + steps) % count) for i in range(count)])]
    ppermute x12, waiting for transfers between devices: 42.7 us -> 50.8 us  [shift(): lax.ppermute(value, axis, [(i, (i + steps) % count) for i in range(count)])]
    all_to_all x3, waiting for transfers between devices: 12.2 us -> 5.26 us  [to_line(): return lax.all_to_all(blocks, 'fsdp', 0, 0)]
    pallas_call x2 -> x4, Pallas kernels: 7.73 us -> 14.2 us  [the longest x1 4.26 us: add_core(): pl.pallas_call(add_core_kernel, in_specs=[pl.BlockSpec(memory_space=pltpu...]
    all_to_all x3 -> x2, starting transfers between devices: 12.2 us -> 8.16 us  [to_chips(): return lax.all_to_all(blocks, 'dp', 0, 0, axis_index_groups=chips_of('dp'))]
    ppermute x20 -> x24, starting transfers between devices: 15.3 us -> 13.2 us  [swap(): return lax.ppermute(value, axis, [(i, i ^ mask) for i in range(count)])]
  transfers between devices with their start and end apart: 39 -> 42, of which waited for: 17 -> 15; matrix products, arithmetic and copies ran while one was open for 10% -> 9% of each run, Pallas kernels for 35% -> 38%
where the time goes in v4:
time: 354 us; the launch traced here: 353 us
  Pallas kernels  140 us (40%)
  waiting for transfers between devices  110 us (31%)
  starting transfers between devices  57.1 us (16%)
  local copies, waits for them, and re-layouts  21.9 us (6%)
  other arithmetic  21.1 us (6%)
    ppermute x12, waiting for transfers between devices, shift(): lax.ppermute(value, axis, [(i, (i + steps) % count) for i in range(count)])  50.8 us
    ppermute x24, waiting for transfers between devices, swap(): return lax.ppermute(value, axis, [(i, i ^ mask) for i in range(count)])  49.1 us
    pallas_call x1, Pallas kernels, scan_backward(): pl.pallas_call(functools.partial(backward_kernel, at), grid=(nb,), in_spe...  34.4 us
    pallas_call x1, Pallas kernels, conv_back(): pl.pallas_call(functools.partial(conv_back_kernel, n_line, n_dp, at), in_...  18.7 us
    pallas_call x1, Pallas kernels, scan_forward(): pl.pallas_call(functools.partial(forward_kernel, at), grid=(nb,), in_spec...  18.3 us
    pallas_call x1, Pallas kernels, gate_block(): pl.pallas_call(functools.partial(gate_kernel, n_line, n_dp, at), in_specs...  16.9 us
    pallas_call x1, Pallas kernels, gate_back(): pl.pallas_call(functools.partial(gate_back_kernel, n_line, at), in_specs=...  16.1 us
    ppermute x12, starting transfers between devices, shift(): lax.ppermute(value, axis, [(i, (i + steps) % count) for i in range(count)])  16.1 us
  transfers between devices with their start and end apart: 42, of which 15 were waited for; matrix products, arithmetic and copies ran while one was open for 9% of the time, Pallas kernels for 38%

profile of v4, /device:TPU:0, one launch (start us, length us, event | category | flops | bytes accessed | tf_op | source)
XLA Modules:
  0.0 352.8 jit_solution(1092439683159674522)
XLA Ops:
  3.2 6.4 %all-to-all-start = ((bf16[4,144,1024]{2,1,0:T(8,128)(2,1)}), bf16[4,144,1024]{2,1,0:T(8,128)(2,1)S(1)}, u32[]{:S(2)}, u32[]{:S(2)}) async-start(bf16[4,144,1024]{2,1,0:T(8,128)(2,1)} %split_columns.1), calls=%async_computation | async-start | bytes 2359296 | tf_op jit(solution)/shard_map/all_to_all | solution.py:859
  21.6 22.5 %collective-permute-done.refs_1_ = bf16[128,2048]{1,0:T(8,128)(2,1)S(1)} collective-permute-done((bf16[128,2048]{1,0:T(8,128)(2,1)S(1)}, bf16[128,2048]{1,0:T(8,128)(2,1)S(1)}, u32[]{:S(2)}, u32[]{:S(2)}) %collective-permute-start) | collective-permute-done | bytes 524320 | tf_op jit(solution)/shard_map/ppermute | solution.py:851
  44.2 5.3 %all-to-all-done = bf16[4,144,1024]{2,1,0:T(8,128)(2,1)S(1)} async-done(((bf16[4,144,1024]{2,1,0:T(8,128)(2,1)}), bf16[4,144,1024]{2,1,0:T(8,128)(2,1)S(1)}, u32[]{:S(2)}, u32[]{:S(2)}) %all-to-all-start) | async-done | bytes 1179680 | tf_op jit(solution)/shard_map/all_to_all | solution.py:859
  52.2 3.7 %all-to-all-start.1 = ((bf16[4,272,1024]{2,1,0:T(8,128)(2,1)}), bf16[4,272,1024]{2,1,0:T(8,128)(2,1)S(1)}, u32[]{:S(2)}, u32[]{:S(2)}) async-start(bf16[4,272,1024]{2,1,0:T(8,128)(2,1)} %broadcast_in_dim.48), calls=%async_computation.1 | async-start | bytes 4456448 | tf_op jit(solution)/shard_map/all_to_all | solution.py:863
  64.5 5.6 %collective-permute-done.5.refs_3_ = bf16[128,2048]{1,0:T(8,128)(2,1)} collective-permute-done((bf16[128,2048]{1,0:T(8,128)(2,1)S(1)}, bf16[128,2048]{1,0:T(8,128)(2,1)}, u32[]{:S(2)}, u32[]{:S(2)}) %collective-permute-start.5) | collective-permute-done | bytes 524320 | tf_op jit(solution)/shard_map/ppermute | solution.py:851
  70.1 20.5 %collective-permute-done.4.refs_2_ = bf16[128,2048]{1,0:T(8,128)(2,1)} collective-permute-done((bf16[128,2048]{1,0:T(8,128)(2,1)S(1)}, bf16[128,2048]{1,0:T(8,128)(2,1)}, u32[]{:S(2)}, u32[]{:S(2)}) %collective-permute-start.4) | collective-permute-done | bytes 524320 | tf_op jit(solution)/shard_map/ppermute | solution.py:851
  92.7 4.4 %all-to-all-start.2 = ((bf16[4,256,1024]{2,1,0:T(8,128)(2,1)}), bf16[4,256,1024]{2,1,0:T(8,128)(2,1)}, u32[]{:S(2)}, u32[]{:S(2)}) async-start(bf16[4,256,1024]{2,1,0:T(8,128)(2,1)} %broadcast_in_dim.49), calls=%async_computation.2 | async-start | bytes 4194304 | tf_op jit(solution)/shard_map/all_to_all | solution.py:863
  98.7 13.2 %project.1 = (f32[1,2048]{1,0:T(1,128)}, bf16[512,2048]{1,0:T(8,128)(2,1)}, bf16[512,1024]{1,0:T(8,128)(2,1)}, bf16[512,1024]{1,0:T(8,128)(2,1)}, bf16[512,1024]...) custom-call(s32[6]{0:T(128)} %pad_add_fusion.info, ...), custom_call_target="tpu_custom_call" | custom-call | flops 1048576 | bytes 65536 | tf_op jit(solution)/shard_map/project/pallas_call | solution.py:547
  114.2 5.7 %collective-permute-done.11 = bf16[640,128]{1,0:T(8,128)(2,1)S(1)} collective-permute-done((bf16[640,128]{1,0:T(8,128)(2,1)}, bf16[640,128]{1,0:T(8,128)(2,1)S(1)}, u32[]{:S(2)}, u32[]{:S(2)}) %collective-permute-start.11) | collective-permute-done | bytes 163872 | tf_op jit(solution)/shard_map/ppermute | solution.py:846
  123.4 10.9 %collective-permute-done.12 = bf16[640,128]{1,0:T(8,128)(2,1)S(1)} collective-permute-done((bf16[640,128]{1,0:T(8,128)(2,1)S(1)}, bf16[640,128]{1,0:T(8,128)(2,1)S(1)}, u32[]{:S(2)}, u32[]{:S(2)}) %collective-permute-start.12) | collective-permute-done | bytes 163872 | tf_op jit(solution)/shard_map/ppermute | solution.py:846
  138.3 18.3 %scan_forward.1 = (f32[512,1024]{1,0:T(8,128)}, f32[8,16,520,128]{3,2,1,0:T(8,128)}) custom-call(f32[512,33]{1,0:T(8,128)} %pad_maximum_fusion.2.bc, bf16[512,128]{1,0:T(8,128)(2,1)} %slice.150.rank, bf16[320,1024]{1,0:T(8,128)(2,1)} %copy-done.2, bf16[512,1024]{1,0:T(8,128)(2,1)} %get-tuple-element.306.act.refs_7_, f32[512,1]{1,0:T(8,128)} %copy-done.8, ...), custom_call_target="tpu_custom_call" | custom-call | flops 1048576 | bytes 65536 | tf_op jit(solution)/shard_map/scan_forward/pallas_call | solution.py:103
  157.9 16.9 %gate_block.1 = (bf16[128,2048]{1,0:T(8,128)(2,1)}, bf16[128,2048]{1,0:T(8,128)(2,1)}, bf16[128,2048]{1,0:T(8,128)(2,1)}, bf16[128,2048]{1,0:T(8,128)(2,1)}, f32...) custom-call(s32[6]{0:T(128)} %pad_add_fusion.info, ...), custom_call_target="tpu_custom_call" | custom-call | flops 1048576 | bytes 65536 | tf_op jit(solution)/shard_map/gate_block/pallas_call | solution.py:607
  176.4 16.1 %gate_back.1 = (f32[512,1024]{1,0:T(8,128)}, bf16[512,1024]{1,0:T(8,128)(2,1)}, bf16[512,2048]{1,0:T(8,128)(2,1)}, bf16[2048,1024]{1,0:T(8,128)(2,1)}) custom-call(s32[6]{0:T(128)} %pad_add_fusion.info, bf16[128,2048]{1,0:T(8,128)(2,1)} %refs_0_.1, bf16[128,2048]{1,0:T(8,128)(2,1)} %copy-done.28, bf16[128,2048]{1,0:T(8,128)(2,1)} %collective-permute-done.17.refs_2_, ...), custom_call_target="tpu_custom_call" | custom-call | flops 1048576 | bytes 65536 | tf_op jit(solution)/shard_map/gate_back/pallas_call | solution.py:652
  193.3 4.6 %all-to-all-start.3 = ((bf16[8,256,1024]{2,1,0:T(8,128)(2,1)}), bf16[8,256,1024]{2,1,0:T(8,128)(2,1)}, u32[]{:S(2)}, u32[]{:S(2)}) async-start(bf16[8,256,1024]{2,1,0:T(8,128)(2,1)} %bitcast.59), calls=%async_computation.3 | async-start | bytes 8388608 | tf_op jit(solution)/shard_map/all_to_all | solution.py:1157
  202.2 34.4 %scan_backward.1 = (bf16[640,128]{1,0:T(8,128)(2,1)}, bf16[512,1024]{1,0:T(8,128)(2,1)}, f32[128,1024]{1,0:T(8,128)}, f32[2,1024]{1,0:T(2,128)}, f32[16,1024]{1,0:T(8,128)}) custom-call(f32[512,33]{1,0:T(8,128)} %pad_maximum_fusion.2.bc, bf16[512,128]{1,0:T(8,128)(2,1)} %slice.150.rank, bf16[320,1024]{1,0:T(8,128)(2,1)} %copy-done.2, ...), custom_call_target="tpu_custom_call" | custom-call | flops 1048576 | bytes 65536 | tf_op jit(solution)/shard_map/scan_backward/pallas_call | solution.py:277
  236.8 6.2 %outer_product.1 = (bf16[512,2048]{1,0:T(8,128)(2,1)}, bf16[512,2048]{1,0:T(8,128)(2,1)}) custom-call(bf16[512,512]{1,0:T(8,128)(2,1)} %get-tuple-element.362.kept, bf16[512,512]{1,0:T(8,128)(2,1)} %get-tuple-element.363.sent, bf16[512,2048]{1,0:T(8,128)(2,1)} %get-tuple-element.364.right), custom_call_target="tpu_custom_call" | custom-call | flops 1048576 | bytes 65536 | tf_op jit(solution)/shard_map/outer_product/pallas_call | solution.py:456
  247.0 4.0 %reduce_sum.39 = bf16[256,1024]{1,0:T(8,128)(2,1)} reduce(bf16[8,256,1024]{2,1,0:T(8,128)(2,1)} %all-to-all-done.3, bf16[]{:T(256)} %constant.45.clone.1), dimensions={0}, to_apply=%region_1.2 | reduce | flops 1835008 | bytes 4718594 | tf_op jit(solution)/shard_map/reduce_sum | solution.py:1169
  252.3 4.0 %chip_halves.1 = (bf16[256,1024]{1,0:T(8,128)(2,1)}, bf16[256,1024]{1,0:T(8,128)(2,1)}, bf16[128,1024]{1,0:T(8,128)(2,1)}, bf16[128,1024]{1,0:T(8,128)(2,1)}, bf...) custom-call(s32[1]{0:T(128)} %bitcast.27.chip, bf16[512,2048]{1,0:T(8,128)(2,1)} %get-tuple-element.372.kept, ...), custom_call_target="tpu_custom_call" | custom-call | flops 1024 | bytes 65536 | tf_op jit(solution)/shard_map/chip_halves/pallas_call | solution.py:1003
  259.9 18.7 %conv_back.1 = (bf16[512,2048]{1,0:T(8,128)(2,1)}, bf16[1024,1024]{1,0:T(8,128)(2,1)}, bf16[1024,1024]{1,0:T(8,128)(2,1)}, f32[4,48,1024]{2,1,0:T(8,128)}, bf16[4,48,1024]{2,1,0:T(8,128)(2,1)}) custom-call(s32[6]{0:T(128)} %pad_add_fusion.info, f32[640,128]{1,0:T(8,128)} %copy-done.9, bf16[640,128]{1,0:T(8,128)(2,1)} %copy-done.35, ...), custom_call_target="tpu_custom_call" | custom-call | flops 1048576 | bytes 65536 | tf_op jit(solution)/shard_map/conv_back/pallas_call | solution.py:805
  279.4 5.1 %all-to-all-start.5 = ((bf16[4,128,2048]{2,1,0:T(8,128)(2,1)}), bf16[4,128,2048]{2,1,0:T(8,128)(2,1)S(1)}, u32[]{:S(2)}, u32[]{:S(2)}) async-start(bf16[4,128,2048]{2,1,0:T(8,128)(2,1)} %bitcast.61), calls=%async_computation.5 | async-start | bytes 4194304 | tf_op jit(solution)/shard_map/all_to_all | solution.py:859
  288.3 4.3 %add_core.1 = (bf16[304,1024]{1,0:T(8,128)(2,1)}, bf16[304,1024]{1,0:T(8,128)(2,1)}, bf16[304,1024]{1,0:T(8,128)(2,1)}, bf16[304,1024]{1,0:T(8,128)(2,1)}) custom-call(s32[1]{0:T(128)} %bitcast.27.chip, bf16[1024,1024]{1,0:T(8,128)(2,1)} %get-tuple-element.414.kept, bf16[1024,1024]{1,0:T(8,128)(2,1)} %collective-permute-done.26.got, ...), custom_call_target="tpu_custom_call" | custom-call | flops 1024 | bytes 65536 | tf_op jit(solution)/shard_map/add_core/pallas_call | solution.py:928
  292.6 5.6 %collective-permute-done.24 = bf16[256,1024]{1,0:T(8,128)(2,1)S(1)} collective-permute-done((bf16[256,1024]{1,0:T(8,128)(2,1)}, bf16[256,1024]{1,0:T(8,128)(2,1)S(1)}, u32[]{:S(2)}, u32[]{:S(2)}) %collective-permute-start.24) | collective-permute-done | bytes 524320 | tf_op jit(solution)/shard_map/ppermute | solution.py:846
  304.6 11.2 %collective-permute-done.28.refs_1_ = bf16[304,1024]{1,0:T(8,128)(2,1)} collective-permute-done((bf16[304,1024]{1,0:T(8,128)(2,1)}, bf16[304,1024]{1,0:T(8,128)(2,1)}, u32[]{:S(2)}, u32[]{:S(2)}) %collective-permute-start.28) | collective-permute-done | bytes 622624 | tf_op jit(solution)/shard_map/ppermute | solution.py:846
  315.8 12.0 %collective-permute-done.29.refs_2_ = bf16[304,1024]{1,0:T(8,128)(2,1)} collective-permute-done((bf16[304,1024]{1,0:T(8,128)(2,1)}, bf16[304,1024]{1,0:T(8,128)(2,1)}, u32[]{:S(2)}, u32[]{:S(2)}) %collective-permute-start.29) | collective-permute-done | bytes 622624 | tf_op jit(solution)/shard_map/ppermute | solution.py:846
  (243 shorter events, 90.4 us)
Async XLA Ops:
  3.2 46.2 %all-to-all-start = ((bf16[4,144,1024]{2,1,0:T(8,128)(2,1)}), bf16[4,144,1024]{2,1,0:T(8,128)(2,1)S(1)}, u32[]{:S(2)}, u32[]{:S(2)}) async-start(bf16[4,144,1024]{2,1,0:T(8,128)(2,1)} %split_columns.1), calls=%async_computation | async-start | bytes 2359296 | tf_op jit(solution)/shard_map/all_to_all | solution.py:859
  9.9 34.3 %collective-permute-start.3 = (bf16[160,2048]{1,0:T(8,128)(2,1)S(1)}, bf16[160,2048]{1,0:T(8,128)(2,1)}, u32[]{:S(2)}, u32[]{:S(2)}) collective-permute-start(bf16[160,2048]{1,0:T(8,128)(2,1)S(1)} %constant_dynamic-update-slice_fusion.refs_0_), channel_id=1, source_target_pairs={{0,24},{4,28},{8,16},{12,20},{16,8},{20,12},{24,0},{28,4},{1,25},{... | collective-permute-start | bytes 1966088 | tf_op jit(solution)/shard_map/ppermute | solution.py:846
  12.4 31.7 %collective-permute-start.2 = (bf16[160,2048]{1,0:T(8,128)(2,1)S(1)}, bf16[160,2048]{1,0:T(8,128)(2,1)}, u32[]{:S(2)}, u32[]{:S(2)}) collective-permute-start(bf16[160,2048]{1,0:T(8,128)(2,1)S(1)} %constant_dynamic-update-slice_fusion.refs_0_), channel_id=1, source_target_pairs={{0,16},{4,20},{8,24},{12,28},{16,0},{20,4},{24,8},{28,12},{1,17},{... | collective-permute-start | bytes 1966088 | tf_op jit(solution)/shard_map/ppermute | solution.py:846
  13.0 31.2 %collective-permute-start.1 = (bf16[160,2048]{1,0:T(8,128)(2,1)S(1)}, bf16[160,2048]{1,0:T(8,128)(2,1)}, u32[]{:S(2)}, u32[]{:S(2)}) collective-permute-start(bf16[160,2048]{1,0:T(8,128)(2,1)S(1)} %constant_dynamic-update-slice_fusion.refs_0_), channel_id=1, source_target_pairs={{0,8},{4,12},{8,0},{12,4},{16,24},{20,28},{24,16},{28,20},{1,9},{5... | collective-permute-start | bytes 1966088 | tf_op jit(solution)/shard_map/ppermute | solution.py:846
  13.5 30.7 %collective-permute-start = (bf16[128,2048]{1,0:T(8,128)(2,1)S(1)}, bf16[128,2048]{1,0:T(8,128)(2,1)S(1)}, u32[]{:S(2)}, u32[]{:S(2)}) collective-permute-start(bf16[128,2048]{1,0:T(8,128)(2,1)S(1)} %copy-done.4), channel_id=1, source_target_pairs={{0,1},{1,2},{2,3},{3,0},{4,5},{5,6},{6,7},{7,4},{8,9},{9,10},{10,1... | collective-permute-start | bytes 1572872 | tf_op jit(solution)/shard_map/ppermute | solution.py:851
  52.2 38.4 %all-to-all-start.1 = ((bf16[4,272,1024]{2,1,0:T(8,128)(2,1)}), bf16[4,272,1024]{2,1,0:T(8,128)(2,1)S(1)}, u32[]{:S(2)}, u32[]{:S(2)}) async-start(bf16[4,272,1024]{2,1,0:T(8,128)(2,1)} %broadcast_in_dim.48), calls=%async_computation.1 | async-start | bytes 4456448 | tf_op jit(solution)/shard_map/all_to_all | solution.py:863
  55.9 34.7 %collective-permute-start.4 = (bf16[128,2048]{1,0:T(8,128)(2,1)S(1)}, bf16[128,2048]{1,0:T(8,128)(2,1)}, u32[]{:S(2)}, u32[]{:S(2)}) collective-permute-start(bf16[128,2048]{1,0:T(8,128)(2,1)S(1)} %copy-done.4), channel_id=1, source_target_pairs={{0,2},{1,3},{2,0},{3,1},{4,6},{5,7},{6,4},{7,5},{8,10},{9,11},{10,... | collective-permute-start | bytes 1572872 | tf_op jit(solution)/shard_map/ppermute | solution.py:851
  92.7 30.0 %all-to-all-start.2 = ((bf16[4,256,1024]{2,1,0:T(8,128)(2,1)}), bf16[4,256,1024]{2,1,0:T(8,128)(2,1)}, u32[]{:S(2)}, u32[]{:S(2)}) async-start(bf16[4,256,1024]{2,1,0:T(8,128)(2,1)} %broadcast_in_dim.49), calls=%async_computation.2 | async-start | bytes 4194304 | tf_op jit(solution)/shard_map/all_to_all | solution.py:863
  97.4 16.6 %collective-permute-start.9 = (bf16[160,2048]{1,0:T(8,128)(2,1)}, bf16[160,2048]{1,0:T(8,128)(2,1)S(1)}, u32[]{:S(2)}, u32[]{:S(2)}) collective-permute-start(bf16[160,2048]{1,0:T(8,128)(2,1)} %copy-done.10), channel_id=1, source_target_pairs={{0,4},{4,0},{8,12},{12,8},{16,20},{20,16},{24,28},{28,24},{1,5},{5... | collective-permute-start | bytes 1966088 | tf_op jit(solution)/shard_map/ppermute | solution.py:846
  97.7 16.4 %collective-permute-start.10 = (bf16[160,2048]{1,0:T(8,128)(2,1)}, bf16[160,2048]{1,0:T(8,128)(2,1)S(1)}, u32[]{:S(2)}, u32[]{:S(2)}) collective-permute-start(bf16[160,2048]{1,0:T(8,128)(2,1)} %collective-permute-done.1.refs_1_), channel_id=1, source_target_pairs={{0,4},{4,0},{8,12},{12,8},{16,20},{20,16},{24,28},{28,24},{1,5},{5... | collective-permute-start | bytes 1966088 | tf_op jit(solution)/shard_map/ppermute | solution.py:846
  98.0 16.1 %collective-permute-start.8 = (bf16[128,2048]{1,0:T(8,128)(2,1)}, bf16[128,2048]{1,0:T(8,128)(2,1)S(1)}, u32[]{:S(2)}, u32[]{:S(2)}) collective-permute-start(bf16[128,2048]{1,0:T(8,128)(2,1)} %refs_0_.1), channel_id=1, source_target_pairs={{0,1},{1,2},{2,3},{3,0},{4,5},{5,6},{6,7},{7,4},{8,9},{9,10},{10,1... | collective-permute-start | bytes 1572872 | tf_op jit(solution)/shard_map/ppermute | solution.py:851
  122.7 33.9 %collective-permute-start.15 = (bf16[4,256,1024]{2,1,0:T(8,128)(2,1)}, bf16[4,256,1024]{2,1,0:T(8,128)(2,1)S(1)}, u32[]{:S(2)}, u32[]{:S(2)}) collective-permute-start(bf16[4,256,1024]{2,1,0:T(8,128)(2,1)} %all-to-all-done.2.own.refs_2_), channel_id=1, source_target_pairs={{0,4},{4,0},{8,12},{12,8},{16,20},{20,16},{24,28},{28,24},{1,5},{5... | collective-permute-start | bytes 6291464 | tf_op jit(solution)/shard_map/ppermute | solution.py:846
  134.3 22.2 %collective-permute-start.16 = (bf16[128,2048]{1,0:T(8,128)(2,1)}, bf16[128,2048]{1,0:T(8,128)(2,1)}, u32[]{:S(2)}, u32[]{:S(2)}) collective-permute-start(bf16[128,2048]{1,0:T(8,128)(2,1)} %refs_0_.1), channel_id=1, source_target_pairs={{0,3},{1,0},{2,1},{3,2},{4,7},{5,4},{6,5},{7,6},{8,11},{9,8},{10,9... | collective-permute-start | bytes 1572872 | tf_op jit(solution)/shard_map/ppermute | solution.py:851
  135.6 39.2 %collective-permute-start.17 = (bf16[128,2048]{1,0:T(8,128)(2,1)}, bf16[128,2048]{1,0:T(8,128)(2,1)}, u32[]{:S(2)}, u32[]{:S(2)}) collective-permute-start(bf16[128,2048]{1,0:T(8,128)(2,1)} %refs_0_.1), channel_id=1, source_target_pairs={{0,2},{1,3},{2,0},{3,1},{4,6},{5,7},{6,4},{7,5},{8,10},{9,11},{10,... | collective-permute-start | bytes 1572872 | tf_op jit(solution)/shard_map/ppermute | solution.py:851
  174.8 17.7 %collective-permute-start.18 = (bf16[128,2048]{1,0:T(8,128)(2,1)}, bf16[128,2048]{1,0:T(8,128)(2,1)S(1)}, u32[]{:S(2)}, u32[]{:S(2)}) collective-permute-start(bf16[128,2048]{1,0:T(8,128)(2,1)} %get-tuple-element.335), channel_id=1, source_target_pairs={{0,1},{1,2},{2,3},{3,0},{4,5},{5,6},{6,7},{7,4},{8,9},{9,10},{10,1... | collective-permute-start | bytes 1572872 | tf_op jit(solution)/shard_map/ppermute | solution.py:851
  193.3 53.7 %all-to-all-start.3 = ((bf16[8,256,1024]{2,1,0:T(8,128)(2,1)}), bf16[8,256,1024]{2,1,0:T(8,128)(2,1)}, u32[]{:S(2)}, u32[]{:S(2)}) async-start(bf16[8,256,1024]{2,1,0:T(8,128)(2,1)} %bitcast.59), calls=%async_computation.3 | async-start | bytes 8388608 | tf_op jit(solution)/shard_map/all_to_all | solution.py:1157
  197.9 38.8 %collective-permute-start.19 = (bf16[128,2048]{1,0:T(8,128)(2,1)S(1)}, bf16[128,2048]{1,0:T(8,128)(2,1)S(1)}, u32[]{:S(2)}, u32[]{:S(2)}) collective-permute-start(bf16[128,2048]{1,0:T(8,128)(2,1)S(1)} %copy-done.48), channel_id=1, source_target_pairs={{0,2},{1,3},{2,0},{3,1},{4,6},{5,7},{6,4},{7,5},{8,10},{9,11},{10,... | collective-permute-start | bytes 1572872 | tf_op jit(solution)/shard_map/ppermute | solution.py:851
  200.1 36.5 %collective-permute-start.20 = (bf16[128,2048]{1,0:T(8,128)(2,1)S(1)}, bf16[128,2048]{1,0:T(8,128)(2,1)S(1)}, u32[]{:S(2)}, u32[]{:S(2)}) collective-permute-start(bf16[128,2048]{1,0:T(8,128)(2,1)S(1)} %copy-done.47), channel_id=1, source_target_pairs={{0,3},{1,0},{2,1},{3,2},{4,7},{5,4},{6,5},{7,6},{8,11},{9,8},{10,9... | collective-permute-start | bytes 1572872 | tf_op jit(solution)/shard_map/ppermute | solution.py:851
  256.3 22.2 %all-to-all-start.4 = ((bf16[4,64,1024]{2,1,0:T(8,128)(2,1)}), bf16[4,64,1024]{2,1,0:T(8,128)(2,1)S(1)}, u32[]{:S(2)}, u32[]{:S(2)}) async-start(bf16[4,64,1024]{2,1,0:T(8,128)(2,1)} %bitcast.29), calls=%async_computation.4 | async-start | bytes 1048576 | tf_op jit(solution)/shard_map/all_to_all | solution.py:859
  279.4 61.9 %all-to-all-start.5 = ((bf16[4,128,2048]{2,1,0:T(8,128)(2,1)}), bf16[4,128,2048]{2,1,0:T(8,128)(2,1)S(1)}, u32[]{:S(2)}, u32[]{:S(2)}) async-start(bf16[4,128,2048]{2,1,0:T(8,128)(2,1)} %bitcast.61), calls=%async_computation.5 | async-start | bytes 4194304 | tf_op jit(solution)/shard_map/all_to_all | solution.py:859
  298.5 17.3 %collective-permute-start.28 = (bf16[304,1024]{1,0:T(8,128)(2,1)}, bf16[304,1024]{1,0:T(8,128)(2,1)}, u32[]{:S(2)}, u32[]{:S(2)}) collective-permute-start(bf16[304,1024]{1,0:T(8,128)(2,1)} %get-tuple-element.433), channel_id=1, source_target_pairs={{0,8},{4,12},{8,0},{12,4},{16,24},{20,28},{24,16},{28,20},{1,9},{5... | collective-permute-start | bytes 1867784 | tf_op jit(solution)/shard_map/ppermute | solution.py:846
  300.0 27.8 %collective-permute-start.29 = (bf16[304,1024]{1,0:T(8,128)(2,1)}, bf16[304,1024]{1,0:T(8,128)(2,1)}, u32[]{:S(2)}, u32[]{:S(2)}) collective-permute-start(bf16[304,1024]{1,0:T(8,128)(2,1)} %get-tuple-element.434), channel_id=1, source_target_pairs={{0,16},{4,20},{8,24},{12,28},{16,0},{20,4},{24,8},{28,12},{1,17},{... | collective-permute-start | bytes 1867784 | tf_op jit(solution)/shard_map/ppermute | solution.py:846
  300.5 27.3 %collective-permute-start.30 = (bf16[304,1024]{1,0:T(8,128)(2,1)}, bf16[304,1024]{1,0:T(8,128)(2,1)}, u32[]{:S(2)}, u32[]{:S(2)}) collective-permute-start(bf16[304,1024]{1,0:T(8,128)(2,1)} %get-tuple-element.435), channel_id=1, source_target_pairs={{0,24},{4,28},{8,16},{12,20},{16,8},{20,12},{24,0},{28,4},{1,25},{... | collective-permute-start | bytes 1867784 | tf_op jit(solution)/shard_map/ppermute | solution.py:846
  332.6 16.3 %collective-permute-start.31 = (bf16[64,1024]{1,0:T(8,128)(2,1)}, bf16[64,1024]{1,0:T(8,128)(2,1)S(1)}, u32[]{:S(2)}, u32[]{:S(2)}) collective-permute-start(bf16[64,1024]{1,0:T(8,128)(2,1)} %get-tuple-element.446), channel_id=1, source_target_pairs={{0,1},{1,2},{2,3},{3,0},{4,5},{5,6},{6,7},{7,4},{8,9},{9,10},{10,1... | collective-permute-start | bytes 393224 | tf_op jit(solution)/shard_map/ppermute | solution.py:851
  (68 other events, 610.2 us)

commit v5 on v4

--- a/solution.py
+++ b/solution.py
@@ -944,30 +944,43 @@
     return total
 
 
-def sum_chips_kernel(count, place, *refs):
-    blocks, (*outs, small) = refs[:count], refs[count:]
+def sum_chips_kernel(count, n_line, at, place, *refs):
+    blocks, outs, (dt_g, x_g, a_g, conv_g, *vectors, column) = (
+        refs[:count], refs[count : count + n_line], refs[count + n_line :]
+    )
     rows = outs[0].shape[0]
     for s, out in enumerate(outs):
-        at = pl.ds(pl.multiple_of(lax.rem(place[0] + s, len(outs)) * rows, rows), rows)
-        out[...] = sum(block[at, :].astype(F32) for block in blocks).astype(BF)
-    first = rows * len(outs)
-    small[...] = sum(block[first:, :].astype(F32) for block in blocks)
-
-
-def sum_chips(place, blocks, n_line, rows):
+        mine = pl.ds(pl.multiple_of(lax.rem(place[0] + s, n_line) * rows, rows), rows)
+        out[...] = sum(block[mine, :].astype(F32) for block in blocks).astype(BF)
+    first, owned = rows * n_line, column.shape[1]
+    small = sum(block[first:, :].astype(F32) for block in blocks)
+    fold = small.shape[0]
+    for b in range(small.shape[1] // owned):
+        column[b * fold : (b + 1) * fold, :] = small[:, b * owned : (b + 1) * owned]
+    dt_g[...], x_g[...], a_g[...] = column[at.dt_w, :], column[at.x_t, :], column[at.a_t, :]
+    rest = column[at.rest, :]
+    conv_g[...] = rest[: at.taps, :]
+    for i, out in enumerate(vectors):
+        out[...] = rest[at.taps + i : at.taps + i + 1, :]
+
+
+def sum_chips(place, blocks, n_line, rows, at, owned):
     full, width = blocks[0].shape
     vmem = pl.BlockSpec(memory_space=pltpu.VMEM)
-    *parts, small = pl.pallas_call(
-        functools.partial(sum_chips_kernel, len(blocks)),
+    small = [(part.stop - part.start, owned) for part in (at.dt_w, at.x_t, at.a_t)]
+    small += [(at.taps, owned)] + [(1, owned)] * 3
+    outs = pl.pallas_call(
+        functools.partial(sum_chips_kernel, len(blocks), n_line, at),
         in_specs=[pl.BlockSpec(memory_space=pltpu.SMEM)] + [vmem] * len(blocks),
-        out_specs=[vmem] * (n_line + 1),
+        out_specs=[vmem] * (n_line + len(small)),
         out_shape=[jax.ShapeDtypeStruct((rows, width), BF)] * n_line
-        + [jax.ShapeDtypeStruct((full - n_line * rows, width), F32)],
+        + [jax.ShapeDtypeStruct(shape, F32) for shape in small],
+        scratch_shapes=[pltpu.VMEM(((full - n_line * rows) * (width // owned), owned), F32)],
         compiler_params=pltpu.CompilerParams(vmem_limit_bytes=61 << 20),
         cost_estimate=small_cost(1 << 10),
         name="sum_chips",
     )(place[None], *blocks)
-    return parts, small
+    return list(outs[:n_line]), list(outs[n_line:])
 
 
 def sent_far(kept, got, u):
@@ -1012,6 +1025,12 @@
     return ChipSum(held, [first, second])
 
 
+def total_kernel(left, right, left_got, right_got, out):
+    half = left.shape[1]
+    out[:, 0:half] = left[...] + left_got[...].astype(F32)
+    out[:, half:] = right[...] + right_got[...].astype(F32)
+
+
 class ChipSum:
     def __init__(self, held, sends=None):
         self.direct = sends is None
@@ -1040,7 +1059,17 @@
     def total(self):
         if self.direct:
             return sum(part.astype(F32) for part in (self.held[0], *self.got))
-        return jnp.concatenate([h + got.astype(F32) for h, got in zip(self.held, self.got)], axis=1)
+        rows, half = self.held[0].shape
+        vmem = pl.BlockSpec(memory_space=pltpu.VMEM)
+        return pl.pallas_call(
+            total_kernel,
+            in_specs=[vmem] * 4,
+            out_specs=vmem,
+            out_shape=jax.ShapeDtypeStruct((rows, 2 * half), F32),
+            compiler_params=pltpu.CompilerParams(vmem_limit_bytes=61 << 20),
+            cost_estimate=small_cost(1 << 10),
+            name="chip_total",
+        )(*self.held, *self.got)
 
 
 def per_device(
@@ -1173,6 +1202,7 @@
     part, got, out_sum.held, out_sum.sends, gate_rows = fence(part, got, out_sum.held, out_sum.sends, gate_rows)
 
     gate_got = to_line(gate_rows.reshape(n_line, in_rows, width))
+    out_sum.first()
     grad_normed, inner_kept, inner_sent, small_kept, small_sent = conv_back(
         info, n_line, n_dp, part, got, grad_u, at, small, activ, conv_out, inner, allowed,
         dt_w_grad, rate_grad, vectors, grad_gate, (inner_own, inner_other), (gate_own, gate_other),
@@ -1184,7 +1214,6 @@
 
     grad_normed = to_line(grad_normed.reshape(n_line, held_slots, model))
     folded = owned % LANES == 0
-    out_sum.first()
     inner_got, small_got = swap(inner_sent, "dp", 1), swap(small_sent, "dp", 1)
     if folded:
         blocks = add_core(inner_kept, inner_got, small_kept, small_got)
@@ -1195,26 +1224,25 @@
     blocks = [swap(block, "dp", 2 * u) if u else block for u, block in enumerate(blocks)]
     out_sum.add()
     if folded:
-        inner_sent, small_sum = sum_chips(place, blocks, n_line, in_rows)
+        inner_sent, small_sum = sum_chips(place, blocks, n_line, in_rows, at, owned)
     else:
         rows = sum(block.astype(F32) for block in blocks).astype(BF).reshape(n_line, in_rows, width)
         inner_sent = [
             lax.dynamic_index_in_dim(rows, lax.rem(place + s, n_line), 0, keepdims=False) for s in range(n_line)
         ]
         small_sum = add_chips_near(small_kept + small_got.astype(F32))
+        tail_g = small_sum[at.rest]
+        small_sum = [small_sum[at.dt_w], small_sum[at.x_t], small_sum[at.a_t], tail_g[:taps]] + [
+            tail_g[taps + i : taps + i + 1] for i in range(3)
+        ]
     inner_sent, small_sum, branches = out_sum.fenced(inner_sent, small_sum, branches)
 
     inner_got = [shift(block, "fsdp", s) if s else block for s, block in enumerate(inner_sent)]
     out_sum.second()
-    grad_normed, small_sum = fence(grad_normed, small_sum)
     grad_normed = jnp.sum(grad_normed.astype(F32), axis=0)
     out_weight_grad = out_sum.total()
-    small_grads = small_sum
-    if folded:
-        small_grads = small_sum.reshape(-1, n_dp, owned).transpose(1, 0, 2).reshape(-1, owned)
-    dt_g, x_g, a_g = small_grads[at.dt_w], small_grads[at.x_t], small_grads[at.a_t]
-    tail_g = small_grads[at.rest]
-    conv_g, conv_b_g, dt_b_g, skip_g = tail_g[:taps], tail_g[taps], tail_g[taps + 1], tail_g[taps + 2]
+    dt_g, x_g, a_g, conv_g, *vectors = small_sum
+    conv_b_g, dt_b_g, skip_g = [value[0] for value in vectors]
     small_out = [conv_g, conv_b_g, x_g.T, dt_g, dt_b_g, a_g.T, skip_g]
     own_f = own_tokens.astype(F32)
     output = (own_f + own_valid * sum(p.astype(F32) for p in branches)).astype(BF)
@@ -1224,9 +1252,7 @@
     token_grad = own_cot.astype(F32) + own_scale * (
         grad_unit - unit * jnp.mean(grad_unit * unit, axis=1, keepdims=True)
     )
-    inner_got, token_grad, output, out_weight_grad, small_out = fence(
-        inner_got, token_grad, output, out_weight_grad, small_out
-    )
+    inner_got, token_grad, output, out_weight_grad = fence(inner_got, token_grad, output, out_weight_grad)
     in_weight_grad, gain_grad = join_columns(place, inner_got, gate_got, in_weight, gain, n_dp)
     return output, token_grad, gain_grad, in_weight_grad, *small_out, out_weight_grad
 

time: 354 us -> 349 us (0.986)
  transfers between devices with their start and end apart: 42 -> 42, of which waited for: 15 -> 14; matrix products, arithmetic and copies ran while one was open for 9% -> 7% of each run, Pallas kernels for 38% -> 39%
where the time goes in v5:
time: 349 us; the launch traced here: 348 us
  Pallas kernels  143 us (41%)
  waiting for transfers between devices  108 us (31%)
  starting transfers between devices  58.3 us (17%)
  local copies, waits for them, and re-layouts  18.5 us (5%)
  other arithmetic  17.8 us (5%)
    ppermute x12, waiting for transfers between devices, shift(): lax.ppermute(value, axis, [(i, (i + steps) % count) for i in range(count)])  50.8 us
    ppermute x24, waiting for transfers between devices, swap(): return lax.ppermute(value, axis, [(i, i ^ mask) for i in range(count)])  47.6 us
    pallas_call x1, Pallas kernels, scan_backward(): pl.pallas_call(functools.partial(backward_kernel, at), grid=(nb,), in_spe...  34.4 us
    pallas_call x1, Pallas kernels, conv_back(): pl.pallas_call(functools.partial(conv_back_kernel, n_line, n_dp, at), in_...  18.7 us
    pallas_call x1, Pallas kernels, scan_forward(): pl.pallas_call(functools.partial(forward_kernel, at), grid=(nb,), in_spec...  18.3 us
    pallas_call x1, Pallas kernels, gate_block(): pl.pallas_call(functools.partial(gate_kernel, n_line, n_dp, at), in_specs...  16.9 us
    ppermute x12, starting transfers between devices, shift(): lax.ppermute(value, axis, [(i, (i + steps) % count) for i in range(count)])  16.6 us
    pallas_call x1, Pallas kernels, gate_back(): pl.pallas_call(functools.partial(gate_back_kernel, n_line, at), in_specs=...  16.1 us
  transfers between devices with their start and end apart: 42, of which 14 were waited for; matrix products, arithmetic and copies ran while one was open for 7% of the time, Pallas kernels for 39%

profile of v5, /device:TPU:0, one launch (start us, length us, event | category | flops | bytes accessed | tf_op | source)
XLA Modules:
  0.0 348.2 jit_solution(5129049809611603171)
XLA Ops:
  3.2 6.4 %all-to-all-start = ((bf16[4,144,1024]{2,1,0:T(8,128)(2,1)}), bf16[4,144,1024]{2,1,0:T(8,128)(2,1)S(1)}, u32[]{:S(2)}, u32[]{:S(2)}) async-start(bf16[4,144,1024]{2,1,0:T(8,128)(2,1)} %split_columns.1), calls=%async_computation | async-start | bytes 2359296 | tf_op jit(solution)/shard_map/all_to_all | solution.py:859
  21.7 22.5 %collective-permute-done.refs_1_ = bf16[128,2048]{1,0:T(8,128)(2,1)S(1)} collective-permute-done((bf16[128,2048]{1,0:T(8,128)(2,1)S(1)}, bf16[128,2048]{1,0:T(8,128)(2,1)S(1)}, u32[]{:S(2)}, u32[]{:S(2)}) %collective-permute-start) | collective-permute-done | bytes 524320 | tf_op jit(solution)/shard_map/ppermute | solution.py:851
  44.2 5.3 %all-to-all-done = bf16[4,144,1024]{2,1,0:T(8,128)(2,1)S(1)} async-done(((bf16[4,144,1024]{2,1,0:T(8,128)(2,1)}), bf16[4,144,1024]{2,1,0:T(8,128)(2,1)S(1)}, u32[]{:S(2)}, u32[]{:S(2)}) %all-to-all-start) | async-done | bytes 1179680 | tf_op jit(solution)/shard_map/all_to_all | solution.py:859
  52.1 3.7 %all-to-all-start.1 = ((bf16[4,272,1024]{2,1,0:T(8,128)(2,1)}), bf16[4,272,1024]{2,1,0:T(8,128)(2,1)S(1)}, u32[]{:S(2)}, u32[]{:S(2)}) async-start(bf16[4,272,1024]{2,1,0:T(8,128)(2,1)} %broadcast_in_dim.48), calls=%async_computation.1 | async-start | bytes 4456448 | tf_op jit(solution)/shard_map/all_to_all | solution.py:863
  64.4 5.7 %collective-permute-done.5.refs_3_ = bf16[128,2048]{1,0:T(8,128)(2,1)} collective-permute-done((bf16[128,2048]{1,0:T(8,128)(2,1)S(1)}, bf16[128,2048]{1,0:T(8,128)(2,1)}, u32[]{:S(2)}, u32[]{:S(2)}) %collective-permute-start.5) | collective-permute-done | bytes 524320 | tf_op jit(solution)/shard_map/ppermute | solution.py:851
  70.1 20.5 %collective-permute-done.4.refs_2_ = bf16[128,2048]{1,0:T(8,128)(2,1)} collective-permute-done((bf16[128,2048]{1,0:T(8,128)(2,1)S(1)}, bf16[128,2048]{1,0:T(8,128)(2,1)}, u32[]{:S(2)}, u32[]{:S(2)}) %collective-permute-start.4) | collective-permute-done | bytes 524320 | tf_op jit(solution)/shard_map/ppermute | solution.py:851
  92.6 4.4 %all-to-all-start.2 = ((bf16[4,256,1024]{2,1,0:T(8,128)(2,1)}), bf16[4,256,1024]{2,1,0:T(8,128)(2,1)}, u32[]{:S(2)}, u32[]{:S(2)}) async-start(bf16[4,256,1024]{2,1,0:T(8,128)(2,1)} %broadcast_in_dim.49), calls=%async_computation.2 | async-start | bytes 4194304 | tf_op jit(solution)/shard_map/all_to_all | solution.py:863
  98.6 13.2 %project.1 = (f32[1,2048]{1,0:T(1,128)}, bf16[512,2048]{1,0:T(8,128)(2,1)}, bf16[512,1024]{1,0:T(8,128)(2,1)}, bf16[512,1024]{1,0:T(8,128)(2,1)}, bf16[512,1024]...) custom-call(s32[6]{0:T(128)} %pad_add_fusion.info, ...), custom_call_target="tpu_custom_call" | custom-call | flops 1048576 | bytes 65536 | tf_op jit(solution)/shard_map/project/pallas_call | solution.py:547
  114.1 5.7 %collective-permute-done.11 = bf16[640,128]{1,0:T(8,128)(2,1)S(1)} collective-permute-done((bf16[640,128]{1,0:T(8,128)(2,1)}, bf16[640,128]{1,0:T(8,128)(2,1)S(1)}, u32[]{:S(2)}, u32[]{:S(2)}) %collective-permute-start.11) | collective-permute-done | bytes 163872 | tf_op jit(solution)/shard_map/ppermute | solution.py:846
  123.4 10.9 %collective-permute-done.12 = bf16[640,128]{1,0:T(8,128)(2,1)S(1)} collective-permute-done((bf16[640,128]{1,0:T(8,128)(2,1)S(1)}, bf16[640,128]{1,0:T(8,128)(2,1)S(1)}, u32[]{:S(2)}, u32[]{:S(2)}) %collective-permute-start.12) | collective-permute-done | bytes 163872 | tf_op jit(solution)/shard_map/ppermute | solution.py:846
  138.3 18.3 %scan_forward.1 = (f32[512,1024]{1,0:T(8,128)}, f32[8,16,520,128]{3,2,1,0:T(8,128)}) custom-call(f32[512,33]{1,0:T(8,128)} %pad_maximum_fusion.1.bc, bf16[512,128]{1,0:T(8,128)(2,1)} %slice.105.rank, bf16[320,1024]{1,0:T(8,128)(2,1)} %copy-done.2, bf16[512,1024]{1,0:T(8,128)(2,1)} %get-tuple-element.309.act.refs_7_, f32[512,1]{1,0:T(8,128)} %copy-done.8, ...), custom_call_target="tpu_custom_call" | custom-call | flops 1048576 | bytes 65536 | tf_op jit(solution)/shard_map/scan_forward/pallas_call | solution.py:103
  158.0 16.9 %gate_block.1 = (bf16[128,2048]{1,0:T(8,128)(2,1)}, bf16[128,2048]{1,0:T(8,128)(2,1)}, bf16[128,2048]{1,0:T(8,128)(2,1)}, bf16[128,2048]{1,0:T(8,128)(2,1)}, f32...) custom-call(s32[6]{0:T(128)} %pad_add_fusion.info, ...), custom_call_target="tpu_custom_call" | custom-call | flops 1048576 | bytes 65536 | tf_op jit(solution)/shard_map/gate_block/pallas_call | solution.py:607
  176.4 16.1 %gate_back.1 = (f32[512,1024]{1,0:T(8,128)}, bf16[512,1024]{1,0:T(8,128)(2,1)}, bf16[512,2048]{1,0:T(8,128)(2,1)}, bf16[2048,1024]{1,0:T(8,128)(2,1)}) custom-call(s32[6]{0:T(128)} %pad_add_fusion.info, bf16[128,2048]{1,0:T(8,128)(2,1)} %refs_0_.1, bf16[128,2048]{1,0:T(8,128)(2,1)} %copy-done.28, bf16[128,2048]{1,0:T(8,128)(2,1)} %collective-permute-done.17.refs_2_, ...), custom_call_target="tpu_custom_call" | custom-call | flops 1048576 | bytes 65536 | tf_op jit(solution)/shard_map/gate_back/pallas_call | solution.py:652
  193.4 4.6 %all-to-all-start.3 = ((bf16[8,256,1024]{2,1,0:T(8,128)(2,1)}), bf16[8,256,1024]{2,1,0:T(8,128)(2,1)}, u32[]{:S(2)}, u32[]{:S(2)}) async-start(bf16[8,256,1024]{2,1,0:T(8,128)(2,1)} %bitcast.49), calls=%async_computation.3 | async-start | bytes 8388608 | tf_op jit(solution)/shard_map/all_to_all | solution.py:1186
  202.3 34.4 %scan_backward.1 = (bf16[640,128]{1,0:T(8,128)(2,1)}, bf16[512,1024]{1,0:T(8,128)(2,1)}, f32[128,1024]{1,0:T(8,128)}, f32[2,1024]{1,0:T(2,128)}, f32[16,1024]{1,0:T(8,128)}) custom-call(f32[512,33]{1,0:T(8,128)} %pad_maximum_fusion.1.bc, bf16[512,128]{1,0:T(8,128)(2,1)} %slice.105.rank, bf16[320,1024]{1,0:T(8,128)(2,1)} %copy-done.2, ...), custom_call_target="tpu_custom_call" | custom-call | flops 1048576 | bytes 65536 | tf_op jit(solution)/shard_map/scan_backward/pallas_call | solution.py:277
  236.9 6.2 %outer_product.1 = (bf16[512,2048]{1,0:T(8,128)(2,1)}, bf16[512,2048]{1,0:T(8,128)(2,1)}) custom-call(bf16[512,512]{1,0:T(8,128)(2,1)} %get-tuple-element.365.kept, bf16[512,512]{1,0:T(8,128)(2,1)} %get-tuple-element.366.sent, bf16[512,2048]{1,0:T(8,128)(2,1)} %get-tuple-element.367.right), custom_call_target="tpu_custom_call" | custom-call | flops 1048576 | bytes 65536 | tf_op jit(solution)/shard_map/outer_product/pallas_call | solution.py:456
  247.1 4.0 %reduce_sum.39 = bf16[256,1024]{1,0:T(8,128)(2,1)} reduce(bf16[8,256,1024]{2,1,0:T(8,128)(2,1)} %all-to-all-done.3, bf16[]{:T(256)} %constant.45.clone.1), dimensions={0}, to_apply=%region_1.2 | reduce | flops 1835008 | bytes 4718594 | tf_op jit(solution)/shard_map/reduce_sum | solution.py:1198
  252.4 4.0 %chip_halves.1 = (bf16[256,1024]{1,0:T(8,128)(2,1)}, bf16[256,1024]{1,0:T(8,128)(2,1)}, bf16[128,1024]{1,0:T(8,128)(2,1)}, bf16[128,1024]{1,0:T(8,128)(2,1)}, bf...) custom-call(s32[1]{0:T(128)} %bitcast.27.chip, bf16[512,2048]{1,0:T(8,128)(2,1)} %get-tuple-element.375.kept, ...), custom_call_target="tpu_custom_call" | custom-call | flops 1024 | bytes 65536 | tf_op jit(solution)/shard_map/chip_halves/pallas_call | solution.py:1016
  261.4 18.7 %conv_back.1 = (bf16[512,2048]{1,0:T(8,128)(2,1)}, bf16[1024,1024]{1,0:T(8,128)(2,1)}, bf16[1024,1024]{1,0:T(8,128)(2,1)}, f32[4,48,1024]{2,1,0:T(8,128)}, bf16[4,48,1024]{2,1,0:T(8,128)(2,1)}) custom-call(s32[6]{0:T(128)} %pad_add_fusion.info, f32[640,128]{1,0:T(8,128)} %copy-done.9, bf16[640,128]{1,0:T(8,128)(2,1)} %copy-done.35, ...), custom_call_target="tpu_custom_call" | custom-call | flops 1048576 | bytes 65536 | tf_op jit(solution)/shard_map/conv_back/pallas_call | solution.py:805
  281.1 5.1 %all-to-all-start.5 = ((bf16[4,128,2048]{2,1,0:T(8,128)(2,1)}), bf16[4,128,2048]{2,1,0:T(8,128)(2,1)S(1)}, u32[]{:S(2)}, u32[]{:S(2)}) async-start(bf16[4,128,2048]{2,1,0:T(8,128)(2,1)} %bitcast.51), calls=%async_computation.5 | async-start | bytes 4194304 | tf_op jit(solution)/shard_map/all_to_all | solution.py:859
  286.7 3.8 %collective-permute-done.27.small_got = bf16[4,48,1024]{2,1,0:T(8,128)(2,1)S(1)} collective-permute-done((bf16[4,48,1024]{2,1,0:T(8,128)(2,1)S(1)}, bf16[4,48,1024]{2,1,0:T(8,128)(2,1)S(1)}, u32[]{:S(2)}, u32[]{:S(2)}) %collective-permute-start.27) | collective-permute-done | bytes 393248 | tf_op jit(solution)/shard_map/ppermute | solution.py:846
  291.3 4.2 %add_core.1 = (bf16[304,1024]{1,0:T(8,128)(2,1)}, bf16[304,1024]{1,0:T(8,128)(2,1)}, bf16[304,1024]{1,0:T(8,128)(2,1)}, bf16[304,1024]{1,0:T(8,128)(2,1)}) custom-call(s32[1]{0:T(128)} %bitcast.27.chip, bf16[1024,1024]{1,0:T(8,128)(2,1)} %get-tuple-element.417.kept, bf16[1024,1024]{1,0:T(8,128)(2,1)} %collective-permute-done.26.got, ...), custom_call_target="tpu_custom_call" | custom-call | flops 1024 | bytes 65536 | tf_op jit(solution)/shard_map/add_core/pallas_call | solution.py:928
  301.6 11.1 %collective-permute-done.28.refs_1_ = bf16[304,1024]{1,0:T(8,128)(2,1)} collective-permute-done((bf16[304,1024]{1,0:T(8,128)(2,1)}, bf16[304,1024]{1,0:T(8,128)(2,1)}, u32[]{:S(2)}, u32[]{:S(2)}) %collective-permute-start.28) | collective-permute-done | bytes 622624 | tf_op jit(solution)/shard_map/ppermute | solution.py:846
  312.7 13.7 %collective-permute-done.29.refs_2_ = bf16[304,1024]{1,0:T(8,128)(2,1)} collective-permute-done((bf16[304,1024]{1,0:T(8,128)(2,1)}, bf16[304,1024]{1,0:T(8,128)(2,1)}, u32[]{:S(2)}, u32[]{:S(2)}) %collective-permute-start.29) | collective-permute-done | bytes 622624 | tf_op jit(solution)/shard_map/ppermute | solution.py:846
  (234 shorter events, 85.9 us)
Async XLA Ops:
  3.2 46.2 %all-to-all-start = ((bf16[4,144,1024]{2,1,0:T(8,128)(2,1)}), bf16[4,144,1024]{2,1,0:T(8,128)(2,1)S(1)}, u32[]{:S(2)}, u32[]{:S(2)}) async-start(bf16[4,144,1024]{2,1,0:T(8,128)(2,1)} %split_columns.1), calls=%async_computation | async-start | bytes 2359296 | tf_op jit(solution)/shard_map/all_to_all | solution.py:859
  9.9 34.3 %collective-permute-start.3 = (bf16[160,2048]{1,0:T(8,128)(2,1)S(1)}, bf16[160,2048]{1,0:T(8,128)(2,1)}, u32[]{:S(2)}, u32[]{:S(2)}) collective-permute-start(bf16[160,2048]{1,0:T(8,128)(2,1)S(1)} %constant_dynamic-update-slice_fusion.refs_0_), channel_id=1, source_target_pairs={{0,24},{4,28},{8,16},{12,20},{16,8},{20,12},{24,0},{28,4},{1,25},{... | collective-permute-start | bytes 1966088 | tf_op jit(solution)/shard_map/ppermute | solution.py:846
  12.4 31.7 %collective-permute-start.2 = (bf16[160,2048]{1,0:T(8,128)(2,1)S(1)}, bf16[160,2048]{1,0:T(8,128)(2,1)}, u32[]{:S(2)}, u32[]{:S(2)}) collective-permute-start(bf16[160,2048]{1,0:T(8,128)(2,1)S(1)} %constant_dynamic-update-slice_fusion.refs_0_), channel_id=1, source_target_pairs={{0,16},{4,20},{8,24},{12,28},{16,0},{20,4},{24,8},{28,12},{1,17},{... | collective-permute-start | bytes 1966088 | tf_op jit(solution)/shard_map/ppermute | solution.py:846
  13.0 31.2 %collective-permute-start.1 = (bf16[160,2048]{1,0:T(8,128)(2,1)S(1)}, bf16[160,2048]{1,0:T(8,128)(2,1)}, u32[]{:S(2)}, u32[]{:S(2)}) collective-permute-start(bf16[160,2048]{1,0:T(8,128)(2,1)S(1)} %constant_dynamic-update-slice_fusion.refs_0_), channel_id=1, source_target_pairs={{0,8},{4,12},{8,0},{12,4},{16,24},{20,28},{24,16},{28,20},{1,9},{5... | collective-permute-start | bytes 1966088 | tf_op jit(solution)/shard_map/ppermute | solution.py:846
  13.5 30.7 %collective-permute-start = (bf16[128,2048]{1,0:T(8,128)(2,1)S(1)}, bf16[128,2048]{1,0:T(8,128)(2,1)S(1)}, u32[]{:S(2)}, u32[]{:S(2)}) collective-permute-start(bf16[128,2048]{1,0:T(8,128)(2,1)S(1)} %copy-done.4), channel_id=1, source_target_pairs={{0,1},{1,2},{2,3},{3,0},{4,5},{5,6},{6,7},{7,4},{8,9},{9,10},{10,1... | collective-permute-start | bytes 1572872 | tf_op jit(solution)/shard_map/ppermute | solution.py:851
  52.1 38.4 %all-to-all-start.1 = ((bf16[4,272,1024]{2,1,0:T(8,128)(2,1)}), bf16[4,272,1024]{2,1,0:T(8,128)(2,1)S(1)}, u32[]{:S(2)}, u32[]{:S(2)}) async-start(bf16[4,272,1024]{2,1,0:T(8,128)(2,1)} %broadcast_in_dim.48), calls=%async_computation.1 | async-start | bytes 4456448 | tf_op jit(solution)/shard_map/all_to_all | solution.py:863
  55.9 34.7 %collective-permute-start.4 = (bf16[128,2048]{1,0:T(8,128)(2,1)S(1)}, bf16[128,2048]{1,0:T(8,128)(2,1)}, u32[]{:S(2)}, u32[]{:S(2)}) collective-permute-start(bf16[128,2048]{1,0:T(8,128)(2,1)S(1)} %copy-done.4), channel_id=1, source_target_pairs={{0,2},{1,3},{2,0},{3,1},{4,6},{5,7},{6,4},{7,5},{8,10},{9,11},{10,... | collective-permute-start | bytes 1572872 | tf_op jit(solution)/shard_map/ppermute | solution.py:851
  92.6 30.1 %all-to-all-start.2 = ((bf16[4,256,1024]{2,1,0:T(8,128)(2,1)}), bf16[4,256,1024]{2,1,0:T(8,128)(2,1)}, u32[]{:S(2)}, u32[]{:S(2)}) async-start(bf16[4,256,1024]{2,1,0:T(8,128)(2,1)} %broadcast_in_dim.49), calls=%async_computation.2 | async-start | bytes 4194304 | tf_op jit(solution)/shard_map/all_to_all | solution.py:863
  97.4 16.6 %collective-permute-start.9 = (bf16[160,2048]{1,0:T(8,128)(2,1)}, bf16[160,2048]{1,0:T(8,128)(2,1)S(1)}, u32[]{:S(2)}, u32[]{:S(2)}) collective-permute-start(bf16[160,2048]{1,0:T(8,128)(2,1)} %copy-done.10), channel_id=1, source_target_pairs={{0,4},{4,0},{8,12},{12,8},{16,20},{20,16},{24,28},{28,24},{1,5},{5... | collective-permute-start | bytes 1966088 | tf_op jit(solution)/shard_map/ppermute | solution.py:846
  97.7 16.4 %collective-permute-start.10 = (bf16[160,2048]{1,0:T(8,128)(2,1)}, bf16[160,2048]{1,0:T(8,128)(2,1)S(1)}, u32[]{:S(2)}, u32[]{:S(2)}) collective-permute-start(bf16[160,2048]{1,0:T(8,128)(2,1)} %collective-permute-done.1.refs_1_), channel_id=1, source_target_pairs={{0,4},{4,0},{8,12},{12,8},{16,20},{20,16},{24,28},{28,24},{1,5},{5... | collective-permute-start | bytes 1966088 | tf_op jit(solution)/shard_map/ppermute | solution.py:846
  122.7 33.9 %collective-permute-start.15 = (bf16[4,256,1024]{2,1,0:T(8,128)(2,1)}, bf16[4,256,1024]{2,1,0:T(8,128)(2,1)S(1)}, u32[]{:S(2)}, u32[]{:S(2)}) collective-permute-start(bf16[4,256,1024]{2,1,0:T(8,128)(2,1)} %all-to-all-done.2.own.refs_2_), channel_id=1, source_target_pairs={{0,4},{4,0},{8,12},{12,8},{16,20},{20,16},{24,28},{28,24},{1,5},{5... | collective-permute-start | bytes 6291464 | tf_op jit(solution)/shard_map/ppermute | solution.py:846
  134.3 22.3 %collective-permute-start.16 = (bf16[128,2048]{1,0:T(8,128)(2,1)}, bf16[128,2048]{1,0:T(8,128)(2,1)}, u32[]{:S(2)}, u32[]{:S(2)}) collective-permute-start(bf16[128,2048]{1,0:T(8,128)(2,1)} %refs_0_.1), channel_id=1, source_target_pairs={{0,3},{1,0},{2,1},{3,2},{4,7},{5,4},{6,5},{7,6},{8,11},{9,8},{10,9... | collective-permute-start | bytes 1572872 | tf_op jit(solution)/shard_map/ppermute | solution.py:851
  135.6 39.3 %collective-permute-start.17 = (bf16[128,2048]{1,0:T(8,128)(2,1)}, bf16[128,2048]{1,0:T(8,128)(2,1)}, u32[]{:S(2)}, u32[]{:S(2)}) collective-permute-start(bf16[128,2048]{1,0:T(8,128)(2,1)} %refs_0_.1), channel_id=1, source_target_pairs={{0,2},{1,3},{2,0},{3,1},{4,6},{5,7},{6,4},{7,5},{8,10},{9,11},{10,... | collective-permute-start | bytes 1572872 | tf_op jit(solution)/shard_map/ppermute | solution.py:851
  174.8 17.7 %collective-permute-start.18 = (bf16[128,2048]{1,0:T(8,128)(2,1)}, bf16[128,2048]{1,0:T(8,128)(2,1)S(1)}, u32[]{:S(2)}, u32[]{:S(2)}) collective-permute-start(bf16[128,2048]{1,0:T(8,128)(2,1)} %get-tuple-element.338), channel_id=1, source_target_pairs={{0,1},{1,2},{2,3},{3,0},{4,5},{5,6},{6,7},{7,4},{8,9},{9,10},{10,1... | collective-permute-start | bytes 1572872 | tf_op jit(solution)/shard_map/ppermute | solution.py:851
  193.4 53.7 %all-to-all-start.3 = ((bf16[8,256,1024]{2,1,0:T(8,128)(2,1)}), bf16[8,256,1024]{2,1,0:T(8,128)(2,1)}, u32[]{:S(2)}, u32[]{:S(2)}) async-start(bf16[8,256,1024]{2,1,0:T(8,128)(2,1)} %bitcast.49), calls=%async_computation.3 | async-start | bytes 8388608 | tf_op jit(solution)/shard_map/all_to_all | solution.py:1186
  198.0 38.8 %collective-permute-start.19 = (bf16[128,2048]{1,0:T(8,128)(2,1)S(1)}, bf16[128,2048]{1,0:T(8,128)(2,1)S(1)}, u32[]{:S(2)}, u32[]{:S(2)}) collective-permute-start(bf16[128,2048]{1,0:T(8,128)(2,1)S(1)} %copy-done.48), channel_id=1, source_target_pairs={{0,2},{1,3},{2,0},{3,1},{4,6},{5,7},{6,4},{7,5},{8,10},{9,11},{10,... | collective-permute-start | bytes 1572872 | tf_op jit(solution)/shard_map/ppermute | solution.py:851
  200.2 36.5 %collective-permute-start.20 = (bf16[128,2048]{1,0:T(8,128)(2,1)S(1)}, bf16[128,2048]{1,0:T(8,128)(2,1)S(1)}, u32[]{:S(2)}, u32[]{:S(2)}) collective-permute-start(bf16[128,2048]{1,0:T(8,128)(2,1)S(1)} %copy-done.47), channel_id=1, source_target_pairs={{0,3},{1,0},{2,1},{3,2},{4,7},{5,4},{6,5},{7,6},{8,11},{9,8},{10,9... | collective-permute-start | bytes 1572872 | tf_op jit(solution)/shard_map/ppermute | solution.py:851
  256.5 23.6 %all-to-all-start.4 = ((bf16[4,64,1024]{2,1,0:T(8,128)(2,1)}), bf16[4,64,1024]{2,1,0:T(8,128)(2,1)S(1)}, u32[]{:S(2)}, u32[]{:S(2)}) async-start(bf16[4,64,1024]{2,1,0:T(8,128)(2,1)} %bitcast.29), calls=%async_computation.4 | async-start | bytes 1048576 | tf_op jit(solution)/shard_map/all_to_all | solution.py:859
  260.0 20.1 %collective-permute-start.24 = (bf16[256,1024]{1,0:T(8,128)(2,1)}, bf16[256,1024]{1,0:T(8,128)(2,1)S(1)}, u32[]{:S(2)}, u32[]{:S(2)}) collective-permute-start(bf16[256,1024]{1,0:T(8,128)(2,1)} %get-tuple-element.388), channel_id=1, source_target_pairs={{0,8},{4,12},{8,0},{12,4},{16,24},{20,28},{24,16},{28,20},{1,9},{5... | collective-permute-start | bytes 1572872 | tf_op jit(solution)/shard_map/ppermute | solution.py:846
  260.5 19.6 %collective-permute-start.25 = (bf16[256,1024]{1,0:T(8,128)(2,1)}, bf16[256,1024]{1,0:T(8,128)(2,1)S(1)}, u32[]{:S(2)}, u32[]{:S(2)}) collective-permute-start(bf16[256,1024]{1,0:T(8,128)(2,1)} %get-tuple-element.389), channel_id=1, source_target_pairs={{0,16},{4,20},{8,24},{12,28},{16,0},{20,4},{24,8},{28,12},{1,17},{... | collective-permute-start | bytes 1572872 | tf_op jit(solution)/shard_map/ppermute | solution.py:846
  281.1 58.7 %all-to-all-start.5 = ((bf16[4,128,2048]{2,1,0:T(8,128)(2,1)}), bf16[4,128,2048]{2,1,0:T(8,128)(2,1)S(1)}, u32[]{:S(2)}, u32[]{:S(2)}) async-start(bf16[4,128,2048]{2,1,0:T(8,128)(2,1)} %bitcast.51), calls=%async_computation.5 | async-start | bytes 4194304 | tf_op jit(solution)/shard_map/all_to_all | solution.py:859
  295.5 17.2 %collective-permute-start.28 = (bf16[304,1024]{1,0:T(8,128)(2,1)}, bf16[304,1024]{1,0:T(8,128)(2,1)}, u32[]{:S(2)}, u32[]{:S(2)}) collective-permute-start(bf16[304,1024]{1,0:T(8,128)(2,1)} %get-tuple-element.436), channel_id=1, source_target_pairs={{0,8},{4,12},{8,0},{12,4},{16,24},{20,28},{24,16},{28,20},{1,9},{5... | collective-permute-start | bytes 1867784 | tf_op jit(solution)/shard_map/ppermute | solution.py:846
  296.7 29.7 %collective-permute-start.29 = (bf16[304,1024]{1,0:T(8,128)(2,1)}, bf16[304,1024]{1,0:T(8,128)(2,1)}, u32[]{:S(2)}, u32[]{:S(2)}) collective-permute-start(bf16[304,1024]{1,0:T(8,128)(2,1)} %get-tuple-element.437), channel_id=1, source_target_pairs={{0,16},{4,20},{8,24},{12,28},{16,0},{20,4},{24,8},{28,12},{1,17},{... | collective-permute-start | bytes 1867784 | tf_op jit(solution)/shard_map/ppermute | solution.py:846
  298.2 28.2 %collective-permute-start.30 = (bf16[304,1024]{1,0:T(8,128)(2,1)}, bf16[304,1024]{1,0:T(8,128)(2,1)}, u32[]{:S(2)}, u32[]{:S(2)}) collective-permute-start(bf16[304,1024]{1,0:T(8,128)(2,1)} %get-tuple-element.438), channel_id=1, source_target_pairs={{0,24},{4,28},{8,16},{12,20},{16,8},{20,12},{24,0},{28,4},{1,25},{... | collective-permute-start | bytes 1867784 | tf_op jit(solution)/shard_map/ppermute | solution.py:846
  (68 other events, 597.0 us)

commit v6 on v5

--- a/solution.py
+++ b/solution.py
@@ -660,6 +660,10 @@
     )(info, *cots, o_nat, gate, y, act, small, valid, normed)
 
 
+def combined(slots, owned):
+    return together(slots) and owned % LANES == 0
+
+
 def together(slots):
     return slots <= 1024
 
@@ -673,6 +677,7 @@
     products_far, refs = (refs[:2], refs[2:]) if together(slots) else ((), refs)
     gi_low, refs = (None, refs) if together(slots) else (refs[0], refs[1:])
     kept, sent, x_grad, vec, ext, gi, tail, grad_normed, column, gp, arrived, left, w_nat, gate_nat, *refs = refs
+    below = combined(slots, width // n_dp)
     halves = ()
     copies = block_copies(w_nat, inner_own, inner_other, info[0], arrived, 0)
     copies += block_copies(gate_nat, gate_own, gate_other, info[0], arrived, n_dp)
@@ -785,7 +790,14 @@
             for rows, source in ((at.dt_w, dtw), (at.x_t, x_grad), (at.a_t, rate_grad), (at.rest, vec)):
                 column[rows, :] = source[:, cols]
             for b in range(width // owned):
-                ref[q, :, b * owned : (b + 1) * owned] = column[b * fold : (b + 1) * fold, :].astype(ref.dtype)
+                cols = slice(b * owned, (b + 1) * owned)
+                value = column[b * fold : (b + 1) * fold, :].astype(ref.dtype)
+                if ref is sent and below:
+                    sent[q * fold : (q + 1) * fold, cols] = value
+                else:
+                    ref[q, :, cols] = value
+    if below:
+        leave(sent, products_far[1].at[pl.ds(model // 2, sent.shape[0])])
     for copy in leaving:
         copy.wait()
 
@@ -796,23 +808,25 @@
     held, model = slots // n_line, 2 * normed_k.shape[1]
     cb = column_block(width, slots)
     owned = width // n_dp
-    tiles, one = owned % LANES == 0, together(slots)
+    one, below = together(slots), combined(slots, owned)
+    tiles = below
     vmem, away = pl.BlockSpec(memory_space=pltpu.VMEM), pl.BlockSpec(memory_space=pl.ANY)
     fold = at.fold(n_dp)
     shape = (n_dp // 2, fold, width) if tiles else (1, at.rows, width)
     later = [*inner_blocks, *gate_blocks] + ([normed_k, normed_s] if one else [])
     low, half = jax.ShapeDtypeStruct((slots, width), BF), jax.ShapeDtypeStruct((model // 2, width), BF)
+    more = n_dp // 2 * fold if below else 0
+    longer = jax.ShapeDtypeStruct((model // 2 + more, width), BF)
     outs = pl.pallas_call(
         functools.partial(conv_back_kernel, n_line, n_dp, at),
         in_specs=[pl.BlockSpec(memory_space=pltpu.SMEM)] + [vmem] * 12 + [away] * len(later),
-        out_specs=[away] + ([away] * 2 if one else [vmem]) + [vmem] * 2,
+        out_specs=[away] + ([away] * 2 if one else [vmem]) + [vmem] * (1 if below else 2),
         out_shape=[jax.ShapeDtypeStruct((slots, model), BF)]
-        + ([half] * 2 if one else [low])
+        + ([half, longer] if one else [low])
+        + [jax.ShapeDtypeStruct(shape, F32)]
+        + ([] if below else [jax.ShapeDtypeStruct(shape if tiles else (SUB, LANES), BF if tiles else F32)]),
+        scratch_shapes=([pltpu.VMEM((more, width), BF)] if below else [])
         + [
-            jax.ShapeDtypeStruct(shape, F32),
-            jax.ShapeDtypeStruct(shape if tiles else (SUB, LANES), BF if tiles else F32),
-        ],
-        scratch_shapes=[
             pltpu.VMEM((at.x_t.stop - at.x_t.start, width), F32),
             pltpu.VMEM((16, width), F32),
             pltpu.VMEM((SUB + held, cb), F32),
@@ -822,7 +836,7 @@
             pltpu.VMEM((n_dp * fold, owned), F32),
             pltpu.VMEM(gp_got.shape, BF),
             pltpu.SemaphoreType.DMA((2 * n_dp + 2,)),
-            pltpu.SemaphoreType.DMA((9,)),
+            pltpu.SemaphoreType.DMA((10,)),
         ]
         + [pltpu.VMEM((model, width), BF)] * 2
         + ([pltpu.VMEM((slots, width), BF)] + [pltpu.VMEM((slots, model // 2), BF)] * 2 if one else [])
@@ -831,14 +845,14 @@
         cost_estimate=small_cost(1 << 20),
         name="conv_back",
     )(info, gp_part, gp_got, gu, small, act, conv_out, inner, allowed, dtw, rate_grad, scan_vec, grad_gate, *later)
-    grad_normed, *products, kept, sent = outs
+    grad_normed, *products, kept, sent = (*outs, None) if below else outs
     if not one:
         products = outer_product(normed_k, normed_s, products[0])
     if not tiles:
         kept, sent = [
             part.reshape(at.rows, n_dp // 2, owned).transpose(1, 0, 2) for part in cores(kept[0], 1)
         ]
-    return grad_normed, *products, kept, sent.astype(BF)
+    return grad_normed, *products, kept, sent if below else sent.astype(BF)
 
 
 def swap(value, axis, mask):
@@ -912,28 +926,29 @@
     return [part.reshape(flat) for part in found]
 
 
-def add_core_kernel(chip, kept, got, small_kept, small_got, *outs):
-    rows = kept.shape[0] // len(outs)
+def add_core_kernel(chip, kept, got, small_kept, *outs):
+    rows, fold = kept.shape[0] // len(outs), small_kept.shape[1]
     for u, out in enumerate(outs):
         q = jnp.bitwise_xor(chip[0], u)
         at = pl.ds(pl.multiple_of(q * rows, rows), rows)
         out[0:rows, :] = (kept[at, :].astype(F32) + got[at, :].astype(F32)).astype(BF)
-        out[rows:, :] = (small_kept[q] + small_got[q].astype(F32)).astype(BF)
-
-
-def add_core(kept, got, small_kept, small_got):
+        below = pl.ds(pl.multiple_of(kept.shape[0] + q * fold, fold), fold)
+        out[rows:, :] = (small_kept[q] + got[below, :].astype(F32)).astype(BF)
+
+
+def add_core(kept, got, small_kept):
     chips, width = lax.axis_size("dp") // 2, kept.shape[1]
     rows = kept.shape[0] // chips + small_kept.shape[1]
     vmem = pl.BlockSpec(memory_space=pltpu.VMEM)
     return pl.pallas_call(
         add_core_kernel,
-        in_specs=[pl.BlockSpec(memory_space=pltpu.SMEM)] + [vmem] * 4,
+        in_specs=[pl.BlockSpec(memory_space=pltpu.SMEM)] + [vmem] * 3,
         out_specs=[vmem] * chips,
         out_shape=[jax.ShapeDtypeStruct((rows, width), BF)] * chips,
         compiler_params=pltpu.CompilerParams(vmem_limit_bytes=61 << 20),
         cost_estimate=small_cost(1 << 10),
         name="add_core",
-    )(lax.div(lax.axis_index("dp"), 2)[None], kept, got, small_kept, small_got)
+    )(lax.div(lax.axis_index("dp"), 2)[None], kept, got, small_kept)
 
 
 def add_chips_near(blocks):
@@ -1213,16 +1228,19 @@
     )
 
     grad_normed = to_line(grad_normed.reshape(n_line, held_slots, model))
-    folded = owned % LANES == 0
-    inner_got, small_got = swap(inner_sent, "dp", 1), swap(small_sent, "dp", 1)
+    folded = combined(slots, owned)
+    out_sum.add()
+    out_sum.second()
+    inner_got, small_got = swap(inner_sent, "dp", 1), None
     if folded:
-        blocks = add_core(inner_kept, inner_got, small_kept, small_got)
+        blocks = add_core(inner_kept, inner_got, small_kept)
     else:
+        small_got = swap(small_sent, "dp", 1)
         blocks = [sent_far(inner_kept, inner_got, u) for u in range(n_dp // 2)]
     blocks, small_kept, small_got, branches = out_sum.fenced(blocks, small_kept, small_got, branches)
 
     blocks = [swap(block, "dp", 2 * u) if u else block for u, block in enumerate(blocks)]
-    out_sum.add()
+    out_weight_grad = out_sum.total()
     if folded:
         inner_sent, small_sum = sum_chips(place, blocks, n_line, in_rows, at, owned)
     else:
@@ -1235,12 +1253,10 @@
         small_sum = [small_sum[at.dt_w], small_sum[at.x_t], small_sum[at.a_t], tail_g[:taps]] + [
             tail_g[taps + i : taps + i + 1] for i in range(3)
         ]
-    inner_sent, small_sum, branches = out_sum.fenced(inner_sent, small_sum, branches)
+    inner_sent, small_sum, branches, out_weight_grad = fence(inner_sent, small_sum, branches, out_weight_grad)
 
     inner_got = [shift(block, "fsdp", s) if s else block for s, block in enumerate(inner_sent)]
-    out_sum.second()
     grad_normed = jnp.sum(grad_normed.astype(F32), axis=0)
-    out_weight_grad = out_sum.total()
     dt_g, x_g, a_g, conv_g, *vectors = small_sum
     conv_b_g, dt_b_g, skip_g = [value[0] for value in vectors]
     small_out = [conv_g, conv_b_g, x_g.T, dt_g, dt_b_g, a_g.T, skip_g]
@@ -1252,7 +1268,7 @@
     token_grad = own_cot.astype(F32) + own_scale * (
         grad_unit - unit * jnp.mean(grad_unit * unit, axis=1, keepdims=True)
     )
-    inner_got, token_grad, output, out_weight_grad = fence(inner_got, token_grad, output, out_weight_grad)
+    inner_got, token_grad, output = fence(inner_got, token_grad, output)
     in_weight_grad, gain_grad = join_columns(place, inner_got, gate_got, in_weight, gain, n_dp)
     return output, token_grad, gain_grad, in_weight_grad, *small_out, out_weight_grad
 

time: 349 us -> 349 us (level)
    ppermute x24 -> x23, waiting for transfers between devices: 47.6 us -> 45.2 us  [swap(): return lax.ppermute(value, axis, [(i, i ^ mask) for i in range(count)])]
    ppermute x24 -> x23, starting transfers between devices: 13.8 us -> 14 us  [swap(): return lax.ppermute(value, axis, [(i, i ^ mask) for i in range(count)])]
  transfers between devices with their start and end apart: 42 -> 41, of which waited for: 14 -> 15; matrix products, arithmetic and copies ran while one was open for 7% -> 8% of each run, Pallas kernels for 39% -> 39%
where the time goes in v6:
time: 349 us; the launch traced here: 348 us
  Pallas kernels  143 us (41%)
  waiting for transfers between devices  107 us (31%)
  starting transfers between devices  58.4 us (17%)
  other arithmetic  19.1 us (5%)
  local copies, waits for them, and re-layouts  17.6 us (5%)
    ppermute x12, waiting for transfers between devices, shift(): lax.ppermute(value, axis, [(i, (i + steps) % count) for i in range(count)])  52.5 us
    ppermute x23, waiting for transfers between devices, swap(): return lax.ppermute(value, axis, [(i, i ^ mask) for i in range(count)])  45.2 us
    pallas_call x1, Pallas kernels, scan_backward(): pl.pallas_call(functools.partial(backward_kernel, at), grid=(nb,), in_spe...  34.4 us
    pallas_call x1, Pallas kernels, conv_back(): pl.pallas_call(functools.partial(conv_back_kernel, n_line, n_dp, at), in_...  18.7 us
    pallas_call x1, Pallas kernels, scan_forward(): pl.pallas_call(functools.partial(forward_kernel, at), grid=(nb,), in_spec...  18.3 us
    pallas_call x1, Pallas kernels, gate_block(): pl.pallas_call(functools.partial(gate_kernel, n_line, n_dp, at), in_specs...  16.9 us
    ppermute x12, starting transfers between devices, shift(): lax.ppermute(value, axis, [(i, (i + steps) % count) for i in range(count)])  16.6 us
    pallas_call x1, Pallas kernels, gate_back(): pl.pallas_call(functools.partial(gate_back_kernel, n_line, at), in_specs=...  16.1 us
  transfers between devices with their start and end apart: 41, of which 15 were waited for; matrix products, arithmetic and copies ran while one was open for 8% of the time, Pallas kernels for 39%

profile of v6, /device:TPU:0, one launch (start us, length us, event | category | flops | bytes accessed | tf_op | source)
XLA Modules:
  0.0 347.9 jit_solution(5997191023320579400)
XLA Ops:
  3.2 6.4 %all-to-all-start = ((bf16[4,144,1024]{2,1,0:T(8,128)(2,1)}), bf16[4,144,1024]{2,1,0:T(8,128)(2,1)S(1)}, u32[]{:S(2)}, u32[]{:S(2)}) async-start(bf16[4,144,1024]{2,1,0:T(8,128)(2,1)} %split_columns.1), calls=%async_computation | async-start | bytes 2359296 | tf_op jit(solution)/shard_map/all_to_all | solution.py:873
  21.6 22.6 %collective-permute-done.refs_1_ = bf16[128,2048]{1,0:T(8,128)(2,1)S(1)} collective-permute-done((bf16[128,2048]{1,0:T(8,128)(2,1)S(1)}, bf16[128,2048]{1,0:T(8,128)(2,1)S(1)}, u32[]{:S(2)}, u32[]{:S(2)}) %collective-permute-start) | collective-permute-done | bytes 524320 | tf_op jit(solution)/shard_map/ppermute | solution.py:865
  44.2 5.3 %all-to-all-done = bf16[4,144,1024]{2,1,0:T(8,128)(2,1)S(1)} async-done(((bf16[4,144,1024]{2,1,0:T(8,128)(2,1)}), bf16[4,144,1024]{2,1,0:T(8,128)(2,1)S(1)}, u32[]{:S(2)}, u32[]{:S(2)}) %all-to-all-start) | async-done | bytes 1179680 | tf_op jit(solution)/shard_map/all_to_all | solution.py:873
  52.1 3.7 %all-to-all-start.1 = ((bf16[4,272,1024]{2,1,0:T(8,128)(2,1)}), bf16[4,272,1024]{2,1,0:T(8,128)(2,1)S(1)}, u32[]{:S(2)}, u32[]{:S(2)}) async-start(bf16[4,272,1024]{2,1,0:T(8,128)(2,1)} %broadcast_in_dim.51), calls=%async_computation.1 | async-start | bytes 4456448 | tf_op jit(solution)/shard_map/all_to_all | solution.py:877
  64.4 5.7 %collective-permute-done.5.refs_3_ = bf16[128,2048]{1,0:T(8,128)(2,1)} collective-permute-done((bf16[128,2048]{1,0:T(8,128)(2,1)S(1)}, bf16[128,2048]{1,0:T(8,128)(2,1)}, u32[]{:S(2)}, u32[]{:S(2)}) %collective-permute-start.5) | collective-permute-done | bytes 524320 | tf_op jit(solution)/shard_map/ppermute | solution.py:865
  70.1 20.5 %collective-permute-done.4.refs_2_ = bf16[128,2048]{1,0:T(8,128)(2,1)} collective-permute-done((bf16[128,2048]{1,0:T(8,128)(2,1)S(1)}, bf16[128,2048]{1,0:T(8,128)(2,1)}, u32[]{:S(2)}, u32[]{:S(2)}) %collective-permute-start.4) | collective-permute-done | bytes 524320 | tf_op jit(solution)/shard_map/ppermute | solution.py:865
  92.6 4.5 %all-to-all-start.2 = ((bf16[4,256,1024]{2,1,0:T(8,128)(2,1)}), bf16[4,256,1024]{2,1,0:T(8,128)(2,1)}, u32[]{:S(2)}, u32[]{:S(2)}) async-start(bf16[4,256,1024]{2,1,0:T(8,128)(2,1)} %broadcast_in_dim.52), calls=%async_computation.2 | async-start | bytes 4194304 | tf_op jit(solution)/shard_map/all_to_all | solution.py:877
  98.7 13.2 %project.1 = (f32[1,2048]{1,0:T(1,128)}, bf16[512,2048]{1,0:T(8,128)(2,1)}, bf16[512,1024]{1,0:T(8,128)(2,1)}, bf16[512,1024]{1,0:T(8,128)(2,1)}, bf16[512,1024]...) custom-call(s32[6]{0:T(128)} %pad_add_fusion.info, ...), custom_call_target="tpu_custom_call" | custom-call | flops 1048576 | bytes 65536 | tf_op jit(solution)/shard_map/project/pallas_call | solution.py:547
  114.1 5.7 %collective-permute-done.11 = bf16[640,128]{1,0:T(8,128)(2,1)S(1)} collective-permute-done((bf16[640,128]{1,0:T(8,128)(2,1)}, bf16[640,128]{1,0:T(8,128)(2,1)S(1)}, u32[]{:S(2)}, u32[]{:S(2)}) %collective-permute-start.11) | collective-permute-done | bytes 163872 | tf_op jit(solution)/shard_map/ppermute | solution.py:860
  123.4 10.9 %collective-permute-done.12 = bf16[640,128]{1,0:T(8,128)(2,1)S(1)} collective-permute-done((bf16[640,128]{1,0:T(8,128)(2,1)S(1)}, bf16[640,128]{1,0:T(8,128)(2,1)S(1)}, u32[]{:S(2)}, u32[]{:S(2)}) %collective-permute-start.12) | collective-permute-done | bytes 163872 | tf_op jit(solution)/shard_map/ppermute | solution.py:860
  138.3 18.3 %scan_forward.1 = (f32[512,1024]{1,0:T(8,128)}, f32[8,16,520,128]{3,2,1,0:T(8,128)}) custom-call(f32[512,33]{1,0:T(8,128)} %pad_maximum_fusion.1.bc, bf16[512,128]{1,0:T(8,128)(2,1)} %slice.105.rank, bf16[320,1024]{1,0:T(8,128)(2,1)} %copy-done.2, bf16[512,1024]{1,0:T(8,128)(2,1)} %get-tuple-element.301.act.refs_7_, f32[512,1]{1,0:T(8,128)} %copy-done.8, ...), custom_call_target="tpu_custom_call" | custom-call | flops 1048576 | bytes 65536 | tf_op jit(solution)/shard_map/scan_forward/pallas_call | solution.py:103
  157.9 16.9 %gate_block.1 = (bf16[128,2048]{1,0:T(8,128)(2,1)}, bf16[128,2048]{1,0:T(8,128)(2,1)}, bf16[128,2048]{1,0:T(8,128)(2,1)}, bf16[128,2048]{1,0:T(8,128)(2,1)}, f32...) custom-call(s32[6]{0:T(128)} %pad_add_fusion.info, ...), custom_call_target="tpu_custom_call" | custom-call | flops 1048576 | bytes 65536 | tf_op jit(solution)/shard_map/gate_block/pallas_call | solution.py:607
  176.4 16.1 %gate_back.1 = (f32[512,1024]{1,0:T(8,128)}, bf16[512,1024]{1,0:T(8,128)(2,1)}, bf16[512,2048]{1,0:T(8,128)(2,1)}, bf16[2048,1024]{1,0:T(8,128)(2,1)}) custom-call(s32[6]{0:T(128)} %pad_add_fusion.info, bf16[128,2048]{1,0:T(8,128)(2,1)} %refs_0_.1, bf16[128,2048]{1,0:T(8,128)(2,1)} %copy-done.24, bf16[128,2048]{1,0:T(8,128)(2,1)} %collective-permute-done.17.refs_2_, ...), custom_call_target="tpu_custom_call" | custom-call | flops 1048576 | bytes 65536 | tf_op jit(solution)/shard_map/gate_back/pallas_call | solution.py:652
  193.3 4.6 %all-to-all-start.3 = ((bf16[8,256,1024]{2,1,0:T(8,128)(2,1)}), bf16[8,256,1024]{2,1,0:T(8,128)(2,1)}, u32[]{:S(2)}, u32[]{:S(2)}) async-start(bf16[8,256,1024]{2,1,0:T(8,128)(2,1)} %bitcast.49), calls=%async_computation.3 | async-start | bytes 8388608 | tf_op jit(solution)/shard_map/all_to_all | solution.py:1201
  202.2 34.4 %scan_backward.1 = (bf16[640,128]{1,0:T(8,128)(2,1)}, bf16[512,1024]{1,0:T(8,128)(2,1)}, f32[128,1024]{1,0:T(8,128)}, f32[2,1024]{1,0:T(2,128)}, f32[16,1024]{1,0:T(8,128)}) custom-call(f32[512,33]{1,0:T(8,128)} %pad_maximum_fusion.1.bc, bf16[512,128]{1,0:T(8,128)(2,1)} %slice.105.rank, bf16[320,1024]{1,0:T(8,128)(2,1)} %copy-done.2, ...), custom_call_target="tpu_custom_call" | custom-call | flops 1048576 | bytes 65536 | tf_op jit(solution)/shard_map/scan_backward/pallas_call | solution.py:277
  236.7 6.2 %outer_product.1 = (bf16[512,2048]{1,0:T(8,128)(2,1)}, bf16[512,2048]{1,0:T(8,128)(2,1)}) custom-call(bf16[512,512]{1,0:T(8,128)(2,1)} %get-tuple-element.357.kept, bf16[512,512]{1,0:T(8,128)(2,1)} %get-tuple-element.358.sent, bf16[512,2048]{1,0:T(8,128)(2,1)} %get-tuple-element.359.right), custom_call_target="tpu_custom_call" | custom-call | flops 1048576 | bytes 65536 | tf_op jit(solution)/shard_map/outer_product/pallas_call | solution.py:456
  247.0 4.0 %reduce_sum.39 = bf16[256,1024]{1,0:T(8,128)(2,1)} reduce(bf16[8,256,1024]{2,1,0:T(8,128)(2,1)} %all-to-all-done.3, bf16[]{:T(256)} %constant.46.clone.1), dimensions={0}, to_apply=%region_1.2 | reduce | flops 1835008 | bytes 4718594 | tf_op jit(solution)/shard_map/reduce_sum | solution.py:1213
  252.3 4.0 %chip_halves.1 = (bf16[256,1024]{1,0:T(8,128)(2,1)}, bf16[256,1024]{1,0:T(8,128)(2,1)}, bf16[128,1024]{1,0:T(8,128)(2,1)}, bf16[128,1024]{1,0:T(8,128)(2,1)}, bf...) custom-call(s32[1]{0:T(128)} %bitcast.27.chip, bf16[512,2048]{1,0:T(8,128)(2,1)} %get-tuple-element.367.kept, ...), custom_call_target="tpu_custom_call" | custom-call | flops 1024 | bytes 65536 | tf_op jit(solution)/shard_map/chip_halves/pallas_call | solution.py:1031
  261.2 18.7 %conv_back.1 = (bf16[512,2048]{1,0:T(8,128)(2,1)}, bf16[1024,1024]{1,0:T(8,128)(2,1)}, bf16[1216,1024]{1,0:T(8,128)(2,1)}, f32[4,48,1024]{2,1,0:T(8,128)}) custom-call(s32[6]{0:T(128)} %pad_add_fusion.info, f32[640,128]{1,0:T(8,128)} %copy-done.9, bf16[640,128]{1,0:T(8,128)(2,1)} %copy-done.33, bf16[512,1024]{1,0:T(8,128)(2,1)} %get-tuple-element.384.gu, ...), custom_call_target="tpu_custom_call" | custom-call | flops 1048576 | bytes 65536 | tf_op jit(solution)/shard_map/conv_back/pallas_call | solution.py:820
  280.8 5.1 %all-to-all-start.5 = ((bf16[4,128,2048]{2,1,0:T(8,128)(2,1)}), bf16[4,128,2048]{2,1,0:T(8,128)(2,1)S(1)}, u32[]{:S(2)}, u32[]{:S(2)}) async-start(bf16[4,128,2048]{2,1,0:T(8,128)(2,1)} %bitcast.51), calls=%async_computation.5 | async-start | bytes 4194304 | tf_op jit(solution)/shard_map/all_to_all | solution.py:873
  292.0 4.2 %add_core.1 = (bf16[304,1024]{1,0:T(8,128)(2,1)}, bf16[304,1024]{1,0:T(8,128)(2,1)}, bf16[304,1024]{1,0:T(8,128)(2,1)}, bf16[304,1024]{1,0:T(8,128)(2,1)}) custom-call(s32[1]{0:T(128)} %bitcast.27.chip, bf16[1024,1024]{1,0:T(8,128)(2,1)} %get-tuple-element.408.kept, bf16[1216,1024]{1,0:T(8,128)(2,1)} %collective-permute-done.28.got, ...), custom_call_target="tpu_custom_call" | custom-call | flops 1024 | bytes 65536 | tf_op jit(solution)/shard_map/add_core/pallas_call | solution.py:943
  305.3 11.1 %collective-permute-done.29.refs_1_ = bf16[304,1024]{1,0:T(8,128)(2,1)} collective-permute-done((bf16[304,1024]{1,0:T(8,128)(2,1)}, bf16[304,1024]{1,0:T(8,128)(2,1)}, u32[]{:S(2)}, u32[]{:S(2)}) %collective-permute-start.29) | collective-permute-done | bytes 622624 | tf_op jit(solution)/shard_map/ppermute | solution.py:860
  316.3 13.0 %collective-permute-done.30.refs_2_ = bf16[304,1024]{1,0:T(8,128)(2,1)} collective-permute-done((bf16[304,1024]{1,0:T(8,128)(2,1)}, bf16[304,1024]{1,0:T(8,128)(2,1)}, u32[]{:S(2)}, u32[]{:S(2)}) %collective-permute-start.30) | collective-permute-done | bytes 622624 | tf_op jit(solution)/shard_map/ppermute | solution.py:860
  338.7 3.6 %fusion.8 = (bf16[128,2048]{1,0:T(8,128)(2,1)}, f32[128,2048]{1,0:T(8,128)}) fusion(bf16[128,2048]{1,0:T(8,128)(2,1)S(1)} %copy-done.5, bf16[128,2048]{1,0:T(8,128)(2,1)} %copy-done.23, bf16[128,2048]{1,0:T(8,128)(2,1)} %copy-done.21, bf16[128,2048]{1,0:T(8,128)(2,1)} %copy-done.20, bf16[128,2048]{1,0:T(8,128)(2,1)} %get-tuple-element.449, ...), kind=kLoop, calls=%fused_computation.13 | loop fusion | flops 4718592 | bytes 5776896 | tf_op jit(solution)/shard_map/convert_element_type | solution.py:1264
  (231 shorter events, 86.7 us)
Async XLA Ops:
  3.2 46.2 %all-to-all-start = ((bf16[4,144,1024]{2,1,0:T(8,128)(2,1)}), bf16[4,144,1024]{2,1,0:T(8,128)(2,1)S(1)}, u32[]{:S(2)}, u32[]{:S(2)}) async-start(bf16[4,144,1024]{2,1,0:T(8,128)(2,1)} %split_columns.1), calls=%async_computation | async-start | bytes 2359296 | tf_op jit(solution)/shard_map/all_to_all | solution.py:873
  9.9 34.3 %collective-permute-start.3 = (bf16[160,2048]{1,0:T(8,128)(2,1)S(1)}, bf16[160,2048]{1,0:T(8,128)(2,1)}, u32[]{:S(2)}, u32[]{:S(2)}) collective-permute-start(bf16[160,2048]{1,0:T(8,128)(2,1)S(1)} %constant_dynamic-update-slice_fusion.refs_0_), channel_id=1, source_target_pairs={{0,24},{4,28},{8,16},{12,20},{16,8},{20,12},{24,0},{28,4},{1,25},{... | collective-permute-start | bytes 1966088 | tf_op jit(solution)/shard_map/ppermute | solution.py:860
  12.4 31.7 %collective-permute-start.2 = (bf16[160,2048]{1,0:T(8,128)(2,1)S(1)}, bf16[160,2048]{1,0:T(8,128)(2,1)}, u32[]{:S(2)}, u32[]{:S(2)}) collective-permute-start(bf16[160,2048]{1,0:T(8,128)(2,1)S(1)} %constant_dynamic-update-slice_fusion.refs_0_), channel_id=1, source_target_pairs={{0,16},{4,20},{8,24},{12,28},{16,0},{20,4},{24,8},{28,12},{1,17},{... | collective-permute-start | bytes 1966088 | tf_op jit(solution)/shard_map/ppermute | solution.py:860
  13.0 31.2 %collective-permute-start.1 = (bf16[160,2048]{1,0:T(8,128)(2,1)S(1)}, bf16[160,2048]{1,0:T(8,128)(2,1)}, u32[]{:S(2)}, u32[]{:S(2)}) collective-permute-start(bf16[160,2048]{1,0:T(8,128)(2,1)S(1)} %constant_dynamic-update-slice_fusion.refs_0_), channel_id=1, source_target_pairs={{0,8},{4,12},{8,0},{12,4},{16,24},{20,28},{24,16},{28,20},{1,9},{5... | collective-permute-start | bytes 1966088 | tf_op jit(solution)/shard_map/ppermute | solution.py:860
  13.5 30.7 %collective-permute-start = (bf16[128,2048]{1,0:T(8,128)(2,1)S(1)}, bf16[128,2048]{1,0:T(8,128)(2,1)S(1)}, u32[]{:S(2)}, u32[]{:S(2)}) collective-permute-start(bf16[128,2048]{1,0:T(8,128)(2,1)S(1)} %copy-done.4), channel_id=1, source_target_pairs={{0,1},{1,2},{2,3},{3,0},{4,5},{5,6},{6,7},{7,4},{8,9},{9,10},{10,1... | collective-permute-start | bytes 1572872 | tf_op jit(solution)/shard_map/ppermute | solution.py:865
  52.1 38.4 %all-to-all-start.1 = ((bf16[4,272,1024]{2,1,0:T(8,128)(2,1)}), bf16[4,272,1024]{2,1,0:T(8,128)(2,1)S(1)}, u32[]{:S(2)}, u32[]{:S(2)}) async-start(bf16[4,272,1024]{2,1,0:T(8,128)(2,1)} %broadcast_in_dim.51), calls=%async_computation.1 | async-start | bytes 4456448 | tf_op jit(solution)/shard_map/all_to_all | solution.py:877
  55.9 34.7 %collective-permute-start.4 = (bf16[128,2048]{1,0:T(8,128)(2,1)S(1)}, bf16[128,2048]{1,0:T(8,128)(2,1)}, u32[]{:S(2)}, u32[]{:S(2)}) collective-permute-start(bf16[128,2048]{1,0:T(8,128)(2,1)S(1)} %copy-done.4), channel_id=1, source_target_pairs={{0,2},{1,3},{2,0},{3,1},{4,6},{5,7},{6,4},{7,5},{8,10},{9,11},{10,... | collective-permute-start | bytes 1572872 | tf_op jit(solution)/shard_map/ppermute | solution.py:865
  92.6 30.1 %all-to-all-start.2 = ((bf16[4,256,1024]{2,1,0:T(8,128)(2,1)}), bf16[4,256,1024]{2,1,0:T(8,128)(2,1)}, u32[]{:S(2)}, u32[]{:S(2)}) async-start(bf16[4,256,1024]{2,1,0:T(8,128)(2,1)} %broadcast_in_dim.52), calls=%async_computation.2 | async-start | bytes 4194304 | tf_op jit(solution)/shard_map/all_to_all | solution.py:877
  97.4 16.6 %collective-permute-start.9 = (bf16[160,2048]{1,0:T(8,128)(2,1)}, bf16[160,2048]{1,0:T(8,128)(2,1)S(1)}, u32[]{:S(2)}, u32[]{:S(2)}) collective-permute-start(bf16[160,2048]{1,0:T(8,128)(2,1)} %copy-done.10), channel_id=1, source_target_pairs={{0,4},{4,0},{8,12},{12,8},{16,20},{20,16},{24,28},{28,24},{1,5},{5... | collective-permute-start | bytes 1966088 | tf_op jit(solution)/shard_map/ppermute | solution.py:860
  97.7 16.4 %collective-permute-start.10 = (bf16[160,2048]{1,0:T(8,128)(2,1)}, bf16[160,2048]{1,0:T(8,128)(2,1)S(1)}, u32[]{:S(2)}, u32[]{:S(2)}) collective-permute-start(bf16[160,2048]{1,0:T(8,128)(2,1)} %collective-permute-done.1.refs_1_), channel_id=1, source_target_pairs={{0,4},{4,0},{8,12},{12,8},{16,20},{20,16},{24,28},{28,24},{1,5},{5... | collective-permute-start | bytes 1966088 | tf_op jit(solution)/shard_map/ppermute | solution.py:860
  122.7 33.9 %collective-permute-start.15 = (bf16[4,256,1024]{2,1,0:T(8,128)(2,1)}, bf16[4,256,1024]{2,1,0:T(8,128)(2,1)S(1)}, u32[]{:S(2)}, u32[]{:S(2)}) collective-permute-start(bf16[4,256,1024]{2,1,0:T(8,128)(2,1)} %all-to-all-done.2.own.refs_2_), channel_id=1, source_target_pairs={{0,4},{4,0},{8,12},{12,8},{16,20},{20,16},{24,28},{28,24},{1,5},{5... | collective-permute-start | bytes 6291464 | tf_op jit(solution)/shard_map/ppermute | solution.py:860
  134.3 22.2 %collective-permute-start.16 = (bf16[128,2048]{1,0:T(8,128)(2,1)}, bf16[128,2048]{1,0:T(8,128)(2,1)}, u32[]{:S(2)}, u32[]{:S(2)}) collective-permute-start(bf16[128,2048]{1,0:T(8,128)(2,1)} %refs_0_.1), channel_id=1, source_target_pairs={{0,3},{1,0},{2,1},{3,2},{4,7},{5,4},{6,5},{7,6},{8,11},{9,8},{10,9... | collective-permute-start | bytes 1572872 | tf_op jit(solution)/shard_map/ppermute | solution.py:865
  135.6 39.2 %collective-permute-start.17 = (bf16[128,2048]{1,0:T(8,128)(2,1)}, bf16[128,2048]{1,0:T(8,128)(2,1)}, u32[]{:S(2)}, u32[]{:S(2)}) collective-permute-start(bf16[128,2048]{1,0:T(8,128)(2,1)} %refs_0_.1), channel_id=1, source_target_pairs={{0,2},{1,3},{2,0},{3,1},{4,6},{5,7},{6,4},{7,5},{8,10},{9,11},{10,... | collective-permute-start | bytes 1572872 | tf_op jit(solution)/shard_map/ppermute | solution.py:865
  174.8 17.7 %collective-permute-start.18 = (bf16[128,2048]{1,0:T(8,128)(2,1)}, bf16[128,2048]{1,0:T(8,128)(2,1)S(1)}, u32[]{:S(2)}, u32[]{:S(2)}) collective-permute-start(bf16[128,2048]{1,0:T(8,128)(2,1)} %get-tuple-element.330), channel_id=1, source_target_pairs={{0,1},{1,2},{2,3},{3,0},{4,5},{5,6},{6,7},{7,4},{8,9},{9,10},{10,1... | collective-permute-start | bytes 1572872 | tf_op jit(solution)/shard_map/ppermute | solution.py:865
  193.3 53.7 %all-to-all-start.3 = ((bf16[8,256,1024]{2,1,0:T(8,128)(2,1)}), bf16[8,256,1024]{2,1,0:T(8,128)(2,1)}, u32[]{:S(2)}, u32[]{:S(2)}) async-start(bf16[8,256,1024]{2,1,0:T(8,128)(2,1)} %bitcast.49), calls=%async_computation.3 | async-start | bytes 8388608 | tf_op jit(solution)/shard_map/all_to_all | solution.py:1201
  197.9 38.8 %collective-permute-start.19 = (bf16[128,2048]{1,0:T(8,128)(2,1)S(1)}, bf16[128,2048]{1,0:T(8,128)(2,1)S(1)}, u32[]{:S(2)}, u32[]{:S(2)}) collective-permute-start(bf16[128,2048]{1,0:T(8,128)(2,1)S(1)} %copy-done.48), channel_id=1, source_target_pairs={{0,2},{1,3},{2,0},{3,1},{4,6},{5,7},{6,4},{7,5},{8,10},{9,11},{10,... | collective-permute-start | bytes 1572872 | tf_op jit(solution)/shard_map/ppermute | solution.py:865
  200.1 36.5 %collective-permute-start.20 = (bf16[128,2048]{1,0:T(8,128)(2,1)S(1)}, bf16[128,2048]{1,0:T(8,128)(2,1)S(1)}, u32[]{:S(2)}, u32[]{:S(2)}) collective-permute-start(bf16[128,2048]{1,0:T(8,128)(2,1)S(1)} %copy-done.47), channel_id=1, source_target_pairs={{0,3},{1,0},{2,1},{3,2},{4,7},{5,4},{6,5},{7,6},{8,11},{9,8},{10,9... | collective-permute-start | bytes 1572872 | tf_op jit(solution)/shard_map/ppermute | solution.py:865
  256.3 23.6 %all-to-all-start.4 = ((bf16[4,64,1024]{2,1,0:T(8,128)(2,1)}), bf16[4,64,1024]{2,1,0:T(8,128)(2,1)S(1)}, u32[]{:S(2)}, u32[]{:S(2)}) async-start(bf16[4,64,1024]{2,1,0:T(8,128)(2,1)} %bitcast.29), calls=%async_computation.4 | async-start | bytes 1048576 | tf_op jit(solution)/shard_map/all_to_all | solution.py:873
  259.8 20.0 %collective-permute-start.24 = (bf16[256,1024]{1,0:T(8,128)(2,1)}, bf16[256,1024]{1,0:T(8,128)(2,1)S(1)}, u32[]{:S(2)}, u32[]{:S(2)}) collective-permute-start(bf16[256,1024]{1,0:T(8,128)(2,1)} %get-tuple-element.380), channel_id=1, source_target_pairs={{0,8},{4,12},{8,0},{12,4},{16,24},{20,28},{24,16},{28,20},{1,9},{5... | collective-permute-start | bytes 1572872 | tf_op jit(solution)/shard_map/ppermute | solution.py:860
  260.4 19.5 %collective-permute-start.25 = (bf16[256,1024]{1,0:T(8,128)(2,1)}, bf16[256,1024]{1,0:T(8,128)(2,1)S(1)}, u32[]{:S(2)}, u32[]{:S(2)}) collective-permute-start(bf16[256,1024]{1,0:T(8,128)(2,1)} %get-tuple-element.381), channel_id=1, source_target_pairs={{0,16},{4,20},{8,24},{12,28},{16,0},{20,4},{24,8},{28,12},{1,17},{... | collective-permute-start | bytes 1572872 | tf_op jit(solution)/shard_map/ppermute | solution.py:860
  280.8 57.1 %all-to-all-start.5 = ((bf16[4,128,2048]{2,1,0:T(8,128)(2,1)}), bf16[4,128,2048]{2,1,0:T(8,128)(2,1)S(1)}, u32[]{:S(2)}, u32[]{:S(2)}) async-start(bf16[4,128,2048]{2,1,0:T(8,128)(2,1)} %bitcast.51), calls=%async_computation.5 | async-start | bytes 4194304 | tf_op jit(solution)/shard_map/all_to_all | solution.py:873
  299.1 17.3 %collective-permute-start.29 = (bf16[304,1024]{1,0:T(8,128)(2,1)}, bf16[304,1024]{1,0:T(8,128)(2,1)}, u32[]{:S(2)}, u32[]{:S(2)}) collective-permute-start(bf16[304,1024]{1,0:T(8,128)(2,1)} %get-tuple-element.420), channel_id=1, source_target_pairs={{0,8},{4,12},{8,0},{12,4},{16,24},{20,28},{24,16},{28,20},{1,9},{5... | collective-permute-start | bytes 1867784 | tf_op jit(solution)/shard_map/ppermute | solution.py:860
  300.6 28.7 %collective-permute-start.30 = (bf16[304,1024]{1,0:T(8,128)(2,1)}, bf16[304,1024]{1,0:T(8,128)(2,1)}, u32[]{:S(2)}, u32[]{:S(2)}) collective-permute-start(bf16[304,1024]{1,0:T(8,128)(2,1)} %get-tuple-element.421), channel_id=1, source_target_pairs={{0,16},{4,20},{8,24},{12,28},{16,0},{20,4},{24,8},{28,12},{1,17},{... | collective-permute-start | bytes 1867784 | tf_op jit(solution)/shard_map/ppermute | solution.py:860
  301.1 28.2 %collective-permute-start.31 = (bf16[304,1024]{1,0:T(8,128)(2,1)}, bf16[304,1024]{1,0:T(8,128)(2,1)}, u32[]{:S(2)}, u32[]{:S(2)}) collective-permute-start(bf16[304,1024]{1,0:T(8,128)(2,1)} %get-tuple-element.422), channel_id=1, source_target_pairs={{0,24},{4,28},{8,16},{12,20},{16,8},{20,12},{24,0},{28,4},{1,25},{... | collective-permute-start | bytes 1867784 | tf_op jit(solution)/shard_map/ppermute | solution.py:860
  (66 other events, 577.9 us)
